TPU v7x, 32 devices: a whole 2x2x4 slice. The times are simulated.
32 devices in a mesh: kpt: 4 (over y, x), pw: 8 (over z, core).
Axes of the slice: x: 2, y: 2, z: 4, core: 2. Of those that a mesh axis runs over, the one named last changes fastest.
Arguments:
- band_coeffs: float32 [4, 2, 2, 393216], P('kpt', None, None, 'pw'), may hold values from -6 to 6
- miller_third: int32 [4, 393216], P('kpt', 'pw'), may hold values from -64 to 63, as said below
- column_slot: int32 [4, 393216], P('kpt', 'pw'), may hold values from 0 to 383, as said below
- column_map: int32 [3072], P('pw'), may hold values from 0 to 16383, as said below
- kpoint_counts: int32 [4], replicated, may hold values from 1 to 12
Outputs:
- density: float32 [256, 128, 128], P('pw', 'kpt')
- hartree: float32 [256, 128, 128], P('pw', 'kpt')
Inputs may be any that keep to these rules, and one draw needn't show every extreme that they name: `miller_third`: on each device of pw and for each k-point, the 49152 entries pair with column_slot so that every pair of a slot and a z index occurs exactly once. `column_slot`: the slot of each coefficient among the 384 columns of the device of pw that holds it. `column_map`: distinct flattened indices x * 128 + y of the 3072 columns with the smallest (s_x / 128)^2 + (s_y / 128)^2 in signed frequencies, ties at the rim taken at random; entries j * 384 to (j + 1) * 384 - 1 are the columns of device j of pw, assigned at random; the same for every k-point.
All inputs are finite; a program needn't handle non-finite values.
Results may differ from a plain program's by a relative error of at most 0.0003.
Values sent between devices are 32-bit elements; how exact they have to be, the bound alone decides.
No kernel may reach another device: no remote copies, remote signals or barrier semaphores. Data moves between devices by JAX's collectives and lax.ppermute only.
A program may use at most 128 MiB of HBM per device.

v0:
```python
import math

import jax
import jax.numpy as jnp
from jax import lax
from jax.sharding import PartitionSpec as P

NX = 128
NY = 128
NZ = 256


SPACING = 0.25


def contract(pattern, former, latter):
    return jnp.einsum(
        pattern, former, latter, precision=lax.Precision.HIGHEST, preferred_element_type=jnp.float32
    )


def phase_tables(first_index, second_index, length):
    product = first_index[:, None] * second_index[None, :] % length
    angle = product.astype(jnp.float32) * (2.0 * math.pi / length)
    return (jnp.cos(angle), jnp.sin(angle))


def signed_freq(values, length):
    return jnp.where(values >= length // 2, values - length, values)


def coulomb(freq_z, freq_x, freq_y):
    wave_z = freq_z.astype(jnp.float32) / (NZ * SPACING)
    wave_x = freq_x.astype(jnp.float32) / (NX * SPACING)
    wave_y = freq_y.astype(jnp.float32) / (NY * SPACING)
    squared = (2.0 * math.pi) ** 2 * (wave_z * wave_z + wave_x * wave_x + wave_y * wave_y)
    anchor = (freq_z == 0) & (freq_x == 0) & (freq_y == 0)
    return jnp.where(anchor, 0.0, 4.0 * math.pi / jnp.where(anchor, 1.0, squared))


def poisson_columns(real_part, imag_part, freq_x, freq_y):
    length = real_part.shape[0]
    steps_z = jnp.arange(length, dtype=jnp.int32)
    cos_z, sin_z = phase_tables(steps_z, steps_z, length)
    spec_real = contract("zk,km->zm", cos_z, real_part) + contract("zk,km->zm", sin_z, imag_part)
    spec_imag = contract("zk,km->zm", cos_z, imag_part) - contract("zk,km->zm", sin_z, real_part)
    kernel = coulomb(signed_freq(steps_z, length)[:, None], freq_x[None, :], freq_y[None, :]) / (
        NX * NY * NZ
    )
    spec_real = spec_real * kernel
    spec_imag = spec_imag * kernel
    back_real = contract("zk,km->zm", cos_z, spec_real) - contract("zk,km->zm", sin_z, spec_imag)
    back_imag = contract("zk,km->zm", sin_z, spec_real) + contract("zk,km->zm", cos_z, spec_imag)
    return (back_real, back_imag)


def forward_planes(field):
    steps_x = jnp.arange(NX, dtype=jnp.int32)
    steps_y = jnp.arange(NY, dtype=jnp.int32)
    cos_y, sin_y = phase_tables(steps_y, steps_y, NY)
    cos_x, sin_x = phase_tables(steps_x, steps_x, NX)
    half_real = contract("pxy,ky->pxk", field, cos_y)
    half_imag = -contract("pxy,ky->pxk", field, sin_y)
    spec_real = contract("kx,pxy->pky", cos_x, half_real) + contract(
        "kx,pxy->pky", sin_x, half_imag
    )
    spec_imag = contract("kx,pxy->pky", cos_x, half_imag) - contract(
        "kx,pxy->pky", sin_x, half_real
    )
    return (spec_real, spec_imag)


def local(band_coeffs, miller_third, column_slot, column_map, kpoint_counts):
    pw_count = lax.axis_size("pw")
    kpt_count = lax.axis_size("kpt")
    pw_index = lax.axis_index("pw")
    kpt_index = lax.axis_index("kpt")
    col_dev = column_map.shape[0]
    ng_dev = column_slot.shape[1]
    band_count = band_coeffs.shape[1]
    z_width = ng_dev // col_dev
    planes = NZ // pw_count
    x_block = NX // kpt_count
    col_total = pw_count * col_dev
    steps_y = jnp.arange(NY, dtype=jnp.int32)
    steps_x = jnp.arange(NX, dtype=jnp.int32)
    cos_y, sin_y = phase_tables(steps_y, steps_y, NY)
    cos_x, sin_x = phase_tables(steps_x, steps_x, NX)
    all_columns = lax.all_gather(column_map, "pw", axis=0, tiled=True)
    position = (miller_third[0] + z_width // 2) * col_dev + column_slot[0]
    source_of = (
        jnp.zeros((ng_dev,), jnp.int32).at[position].set(jnp.arange(ng_dev, dtype=jnp.int32))
    )
    coeff_rows = band_coeffs[0].reshape(band_count * 2, ng_dev).T
    packed = jnp.take(coeff_rows, source_of, axis=0)
    packed = (
        packed.reshape(z_width, col_dev, band_count, 2)
        .transpose(0, 2, 3, 1)
        .reshape(z_width, band_count * 2 * col_dev)
    )
    cos_z, sin_z = phase_tables(
        jnp.arange(NZ, dtype=jnp.int32), jnp.arange(z_width, dtype=jnp.int32) - z_width // 2, NZ
    )
    by_cos = contract("zj,jc->zc", cos_z, packed).reshape(NZ, band_count, 2, col_dev)
    by_sin = contract("zj,jc->zc", sin_z, packed).reshape(NZ, band_count, 2, col_dev)
    pencil = jnp.stack(
        (by_cos[:, :, 0] - by_sin[:, :, 1], by_sin[:, :, 0] + by_cos[:, :, 1]), axis=2
    )
    pencil = pencil.reshape(NZ, band_count * 2 * col_dev)
    arrived = lax.all_to_all(pencil, "pw", split_axis=0, concat_axis=1, tiled=True)
    arrived = arrived.reshape(planes, pw_count, band_count, 2, col_dev).transpose(2, 1, 4, 3, 0)
    arrived = arrived.reshape(band_count, col_total, 2 * planes)
    arrived = jnp.concatenate(
        (arrived, jnp.zeros((band_count, 1, 2 * planes), jnp.float32)), axis=1
    )
    cell_source = (
        jnp.full((NX * NY,), col_total, jnp.int32)
        .at[all_columns]
        .set(jnp.arange(col_total, dtype=jnp.int32))
    )

    def add_band(band, running):
        one_band = lax.dynamic_index_in_dim(arrived, band, 0, keepdims=False)
        placed = jnp.take(one_band, cell_source, axis=0)
        placed = placed.reshape(NX, NY, 2, planes).transpose(2, 3, 0, 1)
        grid_real = placed[0]
        grid_imag = placed[1]
        mixed_real = contract("pxm,ym->pxy", grid_real, cos_y) - contract(
            "pxm,ym->pxy", grid_imag, sin_y
        )
        mixed_imag = contract("pxm,ym->pxy", grid_real, sin_y) + contract(
            "pxm,ym->pxy", grid_imag, cos_y
        )
        wave_real = contract("xm,pmy->pxy", cos_x, mixed_real) - contract(
            "xm,pmy->pxy", sin_x, mixed_imag
        )
        wave_imag = contract("xm,pmy->pxy", sin_x, mixed_real) + contract(
            "xm,pmy->pxy", cos_x, mixed_imag
        )
        return running + wave_real * wave_real + wave_imag * wave_imag

    squares_sum = lax.fori_loop(0, band_count, add_band, jnp.zeros((planes, NX, NY), jnp.float32))
    weight = (
        2.0
        * kpoint_counts[kpt_index].astype(jnp.float32)
        / jnp.sum(kpoint_counts).astype(jnp.float32)
    )
    weight = weight / (ng_dev * pw_count)
    partial_value = weight * squares_sum
    total_density = lax.psum(partial_value, "kpt")
    density = lax.dynamic_slice_in_dim(total_density, kpt_index * x_block, x_block, 1)
    spec_real, spec_imag = forward_planes(total_density)
    rows_pw = NX // pw_count
    pencil_real, pencil_imag = (
        lax.all_to_all(spec_real, "pw", split_axis=1, concat_axis=0, tiled=True),
        lax.all_to_all(spec_imag, "pw", split_axis=1, concat_axis=0, tiled=True),
    )
    local_x = pw_index * rows_pw + jnp.arange(rows_pw, dtype=jnp.int32)
    freq_x = jnp.repeat(signed_freq(local_x, NX), NY)
    freq_y = jnp.tile(signed_freq(steps_y, NY), rows_pw)
    back_real, back_imag = poisson_columns(
        pencil_real.reshape(NZ, rows_pw * NY), pencil_imag.reshape(NZ, rows_pw * NY), freq_x, freq_y
    )
    plane_real, plane_imag = (
        lax.all_to_all(
            back_real.reshape(NZ, rows_pw, NY), "pw", split_axis=0, concat_axis=1, tiled=True
        ),
        lax.all_to_all(
            back_imag.reshape(NZ, rows_pw, NY), "pw", split_axis=0, concat_axis=1, tiled=True
        ),
    )
    own_rows = kpt_index * x_block + jnp.arange(x_block, dtype=jnp.int32)
    cos_rows, sin_rows = phase_tables(own_rows, steps_x, NX)
    rows_real = contract("xk,pky->pxy", cos_rows, plane_real) - contract(
        "xk,pky->pxy", sin_rows, plane_imag
    )
    rows_imag = contract("xk,pky->pxy", sin_rows, plane_real) + contract(
        "xk,pky->pxy", cos_rows, plane_imag
    )
    hartree = contract("pxk,yk->pxy", rows_real, cos_y) - contract("pxk,yk->pxy", rows_imag, sin_y)
    return (density, hartree)


def solution(mesh):
    return jax.shard_map(
        local,
        mesh=mesh,
        in_specs=(P("kpt", None, None, "pw"), P("kpt", "pw"), P("kpt", "pw"), P("pw"), P()),
        out_specs=(P("pw", "kpt", None), P("pw", "kpt", None)),
        check_vma=False,
    )
```

profile of v0, /device:TPU:0, one launch (start us, length us, event | category | flops | bytes accessed | tf_op | source)
XLA Modules:
  0.0 1010.1 jit_solution(5045536480382023026)
XLA Ops:
  8.6 179.9 %scatter_custom_fusion.1 = s32[49152]{0:T(1024)S(1)} fusion(s32[49152]{0:T(1024)S(1)} %bitcast.258, s32[49152]{0:T(1024)S(1)} %iota.57, s32[]{:T(128)} %constant.171.clone.1), kind=kCustom, calls=%fused_computation.148 | custom fusion | bytes 196612 | tf_op jit(solution)/shard_map/scatter | solution.py:92
  189.4 12.5 %copy.67 = f32[4,49152]{0,1:T(8,128)} copy(f32[4,49152]{1,0:T(4,128)S(1)} %reshape_squeeze.3) | data formatting | bytes 1572864 | tf_op jit(solution)/shard_map/reshape;squeeze | solution.py:94
  201.9 171.2 %gather_fusion.1 = f32[49152,4]{1,0:T(8,128)} fusion(f32[49152,4]{1,0:T(8,128)} %bitcast.238, s32[49152]{0:T(1024)S(1)} %fusion.103), kind=kCustom, calls=%fused_computation.1 | custom fusion | bytes 1769472 | tf_op jit(solution)/shard_map/jit(_take)/gather | solution.py:95
  373.1 13.8 %copy.68 = f32[49152,4]{0,1:T(4,128)S(1)} copy(f32[49152,4]{1,0:T(8,128)} %gather_fusion.1) | data formatting | bytes 1572864 | tf_op jit(solution)/shard_map/jit(_take)/gather | solution.py:95
  395.1 6.5 all-to-all-start
  404.3 40.9 %all-gather = s32[8,1,384]{2,1,0:T(1,128)S(1)} all-gather(s32[1,1,384]{2,1,0:T(1,128)S(1)} %reshape.256), channel_id=1, replica_groups=mesh['kpt'=4,'pw'=8] {'pw'}, dimensions={0}, use_global_device_ids=true | all-gather | bytes 13824 | tf_op jit(solution)/shard_map/all_gather | solution.py:89
  445.2 11.8 %scatter_custom_fusion = s32[16384]{0:T(1024)S(1)} fusion(s32[3072]{0:T(1024)S(1)} %compare_select_fusion.4, s32[3072]{0:T(1024)S(1)} %iota.55, s32[]{:T(128)} %constant.185.clone.1), kind=kCustom, calls=%fused_computation.172 | custom fusion | bytes 65540 | tf_op jit(solution)/shard_map/scatter | solution.py:119
  465.7 210.5 %while.16 = (s32[]{:T(128)}, f32[32,128,128]{1,2,0:T(8,128)}, s32[16384]{0:T(1024)S(1)}, f32[2,3073,64]{1,2,0:T(8,128)}, s32[]{:T(128)}, /*index=5*/s32[]{:T(128)}) while((s32[]{:T(128)}, f32[32,128,128]{1,2,0:T(8,128)}, s32[16384]{0:T(1024)S(1)}, f32[2,3073,64]{1,2,0:T(8,128)}, s32[]{:T(128)}, ...), condition=%wide.region_4.5_spmd.clone.clone, body=%wide.region_3.4_spmd.clone.clone.sunk | while | flops 6450216960 | bytes 83264592 | solution.py:142
  483.3 54.8 %gather_fusion = f32[16384,64]{1,0:T(8,128)} fusion(f32[3073,64]{1,0:T(8,128)S(1)} %bitcast.237, s32[16384]{0:T(1024)S(1)} %broadcast_clamp_fusion.2), kind=kCustom, calls=%fused_computation.clone.clone.1 | custom fusion | bytes 8454144 | tf_op jit(solution)/shard_map/while/body/eval_jaxpr/jit(_take)/gather | solution.py:124
  538.0 6.8 copy.127
  552.6 4.9 fusion.323
  561.8 5.0 fusion.319
  566.8 5.0 fusion.320
  571.8 6.7 bitcast_add_fusion.3
  580.3 54.8 %gather_fusion = f32[16384,64]{1,0:T(8,128)} fusion(f32[3073,64]{1,0:T(8,128)S(1)} %bitcast.237, s32[16384]{0:T(1024)S(1)} %broadcast_clamp_fusion.2), kind=kCustom, calls=%fused_computation.clone.clone.1 | custom fusion | bytes 8454144 | tf_op jit(solution)/shard_map/while/body/eval_jaxpr/jit(_take)/gather | solution.py:124
  635.1 6.8 copy.127
  649.6 4.9 fusion.323
  658.8 5.0 fusion.319
  663.8 5.0 fusion.320
  668.8 7.0 bitcast_add_fusion.3
  679.7 68.0 %all-reduce.3.cloned.1.call-done = f32[32,128,128]{2,1,0:T(8,128)} async-done(((f32[32,128,128]{2,1,0:T(8,128)}), f32[32,128,128]{2,1,0:T(8,128)}) %all-reduce.3.cloned.1.call-update) | async-done | bytes 2097168 | tf_op jit(solution)/shard_map/psum | solution.py:150
  755.9 5.0 subtract_bitcast_fusion
  764.0 4.8 all-to-all-start.2
  772.6 5.0 add_bitcast_fusion
  780.7 37.3 %all-to-all-done.2 = f32[32,128,128]{2,0,1:T(8,128)} async-done(((f32[32,128,128]{2,0,1:T(8,128)}), f32[32,128,128]{2,0,1:T(8,128)}, u32[]{:S(2)}, u32[]{:S(2)}) %all-to-all-start.2) | async-done | bytes 2097184 | tf_op jit(solution)/shard_map/all_to_all | solution.py:156
  825.9 4.6 fusion.71
  830.5 40.0 %all-to-all-done.1 = f32[32,128,128]{2,0,1:T(8,128)S(1)} async-done(((f32[32,128,128]{2,0,1:T(8,128)}), f32[32,128,128]{2,0,1:T(8,128)S(1)}, u32[]{:S(2)}, u32[]{:S(2)}) %all-to-all-start.1) | async-done | bytes 2097184 | tf_op jit(solution)/shard_map/all_to_all | solution.py:155
  875.1 4.5 fusion.69
  891.2 4.5 all-to-all-start.3
  895.7 4.5 fusion.116
  904.9 39.9 %all-to-all-done.3 = f32[256,16,128]{2,1,0:T(8,128)} async-done(((f32[256,16,128]{2,1,0:T(8,128)}), f32[256,16,128]{2,1,0:T(8,128)}, u32[]{:S(2)}, u32[]{:S(2)}) %all-to-all-start.3) | async-done | bytes 2097184 | tf_op jit(solution)/shard_map/all_to_all | solution.py:165
  955.1 42.5 %all-to-all-done.4 = f32[256,16,128]{2,1,0:T(8,128)S(1)} async-done(((f32[256,16,128]{2,1,0:T(8,128)}), f32[256,16,128]{2,1,0:T(8,128)S(1)}, u32[]{:S(2)}, u32[]{:S(2)}) %all-to-all-start.4) | async-done | bytes 2097184 | tf_op jit(solution)/shard_map/all_to_all | solution.py:168
  (106 shorter events, 113.8 us)
Async XLA Ops:
  7.2 181.5 %copy-start.6 = (f32[1,2,2,49152]{3,2,1,0:T(2,128)S(1)}, f32[1,2,2,49152]{3,2,1,0:T(2,128)}, u32[]{:S(2)}) copy-start(f32[1,2,2,49152]{3,2,1,0:T(2,128)} %param.7) | copy-start | bytes 2359300
  395.1 6.5 copy-start.7
  395.1 6.5 copy-start.8
  395.1 62.0 %all-to-all-start = ((f32[8,32,1536]{2,1,0:T(8,128)}), f32[8,32,1536]{2,1,0:T(8,128)S(1)}, u32[]{:S(2)}, u32[]{:S(2)}) async-start(f32[8,32,1536]{2,1,0:T(8,128)} %all_to_all.60), calls=%async_computation | async-start | bytes 3145728 | tf_op jit(solution)/shard_map/all_to_all | solution.py:110
  401.5 346.2 %all-reduce.3.cloned.1.call-start = ((), (), s32[]{:S(2)}) async-start(), calls=%async_computation.5 | async-start | bytes 4194304 | tf_op jit(solution)/shard_map/psum | solution.py:150
  751.5 2.2 copy-start
  751.6 2.3 copy-start.1
  764.0 54.0 %all-to-all-start.2 = ((f32[32,128,128]{2,0,1:T(8,128)}), f32[32,128,128]{2,0,1:T(8,128)}, u32[]{:S(2)}, u32[]{:S(2)}) async-start(f32[32,128,128]{2,0,1:T(8,128)} %copy.82), calls=%async_computation.2 | async-start | bytes 4194304 | tf_op jit(solution)/shard_map/all_to_all | solution.py:156
  818.0 52.6 %all-to-all-start.1 = ((f32[32,128,128]{2,0,1:T(8,128)}), f32[32,128,128]{2,0,1:T(8,128)S(1)}, u32[]{:S(2)}, u32[]{:S(2)}) async-start(f32[32,128,128]{2,0,1:T(8,128)} %copy.77), calls=%async_computation.1 | async-start | bytes 4194304 | tf_op jit(solution)/shard_map/all_to_all | solution.py:155
  824.6 1.3 copy-start.2
  871.7 3.3 copy-start.5
  875.0 4.5 copy-start.3
  883.7 2.9 copy-start.4
  891.2 53.6 %all-to-all-start.3 = ((f32[256,16,128]{2,1,0:T(8,128)}), f32[256,16,128]{2,1,0:T(8,128)}, u32[]{:S(2)}, u32[]{:S(2)}) async-start(f32[256,16,128]{2,1,0:T(8,128)} %bitcast.249), calls=%async_computation.3 | async-start | bytes 4194304 | tf_op jit(solution)/shard_map/all_to_all | solution.py:165
  944.8 52.8 %all-to-all-start.4 = ((f32[256,16,128]{2,1,0:T(8,128)}), f32[256,16,128]{2,1,0:T(8,128)S(1)}, u32[]{:S(2)}, u32[]{:S(2)}) async-start(f32[256,16,128]{2,1,0:T(8,128)} %bitcast.79), calls=%async_computation.4 | async-start | bytes 4194304 | tf_op jit(solution)/shard_map/all_to_all | solution.py:168
Sparse Core Ops, SparseCore 0:
  679.8 67.8 all-reduce.2
where the time goes:
time: 1020 us; the launch traced here: 1010 us
  local copies, waits for them, and re-layouts  557 us (55%)
  waiting for transfers between devices  228 us (22%)
  matrix products  124 us (12%)
  blocking collectives  40.9 us (4%)
  starting transfers between devices  23.3 us (2%)
  loops' own time  16.3 us (2%)
  between operations  16.2 us (2%)
    gather x2, local copies, waits for them, and re-layouts, local(): packed = jnp.take(coeff_rows, source_of, axis=0)  185 us
    scatter x1, local copies, waits for them, and re-layouts, local(): jnp.zeros((ng_dev,), jnp.int32).at[position]  180 us
    dot_general x38, matrix products, contract(): jnp.einsum(pattern, former, latter, precision=lax.Precision.HIGHEST, pref...  124 us
    gather x4, local copies, waits for them, and re-layouts, add_band(): placed = jnp.take(one_band, cell_source, axis=0)  123 us
    psum x1, waiting for transfers between devices, local(): total_density = lax.psum(partial_value, 'kpt')  68 us
    all_to_all x1, waiting for transfers between devices, local(): lax.all_to_all(back_imag.reshape(NZ, rows_pw, NY), 'pw', split_axis=0, co...  42.5 us
    all_gather x1, blocking collectives, local(): all_columns = lax.all_gather(column_map, 'pw', axis=0, tiled=True)  40.9 us
    all_to_all x1, waiting for transfers between devices, local(): lax.all_to_all(spec_real, 'pw', split_axis=1, concat_axis=0, tiled=True)  40 us
  transfers between devices with their start and end apart: 6, of which 5 were waited for; matrix products, arithmetic and copies ran while one was open for 5% of the time, Pallas kernels for 0%

commit v1 on v0

--- a/solution.py
+++ b/solution.py
@@ -1,8 +1,12 @@
+import functools
 import math
 
 import jax
 import jax.numpy as jnp
+import numpy as np
 from jax import lax
+from jax.experimental import pallas as pl
+from jax.experimental.pallas import tpu as pltpu
 from jax.sharding import PartitionSpec as P
 
 NX = 128
@@ -70,7 +74,7 @@
     return (spec_real, spec_imag)
 
 
-def local(band_coeffs, miller_third, column_slot, column_map, kpoint_counts):
+def local_general(band_coeffs, miller_third, column_slot, column_map, kpoint_counts):
     pw_count = lax.axis_size("pw")
     kpt_count = lax.axis_size("kpt")
     pw_index = lax.axis_index("pw")
@@ -181,9 +185,463 @@
     return (density, hartree)
 
 
+LANES = 128
+HALF = 64
+VMEM_LIMIT = 56 * 1024 * 1024
+NN = (((1,), (0,)), ((), ()))
+NT = (((1,), (1,)), ((), ()))
+TN = (((0,), (0,)), ((), ()))
+
+
+def pieces(value):
+    high = value.astype(jnp.bfloat16)
+    low = (value - high.astype(jnp.float32)).astype(jnp.bfloat16)
+    return high, low
+
+
+def mul(former, latter, dims):
+    return lax.dot_general(former, latter, dims, preferred_element_type=jnp.float32)
+
+
+def mul3(former, latter, dims):
+    return (
+        mul(former[0], latter[0], dims)
+        + mul(former[0], latter[1], dims)
+        + mul(former[1], latter[0], dims)
+    )
+
+
+def table(values):
+    high = values.astype(np.float32).astype(jnp.bfloat16)
+    low = (values - high.astype(np.float64)).astype(np.float32).astype(jnp.bfloat16)
+    return jnp.asarray(np.stack((high, low)))
+
+
+def angles(former, latter, length):
+    return np.outer(former, latter) % length * (2.0 * np.pi / length)
+
+
+def tables(kpts, pws, planes):
+    count = kpts * pws
+    low_freq = np.arange(HALF) - HALF // 2
+    grid_x, grid_y, grid_z = np.arange(NX), np.arange(NY), np.arange(NZ)
+    own_y = np.arange(HALF)
+
+    device = np.arange(count)
+    plane_of = (
+        (device % pws)[:, None] * (NZ // pws)
+        + (device // pws)[:, None] * planes
+        + np.arange(planes)[None, :]
+    )
+    return_table = {}
+
+    def pencil(z_width):
+        angle = angles(plane_of.ravel(), np.arange(z_width) - z_width // 2, NZ)
+        cos, sin = (
+            part.reshape(count, 1, planes, z_width) for part in (np.cos(angle), np.sin(angle))
+        )
+        real = np.concatenate((cos, -sin), axis=3)
+        imag = np.concatenate((sin, cos), axis=3)
+        return np.concatenate((real, imag), axis=1).reshape(-1, 2 * z_width)
+
+    return_table["pencil"] = pencil
+
+    angle = angles(low_freq, grid_y, NY)
+    cos, sin = np.cos(angle), np.sin(angle)
+    return_table["wave_y"] = np.block([[cos, sin], [-sin, cos]])
+
+    angle = angles(grid_x, low_freq, NX)
+    cos, sin = np.cos(angle), np.sin(angle)
+    return_table["wave_x"] = np.block([[cos, -sin], [sin, cos]])
+
+    angle = angles(own_y, grid_y, NY)
+    cos, sin = np.cos(angle), np.sin(angle)
+    return_table["forth_y"] = np.stack((cos, -sin), axis=1).reshape(2 * HALF, NY)
+    twice = np.where(own_y == 0, 1.0, 2.0)[:, None]
+    return_table["back_y"] = np.stack((twice * cos, -twice * sin), axis=1).reshape(2 * HALF, NY)
+
+    angle = angles(grid_z, plane_of.ravel(), NZ)
+    return_table["forth_z"] = np.concatenate((np.cos(angle), np.sin(angle)), axis=0)
+    own = NZ // pws
+    merged = own // 8
+    order = (
+        np.arange(pws)[None, :, None] * own
+        + np.arange(8)[None, None, :] * merged
+        + np.arange(merged)[:, None, None]
+    )
+    angle = angles(order.ravel(), grid_z, NZ)
+    return_table["back_z"] = np.concatenate((np.cos(angle), np.sin(angle)), axis=0)
+
+    angle = angles(grid_x, grid_x, NX)
+    return_table["both_x"] = np.concatenate((np.cos(angle), np.sin(angle)), axis=1)
+    return return_table
+
+
+def pack_kernel(step_width, coeff_ref, miller_ref, slot_ref, pencil_ref, out_ref, total):
+    step = pl.program_id(0)
+    slots = out_ref.shape[1]
+    width = pencil_ref.shape[2] // 2
+    chunk = coeff_ref.shape[3]
+
+    @pl.when(step == 0)
+    def _():
+        total[...] = jnp.zeros_like(total)
+
+    one = jnp.ones((LANES, step_width), jnp.bfloat16)
+    zero = jnp.zeros((LANES, step_width), jnp.bfloat16)
+    steps = lax.broadcasted_iota(jnp.int32, (LANES, step_width), 0)
+    steps = steps.astype(jnp.float32).astype(jnp.bfloat16)
+    for start in range(0, chunk, step_width):
+        part = pl.ds(start, step_width)
+        slot = slot_ref[:, part].astype(jnp.float32)
+        depth = (miller_ref[:, part] + width // 2).astype(jnp.float32).astype(jnp.bfloat16)
+        chosen = jnp.concatenate(
+            [
+                jnp.where((slot - first).astype(jnp.bfloat16) == steps, one, zero)
+                for first in range(0, slots, LANES)
+            ],
+            axis=0,
+        )
+        here = depth == steps
+        high, low = pieces(coeff_ref[0, 0, :, part])
+        spread = jnp.concatenate(
+            [jnp.where(here, piece[c : c + 1], zero) for piece in (high, low) for c in range(2)],
+            axis=0,
+        )
+        total[...] += mul(chosen, spread, NT)
+
+    @pl.when(step == pl.num_programs(0) - 1)
+    def _():
+        both = (
+            total[:, : 2 * width].astype(jnp.bfloat16),
+            total[:, 2 * width :].astype(jnp.bfloat16),
+        )
+        out_ref[...] = mul3((pencil_ref[0], pencil_ref[1]), both, NT)
+
+
+def pack_band(band, coeffs, miller, slot, pencil, slots):
+    total = miller.shape[1]
+    width = pencil.shape[2] // 2
+    chunk = 4096 if total % 4096 == 0 else total
+    return pl.pallas_call(
+        functools.partial(pack_kernel, 1024 if chunk % 1024 == 0 else chunk),
+        grid=(total // chunk,),
+        in_specs=[
+            pl.BlockSpec((1, 1, 2, chunk), lambda i: (0, band, 0, i)),
+            pl.BlockSpec((1, chunk), lambda i: (0, i)),
+            pl.BlockSpec((1, chunk), lambda i: (0, i)),
+            pl.BlockSpec(pencil.shape, lambda i: (0, 0, 0)),
+        ],
+        out_specs=pl.BlockSpec((pencil.shape[1], slots), lambda i: (0, 0)),
+        out_shape=jax.ShapeDtypeStruct((pencil.shape[1], slots), jnp.float32),
+        scratch_shapes=[pltpu.VMEM((slots, 4 * width), jnp.float32)],
+        compiler_params=pltpu.CompilerParams(vmem_limit_bytes=VMEM_LIMIT),
+        cost_estimate=pl.CostEstimate(
+            flops=2 * total * slots * 4 * width, bytes_accessed=16 * total, transcendentals=0
+        ),
+        name="pack_band",
+    )(coeffs, miller, slot, pencil)
+
+
+def wave_kernel(kpts, has_former, is_last, *refs):
+    weight_ref, came_ref, column_ref, wave_y_ref, wave_x_ref, forth_ref = refs[:6]
+    rest = list(refs[6:])
+    former_ref = rest.pop(0) if has_former else None
+    density_ref = rest.pop(0)
+    send_ref = rest.pop(0) if is_last else None
+    values, grid = rest
+    planes = density_ref.shape[1]
+    slots = came_ref.shape[2]
+    pws = came_ref.shape[0] // kpts
+    rows = kpts * 2 * planes
+
+    for j in range(pws):
+        block = jnp.concatenate([came_ref[k * pws + j] for k in range(kpts)], axis=0)
+        high, low = pieces(block)
+        values[0:rows, pl.ds(j * slots, slots)] = high
+        values[rows : 2 * rows, pl.ds(j * slots, slots)] = low
+
+    column = column_ref[...]
+    cell = ((column // NY + NX // 2) % NX - HALF // 2) * HALF
+    cell = cell + (column % NY + NY // 2) % NY - HALF // 2
+    cell = cell.astype(jnp.float32)
+    total = cell.shape[1]
+    tile = 4 * HALF
+    steps = lax.broadcasted_iota(jnp.int32, (tile, total), 0).astype(jnp.float32)
+    steps = steps.astype(jnp.bfloat16)
+    one = jnp.ones((tile, total), jnp.bfloat16)
+    zero = jnp.zeros((tile, total), jnp.bfloat16)
+    left = lax.broadcasted_iota(jnp.int32, (kpts * planes, LANES), 1) < HALF
+
+    def place(t, unused):
+        near = (cell - (t * tile).astype(jnp.float32)).astype(jnp.bfloat16)
+        chosen = jnp.where(near == steps, one, zero)
+        found = mul(values[...], chosen, NT)
+        found = found[:rows] + found[rows:]
+        for h in range(2):
+            real, imag = (
+                jnp.concatenate(
+                    [
+                        found[(2 * k + c) * planes : (2 * k + c + 1) * planes, h * LANES : (h + 1) * LANES]
+                        for k in range(kpts)
+                    ],
+                    axis=0,
+                )
+                for c in range(2)
+            )
+            even = jnp.where(left, real, pltpu.roll(imag, HALF, 1))
+            odd = jnp.where(left, pltpu.roll(real, HALF, 1), imag)
+            grid[pl.ds(t * 4 + 2 * h, kpts * planes, stride=HALF), :] = even
+            grid[pl.ds(t * 4 + 2 * h + 1, kpts * planes, stride=HALF), :] = odd
+        return unused
+
+    lax.fori_loop(0, HALF // 4, place, 0)
+
+    first_row = lax.broadcasted_iota(jnp.int32, (2 * HALF, NX), 0) == 0
+
+    def transform(p, unused):
+        lines = jnp.concatenate(
+            [
+                grid[pl.ds(pl.multiple_of((k * planes + p) * HALF, HALF), HALF), :]
+                for k in range(kpts)
+            ],
+            axis=0,
+        )
+        mixed = mul3(pieces(lines), (wave_y_ref[0], wave_y_ref[1]), NN)
+        mixed = jnp.concatenate(
+            [
+                jnp.concatenate(
+                    [mixed[k * HALF : (k + 1) * HALF, c * NY : (c + 1) * NY] for k in range(kpts)],
+                    axis=1,
+                )
+                for c in range(2)
+            ],
+            axis=0,
+        )
+        wave = mul3((wave_x_ref[0], wave_x_ref[1]), pieces(mixed), NN)
+        square = wave[:NX] * wave[:NX] + wave[NX:] * wave[NX:]
+        density = weight_ref[0] * square[:, :NY]
+        for k in range(1, kpts):
+            density = density + weight_ref[k] * square[:, k * NY : (k + 1) * NY]
+        blocks = density_ref.shape[0]
+        block = NX // blocks
+        if has_former:
+            density = density + jnp.concatenate([former_ref[a, p] for a in range(blocks)], axis=0)
+        for a in range(blocks):
+            density_ref[a, p] = density[a * block : (a + 1) * block]
+        if is_last:
+            level = jnp.mean(density[:8], axis=(0, 1), keepdims=True)
+            half = mul3((forth_ref[0], forth_ref[1]), pieces(density - level), NT)
+            half = half + jnp.where(first_row, level * NY, 0.0)
+            send_ref[pl.ds(p, 2 * HALF, stride=planes), :] = half
+        return unused
+
+    lax.fori_loop(0, planes, transform, 0)
+
+
+def wave_band(kpts, weight, came, column, wave_y, wave_x, forth, former, is_last):
+    planes = came.shape[1] // 2
+    block = NX // kpts
+    vmem = pl.BlockSpec(memory_space=pltpu.VMEM)
+    operands = [weight, came, column, wave_y, wave_x, forth]
+    if former is not None:
+        operands.append(former)
+    out_shape = [jax.ShapeDtypeStruct((kpts, planes, block, NY), jnp.float32)]
+    if is_last:
+        out_shape.append(jax.ShapeDtypeStruct((2 * HALF * planes, NX), jnp.float32))
+    total = column.shape[1]
+    rows = kpts * 2 * planes
+    return pl.pallas_call(
+        functools.partial(wave_kernel, kpts, former is not None, is_last),
+        in_specs=[pl.BlockSpec(memory_space=pltpu.SMEM)] + [vmem] * (len(operands) - 1),
+        out_specs=[vmem] * len(out_shape),
+        out_shape=out_shape,
+        scratch_shapes=[
+            pltpu.VMEM((2 * rows, total), jnp.bfloat16),
+            pltpu.VMEM((kpts * planes * HALF, LANES), jnp.float32),
+        ],
+        compiler_params=pltpu.CompilerParams(vmem_limit_bytes=VMEM_LIMIT),
+        cost_estimate=pl.CostEstimate(
+            flops=4 * rows * total * HALF * HALF, bytes_accessed=4 * came.size, transcendentals=0
+        ),
+        name="wave_band",
+    )(*operands)
+
+
+def poisson_kernel(pws, first_ref, came_ref, forth_ref, back_ref, both_x_ref, send_ref):
+    count, parts, planes, unused = came_ref.shape
+    pairs = parts // 2
+    forth = (forth_ref[0], forth_ref[1])
+    back = (back_ref[0], back_ref[1])
+    both_x = (both_x_ref[0], both_x_ref[1])
+
+    fields = [came_ref[:, i].reshape(NZ, NX) for i in range(parts)]
+    level = jnp.mean(fields[0], axis=(0, 1), keepdims=True)
+    fields[0] = fields[0] - jnp.where(first_ref[0] == 0, level, 0.0)
+    field = jnp.concatenate(fields, axis=1)
+    turned = mul3(forth, pieces(field), NN)
+
+    def part(array, half, i):
+        return array[half * NZ : (half + 1) * NZ, i * NX : (i + 1) * NX]
+
+    lines = []
+    for q in range(pairs):
+        lines.append(part(turned, 0, 2 * q) + part(turned, 1, 2 * q + 1))
+        lines.append(part(turned, 0, 2 * q + 1) - part(turned, 1, 2 * q))
+    spectrum = mul3(pieces(jnp.concatenate(lines, axis=0)), both_x, NN)
+
+    step_z = lax.broadcasted_iota(jnp.int32, (NZ, NX), 0)
+    step_x = lax.broadcasted_iota(jnp.int32, (NZ, NX), 1)
+    lines = []
+    for q in range(pairs):
+        real = spectrum[2 * q * NZ : (2 * q + 1) * NZ]
+        imag = spectrum[(2 * q + 1) * NZ : (2 * q + 2) * NZ]
+        freq_y = jnp.full((NZ, NX), first_ref[0] + q, jnp.int32)
+        kernel = coulomb(signed_freq(step_z, NZ), signed_freq(step_x, NX), freq_y)
+        kernel = kernel * (1.0 / (NX * NY * NZ))
+        lines.append((real[:, :NX] + imag[:, NX:]) * kernel)
+        lines.append((imag[:, :NX] - real[:, NX:]) * kernel)
+    turned = mul3(pieces(jnp.concatenate(lines, axis=0)), both_x, NN)
+    lines = []
+    for q in range(pairs):
+        real = turned[2 * q * NZ : (2 * q + 1) * NZ]
+        imag = turned[(2 * q + 1) * NZ : (2 * q + 2) * NZ]
+        lines.append(real[:, :NX] - imag[:, NX:])
+        lines.append(real[:, NX:] + imag[:, :NX])
+    turned = mul3(back, pieces(jnp.concatenate(lines, axis=1)), NN)
+
+    kpts = count // pws
+    merged = NZ // pws // 8
+    block = NX // kpts
+    rows = pws * 8
+    lane = lax.broadcasted_iota(jnp.int32, (rows, LANES), 1) // block
+    for q in range(pairs):
+        real = part(turned, 0, 2 * q) - part(turned, 1, 2 * q + 1)
+        imag = part(turned, 0, 2 * q + 1) + part(turned, 1, 2 * q)
+        for c, value in enumerate((real, imag)):
+            for a in range(kpts):
+                packed = None
+                for m in range(merged):
+                    piece = value[m * rows : (m + 1) * rows]
+                    shift = (m - a) * block % LANES
+                    if shift:
+                        piece = pltpu.roll(piece, shift, 1)
+                    packed = piece if m == 0 else jnp.where(lane == m, piece, packed)
+                send_ref[a * pws : (a + 1) * pws, 2 * q + c] = packed.reshape(pws, 8, LANES)
+
+
+def poisson(pws, first, came, forth, back, both_x):
+    vmem = pl.BlockSpec(memory_space=pltpu.VMEM)
+    count, parts, unused, unused = came.shape
+    return pl.pallas_call(
+        functools.partial(poisson_kernel, pws),
+        in_specs=[pl.BlockSpec(memory_space=pltpu.SMEM)] + [vmem] * 4,
+        out_specs=vmem,
+        out_shape=jax.ShapeDtypeStruct((count, parts, 8, LANES), jnp.float32),
+        compiler_params=pltpu.CompilerParams(vmem_limit_bytes=VMEM_LIMIT),
+        name="poisson",
+    )(first, came, forth, back, both_x)
+
+
+def finish_kernel(came_ref, back_ref, out_ref):
+    back = (back_ref[0], back_ref[1])
+    planes, block, unused = out_ref.shape
+    merged = planes // 8
+    for h in range(8):
+        lines = came_ref[pl.ds(h, 2 * HALF, stride=8), :]
+        field = mul3(pieces(lines), back, TN)
+        out_ref[h * merged : (h + 1) * merged] = field.reshape(merged, block, NY)
+
+
+def finish(planes, block, came, back_y):
+    vmem = pl.BlockSpec(memory_space=pltpu.VMEM)
+    return pl.pallas_call(
+        finish_kernel,
+        in_specs=[vmem] * 2,
+        out_specs=vmem,
+        out_shape=jax.ShapeDtypeStruct((planes, block, NY), jnp.float32),
+        compiler_params=pltpu.CompilerParams(vmem_limit_bytes=VMEM_LIMIT),
+        name="finish",
+    )(came, back_y)
+
+
+def local_planes(band_coeffs, miller_third, column_slot, column_map, kpoint_counts):
+    pws = lax.axis_size("pw")
+    kpts = lax.axis_size("kpt")
+    count = pws * kpts
+    everyone = ("kpt", "pw")
+    slots = column_map.shape[0]
+    band_count = band_coeffs.shape[1]
+    z_width = column_slot.shape[1] // slots
+    planes = NZ // count
+    parts = 2 * HALF // count
+    made = tables(kpts, pws, planes)
+    pencil = table(made["pencil"](z_width))
+    wave_y, wave_x, forth_y, back_y, forth_z, back_z, both_x = (
+        table(made[name])
+        for name in ("wave_y", "wave_x", "forth_y", "back_y", "forth_z", "back_z", "both_x")
+    )
+
+    columns = lax.all_to_all(
+        jnp.broadcast_to(column_map[None, None, :], (pws, 1, slots)),
+        "pw",
+        split_axis=0,
+        concat_axis=0,
+        tiled=True,
+    ).reshape(1, pws * slots)
+    weight = (
+        2.0 * kpoint_counts.astype(jnp.float32) / jnp.sum(kpoint_counts).astype(jnp.float32)
+    ) / (column_slot.shape[1] * pws)
+
+    arrived = []
+    for band in range(band_count):
+        packed = pack_band(band, band_coeffs, miller_third, column_slot, pencil, slots)
+        arrived.append(
+            lax.all_to_all(
+                packed.reshape(count, 2 * planes, slots),
+                everyone,
+                split_axis=0,
+                concat_axis=0,
+                tiled=True,
+            )
+        )
+    former = None
+    for band in range(band_count):
+        is_last = band == band_count - 1
+        made_here = wave_band(
+            kpts, weight, arrived[band], columns, wave_y, wave_x, forth_y, former, is_last
+        )
+        former = made_here[0]
+    half = made_here[1].reshape(count, parts, planes, NX)
+    half = lax.all_to_all(half, everyone, split_axis=0, concat_axis=0, tiled=True)
+    density = lax.all_to_all(former, "kpt", split_axis=0, concat_axis=0, tiled=True)
+    density = density.reshape(NZ // pws, NX // kpts, NY)
+    device = lax.axis_index("kpt") * pws + lax.axis_index("pw")
+    first = (device * (parts // 2)).astype(jnp.int32).reshape(1)
+    back = poisson(pws, first, half, forth_z, back_z, both_x)
+    back = lax.all_to_all(back, everyone, split_axis=0, concat_axis=0, tiled=True)
+    back = back.reshape(count * parts * 8, LANES)
+    hartree = finish(NZ // pws, NX // kpts, back, back_y)
+    return (density, hartree)
+
+
+def fits_planes(kpts, pws):
+    count = kpts * pws
+    own = NZ // pws
+    return (
+        NZ % count == 0
+        and NZ // count == 8
+        and 2 * HALF % (2 * count) == 0
+        and NX % kpts == 0
+        and own % 8 == 0
+        and own // 8 * (NX // kpts) == LANES
+    )
+
+
 def solution(mesh):
+    chosen = local_planes if fits_planes(mesh.shape["kpt"], mesh.shape["pw"]) else local_general
     return jax.shard_map(
-        local,
+        chosen,
         mesh=mesh,
         in_specs=(P("kpt", None, None, "pw"), P("kpt", "pw"), P("kpt", "pw"), P("pw"), P()),
         out_specs=(P("pw", "kpt", None), P("pw", "kpt", None)),

time: 1020 us -> 175 us (0.17)
  local copies, waits for them, and re-layouts: 557 us -> 5.29 us
  waiting for transfers between devices: 228 us -> 19.5 us
  matrix products: 124 us -> 0 us
  Pallas kernels: 0 us -> 101 us
  blocking collectives: 40.9 us -> 22.3 us
  loops' own time: 16.3 us -> 0 us
  between operations: 16.2 us -> 1.35 us
    gather x6 -> x0, local copies, waits for them, and re-layouts: 308 us -> none  [the longest x2 185 us: local(): packed = jnp.take(coeff_rows, source_of, axis=0)]
    scatter x2 -> x0, local copies, waits for them, and re-layouts: 192 us -> none  [the longest x1 180 us: local(): jnp.zeros((ng_dev,), jnp.int32).at[position]]
    all_to_all x5, waiting for transfers between devices: 160 us -> 19.5 us  [the longest x1 16.4 us: local_planes(): lax.all_to_all(back, everyone, split_axis=0, concat_axis=0, tiled=True)]
    dot_general x38 -> x0, matrix products: 124 us -> none  [contract(): jnp.einsum(pattern, former, latter, precision=lax.Precision.HIGHEST, pref...]
    pallas_call x0 -> x6, Pallas kernels: none -> 101 us  [the longest x2 50.2 us: pack_band(): pl.pallas_call(functools.partial(pack_kernel, 1024 if chunk % 1024 == 0 e...]
    psum x1 -> x0, waiting for transfers between devices: 68 us -> none  [local(): total_density = lax.psum(partial_value, 'kpt')]
    all_gather x1 -> x0, blocking collectives: 40.9 us -> none  [local(): all_columns = lax.all_gather(column_map, 'pw', axis=0, tiled=True)]
    all_to_all x0 -> x1, blocking collectives: none -> 22.3 us  [local_planes(): lax.all_to_all(half, everyone, split_axis=0, concat_axis=0, tiled=True)]
  transfers between devices with their start and end apart: 6 -> 5, of which waited for: 5 -> 2; matrix products, arithmetic and copies ran while one was open for 5% -> 1% of each run, Pallas kernels for 0% -> 43%
where the time goes in v1:
time: 175 us
  Pallas kernels  101 us (58%)
  starting transfers between devices  24.3 us (14%)
  blocking collectives  22.3 us (13%)
  waiting for transfers between devices  19.5 us (11%)
  local copies, waits for them, and re-layouts  5.29 us (3%)
    pallas_call x2, Pallas kernels, pack_band(): pl.pallas_call(functools.partial(pack_kernel, 1024 if chunk % 1024 == 0 e...  50.2 us
    pallas_call x2, Pallas kernels, wave_band(): pl.pallas_call(functools.partial(wave_kernel, kpts, former is not None, i...  43.1 us
    all_to_all x1, blocking collectives, local_planes(): lax.all_to_all(half, everyone, split_axis=0, concat_axis=0, tiled=True)  22.3 us
    all_to_all x1, waiting for transfers between devices, local_planes(): lax.all_to_all(back, everyone, split_axis=0, concat_axis=0, tiled=True)  16.4 us
    all_to_all x2, starting transfers between devices, local_planes(): lax.all_to_all(packed.reshape(count, 2 * planes, slots), everyone, split_...  11.9 us
    all_to_all x1, starting transfers between devices, local_planes(): lax.all_to_all(jnp.broadcast_to(column_map[None, None, :], (pws, 1, slots...  6.33 us
    pallas_call x1, Pallas kernels, poisson(): pl.pallas_call(functools.partial(poisson_kernel, pws), in_specs=[pl.Block...  5.32 us
    unnamed x11, local copies, waits for them, and re-layouts  4 us
  transfers between devices with their start and end apart: 5, of which 2 were waited for; matrix products, arithmetic and copies ran while one was open for 1% of the time, Pallas kernels for 43%

profile of v1, /device:TPU:0, one launch (start us, length us, event | category | flops | bytes accessed | tf_op | source)
XLA Modules:
  0.0 174.7 jit_solution(5899946366972532936)
XLA Ops:
  0.6 1.3 broadcast_in_dim.2
  1.9 6.3 %all-to-all-start.1 = ((s32[8,1,384]{2,1,0:T(1,128)}), s32[8,1,384]{2,1,0:T(1,128)S(1)}, u32[]{:S(2)}, u32[]{:S(2)}) async-start(s32[8,1,384]{2,1,0:T(1,128)} %broadcast_in_dim.2), calls=%async_computation.1 | async-start | bytes 24576 | tf_op jit(solution)/shard_map/all_to_all | solution.py:585
  8.2 25.1 %pack_band.3 = f32[512,384]{1,0:T(8,128)} custom-call(f32[1,2,2,49152]{3,2,1,0:T(2,128)} %coeff_ref.3, s32[1,49152]{1,0:T(1,128)} %miller_ref.3, s32[1,49152]{1,0:T(1,128)} %slot_ref.3, bf16[2,512,256]{2,1,0:T(8,128)(2,1)} %constant.35.clone.pencil_ref), custom_call_target="tpu_custom_call" | custom-call | flops 19327352832 | bytes 786432 | tf_op jit(solution)/shard_map/pack_band/pallas_call | solution.py:326
  33.3 0.0 all-to-all-done.1
  33.3 0.0 copy-start.3
  33.3 0.6 copy-done.3
  33.9 6.1 %all-to-all-start.2 = ((f32[32,16,384]{2,1,0:T(8,128)}), f32[32,16,384]{2,1,0:T(8,128)S(1)}, u32[]{:S(2)}, u32[]{:S(2)}) async-start(f32[32,16,384]{2,1,0:T(8,128)} %bitcast.10), calls=%async_computation.2 | async-start | bytes 1572864 | tf_op jit(solution)/shard_map/all_to_all | solution.py:600
  40.0 25.1 %pack_band.2 = f32[512,384]{1,0:T(8,128)} custom-call(f32[1,2,2,49152]{3,2,1,0:T(2,128)} %coeff_ref.3, s32[1,49152]{1,0:T(1,128)} %miller_ref.3, s32[1,49152]{1,0:T(1,128)} %slot_ref.3, bf16[2,512,256]{2,1,0:T(8,128)(2,1)} %constant.35.clone.pencil_ref), custom_call_target="tpu_custom_call" | custom-call | flops 19327352832 | bytes 786432 | tf_op jit(solution)/shard_map/pack_band/pallas_call | solution.py:326
  65.1 0.0 all-to-all-done.2.refs_1_
  65.1 0.0 copy-start.2
  65.1 0.0 copy-start.4
  65.1 0.9 copy-done.2
  66.0 5.8 %all-to-all-start = ((f32[32,16,384]{2,1,0:T(8,128)}), f32[32,16,384]{2,1,0:T(8,128)S(1)}, u32[]{:S(2)}, u32[]{:S(2)}) async-start(f32[32,16,384]{2,1,0:T(8,128)} %bitcast.9), calls=%async_computation | async-start | bytes 1572864 | tf_op jit(solution)/shard_map/all_to_all | solution.py:600
  71.9 0.0 copy-done.4
  71.9 0.6 reduce_sum.9
  73.2 0.5 divide_multiply_fusion.refs_0_
  73.7 20.2 %wave_band.2.refs_6_ = f32[4,8,32,128]{3,2,1,0:T(8,128)} custom-call(f32[4]{0:T(128)} %divide_multiply_fusion.refs_0_, f32[32,16,384]{2,1,0:T(8,128)} %copy-done.2, s32[1,3072]{1,0:T(1,128)} %bitcast.12, bf16[2,128,256]{2,1,0:T(8,128)(2,1)} %constant.36.clone.refs_3_, bf16[2,256,128]{2,1,0:T(8,128)(2,1)} %constant.37.clone.refs_4_, ...), custom_call_target="tpu_custom_call" | custom-call | flops 3221225472 | bytes 786432 | tf_op jit(solution)/shard_map/wave_band/pallas_call | solution.py:454
  93.8 0.0 all-to-all-done.refs_1_
  93.8 0.0 copy-start.1
  93.8 0.9 copy-done.1
  94.7 22.9 %wave_band.3 = (f32[4,8,32,128]{3,2,1,0:T(8,128)}, f32[1024,128]{1,0:T(8,128)}) custom-call(f32[4]{0:T(128)} %divide_multiply_fusion.refs_0_, f32[32,16,384]{2,1,0:T(8,128)} %copy-done.1, s32[1,3072]{1,0:T(1,128)} %bitcast.13, bf16[2,128,256]{2,1,0:T(8,128)(2,1)} %constant.36.clone.refs_3_, bf16[2,256,128]{2,1,0:T(8,128)(2,1)} %constant.37.clone.refs_4_, ...), custom_call_target="tpu_custom_call" | custom-call | flops 3221225472 | bytes 786432 | tf_op jit(solution)/shard_map/wave_band/pallas_call | solution.py:454
  117.7 22.3 %all_to_all.30.came_ref = f32[32,4,8,128]{3,2,1,0:T(8,128)} all-to-all(f32[32,4,8,128]{3,2,1,0:T(8,128)} %bitcast.11), channel_id=1, replica_groups=mesh['kpt'=4,'pw'=8] {'kpt','pw'}, dimensions={0} | all-to-all | bytes 1048576 | tf_op jit(solution)/shard_map/all_to_all | solution.py:616
  140.0 3.5 %all-to-all-start.3 = ((f32[4,8,32,128]{3,2,1,0:T(8,128)}), f32[4,8,32,128]{3,2,1,0:T(8,128)S(1)}, u32[]{:S(2)}, u32[]{:S(2)}) async-start(f32[4,8,32,128]{3,2,1,0:T(8,128)} %get-tuple-element.4), calls=%async_computation.3 | async-start | bytes 1048576 | tf_op jit(solution)/shard_map/all_to_all | solution.py:617
  143.4 5.3 %poisson.1 = f32[32,4,8,128]{3,2,1,0:T(8,128)} custom-call(s32[1]{0:T(128)} %bitcast.4.first_ref, f32[32,4,8,128]{3,2,1,0:T(8,128)} %all_to_all.30.came_ref, bf16[2,512,256]{2,1,0:T(8,128)(2,1)} %constant.40.clone.forth_ref, bf16[2,512,256]{2,1,0:T(8,128)(2,1)} %constant.41.clone.back_ref, bf16[2,128,256]{2,1,0:T(8,128)(2,1)} %constant.42.clone.both_x_ref), custom_call_target="tpu_custom_call" | custom-call | tf_op jit(solution)/shard_map/poisson/pallas_call | solution.py:536
  148.8 3.1 %all-to-all-done.3 = f32[4,8,32,128]{3,2,1,0:T(8,128)S(1)} async-done(((f32[4,8,32,128]{3,2,1,0:T(8,128)}), f32[4,8,32,128]{3,2,1,0:T(8,128)S(1)}, u32[]{:S(2)}, u32[]{:S(2)}) %all-to-all-start.3) | async-done | bytes 524320 | tf_op jit(solution)/shard_map/all_to_all | solution.py:617
  151.9 2.6 %all-to-all-start.5 = ((f32[32,4,8,128]{3,2,1,0:T(8,128)}), f32[32,4,8,128]{3,2,1,0:T(8,128)S(1)}, u32[]{:S(2)}, u32[]{:S(2)}) async-start(f32[32,4,8,128]{3,2,1,0:T(8,128)} %poisson.1), calls=%async_computation.5 | async-start | bytes 1048576 | tf_op jit(solution)/shard_map/all_to_all | solution.py:622
  154.5 16.4 %all-to-all-done.5 = f32[32,4,8,128]{3,2,1,0:T(8,128)S(1)} async-done(((f32[32,4,8,128]{3,2,1,0:T(8,128)}), f32[32,4,8,128]{3,2,1,0:T(8,128)S(1)}, u32[]{:S(2)}, u32[]{:S(2)}) %all-to-all-start.5) | async-done | bytes 524320 | tf_op jit(solution)/shard_map/all_to_all | solution.py:622
  170.8 0.0 copy-start
  170.8 0.8 copy-done
  171.6 2.2 %finish.1 = f32[32,32,128]{2,1,0:T(8,128)} custom-call(f32[1024,128]{1,0:T(8,128)} %bitcast.8, bf16[2,128,128]{2,1,0:T(8,128)(2,1)} %constant.39.clone.back_ref), custom_call_target="tpu_custom_call" | custom-call | tf_op jit(solution)/shard_map/finish/pallas_call | solution.py:558
  173.9 0.8 copy.16
Async XLA Ops:
  1.9 31.4 %all-to-all-start.1 = ((s32[8,1,384]{2,1,0:T(1,128)}), s32[8,1,384]{2,1,0:T(1,128)S(1)}, u32[]{:S(2)}, u32[]{:S(2)}) async-start(s32[8,1,384]{2,1,0:T(1,128)} %broadcast_in_dim.2), calls=%async_computation.1 | async-start | bytes 24576 | tf_op jit(solution)/shard_map/all_to_all | solution.py:585
  33.3 0.6 copy-start.3
  33.9 31.2 %all-to-all-start.2 = ((f32[32,16,384]{2,1,0:T(8,128)}), f32[32,16,384]{2,1,0:T(8,128)S(1)}, u32[]{:S(2)}, u32[]{:S(2)}) async-start(f32[32,16,384]{2,1,0:T(8,128)} %bitcast.10), calls=%async_computation.2 | async-start | bytes 1572864 | tf_op jit(solution)/shard_map/all_to_all | solution.py:600
  65.1 0.9 copy-start.2
  65.1 6.8 %copy-start.4 = (s32[4]{0:T(128)S(1)}, s32[4]{0:T(128)}, u32[]{:S(2)}) copy-start(s32[4]{0:T(128)} %param.17) | copy-start | bytes 52
  66.0 27.8 %all-to-all-start = ((f32[32,16,384]{2,1,0:T(8,128)}), f32[32,16,384]{2,1,0:T(8,128)S(1)}, u32[]{:S(2)}, u32[]{:S(2)}) async-start(f32[32,16,384]{2,1,0:T(8,128)} %bitcast.9), calls=%async_computation | async-start | bytes 1572864 | tf_op jit(solution)/shard_map/all_to_all | solution.py:600
  93.8 0.9 copy-start.1
  140.0 11.9 %all-to-all-start.3 = ((f32[4,8,32,128]{3,2,1,0:T(8,128)}), f32[4,8,32,128]{3,2,1,0:T(8,128)S(1)}, u32[]{:S(2)}, u32[]{:S(2)}) async-start(f32[4,8,32,128]{3,2,1,0:T(8,128)} %get-tuple-element.4), calls=%async_computation.3 | async-start | bytes 1048576 | tf_op jit(solution)/shard_map/all_to_all | solution.py:617
  151.9 19.0 %all-to-all-start.5 = ((f32[32,4,8,128]{3,2,1,0:T(8,128)}), f32[32,4,8,128]{3,2,1,0:T(8,128)S(1)}, u32[]{:S(2)}, u32[]{:S(2)}) async-start(f32[32,4,8,128]{3,2,1,0:T(8,128)} %poisson.1), calls=%async_computation.5 | async-start | bytes 1048576 | tf_op jit(solution)/shard_map/all_to_all | solution.py:622
  170.8 0.8 copy-start

commit v2 on v1

--- a/solution.py
+++ b/solution.py
@@ -204,10 +204,11 @@
 
 
 def mul3(former, latter, dims):
-    return (
-        mul(former[0], latter[0], dims)
-        + mul(former[0], latter[1], dims)
-        + mul(former[1], latter[0], dims)
+    (of_former,), (of_latter,) = dims[0]
+    return mul(
+        jnp.concatenate((former[0], former[0], former[1]), axis=of_former),
+        jnp.concatenate((latter[0], latter[1], latter[0]), axis=of_latter),
+        dims,
     )
 
 
@@ -277,95 +278,140 @@
     return return_table
 
 
-def pack_kernel(step_width, coeff_ref, miller_ref, slot_ref, pencil_ref, out_ref, total):
-    step = pl.program_id(0)
-    slots = out_ref.shape[1]
-    width = pencil_ref.shape[2] // 2
-    chunk = coeff_ref.shape[3]
-
-    @pl.when(step == 0)
-    def _():
-        total[...] = jnp.zeros_like(total)
+def pack_kernel(width, has_column, *refs):
+    coeff_ref, miller_ref, slot_ref, pencil_ref = refs[:4]
+    rest = list(refs[4:])
+    column_ref = rest.pop(0) if has_column else None
+    out_ref, total, chosen_a, spread_a, chosen_b, spread_b = rest
+    slots, step_width = chosen_a.shape
+    count = out_ref.shape[0]
+    rows = pencil_ref.shape[1] // count
+    step_count = miller_ref.shape[1] // step_width
 
     one = jnp.ones((LANES, step_width), jnp.bfloat16)
     zero = jnp.zeros((LANES, step_width), jnp.bfloat16)
     steps = lax.broadcasted_iota(jnp.int32, (LANES, step_width), 0)
     steps = steps.astype(jnp.float32).astype(jnp.bfloat16)
-    for start in range(0, chunk, step_width):
-        part = pl.ds(start, step_width)
+
+    def build(step, chosen_ref, spread_ref):
+        part = pl.ds(pl.multiple_of(step * step_width, step_width), step_width)
         slot = slot_ref[:, part].astype(jnp.float32)
         depth = (miller_ref[:, part] + width // 2).astype(jnp.float32).astype(jnp.bfloat16)
-        chosen = jnp.concatenate(
-            [
-                jnp.where((slot - first).astype(jnp.bfloat16) == steps, one, zero)
-                for first in range(0, slots, LANES)
-            ],
-            axis=0,
-        )
+        for first in range(0, slots, LANES):
+            found = (slot - first).astype(jnp.bfloat16) == steps
+            chosen_ref[first : first + LANES] = jnp.where(found, one, zero)
         here = depth == steps
-        high, low = pieces(coeff_ref[0, 0, :, part])
-        spread = jnp.concatenate(
-            [jnp.where(here, piece[c : c + 1], zero) for piece in (high, low) for c in range(2)],
-            axis=0,
-        )
-        total[...] += mul(chosen, spread, NT)
-
-    @pl.when(step == pl.num_programs(0) - 1)
-    def _():
-        both = (
-            total[:, : 2 * width].astype(jnp.bfloat16),
-            total[:, 2 * width :].astype(jnp.bfloat16),
-        )
-        out_ref[...] = mul3((pencil_ref[0], pencil_ref[1]), both, NT)
-
-
-def pack_band(band, coeffs, miller, slot, pencil, slots):
+        for at, piece in enumerate(pieces(coeff_ref[0, 0, :, part])):
+            for c in range(2):
+                first = (2 * at + c) * LANES
+                spread_ref[first : first + LANES] = jnp.where(here, piece[c : c + 1], zero)
+
+    def use(chosen_ref, spread_ref):
+        total[...] += mul(chosen_ref[...], spread_ref[...], NT)
+
+    total[...] = jnp.zeros_like(total)
+    build(0, chosen_a, spread_a)
+
+    def two_steps(i, unused):
+        build(2 * i + 1, chosen_b, spread_b)
+        use(chosen_a, spread_a)
+        build(jnp.minimum(2 * i + 2, step_count - 1), chosen_a, spread_a)
+        use(chosen_b, spread_b)
+        return unused
+
+    lax.fori_loop(0, step_count // 2, two_steps, 0)
+    if step_count % 2:
+        use(chosen_a, spread_a)
+
+    both = (
+        total[:, : 2 * width].astype(jnp.bfloat16),
+        total[:, 2 * width :].astype(jnp.bfloat16),
+    )
+    pencils = mul3((pencil_ref[0], pencil_ref[1]), both, NT)
+    tiles = slots // LANES
+    for t in range(tiles):
+        tile = pencils[:, t * LANES : (t + 1) * LANES].reshape(count, rows, LANES)
+        out_ref[:, t * rows : (t + 1) * rows] = tile
+    if has_column:
+        column = column_ref[...].astype(jnp.float32)
+        column = [column[:, t * LANES : (t + 1) * LANES] for t in range(tiles)]
+        blank = [jnp.zeros((8 - tiles, LANES), jnp.float32)]
+        column = jnp.concatenate(column + blank, axis=0)
+        out_ref[:, tiles * rows :] = jnp.broadcast_to(column[None], (count, 8, LANES))
+
+
+def pack_band(band, count, coeffs, miller, slot, pencil, slots, column):
     total = miller.shape[1]
     width = pencil.shape[2] // 2
-    chunk = 4096 if total % 4096 == 0 else total
+    rows = pencil.shape[1] // count * (slots // LANES)
+    step_width = 1024 if total % 1024 == 0 else total
+    operands = [coeffs, miller, slot, pencil]
+    if column is not None:
+        operands.append(column)
+        rows += 8
+    one_band = pl.BlockSpec((1, 1, 2, total), lambda i: (0, band, 0, 0))
+    buffers = [
+        pltpu.VMEM((slots, step_width), jnp.bfloat16),
+        pltpu.VMEM((4 * width, step_width), jnp.bfloat16),
+    ]
     return pl.pallas_call(
-        functools.partial(pack_kernel, 1024 if chunk % 1024 == 0 else chunk),
-        grid=(total // chunk,),
-        in_specs=[
-            pl.BlockSpec((1, 1, 2, chunk), lambda i: (0, band, 0, i)),
-            pl.BlockSpec((1, chunk), lambda i: (0, i)),
-            pl.BlockSpec((1, chunk), lambda i: (0, i)),
-            pl.BlockSpec(pencil.shape, lambda i: (0, 0, 0)),
-        ],
-        out_specs=pl.BlockSpec((pencil.shape[1], slots), lambda i: (0, 0)),
-        out_shape=jax.ShapeDtypeStruct((pencil.shape[1], slots), jnp.float32),
-        scratch_shapes=[pltpu.VMEM((slots, 4 * width), jnp.float32)],
+        functools.partial(pack_kernel, width, column is not None),
+        grid=(1,),
+        in_specs=[one_band]
+        + [pl.BlockSpec(x.shape, lambda i, n=x.ndim: (0,) * n) for x in operands[1:]],
+        out_specs=pl.BlockSpec((count, rows, LANES), lambda i: (0, 0, 0)),
+        out_shape=jax.ShapeDtypeStruct((count, rows, LANES), jnp.float32),
+        scratch_shapes=[pltpu.VMEM((slots, 4 * width), jnp.float32)] + buffers + buffers,
         compiler_params=pltpu.CompilerParams(vmem_limit_bytes=VMEM_LIMIT),
         cost_estimate=pl.CostEstimate(
             flops=2 * total * slots * 4 * width, bytes_accessed=16 * total, transcendentals=0
         ),
         name="pack_band",
-    )(coeffs, miller, slot, pencil)
-
-
-def wave_kernel(kpts, has_former, is_last, *refs):
-    weight_ref, came_ref, column_ref, wave_y_ref, wave_x_ref, forth_ref = refs[:6]
-    rest = list(refs[6:])
-    former_ref = rest.pop(0) if has_former else None
+    )(*operands)
+
+
+def wave_kernel(kpts, tiles, scale, is_first, is_last, *refs):
+    count_ref, came_ref, wave_y_ref, wave_x_ref = refs[:4]
+    rest = list(refs[4:])
+    forth_ref = rest.pop(0) if is_last else None
+    former_ref, cell_ref = (None, None) if is_first else (rest.pop(0), rest.pop(0))
     density_ref = rest.pop(0)
+    cell_out = rest.pop(0) if is_first and not is_last else None
     send_ref = rest.pop(0) if is_last else None
-    values, grid = rest
-    planes = density_ref.shape[1]
-    slots = came_ref.shape[2]
+    values, grid, chosen_a, chosen_b = rest
+    blocks, planes, block, unused = density_ref.shape
+    part_rows = 2 * planes
     pws = came_ref.shape[0] // kpts
-    rows = kpts * 2 * planes
+    rows = kpts * part_rows
+    total = values.shape[1]
 
     for j in range(pws):
-        block = jnp.concatenate([came_ref[k * pws + j] for k in range(kpts)], axis=0)
-        high, low = pieces(block)
-        values[0:rows, pl.ds(j * slots, slots)] = high
-        values[rows : 2 * rows, pl.ds(j * slots, slots)] = low
-
-    column = column_ref[...]
-    cell = ((column // NY + NX // 2) % NX - HALF // 2) * HALF
-    cell = cell + (column % NY + NY // 2) % NY - HALF // 2
-    cell = cell.astype(jnp.float32)
-    total = cell.shape[1]
+        for t in range(tiles):
+            taken = jnp.concatenate(
+                [came_ref[k * pws + j, t * part_rows : (t + 1) * part_rows] for k in range(kpts)],
+                axis=0,
+            )
+            high, low = pieces(taken)
+            first = (j * tiles + t) * LANES
+            values[0:rows, first : first + LANES] = high
+            values[rows : 2 * rows, first : first + LANES] = low
+
+    if is_first:
+        column = jnp.concatenate(
+            [
+                came_ref[j, tiles * part_rows + t : tiles * part_rows + t + 1]
+                for j in range(pws)
+                for t in range(tiles)
+            ],
+            axis=1,
+        ).astype(jnp.int32)
+        cell = ((column // NY + NX // 2) % NX - HALF // 2) * HALF
+        cell = cell + (column % NY + NY // 2) % NY - HALF // 2
+        cell = cell.astype(jnp.float32)
+        if cell_out is not None:
+            cell_out[...] = cell
+    else:
+        cell = cell_ref[...]
     tile = 4 * HALF
     steps = lax.broadcasted_iota(jnp.int32, (tile, total), 0).astype(jnp.float32)
     steps = steps.astype(jnp.bfloat16)
@@ -373,10 +419,12 @@
     zero = jnp.zeros((tile, total), jnp.bfloat16)
     left = lax.broadcasted_iota(jnp.int32, (kpts * planes, LANES), 1) < HALF
 
-    def place(t, unused):
+    def build(t, chosen_ref):
         near = (cell - (t * tile).astype(jnp.float32)).astype(jnp.bfloat16)
-        chosen = jnp.where(near == steps, one, zero)
-        found = mul(values[...], chosen, NT)
+        chosen_ref[...] = jnp.where(near == steps, one, zero)
+
+    def place(t, chosen_ref):
+        found = mul(values[...], chosen_ref[...], NT)
         found = found[:rows] + found[rows:]
         for h in range(2):
             real, imag = (
@@ -393,13 +441,32 @@
             odd = jnp.where(left, pltpu.roll(real, HALF, 1), imag)
             grid[pl.ds(t * 4 + 2 * h, kpts * planes, stride=HALF), :] = even
             grid[pl.ds(t * 4 + 2 * h + 1, kpts * planes, stride=HALF), :] = odd
+
+    build(jnp.int32(0), chosen_a)
+
+    def two_tiles(i, unused):
+        build(2 * i + 1, chosen_b)
+        place(2 * i, chosen_a)
+        build(2 * i + 2, chosen_a)
+        place(2 * i + 1, chosen_b)
         return unused
 
-    lax.fori_loop(0, HALF // 4, place, 0)
-
+    lax.fori_loop(0, HALF // 8, two_tiles, 0)
+
+    sum_of = count_ref[0]
+    for k in range(1, kpts):
+        sum_of = sum_of + count_ref[k]
+
+    def spread(number):
+        return jnp.full((8, NY), number, jnp.int32).astype(jnp.float32)
+
+    weights = [
+        jnp.concatenate([spread(count_ref[k]) / spread(sum_of) * scale] * (NX // 8), axis=0)
+        for k in range(kpts)
+    ]
     first_row = lax.broadcasted_iota(jnp.int32, (2 * HALF, NX), 0) == 0
 
-    def transform(p, unused):
+    def transform(p):
         lines = jnp.concatenate(
             [
                 grid[pl.ds(pl.multiple_of((k * planes + p) * HALF, HALF), HALF), :]
@@ -420,12 +487,10 @@
         )
         wave = mul3((wave_x_ref[0], wave_x_ref[1]), pieces(mixed), NN)
         square = wave[:NX] * wave[:NX] + wave[NX:] * wave[NX:]
-        density = weight_ref[0] * square[:, :NY]
+        density = weights[0] * square[:, :NY]
         for k in range(1, kpts):
-            density = density + weight_ref[k] * square[:, k * NY : (k + 1) * NY]
-        blocks = density_ref.shape[0]
-        block = NX // blocks
-        if has_former:
+            density = density + weights[k] * square[:, k * NY : (k + 1) * NY]
+        if former_ref is not None:
             density = density + jnp.concatenate([former_ref[a, p] for a in range(blocks)], axis=0)
         for a in range(blocks):
             density_ref[a, p] = density[a * block : (a + 1) * block]
@@ -434,31 +499,43 @@
             half = mul3((forth_ref[0], forth_ref[1]), pieces(density - level), NT)
             half = half + jnp.where(first_row, level * NY, 0.0)
             send_ref[pl.ds(p, 2 * HALF, stride=planes), :] = half
+
+    together = 4
+
+    def some_planes(i, unused):
+        for s in range(together):
+            transform(together * i + s)
         return unused
 
-    lax.fori_loop(0, planes, transform, 0)
-
-
-def wave_band(kpts, weight, came, column, wave_y, wave_x, forth, former, is_last):
-    planes = came.shape[1] // 2
+    lax.fori_loop(0, planes // together, some_planes, 0)
+
+
+def wave_band(kpts, tiles, total, scale, counts, came, wave_y, wave_x, forth, former, cell):
+    planes = NZ // came.shape[0]
     block = NX // kpts
+    is_first, is_last = former is None, forth is not None
     vmem = pl.BlockSpec(memory_space=pltpu.VMEM)
-    operands = [weight, came, column, wave_y, wave_x, forth]
-    if former is not None:
-        operands.append(former)
+    operands = [counts, came, wave_y, wave_x]
+    if is_last:
+        operands.append(forth)
+    if not is_first:
+        operands += [former, cell]
     out_shape = [jax.ShapeDtypeStruct((kpts, planes, block, NY), jnp.float32)]
+    if is_first and not is_last:
+        out_shape.append(jax.ShapeDtypeStruct((1, total), jnp.float32))
     if is_last:
         out_shape.append(jax.ShapeDtypeStruct((2 * HALF * planes, NX), jnp.float32))
-    total = column.shape[1]
     rows = kpts * 2 * planes
     return pl.pallas_call(
-        functools.partial(wave_kernel, kpts, former is not None, is_last),
+        functools.partial(wave_kernel, kpts, tiles, scale, is_first, is_last),
         in_specs=[pl.BlockSpec(memory_space=pltpu.SMEM)] + [vmem] * (len(operands) - 1),
         out_specs=[vmem] * len(out_shape),
         out_shape=out_shape,
         scratch_shapes=[
             pltpu.VMEM((2 * rows, total), jnp.bfloat16),
             pltpu.VMEM((kpts * planes * HALF, LANES), jnp.float32),
+            pltpu.VMEM((4 * HALF, total), jnp.bfloat16),
+            pltpu.VMEM((4 * HALF, total), jnp.bfloat16),
         ],
         compiler_params=pltpu.CompilerParams(vmem_limit_bytes=VMEM_LIMIT),
         cost_estimate=pl.CostEstimate(
@@ -565,6 +642,10 @@
     )(came, back_y)
 
 
+def exchange(array, axes):
+    return lax.all_to_all(array, axes, split_axis=0, concat_axis=0, tiled=True)
+
+
 def local_planes(band_coeffs, miller_third, column_slot, column_map, kpoint_counts):
     pws = lax.axis_size("pw")
     kpts = lax.axis_size("kpt")
@@ -582,44 +663,39 @@
         for name in ("wave_y", "wave_x", "forth_y", "back_y", "forth_z", "back_z", "both_x")
     )
 
-    columns = lax.all_to_all(
-        jnp.broadcast_to(column_map[None, None, :], (pws, 1, slots)),
-        "pw",
-        split_axis=0,
-        concat_axis=0,
-        tiled=True,
-    ).reshape(1, pws * slots)
-    weight = (
-        2.0 * kpoint_counts.astype(jnp.float32) / jnp.sum(kpoint_counts).astype(jnp.float32)
-    ) / (column_slot.shape[1] * pws)
-
+    tiles = slots // LANES
+    scale = 2.0 / (column_slot.shape[1] * pws)
     arrived = []
     for band in range(band_count):
-        packed = pack_band(band, band_coeffs, miller_third, column_slot, pencil, slots)
-        arrived.append(
-            lax.all_to_all(
-                packed.reshape(count, 2 * planes, slots),
-                everyone,
-                split_axis=0,
-                concat_axis=0,
-                tiled=True,
-            )
-        )
-    former = None
+        column = column_map.reshape(1, slots) if band == 0 else None
+        packed = pack_band(
+            band, count, band_coeffs, miller_third, column_slot, pencil, slots, column
+        )
+        arrived.append(exchange(packed, everyone))
+    former = cell = None
     for band in range(band_count):
-        is_last = band == band_count - 1
-        made_here = wave_band(
-            kpts, weight, arrived[band], columns, wave_y, wave_x, forth_y, former, is_last
-        )
-        former = made_here[0]
-    half = made_here[1].reshape(count, parts, planes, NX)
-    half = lax.all_to_all(half, everyone, split_axis=0, concat_axis=0, tiled=True)
-    density = lax.all_to_all(former, "kpt", split_axis=0, concat_axis=0, tiled=True)
-    density = density.reshape(NZ // pws, NX // kpts, NY)
+        forth = forth_y if band == band_count - 1 else None
+        former, other = wave_band(
+            kpts,
+            tiles,
+            pws * slots,
+            scale,
+            kpoint_counts,
+            arrived[band],
+            wave_y,
+            wave_x,
+            forth,
+            former,
+            cell,
+        )
+        cell = other if band == 0 else cell
+    half = exchange(other.reshape(count, parts, planes, NX), everyone)
     device = lax.axis_index("kpt") * pws + lax.axis_index("pw")
     first = (device * (parts // 2)).astype(jnp.int32).reshape(1)
     back = poisson(pws, first, half, forth_z, back_z, both_x)
-    back = lax.all_to_all(back, everyone, split_axis=0, concat_axis=0, tiled=True)
+    back, former = lax.optimization_barrier((back, former))
+    back = exchange(back, everyone)
+    density = exchange(former, "kpt").reshape(NZ // pws, NX // kpts, NY)
     back = back.reshape(count * parts * 8, LANES)
     hartree = finish(NZ // pws, NX // kpts, back, back_y)
     return (density, hartree)

time: 175 us -> 172 us (0.983)
  waiting for transfers between devices: 19.5 us -> 38.3 us
  blocking collectives: 22.3 us -> 11.4 us
  starting transfers between devices: 24.3 us -> 18.3 us
  Pallas kernels: 101 us -> 98.4 us
    all_to_all x5 -> x4, waiting for transfers between devices: 19.5 us -> 38.3 us  [exchange(): return lax.all_to_all(array, axes, split_axis=0, concat_axis=0, tiled=True)]
    all_to_all x1, blocking collectives: 22.3 us -> 11.4 us  [exchange(): return lax.all_to_all(array, axes, split_axis=0, concat_axis=0, tiled=True)]
    all_to_all x5 -> x4, starting transfers between devices: 24.3 us -> 18.3 us  [exchange(): return lax.all_to_all(array, axes, split_axis=0, concat_axis=0, tiled=True)]
    pallas_call x4, Pallas kernels: 93.3 us -> 91.3 us  [the longest x2 56.4 us: pack_band(): pl.pallas_call(functools.partial(pack_kernel, width, column is not None),...]
  transfers between devices with their start and end apart: 5 -> 4, of which waited for: 2 -> 3; matrix products, arithmetic and copies ran while one was open for 1% -> 0% of each run, Pallas kernels for 43% -> 26%
where the time goes in v2:
time: 172 us
  Pallas kernels  98.4 us (57%)
  waiting for transfers between devices  38.3 us (22%)
  starting transfers between devices  18.3 us (11%)
  blocking collectives  11.4 us (7%)
  local copies, waits for them, and re-layouts  4.54 us (3%)
    pallas_call x2, Pallas kernels, pack_band(): pl.pallas_call(functools.partial(pack_kernel, width, column is not None),...  56.4 us
    all_to_all x4, waiting for transfers between devices, exchange(): return lax.all_to_all(array, axes, split_axis=0, concat_axis=0, tiled=True)  38.3 us
    pallas_call x2, Pallas kernels, wave_band(): pl.pallas_call(functools.partial(wave_kernel, kpts, tiles, scale, is_firs...  34.9 us
    all_to_all x4, starting transfers between devices, exchange(): return lax.all_to_all(array, axes, split_axis=0, concat_axis=0, tiled=True)  18.3 us
    all_to_all x1, blocking collectives, exchange(): return lax.all_to_all(array, axes, split_axis=0, concat_axis=0, tiled=True)  11.4 us
    pallas_call x1, Pallas kernels, poisson(): pl.pallas_call(functools.partial(poisson_kernel, pws), in_specs=[pl.Block...  4.81 us
  transfers between devices with their start and end apart: 4, of which 3 were waited for; matrix products, arithmetic and copies ran while one was open for 0% of the time, Pallas kernels for 26%

profile of v2, /device:TPU:0, one launch (start us, length us, event | category | flops | bytes accessed | tf_op | source)
XLA Modules:
  0.0 171.6 jit_solution(9392235199853270034)
XLA Ops:
  0.6 1.2 reshape.20.refs_4_
  1.9 28.3 %pack_band.3 = f32[32,56,128]{2,1,0:T(8,128)} custom-call(f32[1,2,2,49152]{3,2,1,0:T(2,128)} %refs_0_.5, s32[1,49152]{1,0:T(1,128)} %refs_1_.3, s32[1,49152]{1,0:T(1,128)} %refs_2_.5, bf16[2,512,256]{2,1,0:T(8,128)(2,1)} %constant.28.clone.refs_3_, s32[1,384]{1,0:T(1,128)} %reshape.20.refs_4_), custom_call_target="tpu_custom_call" | custom-call | flops 19327352832 | bytes 786432 | tf_op jit(solution)/shard_map/pack_band/pallas_call | solution.py:357
  30.2 7.3 %all-to-all-start.1 = ((f32[32,56,128]{2,1,0:T(8,128)}), f32[32,56,128]{2,1,0:T(8,128)S(1)}, u32[]{:S(2)}, u32[]{:S(2)}) async-start(f32[32,56,128]{2,1,0:T(8,128)} %pack_band.3), calls=%async_computation.1 | async-start | bytes 1835008 | tf_op jit(solution)/shard_map/all_to_all | solution.py:646
  37.5 28.1 %pack_band.2 = f32[32,48,128]{2,1,0:T(8,128)} custom-call(f32[1,2,2,49152]{3,2,1,0:T(2,128)} %refs_0_.5, s32[1,49152]{1,0:T(1,128)} %refs_1_.3, s32[1,49152]{1,0:T(1,128)} %refs_2_.5, bf16[2,512,256]{2,1,0:T(8,128)(2,1)} %constant.28.clone.refs_3_), custom_call_target="tpu_custom_call" | custom-call | flops 19327352832 | bytes 786432 | tf_op jit(solution)/shard_map/pack_band/pallas_call | solution.py:357
  65.6 0.0 all-to-all-done.1.refs_1_
  65.6 0.0 copy-start.2
  65.6 5.8 %all-to-all-start = ((f32[32,48,128]{2,1,0:T(8,128)}), f32[32,48,128]{2,1,0:T(8,128)S(1)}, u32[]{:S(2)}, u32[]{:S(2)}) async-start(f32[32,48,128]{2,1,0:T(8,128)} %pack_band.2), calls=%async_computation | async-start | bytes 1572864 | tf_op jit(solution)/shard_map/all_to_all | solution.py:646
  71.4 0.0 copy-done.2
  71.4 16.4 %wave_band.2 = (f32[4,8,32,128]{3,2,1,0:T(8,128)}, f32[1,3072]{1,0:T(1,128)}) custom-call(s32[4]{0:T(128)} %refs_0_.7, f32[32,56,128]{2,1,0:T(8,128)} %copy-done.2, bf16[2,128,256]{2,1,0:T(8,128)(2,1)} %constant.29.clone.refs_2_, bf16[2,256,128]{2,1,0:T(8,128)(2,1)} %constant.30.clone.refs_3_), custom_call_target="tpu_custom_call" | custom-call | flops 3221225472 | bytes 917504 | tf_op jit(solution)/shard_map/wave_band/pallas_call | solution.py:529
  87.8 5.6 %all-to-all-done.refs_1_ = f32[32,48,128]{2,1,0:T(8,128)S(1)} async-done(((f32[32,48,128]{2,1,0:T(8,128)}), f32[32,48,128]{2,1,0:T(8,128)S(1)}, u32[]{:S(2)}, u32[]{:S(2)}) %all-to-all-start) | async-done | bytes 786464 | tf_op jit(solution)/shard_map/all_to_all | solution.py:646
  93.4 0.0 copy-start.3
  93.4 0.9 copy-done.3
  94.3 18.5 %wave_band.3 = (f32[4,8,32,128]{3,2,1,0:T(8,128)}, f32[1024,128]{1,0:T(8,128)}) custom-call(s32[4]{0:T(128)} %refs_0_.7, f32[32,48,128]{2,1,0:T(8,128)} %copy-done.3, bf16[2,128,256]{2,1,0:T(8,128)(2,1)} %constant.29.clone.refs_2_, bf16[2,256,128]{2,1,0:T(8,128)(2,1)} %constant.30.clone.refs_3_, bf16[2,128,128]{2,1,0:T(8,128)(2,1)} %constant.31.clone.refs_4_, ...), custom_call_target="tpu_custom_call" | custom-call | flops 3221225472 | bytes 786432 | tf_op jit(solution)/shard_map/wave_band/pallas_call | solution.py:529
  112.8 2.6 %all-to-all-start.2 = ((f32[32,4,8,128]{3,2,1,0:T(8,128)}), f32[32,4,8,128]{3,2,1,0:T(8,128)S(1)}, u32[]{:S(2)}, u32[]{:S(2)}) async-start(f32[32,4,8,128]{3,2,1,0:T(8,128)} %bitcast.6), calls=%async_computation.2 | async-start | bytes 1048576 | tf_op jit(solution)/shard_map/all_to_all | solution.py:646
  115.4 16.3 %all-to-all-done.2.came_ref = f32[32,4,8,128]{3,2,1,0:T(8,128)S(1)} async-done(((f32[32,4,8,128]{3,2,1,0:T(8,128)}), f32[32,4,8,128]{3,2,1,0:T(8,128)S(1)}, u32[]{:S(2)}, u32[]{:S(2)}) %all-to-all-start.2) | async-done | bytes 524320 | tf_op jit(solution)/shard_map/all_to_all | solution.py:646
  131.8 0.0 copy-start
  131.8 0.8 copy-done
  132.6 0.0 copy-start.4
  132.6 4.8 %poisson.1 = f32[32,4,8,128]{3,2,1,0:T(8,128)} custom-call(s32[1]{0:T(128)} %bitcast.first_ref, f32[32,4,8,128]{3,2,1,0:T(8,128)} %copy-done, bf16[2,512,256]{2,1,0:T(8,128)(2,1)} %constant.33.clone.forth_ref, bf16[2,512,256]{2,1,0:T(8,128)(2,1)} %constant.34.clone.back_ref, bf16[2,128,256]{2,1,0:T(8,128)(2,1)} %constant.35.clone.both_x_ref), custom_call_target="tpu_custom_call" | custom-call | tf_op jit(solution)/shard_map/poisson/pallas_call | solution.py:613
  137.4 0.0 copy-done.4
  137.4 11.4 %all_to_all.25 = f32[4,8,32,128]{3,2,1,0:T(8,128)S(1)} all-to-all(f32[4,8,32,128]{3,2,1,0:T(8,128)S(1)} %copy-done.4), channel_id=1, replica_groups=mesh['kpt'=4,'pw'=8] {'kpt'}, dimensions={0} | all-to-all | bytes 1048576 | tf_op jit(solution)/shard_map/all_to_all | solution.py:646
  148.8 2.6 %all-to-all-start.4 = ((f32[32,4,8,128]{3,2,1,0:T(8,128)}), f32[32,4,8,128]{3,2,1,0:T(8,128)S(1)}, u32[]{:S(2)}, u32[]{:S(2)}) async-start(f32[32,4,8,128]{3,2,1,0:T(8,128)} %poisson.1), calls=%async_computation.4 | async-start | bytes 1048576 | tf_op jit(solution)/shard_map/all_to_all | solution.py:646
  151.4 16.4 %all-to-all-done.4 = f32[32,4,8,128]{3,2,1,0:T(8,128)S(1)} async-done(((f32[32,4,8,128]{3,2,1,0:T(8,128)}), f32[32,4,8,128]{3,2,1,0:T(8,128)S(1)}, u32[]{:S(2)}, u32[]{:S(2)}) %all-to-all-start.4) | async-done | bytes 524320 | tf_op jit(solution)/shard_map/all_to_all | solution.py:646
  167.7 0.0 copy-start.1
  167.7 0.8 copy-done.1
  168.5 2.2 %finish.1 = f32[32,32,128]{2,1,0:T(8,128)} custom-call(f32[1024,128]{1,0:T(8,128)} %bitcast.5, bf16[2,128,128]{2,1,0:T(8,128)(2,1)} %constant.32.clone.back_ref), custom_call_target="tpu_custom_call" | custom-call | tf_op jit(solution)/shard_map/finish/pallas_call | solution.py:635
  170.8 0.8 copy.16
Async XLA Ops:
  30.2 35.4 %all-to-all-start.1 = ((f32[32,56,128]{2,1,0:T(8,128)}), f32[32,56,128]{2,1,0:T(8,128)S(1)}, u32[]{:S(2)}, u32[]{:S(2)}) async-start(f32[32,56,128]{2,1,0:T(8,128)} %pack_band.3), calls=%async_computation.1 | async-start | bytes 1835008 | tf_op jit(solution)/shard_map/all_to_all | solution.py:646
  65.6 5.8 %copy-start.2 = (f32[32,56,128]{2,1,0:T(8,128)}, f32[32,56,128]{2,1,0:T(8,128)S(1)}, u32[]{:S(2)}) copy-start(f32[32,56,128]{2,1,0:T(8,128)S(1)} %all-to-all-done.1.refs_1_) | copy-start | bytes 2752516
  65.6 27.8 %all-to-all-start = ((f32[32,48,128]{2,1,0:T(8,128)}), f32[32,48,128]{2,1,0:T(8,128)S(1)}, u32[]{:S(2)}, u32[]{:S(2)}) async-start(f32[32,48,128]{2,1,0:T(8,128)} %pack_band.2), calls=%async_computation | async-start | bytes 1572864 | tf_op jit(solution)/shard_map/all_to_all | solution.py:646
  93.4 0.9 copy-start.3
  112.8 19.0 %all-to-all-start.2 = ((f32[32,4,8,128]{3,2,1,0:T(8,128)}), f32[32,4,8,128]{3,2,1,0:T(8,128)S(1)}, u32[]{:S(2)}, u32[]{:S(2)}) async-start(f32[32,4,8,128]{3,2,1,0:T(8,128)} %bitcast.6), calls=%async_computation.2 | async-start | bytes 1048576 | tf_op jit(solution)/shard_map/all_to_all | solution.py:646
  131.8 0.8 copy-start
  132.6 4.8 %copy-start.4 = (f32[4,8,32,128]{3,2,1,0:T(8,128)S(1)}, f32[4,8,32,128]{3,2,1,0:T(8,128)}, u32[]{:S(2)}) copy-start(f32[4,8,32,128]{3,2,1,0:T(8,128)} %get-tuple-element.12) | copy-start | bytes 1572868
  148.8 19.0 %all-to-all-start.4 = ((f32[32,4,8,128]{3,2,1,0:T(8,128)}), f32[32,4,8,128]{3,2,1,0:T(8,128)S(1)}, u32[]{:S(2)}, u32[]{:S(2)}) async-start(f32[32,4,8,128]{3,2,1,0:T(8,128)} %poisson.1), calls=%async_computation.4 | async-start | bytes 1048576 | tf_op jit(solution)/shard_map/all_to_all | solution.py:646
  167.7 0.8 copy-start.1

commit v3 on v2

--- a/solution.py
+++ b/solution.py
@@ -278,55 +278,83 @@
     return return_table
 
 
+def spread_lanes(row):
+    return jnp.transpose(jnp.broadcast_to(row, (LANES, row.shape[1])))
+
+
+def one_hot_lanes(row, lanes):
+    column = spread_lanes(row.astype(jnp.float32)).astype(jnp.bfloat16)
+    step = lax.broadcasted_iota(jnp.int32, column.shape, 1)
+    one = jnp.ones(column.shape, jnp.bfloat16)
+    zero = jnp.zeros(column.shape, jnp.bfloat16)
+    return jnp.concatenate(
+        [
+            jnp.where(column == (step + first).astype(jnp.float32).astype(jnp.bfloat16), one, zero)
+            for first in range(0, lanes, LANES)
+        ],
+        axis=1,
+    )
+
+
 def pack_kernel(width, has_column, *refs):
     coeff_ref, miller_ref, slot_ref, pencil_ref = refs[:4]
     rest = list(refs[4:])
     column_ref = rest.pop(0) if has_column else None
-    out_ref, total, chosen_a, spread_a, chosen_b, spread_b = rest
-    slots, step_width = chosen_a.shape
+    out_ref, total = rest
+    half = total.shape[0] // 4
+    slots = 2 * half
     count = out_ref.shape[0]
     rows = pencil_ref.shape[1] // count
-    step_count = miller_ref.shape[1] // step_width
-
-    one = jnp.ones((LANES, step_width), jnp.bfloat16)
-    zero = jnp.zeros((LANES, step_width), jnp.bfloat16)
-    steps = lax.broadcasted_iota(jnp.int32, (LANES, step_width), 0)
+    size = miller_ref.shape[1]
+    step_width = 1024 if size % 1024 == 0 else size
+    together = 4 if size % (4 * step_width) == 0 else 1
+
+    zero = jnp.zeros((half, step_width), jnp.bfloat16)
+    steps = lax.broadcasted_iota(jnp.int32, (half, step_width), 0)
     steps = steps.astype(jnp.float32).astype(jnp.bfloat16)
 
-    def build(step, chosen_ref, spread_ref):
+    def add(step):
         part = pl.ds(pl.multiple_of(step * step_width, step_width), step_width)
-        slot = slot_ref[:, part].astype(jnp.float32)
-        depth = (miller_ref[:, part] + width // 2).astype(jnp.float32).astype(jnp.bfloat16)
-        for first in range(0, slots, LANES):
-            found = (slot - first).astype(jnp.bfloat16) == steps
-            chosen_ref[first : first + LANES] = jnp.where(found, one, zero)
-        here = depth == steps
-        for at, piece in enumerate(pieces(coeff_ref[0, 0, :, part])):
-            for c in range(2):
-                first = (2 * at + c) * LANES
-                spread_ref[first : first + LANES] = jnp.where(here, piece[c : c + 1], zero)
-
-    def use(chosen_ref, spread_ref):
-        total[...] += mul(chosen_ref[...], spread_ref[...], NT)
+        slot = slot_ref[:, part]
+        second = slot >= half
+        row = jnp.where(second, slot - half, slot).astype(jnp.float32).astype(jnp.bfloat16)
+        lane = miller_ref[:, part] + width // 2
+        lane = jnp.where(second, lane + width, lane)
+        here = row == steps
+        spread = jnp.concatenate(
+            [
+                jnp.where(here, piece[c : c + 1], zero)
+                for piece in pieces(coeff_ref[0, 0, :, part])
+                for c in range(2)
+            ],
+            axis=0,
+        )
+        total[...] += mul(spread, one_hot_lanes(lane, 2 * width), NN)
 
     total[...] = jnp.zeros_like(total)
-    build(0, chosen_a, spread_a)
-
-    def two_steps(i, unused):
-        build(2 * i + 1, chosen_b, spread_b)
-        use(chosen_a, spread_a)
-        build(jnp.minimum(2 * i + 2, step_count - 1), chosen_a, spread_a)
-        use(chosen_b, spread_b)
+
+    def some_steps(i, unused):
+        for s in range(together):
+            add(together * i + s)
         return unused
 
-    lax.fori_loop(0, step_count // 2, two_steps, 0)
-    if step_count % 2:
-        use(chosen_a, spread_a)
-
-    both = (
-        total[:, : 2 * width].astype(jnp.bfloat16),
-        total[:, 2 * width :].astype(jnp.bfloat16),
-    )
+    lax.fori_loop(0, size // (together * step_width), some_steps, 0)
+
+    both = []
+    for at in range(2):
+        parts = [
+            total[(2 * at + c) * half : (2 * at + c + 1) * half].astype(jnp.bfloat16)
+            for c in range(2)
+        ]
+        both.append(
+            jnp.concatenate(
+                [
+                    jnp.concatenate([part[:, h * width : (h + 1) * width] for part in parts], axis=1)
+                    for h in range(2)
+                ],
+                axis=0,
+            )
+        )
     pencils = mul3((pencil_ref[0], pencil_ref[1]), both, NT)
     tiles = slots // LANES
     for t in range(tiles):
@@ -344,16 +372,11 @@
     total = miller.shape[1]
     width = pencil.shape[2] // 2
     rows = pencil.shape[1] // count * (slots // LANES)
-    step_width = 1024 if total % 1024 == 0 else total
     operands = [coeffs, miller, slot, pencil]
     if column is not None:
         operands.append(column)
         rows += 8
     one_band = pl.BlockSpec((1, 1, 2, total), lambda i: (0, band, 0, 0))
-    buffers = [
-        pltpu.VMEM((slots, step_width), jnp.bfloat16),
-        pltpu.VMEM((4 * width, step_width), jnp.bfloat16),
-    ]
     return pl.pallas_call(
         functools.partial(pack_kernel, width, column is not None),
         grid=(1,),
@@ -361,7 +384,7 @@
         + [pl.BlockSpec(x.shape, lambda i, n=x.ndim: (0,) * n) for x in operands[1:]],
         out_specs=pl.BlockSpec((count, rows, LANES), lambda i: (0, 0, 0)),
         out_shape=jax.ShapeDtypeStruct((count, rows, LANES), jnp.float32),
-        scratch_shapes=[pltpu.VMEM((slots, 4 * width), jnp.float32)] + buffers + buffers,
+        scratch_shapes=[pltpu.VMEM((2 * slots, 2 * width), jnp.float32)],
         compiler_params=pltpu.CompilerParams(vmem_limit_bytes=VMEM_LIMIT),
         cost_estimate=pl.CostEstimate(
             flops=2 * total * slots * 4 * width, bytes_accessed=16 * total, transcendentals=0
@@ -371,15 +394,16 @@
 
 
 def wave_kernel(kpts, tiles, scale, is_first, is_last, *refs):
-    count_ref, came_ref, wave_y_ref, wave_x_ref = refs[:4]
-    rest = list(refs[4:])
+    own_ref, count_ref, came_ref, wave_y_ref, wave_x_ref = refs[:5]
+    rest = list(refs[5:])
     forth_ref = rest.pop(0) if is_last else None
     former_ref, cell_ref = (None, None) if is_first else (rest.pop(0), rest.pop(0))
-    density_ref = rest.pop(0)
+    density_refs = [rest.pop(0) for _ in range(kpts if is_last else 1)]
     cell_out = rest.pop(0) if is_first and not is_last else None
     send_ref = rest.pop(0) if is_last else None
-    values, grid, chosen_a, chosen_b = rest
-    blocks, planes, block, unused = density_ref.shape
+    values, grid, chosen, whole = rest
+    planes = density_refs[0].shape[0]
+    block = NX // kpts
     part_rows = 2 * planes
     pws = came_ref.shape[0] // kpts
     rows = kpts * part_rows
@@ -413,18 +437,13 @@
     else:
         cell = cell_ref[...]
     tile = 4 * HALF
-    steps = lax.broadcasted_iota(jnp.int32, (tile, total), 0).astype(jnp.float32)
-    steps = steps.astype(jnp.bfloat16)
-    one = jnp.ones((tile, total), jnp.bfloat16)
-    zero = jnp.zeros((tile, total), jnp.bfloat16)
+    high = jnp.floor(cell * (1.0 / tile))
+    chosen[...] = one_hot_lanes(cell - high * tile, tile)
+    high = high.astype(jnp.bfloat16)
     left = lax.broadcasted_iota(jnp.int32, (kpts * planes, LANES), 1) < HALF
-
-    def build(t, chosen_ref):
-        near = (cell - (t * tile).astype(jnp.float32)).astype(jnp.bfloat16)
-        chosen_ref[...] = jnp.where(near == steps, one, zero)
-
-    def place(t, chosen_ref):
-        found = mul(values[...], chosen_ref[...], NT)
+    together = 4
+
+    def place(t, found):
         found = found[:rows] + found[rows:]
         for h in range(2):
             real, imag = (
@@ -442,16 +461,18 @@
             grid[pl.ds(t * 4 + 2 * h, kpts * planes, stride=HALF), :] = even
             grid[pl.ds(t * 4 + 2 * h + 1, kpts * planes, stride=HALF), :] = odd
 
-    build(jnp.int32(0), chosen_a)
-
-    def two_tiles(i, unused):
-        build(2 * i + 1, chosen_b)
-        place(2 * i, chosen_a)
-        build(2 * i + 2, chosen_a)
-        place(2 * i + 1, chosen_b)
+    def some_tiles(i, unused):
+        held = values[...]
+        kept = []
+        for s in range(together):
+            here = high == (together * i + s).astype(jnp.float32).astype(jnp.bfloat16)
+            kept.append(jnp.where(here, held, jnp.zeros_like(held)))
+        found = mul(jnp.concatenate(kept, axis=0), chosen[...], NN)
+        for s in range(together):
+            place(together * i + s, found[2 * rows * s : 2 * rows * (s + 1)])
         return unused
 
-    lax.fori_loop(0, HALF // 8, two_tiles, 0)
+    lax.fori_loop(0, HALF // 4 // together, some_tiles, 0)
 
     sum_of = count_ref[0]
     for k in range(1, kpts):
@@ -491,17 +512,20 @@
         for k in range(1, kpts):
             density = density + weights[k] * square[:, k * NY : (k + 1) * NY]
         if former_ref is not None:
-            density = density + jnp.concatenate([former_ref[a, p] for a in range(blocks)], axis=0)
-        for a in range(blocks):
-            density_ref[a, p] = density[a * block : (a + 1) * block]
+            density = density + former_ref[p]
+        if is_last:
+            whole[...] = density
+            for s, density_ref in enumerate(density_refs):
+                first = pl.multiple_of(lax.rem(own_ref[0] + s, kpts) * block, block)
+                density_ref[p] = whole[pl.ds(first, block), :]
+        else:
+            density_refs[0][p] = density
         if is_last:
             level = jnp.mean(density[:8], axis=(0, 1), keepdims=True)
             half = mul3((forth_ref[0], forth_ref[1]), pieces(density - level), NT)
             half = half + jnp.where(first_row, level * NY, 0.0)
             send_ref[pl.ds(p, 2 * HALF, stride=planes), :] = half
 
-    together = 4
-
     def some_planes(i, unused):
         for s in range(together):
             transform(together * i + s)
@@ -510,17 +534,20 @@
     lax.fori_loop(0, planes // together, some_planes, 0)
 
 
-def wave_band(kpts, tiles, total, scale, counts, came, wave_y, wave_x, forth, former, cell):
+def wave_band(kpts, tiles, total, scale, own, counts, came, wave_y, wave_x, forth, former, cell):
     planes = NZ // came.shape[0]
     block = NX // kpts
     is_first, is_last = former is None, forth is not None
     vmem = pl.BlockSpec(memory_space=pltpu.VMEM)
-    operands = [counts, came, wave_y, wave_x]
+    operands = [own, counts, came, wave_y, wave_x]
     if is_last:
         operands.append(forth)
     if not is_first:
         operands += [former, cell]
-    out_shape = [jax.ShapeDtypeStruct((kpts, planes, block, NY), jnp.float32)]
+    if is_last:
+        out_shape = [jax.ShapeDtypeStruct((planes, block, NY), jnp.float32)] * kpts
+    else:
+        out_shape = [jax.ShapeDtypeStruct((planes, NX, NY), jnp.float32)]
     if is_first and not is_last:
         out_shape.append(jax.ShapeDtypeStruct((1, total), jnp.float32))
     if is_last:
@@ -528,14 +555,14 @@
     rows = kpts * 2 * planes
     return pl.pallas_call(
         functools.partial(wave_kernel, kpts, tiles, scale, is_first, is_last),
-        in_specs=[pl.BlockSpec(memory_space=pltpu.SMEM)] + [vmem] * (len(operands) - 1),
+        in_specs=[pl.BlockSpec(memory_space=pltpu.SMEM)] * 2 + [vmem] * (len(operands) - 2),
         out_specs=[vmem] * len(out_shape),
         out_shape=out_shape,
         scratch_shapes=[
             pltpu.VMEM((2 * rows, total), jnp.bfloat16),
             pltpu.VMEM((kpts * planes * HALF, LANES), jnp.float32),
-            pltpu.VMEM((4 * HALF, total), jnp.bfloat16),
-            pltpu.VMEM((4 * HALF, total), jnp.bfloat16),
+            pltpu.VMEM((total, 4 * HALF), jnp.bfloat16),
+            pltpu.VMEM((NX, NY), jnp.float32),
         ],
         compiler_params=pltpu.CompilerParams(vmem_limit_bytes=VMEM_LIMIT),
         cost_estimate=pl.CostEstimate(
@@ -620,26 +647,31 @@
     )(first, came, forth, back, both_x)
 
 
-def finish_kernel(came_ref, back_ref, out_ref):
+def finish_kernel(own_ref, came_ref, back_ref, *refs):
+    block_refs, density_ref, out_ref = refs[:-2], refs[-2], refs[-1]
+    kpts = len(block_refs)
     back = (back_ref[0], back_ref[1])
     planes, block, unused = out_ref.shape
     merged = planes // 8
+    for s, block_ref in enumerate(block_refs):
+        sender = lax.rem(own_ref[0] + kpts - s, kpts)
+        density_ref[pl.ds(sender * (planes // kpts), planes // kpts)] = block_ref[...]
     for h in range(8):
         lines = came_ref[pl.ds(h, 2 * HALF, stride=8), :]
         field = mul3(pieces(lines), back, TN)
         out_ref[h * merged : (h + 1) * merged] = field.reshape(merged, block, NY)
 
 
-def finish(planes, block, came, back_y):
+def finish(planes, block, own, came, back_y, blocks):
     vmem = pl.BlockSpec(memory_space=pltpu.VMEM)
     return pl.pallas_call(
         finish_kernel,
-        in_specs=[vmem] * 2,
-        out_specs=vmem,
-        out_shape=jax.ShapeDtypeStruct((planes, block, NY), jnp.float32),
+        in_specs=[pl.BlockSpec(memory_space=pltpu.SMEM)] + [vmem] * (2 + len(blocks)),
+        out_specs=[vmem] * 2,
+        out_shape=[jax.ShapeDtypeStruct((planes, block, NY), jnp.float32)] * 2,
         compiler_params=pltpu.CompilerParams(vmem_limit_bytes=VMEM_LIMIT),
         name="finish",
-    )(came, back_y)
+    )(own, came, back_y, *blocks)
 
 
 def exchange(array, axes):
@@ -672,14 +704,16 @@
             band, count, band_coeffs, miller_third, column_slot, pencil, slots, column
         )
         arrived.append(exchange(packed, everyone))
+    own = lax.axis_index("kpt").astype(jnp.int32).reshape(1)
     former = cell = None
     for band in range(band_count):
         forth = forth_y if band == band_count - 1 else None
-        former, other = wave_band(
+        *made_here, other = wave_band(
             kpts,
             tiles,
             pws * slots,
             scale,
+            own,
             kpoint_counts,
             arrived[band],
             wave_y,
@@ -688,17 +722,18 @@
             former,
             cell,
         )
+        former = made_here[0]
         cell = other if band == 0 else cell
     half = exchange(other.reshape(count, parts, planes, NX), everyone)
+    blocks = [made_here[0]] + [
+        lax.ppermute(made_here[s], "kpt", [(a, (a + s) % kpts) for a in range(kpts)])
+        for s in range(1, kpts)
+    ]
     device = lax.axis_index("kpt") * pws + lax.axis_index("pw")
     first = (device * (parts // 2)).astype(jnp.int32).reshape(1)
     back = poisson(pws, first, half, forth_z, back_z, both_x)
-    back, former = lax.optimization_barrier((back, former))
-    back = exchange(back, everyone)
-    density = exchange(former, "kpt").reshape(NZ // pws, NX // kpts, NY)
-    back = back.reshape(count * parts * 8, LANES)
-    hartree = finish(NZ // pws, NX // kpts, back, back_y)
-    return (density, hartree)
+    back = exchange(back, everyone).reshape(count * parts * 8, LANES)
+    return tuple(finish(NZ // pws, NX // kpts, own, back, back_y, blocks))
 
 
 def fits_planes(kpts, pws):
@@ -714,10 +749,18 @@
     )
 
 
+def local(band_coeffs, miller_third, column_slot, column_map, kpoint_counts):
+    slots = column_map.shape[0]
+    plain = slots % LANES == 0 and slots // LANES <= 8 and slots // 2 <= 256
+    plain = plain and column_slot.shape[1] == slots * LANES
+    fits = plain and fits_planes(lax.axis_size("kpt"), lax.axis_size("pw"))
+    chosen = local_planes if fits else local_general
+    return chosen(band_coeffs, miller_third, column_slot, column_map, kpoint_counts)
+
+
 def solution(mesh):
-    chosen = local_planes if fits_planes(mesh.shape["kpt"], mesh.shape["pw"]) else local_general
     return jax.shard_map(
-        chosen,
+        local,
         mesh=mesh,
         in_specs=(P("kpt", None, None, "pw"), P("kpt", "pw"), P("kpt", "pw"), P("pw"), P()),
         out_specs=(P("pw", "kpt", None), P("pw", "kpt", None)),

time: 172 us -> 150 us (0.87)
  Pallas kernels: 98.4 us -> 82.1 us
  blocking collectives: 11.4 us -> 0 us
  starting transfers between devices: 18.3 us -> 23.1 us
    all_to_all x1 -> x0, blocking collectives: 11.4 us -> none  [exchange(): return lax.all_to_all(array, axes, split_axis=0, concat_axis=0, tiled=True)]
    pallas_call x2, Pallas kernels: 34.9 us -> 23.7 us  [wave_band(): pl.pallas_call(functools.partial(wave_kernel, kpts, tiles, scale, is_firs...]
    ppermute x0 -> x3, waiting for transfers between devices: none -> 9.07 us  [local_planes(): lax.ppermute(made_here[s], 'kpt', [(a, (a + s) % kpts) for a in range(kpt...]
    all_to_all x4, waiting for transfers between devices: 38.3 us -> 30.4 us  [exchange(): return lax.all_to_all(array, axes, split_axis=0, concat_axis=0, tiled=True)]
    pallas_call x2, Pallas kernels: 56.4 us -> 51.1 us  [pack_band(): pl.pallas_call(functools.partial(pack_kernel, width, column is not None),...]
    ppermute x0 -> x3, starting transfers between devices: none -> 4.63 us  [local_planes(): lax.ppermute(made_here[s], 'kpt', [(a, (a + s) % kpts) for a in range(kpt...]
  transfers between devices with their start and end apart: 4 -> 7, of which waited for: 3 -> 5; matrix products, arithmetic and copies ran while one was open for 0% -> 0% of each run, Pallas kernels for 26% -> 24%
where the time goes in v3:
time: 150 us; the launch traced here: 149 us
  Pallas kernels  82.1 us (55%)
  waiting for transfers between devices  39.5 us (26%)
  starting transfers between devices  23.1 us (15%)
  local copies, waits for them, and re-layouts  3.75 us (2%)
    pallas_call x2, Pallas kernels, pack_band(): pl.pallas_call(functools.partial(pack_kernel, width, column is not None),...  51.1 us
    all_to_all x4, waiting for transfers between devices, exchange(): return lax.all_to_all(array, axes, split_axis=0, concat_axis=0, tiled=True)  30.4 us
    pallas_call x2, Pallas kernels, wave_band(): pl.pallas_call(functools.partial(wave_kernel, kpts, tiles, scale, is_firs...  23.7 us
    all_to_all x4, starting transfers between devices, exchange(): return lax.all_to_all(array, axes, split_axis=0, concat_axis=0, tiled=True)  18.5 us
    ppermute x3, waiting for transfers between devices, local_planes(): lax.ppermute(made_here[s], 'kpt', [(a, (a + s) % kpts) for a in range(kpt...  9.07 us
    pallas_call x1, Pallas kernels, poisson(): pl.pallas_call(functools.partial(poisson_kernel, pws), in_specs=[pl.Block...  4.75 us
    ppermute x3, starting transfers between devices, local_planes(): lax.ppermute(made_here[s], 'kpt', [(a, (a + s) % kpts) for a in range(kpt...  4.63 us
  transfers between devices with their start and end apart: 7, of which 5 were waited for; matrix products, arithmetic and copies ran while one was open for 0% of the time, Pallas kernels for 24%

profile of v3, /device:TPU:0, one launch (start us, length us, event | category | flops | bytes accessed | tf_op | source)
XLA Modules:
  0.0 149.2 jit_solution(8967916199257042475)
XLA Ops:
  0.6 1.2 reshape.21.refs_4_
  1.9 25.5 %pack_band.3 = f32[32,56,128]{2,1,0:T(8,128)} custom-call(f32[1,2,2,49152]{3,2,1,0:T(2,128)} %refs_0_.3, s32[1,49152]{1,0:T(1,128)} %refs_1_.5, s32[1,49152]{1,0:T(1,128)} %refs_2_.3, bf16[2,512,256]{2,1,0:T(8,128)(2,1)} %constant.28.clone.refs_3_, s32[1,384]{1,0:T(1,128)} %reshape.21.refs_4_), custom_call_target="tpu_custom_call" | custom-call | flops 19327352832 | bytes 786432 | tf_op jit(solution)/shard_map/pack_band/pallas_call | solution.py:380
  27.4 7.3 %all-to-all-start.1 = ((f32[32,56,128]{2,1,0:T(8,128)}), f32[32,56,128]{2,1,0:T(8,128)S(1)}, u32[]{:S(2)}, u32[]{:S(2)}) async-start(f32[32,56,128]{2,1,0:T(8,128)} %pack_band.3), calls=%async_computation.1 | async-start | bytes 1835008 | tf_op jit(solution)/shard_map/all_to_all | solution.py:678
  34.7 25.5 %pack_band.2 = f32[32,48,128]{2,1,0:T(8,128)} custom-call(f32[1,2,2,49152]{3,2,1,0:T(2,128)} %refs_0_.3, s32[1,49152]{1,0:T(1,128)} %refs_1_.5, s32[1,49152]{1,0:T(1,128)} %refs_2_.3, bf16[2,512,256]{2,1,0:T(8,128)(2,1)} %constant.28.clone.refs_3_), custom_call_target="tpu_custom_call" | custom-call | flops 19327352832 | bytes 786432 | tf_op jit(solution)/shard_map/pack_band/pallas_call | solution.py:380
  60.3 0.0 all-to-all-done.1.refs_2_
  60.3 5.8 %all-to-all-start = ((f32[32,48,128]{2,1,0:T(8,128)}), f32[32,48,128]{2,1,0:T(8,128)S(1)}, u32[]{:S(2)}, u32[]{:S(2)}) async-start(f32[32,48,128]{2,1,0:T(8,128)} %pack_band.2), calls=%async_computation | async-start | bytes 1572864 | tf_op jit(solution)/shard_map/all_to_all | solution.py:678
  66.1 0.0 copy-done.2
  66.1 10.5 %wave_band.2 = (f32[8,128,128]{2,1,0:T(8,128)}, f32[1,3072]{1,0:T(1,128)}) custom-call(s32[1]{0:T(128)} %bitcast.refs_0_.own_ref, s32[4]{0:T(128)} %refs_1_.7, f32[32,56,128]{2,1,0:T(8,128)} %copy-done.2, bf16[2,128,256]{2,1,0:T(8,128)(2,1)} %constant.29.clone.refs_3_, bf16[2,256,128]{2,1,0:T(8,128)(2,1)} %constant.30.clone.refs_4_), custom_call_target="tpu_custom_call" | custom-call | flops 3221225472 | bytes 917504 | tf_op jit(solution)/shard_map/wave_band/pallas_call | solution.py:556
  76.6 11.4 %all-to-all-done.refs_2_ = f32[32,48,128]{2,1,0:T(8,128)S(1)} async-done(((f32[32,48,128]{2,1,0:T(8,128)}), f32[32,48,128]{2,1,0:T(8,128)S(1)}, u32[]{:S(2)}, u32[]{:S(2)}) %all-to-all-start) | async-done | bytes 786464 | tf_op jit(solution)/shard_map/all_to_all | solution.py:678
  88.1 0.0 copy-start.3
  88.1 0.9 copy-done.3
  89.0 13.2 %wave_band.3 = (f32[8,32,128]{2,1,0:T(8,128)}, f32[8,32,128]{2,1,0:T(8,128)}, f32[8,32,128]{2,1,0:T(8,128)}, f32[8,32,128]{2,1,0:T(8,128)}, f32[1024,128]{1,0:T(8,128)}) custom-call(s32[1]{0:T(128)} %bitcast.refs_0_.own_ref, s32[4]{0:T(128)} %refs_1_.7, f32[32,48,128]{2,1,0:T(8,128)} %copy-done.3, bf16[2,128,256]{2,1,0:T(8,128)(2,1)} %constant.29.clone.refs_3_, ...), custom_call_target="tpu_custom_call" | custom-call | flops 3221225472 | bytes 786432 | tf_op jit(solution)/shard_map/wave_band/pallas_call | solution.py:556
  102.2 2.6 %all-to-all-start.2 = ((f32[32,4,8,128]{3,2,1,0:T(8,128)}), f32[32,4,8,128]{3,2,1,0:T(8,128)S(1)}, u32[]{:S(2)}, u32[]{:S(2)}) async-start(f32[32,4,8,128]{3,2,1,0:T(8,128)} %bitcast.5), calls=%async_computation.2 | async-start | bytes 1048576 | tf_op jit(solution)/shard_map/all_to_all | solution.py:678
  104.8 16.3 %all-to-all-done.2.came_ref = f32[32,4,8,128]{3,2,1,0:T(8,128)S(1)} async-done(((f32[32,4,8,128]{3,2,1,0:T(8,128)}), f32[32,4,8,128]{3,2,1,0:T(8,128)S(1)}, u32[]{:S(2)}, u32[]{:S(2)}) %all-to-all-start.2) | async-done | bytes 524320 | tf_op jit(solution)/shard_map/all_to_all | solution.py:678
  121.1 0.8 copy-done
  121.9 4.8 %poisson.1 = f32[32,4,8,128]{3,2,1,0:T(8,128)} custom-call(s32[1]{0:T(128)} %bitcast.1.first_ref, f32[32,4,8,128]{3,2,1,0:T(8,128)} %copy-done, bf16[2,512,256]{2,1,0:T(8,128)(2,1)} %constant.33.clone.forth_ref, bf16[2,512,256]{2,1,0:T(8,128)(2,1)} %constant.34.clone.back_ref, bf16[2,128,256]{2,1,0:T(8,128)(2,1)} %constant.35.clone.both_x_ref), custom_call_target="tpu_custom_call" | custom-call | tf_op jit(solution)/shard_map/poisson/pallas_call | solution.py:640
  126.7 2.8 %all-to-all-start.3 = ((f32[32,4,8,128]{3,2,1,0:T(8,128)}), f32[32,4,8,128]{3,2,1,0:T(8,128)S(1)}, u32[]{:S(2)}, u32[]{:S(2)}) async-start(f32[32,4,8,128]{3,2,1,0:T(8,128)} %poisson.1), calls=%async_computation.3 | async-start | bytes 1048576 | tf_op jit(solution)/shard_map/all_to_all | solution.py:678
  129.4 0.0 copy-done.9
  129.4 1.7 %collective-permute-start = (f32[8,32,128]{2,1,0:T(8,128)S(1)}, f32[8,32,128]{2,1,0:T(8,128)S(1)}, u32[]{:S(2)}, u32[]{:S(2)}) collective-permute-start(f32[8,32,128]{2,1,0:T(8,128)S(1)} %copy-done.9), channel_id=1, source_target_pairs={{0,8},{8,16},{16,24},{24,0},{1,9},{9,17},{17,25},{25,1},{2,10},{10... | collective-permute-start | bytes 393224 | tf_op jit(solution)/shard_map/ppermute | solution.py:729
  131.1 0.0 copy-done.8
  131.1 1.5 %collective-permute-start.1 = (f32[8,32,128]{2,1,0:T(8,128)S(1)}, f32[8,32,128]{2,1,0:T(8,128)S(1)}, u32[]{:S(2)}, u32[]{:S(2)}) collective-permute-start(f32[8,32,128]{2,1,0:T(8,128)S(1)} %copy-done.8), channel_id=1, source_target_pairs={{0,16},{8,24},{16,0},{24,8},{1,17},{9,25},{17,1},{25,9},{2,18},{10... | collective-permute-start | bytes 393224 | tf_op jit(solution)/shard_map/ppermute | solution.py:729
  132.6 0.0 copy-done.7
  132.6 1.4 collective-permute-start.2
  134.1 6.2 %collective-permute-done.refs_1_ = f32[8,32,128]{2,1,0:T(8,128)S(1)} collective-permute-done((f32[8,32,128]{2,1,0:T(8,128)S(1)}, f32[8,32,128]{2,1,0:T(8,128)S(1)}, u32[]{:S(2)}, u32[]{:S(2)}) %collective-permute-start) | collective-permute-done | bytes 131104 | tf_op jit(solution)/shard_map/ppermute | solution.py:729
  140.3 2.9 %collective-permute-done.1.refs_2_ = f32[8,32,128]{2,1,0:T(8,128)S(1)} collective-permute-done((f32[8,32,128]{2,1,0:T(8,128)S(1)}, f32[8,32,128]{2,1,0:T(8,128)S(1)}, u32[]{:S(2)}, u32[]{:S(2)}) %collective-permute-start.1) | collective-permute-done | bytes 131104 | tf_op jit(solution)/shard_map/ppermute | solution.py:729
  143.2 0.0 collective-permute-done.2.refs_3_
  143.2 2.6 %all-to-all-done.3 = f32[32,4,8,128]{3,2,1,0:T(8,128)S(1)} async-done(((f32[32,4,8,128]{3,2,1,0:T(8,128)}), f32[32,4,8,128]{3,2,1,0:T(8,128)S(1)}, u32[]{:S(2)}, u32[]{:S(2)}) %all-to-all-start.3) | async-done | bytes 524320 | tf_op jit(solution)/shard_map/all_to_all | solution.py:678
  145.8 0.0 copy-done.4
  145.8 0.0 copy-done.5
  145.8 0.0 copy-done.6
  145.8 0.8 copy-done.1
  146.6 2.6 %finish.1 = (f32[32,32,128]{2,1,0:T(8,128)}, f32[32,32,128]{2,1,0:T(8,128)}) custom-call(s32[1]{0:T(128)} %bitcast.refs_0_.own_ref, f32[1024,128]{1,0:T(8,128)} %bitcast.4, bf16[2,128,128]{2,1,0:T(8,128)(2,1)} %constant.32.clone.back_ref, f32[8,32,128]{2,1,0:T(8,128)} %get-tuple-element.12.refs_0_, f32[8,32,128]{2,1,0:T(8,128)} %copy-done.4, ...), custom_call_target="tpu_custom_call" | custom-call | tf_op jit(solution)/shard_map/finish/pallas_call | solution.py:667
  (9 shorter events, 0.0 us)
Async XLA Ops:
  27.4 32.9 %all-to-all-start.1 = ((f32[32,56,128]{2,1,0:T(8,128)}), f32[32,56,128]{2,1,0:T(8,128)S(1)}, u32[]{:S(2)}, u32[]{:S(2)}) async-start(f32[32,56,128]{2,1,0:T(8,128)} %pack_band.3), calls=%async_computation.1 | async-start | bytes 1835008 | tf_op jit(solution)/shard_map/all_to_all | solution.py:678
  60.3 5.9 %copy-start.2 = (f32[32,56,128]{2,1,0:T(8,128)}, f32[32,56,128]{2,1,0:T(8,128)S(1)}, u32[]{:S(2)}) copy-start(f32[32,56,128]{2,1,0:T(8,128)S(1)} %all-to-all-done.1.refs_2_) | copy-start | bytes 2752516
  60.3 27.8 %all-to-all-start = ((f32[32,48,128]{2,1,0:T(8,128)}), f32[32,48,128]{2,1,0:T(8,128)S(1)}, u32[]{:S(2)}, u32[]{:S(2)}) async-start(f32[32,48,128]{2,1,0:T(8,128)} %pack_band.2), calls=%async_computation | async-start | bytes 1572864 | tf_op jit(solution)/shard_map/all_to_all | solution.py:678
  88.1 0.9 copy-start.3
  102.2 19.0 %all-to-all-start.2 = ((f32[32,4,8,128]{3,2,1,0:T(8,128)}), f32[32,4,8,128]{3,2,1,0:T(8,128)S(1)}, u32[]{:S(2)}, u32[]{:S(2)}) async-start(f32[32,4,8,128]{3,2,1,0:T(8,128)} %bitcast.5), calls=%async_computation.2 | async-start | bytes 1048576 | tf_op jit(solution)/shard_map/all_to_all | solution.py:678
  121.1 0.8 copy-start
  126.7 2.8 %copy-start.9 = (f32[8,32,128]{2,1,0:T(8,128)S(1)}, f32[8,32,128]{2,1,0:T(8,128)}, u32[]{:S(2)}) copy-start(f32[8,32,128]{2,1,0:T(8,128)} %get-tuple-element.13) | copy-start | bytes 393220
  126.7 4.5 %copy-start.8 = (f32[8,32,128]{2,1,0:T(8,128)S(1)}, f32[8,32,128]{2,1,0:T(8,128)}, u32[]{:S(2)}) copy-start(f32[8,32,128]{2,1,0:T(8,128)} %get-tuple-element.14) | copy-start | bytes 393220
  126.7 6.0 %copy-start.7 = (f32[8,32,128]{2,1,0:T(8,128)S(1)}, f32[8,32,128]{2,1,0:T(8,128)}, u32[]{:S(2)}) copy-start(f32[8,32,128]{2,1,0:T(8,128)} %get-tuple-element.15) | copy-start | bytes 393220
  126.7 19.1 %all-to-all-start.3 = ((f32[32,4,8,128]{3,2,1,0:T(8,128)}), f32[32,4,8,128]{3,2,1,0:T(8,128)S(1)}, u32[]{:S(2)}, u32[]{:S(2)}) async-start(f32[32,4,8,128]{3,2,1,0:T(8,128)} %poisson.1), calls=%async_computation.3 | async-start | bytes 1048576 | tf_op jit(solution)/shard_map/all_to_all | solution.py:678
  129.4 10.8 %collective-permute-start = (f32[8,32,128]{2,1,0:T(8,128)S(1)}, f32[8,32,128]{2,1,0:T(8,128)S(1)}, u32[]{:S(2)}, u32[]{:S(2)}) collective-permute-start(f32[8,32,128]{2,1,0:T(8,128)S(1)} %copy-done.9), channel_id=1, source_target_pairs={{0,8},{8,16},{16,24},{24,0},{1,9},{9,17},{17,25},{25,1},{2,10},{10... | collective-permute-start | bytes 393224 | tf_op jit(solution)/shard_map/ppermute | solution.py:729
  131.1 12.0 %collective-permute-start.1 = (f32[8,32,128]{2,1,0:T(8,128)S(1)}, f32[8,32,128]{2,1,0:T(8,128)S(1)}, u32[]{:S(2)}, u32[]{:S(2)}) collective-permute-start(f32[8,32,128]{2,1,0:T(8,128)S(1)} %copy-done.8), channel_id=1, source_target_pairs={{0,16},{8,24},{16,0},{24,8},{1,17},{9,25},{17,1},{25,9},{2,18},{10... | collective-permute-start | bytes 393224 | tf_op jit(solution)/shard_map/ppermute | solution.py:729
  132.6 10.5 %collective-permute-start.2 = (f32[8,32,128]{2,1,0:T(8,128)S(1)}, f32[8,32,128]{2,1,0:T(8,128)S(1)}, u32[]{:S(2)}, u32[]{:S(2)}) collective-permute-start(f32[8,32,128]{2,1,0:T(8,128)S(1)} %copy-done.7), channel_id=1, source_target_pairs={{0,24},{8,0},{16,8},{24,16},{1,25},{9,1},{17,9},{25,17},{2,26},{10... | collective-permute-start | bytes 393224 | tf_op jit(solution)/shard_map/ppermute | solution.py:729
  140.3 5.5 %copy-start.4 = (f32[8,32,128]{2,1,0:T(8,128)}, f32[8,32,128]{2,1,0:T(8,128)S(1)}, u32[]{:S(2)}) copy-start(f32[8,32,128]{2,1,0:T(8,128)S(1)} %collective-permute-done.refs_1_) | copy-start | bytes 393220
  143.2 2.6 %copy-start.5 = (f32[8,32,128]{2,1,0:T(8,128)}, f32[8,32,128]{2,1,0:T(8,128)S(1)}, u32[]{:S(2)}) copy-start(f32[8,32,128]{2,1,0:T(8,128)S(1)} %collective-permute-done.1.refs_2_) | copy-start | bytes 393220
  143.2 2.6 %copy-start.6 = (f32[8,32,128]{2,1,0:T(8,128)}, f32[8,32,128]{2,1,0:T(8,128)S(1)}, u32[]{:S(2)}) copy-start(f32[8,32,128]{2,1,0:T(8,128)S(1)} %collective-permute-done.2.refs_3_) | copy-start | bytes 393220
  145.8 0.8 copy-start.1

commit v4 on v3

--- a/solution.py
+++ b/solution.py
@@ -283,7 +283,7 @@
 
 
 def one_hot_lanes(row, lanes):
-    column = spread_lanes(row.astype(jnp.float32)).astype(jnp.bfloat16)
+    column = spread_lanes(row.astype(jnp.float32).astype(jnp.bfloat16))
     step = lax.broadcasted_iota(jnp.int32, column.shape, 1)
     one = jnp.ones(column.shape, jnp.bfloat16)
     zero = jnp.zeros(column.shape, jnp.bfloat16)
@@ -361,8 +361,10 @@
         tile = pencils[:, t * LANES : (t + 1) * LANES].reshape(count, rows, LANES)
         out_ref[:, t * rows : (t + 1) * rows] = tile
     if has_column:
-        column = column_ref[...].astype(jnp.float32)
-        column = [column[:, t * LANES : (t + 1) * LANES] for t in range(tiles)]
+        column = [
+            column_ref[t * LANES : (t + 1) * LANES].astype(jnp.float32).reshape(1, LANES)
+            for t in range(tiles)
+        ]
         blank = [jnp.zeros((8 - tiles, LANES), jnp.float32)]
         column = jnp.concatenate(column + blank, axis=0)
         out_ref[:, tiles * rows :] = jnp.broadcast_to(column[None], (count, 8, LANES))
@@ -699,7 +701,7 @@
     scale = 2.0 / (column_slot.shape[1] * pws)
     arrived = []
     for band in range(band_count):
-        column = column_map.reshape(1, slots) if band == 0 else None
+        column = column_map if band == 0 else None
         packed = pack_band(
             band, count, band_coeffs, miller_third, column_slot, pencil, slots, column
         )

time: 150 us -> 148 us (0.987)
  no operation moved by 1% of the time
where the time goes in v4:
time: 148 us; the launch traced here: 147 us
  Pallas kernels  81.2 us (55%)
  waiting for transfers between devices  39.6 us (27%)
  starting transfers between devices  23.1 us (16%)
  local copies, waits for them, and re-layouts  2.5 us (2%)
    pallas_call x2, Pallas kernels, pack_band(): pl.pallas_call(functools.partial(pack_kernel, width, column is not None),...  50.3 us
    all_to_all x4, waiting for transfers between devices, exchange(): return lax.all_to_all(array, axes, split_axis=0, concat_axis=0, tiled=True)  30.5 us
    pallas_call x2, Pallas kernels, wave_band(): pl.pallas_call(functools.partial(wave_kernel, kpts, tiles, scale, is_firs...  23.6 us
    all_to_all x4, starting transfers between devices, exchange(): return lax.all_to_all(array, axes, split_axis=0, concat_axis=0, tiled=True)  18.5 us
    ppermute x3, waiting for transfers between devices, local_planes(): lax.ppermute(made_here[s], 'kpt', [(a, (a + s) % kpts) for a in range(kpt...  9.07 us
    pallas_call x1, Pallas kernels, poisson(): pl.pallas_call(functools.partial(poisson_kernel, pws), in_specs=[pl.Block...  4.75 us
    ppermute x3, starting transfers between devices, local_planes(): lax.ppermute(made_here[s], 'kpt', [(a, (a + s) % kpts) for a in range(kpt...  4.63 us
  transfers between devices with their start and end apart: 7, of which 5 were waited for; matrix products, arithmetic and copies ran while one was open for 0% of the time, Pallas kernels for 24%

profile of v4, /device:TPU:0, one launch (start us, length us, event | category | flops | bytes accessed | tf_op | source)
XLA Modules:
  0.0 147.1 jit_solution(33934997162516151)
XLA Ops:
  0.6 25.1 %pack_band.3 = f32[32,56,128]{2,1,0:T(8,128)} custom-call(f32[1,2,2,49152]{3,2,1,0:T(2,128)} %refs_0_.3, s32[1,49152]{1,0:T(1,128)} %refs_1_.5, s32[1,49152]{1,0:T(1,128)} %refs_2_.3, bf16[2,512,256]{2,1,0:T(8,128)(2,1)} %constant.28.clone.refs_3_, s32[384]{0:T(512)} %refs_4_.3), custom_call_target="tpu_custom_call" | custom-call | flops 19327352832 | bytes 786432 | tf_op jit(solution)/shard_map/pack_band/pallas_call | solution.py:382
  25.8 7.3 %all-to-all-start.1 = ((f32[32,56,128]{2,1,0:T(8,128)}), f32[32,56,128]{2,1,0:T(8,128)S(1)}, u32[]{:S(2)}, u32[]{:S(2)}) async-start(f32[32,56,128]{2,1,0:T(8,128)} %pack_band.3), calls=%async_computation.1 | async-start | bytes 1835008 | tf_op jit(solution)/shard_map/all_to_all | solution.py:680
  33.1 25.2 %pack_band.2 = f32[32,48,128]{2,1,0:T(8,128)} custom-call(f32[1,2,2,49152]{3,2,1,0:T(2,128)} %refs_0_.3, s32[1,49152]{1,0:T(1,128)} %refs_1_.5, s32[1,49152]{1,0:T(1,128)} %refs_2_.3, bf16[2,512,256]{2,1,0:T(8,128)(2,1)} %constant.28.clone.refs_3_), custom_call_target="tpu_custom_call" | custom-call | flops 19327352832 | bytes 786432 | tf_op jit(solution)/shard_map/pack_band/pallas_call | solution.py:382
  58.3 0.0 all-to-all-done.1.refs_2_
  58.3 0.0 copy-start.2
  58.3 5.8 %all-to-all-start = ((f32[32,48,128]{2,1,0:T(8,128)}), f32[32,48,128]{2,1,0:T(8,128)S(1)}, u32[]{:S(2)}, u32[]{:S(2)}) async-start(f32[32,48,128]{2,1,0:T(8,128)} %pack_band.2), calls=%async_computation | async-start | bytes 1572864 | tf_op jit(solution)/shard_map/all_to_all | solution.py:680
  64.1 0.0 copy-done.2
  64.1 10.4 %wave_band.2 = (f32[8,128,128]{2,1,0:T(8,128)}, f32[1,3072]{1,0:T(1,128)}) custom-call(s32[1]{0:T(128)} %bitcast.refs_0_.own_ref, s32[4]{0:T(128)} %refs_1_.7, f32[32,56,128]{2,1,0:T(8,128)} %copy-done.2, bf16[2,128,256]{2,1,0:T(8,128)(2,1)} %constant.29.clone.refs_3_, bf16[2,256,128]{2,1,0:T(8,128)(2,1)} %constant.30.clone.refs_4_), custom_call_target="tpu_custom_call" | custom-call | flops 3221225472 | bytes 917504 | tf_op jit(solution)/shard_map/wave_band/pallas_call | solution.py:558
  74.6 11.5 %all-to-all-done.refs_2_ = f32[32,48,128]{2,1,0:T(8,128)S(1)} async-done(((f32[32,48,128]{2,1,0:T(8,128)}), f32[32,48,128]{2,1,0:T(8,128)S(1)}, u32[]{:S(2)}, u32[]{:S(2)}) %all-to-all-start) | async-done | bytes 786464 | tf_op jit(solution)/shard_map/all_to_all | solution.py:680
  86.1 0.0 copy-start.3
  86.1 0.9 copy-done.3
  87.0 13.1 %wave_band.3 = (f32[8,32,128]{2,1,0:T(8,128)}, f32[8,32,128]{2,1,0:T(8,128)}, f32[8,32,128]{2,1,0:T(8,128)}, f32[8,32,128]{2,1,0:T(8,128)}, f32[1024,128]{1,0:T(8,128)}) custom-call(s32[1]{0:T(128)} %bitcast.refs_0_.own_ref, s32[4]{0:T(128)} %refs_1_.7, f32[32,48,128]{2,1,0:T(8,128)} %copy-done.3, bf16[2,128,256]{2,1,0:T(8,128)(2,1)} %constant.29.clone.refs_3_, ...), custom_call_target="tpu_custom_call" | custom-call | flops 3221225472 | bytes 786432 | tf_op jit(solution)/shard_map/wave_band/pallas_call | solution.py:558
  100.1 2.6 %all-to-all-start.2 = ((f32[32,4,8,128]{3,2,1,0:T(8,128)}), f32[32,4,8,128]{3,2,1,0:T(8,128)S(1)}, u32[]{:S(2)}, u32[]{:S(2)}) async-start(f32[32,4,8,128]{3,2,1,0:T(8,128)} %bitcast.5), calls=%async_computation.2 | async-start | bytes 1048576 | tf_op jit(solution)/shard_map/all_to_all | solution.py:680
  102.8 16.3 %all-to-all-done.2.came_ref = f32[32,4,8,128]{3,2,1,0:T(8,128)S(1)} async-done(((f32[32,4,8,128]{3,2,1,0:T(8,128)}), f32[32,4,8,128]{3,2,1,0:T(8,128)S(1)}, u32[]{:S(2)}, u32[]{:S(2)}) %all-to-all-start.2) | async-done | bytes 524320 | tf_op jit(solution)/shard_map/all_to_all | solution.py:680
  119.1 0.8 copy-done
  119.9 4.8 %poisson.1 = f32[32,4,8,128]{3,2,1,0:T(8,128)} custom-call(s32[1]{0:T(128)} %bitcast.1.first_ref, f32[32,4,8,128]{3,2,1,0:T(8,128)} %copy-done, bf16[2,512,256]{2,1,0:T(8,128)(2,1)} %constant.33.clone.forth_ref, bf16[2,512,256]{2,1,0:T(8,128)(2,1)} %constant.34.clone.back_ref, bf16[2,128,256]{2,1,0:T(8,128)(2,1)} %constant.35.clone.both_x_ref), custom_call_target="tpu_custom_call" | custom-call | tf_op jit(solution)/shard_map/poisson/pallas_call | solution.py:642
  124.6 2.8 %all-to-all-start.3 = ((f32[32,4,8,128]{3,2,1,0:T(8,128)}), f32[32,4,8,128]{3,2,1,0:T(8,128)S(1)}, u32[]{:S(2)}, u32[]{:S(2)}) async-start(f32[32,4,8,128]{3,2,1,0:T(8,128)} %poisson.1), calls=%async_computation.3 | async-start | bytes 1048576 | tf_op jit(solution)/shard_map/all_to_all | solution.py:680
  127.4 0.0 copy-done.9
  127.4 1.7 %collective-permute-start = (f32[8,32,128]{2,1,0:T(8,128)S(1)}, f32[8,32,128]{2,1,0:T(8,128)S(1)}, u32[]{:S(2)}, u32[]{:S(2)}) collective-permute-start(f32[8,32,128]{2,1,0:T(8,128)S(1)} %copy-done.9), channel_id=1, source_target_pairs={{0,8},{8,16},{16,24},{24,0},{1,9},{9,17},{17,25},{25,1},{2,10},{10... | collective-permute-start | bytes 393224 | tf_op jit(solution)/shard_map/ppermute | solution.py:731
  129.1 0.0 copy-done.8
  129.1 1.5 %collective-permute-start.1 = (f32[8,32,128]{2,1,0:T(8,128)S(1)}, f32[8,32,128]{2,1,0:T(8,128)S(1)}, u32[]{:S(2)}, u32[]{:S(2)}) collective-permute-start(f32[8,32,128]{2,1,0:T(8,128)S(1)} %copy-done.8), channel_id=1, source_target_pairs={{0,16},{8,24},{16,0},{24,8},{1,17},{9,25},{17,1},{25,9},{2,18},{10... | collective-permute-start | bytes 393224 | tf_op jit(solution)/shard_map/ppermute | solution.py:731
  130.6 0.0 copy-done.7
  130.6 1.4 collective-permute-start.2
  132.1 6.2 %collective-permute-done.refs_1_ = f32[8,32,128]{2,1,0:T(8,128)S(1)} collective-permute-done((f32[8,32,128]{2,1,0:T(8,128)S(1)}, f32[8,32,128]{2,1,0:T(8,128)S(1)}, u32[]{:S(2)}, u32[]{:S(2)}) %collective-permute-start) | collective-permute-done | bytes 131104 | tf_op jit(solution)/shard_map/ppermute | solution.py:731
  138.2 2.9 %collective-permute-done.1.refs_2_ = f32[8,32,128]{2,1,0:T(8,128)S(1)} collective-permute-done((f32[8,32,128]{2,1,0:T(8,128)S(1)}, f32[8,32,128]{2,1,0:T(8,128)S(1)}, u32[]{:S(2)}, u32[]{:S(2)}) %collective-permute-start.1) | collective-permute-done | bytes 131104 | tf_op jit(solution)/shard_map/ppermute | solution.py:731
  141.1 0.0 collective-permute-done.2.refs_3_
  141.1 2.6 %all-to-all-done.3 = f32[32,4,8,128]{3,2,1,0:T(8,128)S(1)} async-done(((f32[32,4,8,128]{3,2,1,0:T(8,128)}), f32[32,4,8,128]{3,2,1,0:T(8,128)S(1)}, u32[]{:S(2)}, u32[]{:S(2)}) %all-to-all-start.3) | async-done | bytes 524320 | tf_op jit(solution)/shard_map/all_to_all | solution.py:680
  143.8 0.0 copy-done.4
  143.8 0.0 copy-done.5
  143.8 0.0 copy-done.6
  143.8 0.8 copy-done.1
  144.6 2.6 %finish.1 = (f32[32,32,128]{2,1,0:T(8,128)}, f32[32,32,128]{2,1,0:T(8,128)}) custom-call(s32[1]{0:T(128)} %bitcast.refs_0_.own_ref, f32[1024,128]{1,0:T(8,128)} %bitcast.4, bf16[2,128,128]{2,1,0:T(8,128)(2,1)} %constant.32.clone.back_ref, f32[8,32,128]{2,1,0:T(8,128)} %get-tuple-element.12.refs_0_, f32[8,32,128]{2,1,0:T(8,128)} %copy-done.4, ...), custom_call_target="tpu_custom_call" | custom-call | tf_op jit(solution)/shard_map/finish/pallas_call | solution.py:669
  (8 shorter events, 0.0 us)
Async XLA Ops:
  25.8 32.5 %all-to-all-start.1 = ((f32[32,56,128]{2,1,0:T(8,128)}), f32[32,56,128]{2,1,0:T(8,128)S(1)}, u32[]{:S(2)}, u32[]{:S(2)}) async-start(f32[32,56,128]{2,1,0:T(8,128)} %pack_band.3), calls=%async_computation.1 | async-start | bytes 1835008 | tf_op jit(solution)/shard_map/all_to_all | solution.py:680
  58.3 5.9 %copy-start.2 = (f32[32,56,128]{2,1,0:T(8,128)}, f32[32,56,128]{2,1,0:T(8,128)S(1)}, u32[]{:S(2)}) copy-start(f32[32,56,128]{2,1,0:T(8,128)S(1)} %all-to-all-done.1.refs_2_) | copy-start | bytes 2752516
  58.3 27.8 %all-to-all-start = ((f32[32,48,128]{2,1,0:T(8,128)}), f32[32,48,128]{2,1,0:T(8,128)S(1)}, u32[]{:S(2)}, u32[]{:S(2)}) async-start(f32[32,48,128]{2,1,0:T(8,128)} %pack_band.2), calls=%async_computation | async-start | bytes 1572864 | tf_op jit(solution)/shard_map/all_to_all | solution.py:680
  86.1 0.9 copy-start.3
  100.1 19.0 %all-to-all-start.2 = ((f32[32,4,8,128]{3,2,1,0:T(8,128)}), f32[32,4,8,128]{3,2,1,0:T(8,128)S(1)}, u32[]{:S(2)}, u32[]{:S(2)}) async-start(f32[32,4,8,128]{3,2,1,0:T(8,128)} %bitcast.5), calls=%async_computation.2 | async-start | bytes 1048576 | tf_op jit(solution)/shard_map/all_to_all | solution.py:680
  119.1 0.8 copy-start
  124.6 2.8 %copy-start.9 = (f32[8,32,128]{2,1,0:T(8,128)S(1)}, f32[8,32,128]{2,1,0:T(8,128)}, u32[]{:S(2)}) copy-start(f32[8,32,128]{2,1,0:T(8,128)} %get-tuple-element.13) | copy-start | bytes 393220
  124.6 4.5 %copy-start.8 = (f32[8,32,128]{2,1,0:T(8,128)S(1)}, f32[8,32,128]{2,1,0:T(8,128)}, u32[]{:S(2)}) copy-start(f32[8,32,128]{2,1,0:T(8,128)} %get-tuple-element.14) | copy-start | bytes 393220
  124.6 6.0 %copy-start.7 = (f32[8,32,128]{2,1,0:T(8,128)S(1)}, f32[8,32,128]{2,1,0:T(8,128)}, u32[]{:S(2)}) copy-start(f32[8,32,128]{2,1,0:T(8,128)} %get-tuple-element.15) | copy-start | bytes 393220
  124.6 19.1 %all-to-all-start.3 = ((f32[32,4,8,128]{3,2,1,0:T(8,128)}), f32[32,4,8,128]{3,2,1,0:T(8,128)S(1)}, u32[]{:S(2)}, u32[]{:S(2)}) async-start(f32[32,4,8,128]{3,2,1,0:T(8,128)} %poisson.1), calls=%async_computation.3 | async-start | bytes 1048576 | tf_op jit(solution)/shard_map/all_to_all | solution.py:680
  127.4 10.8 %collective-permute-start = (f32[8,32,128]{2,1,0:T(8,128)S(1)}, f32[8,32,128]{2,1,0:T(8,128)S(1)}, u32[]{:S(2)}, u32[]{:S(2)}) collective-permute-start(f32[8,32,128]{2,1,0:T(8,128)S(1)} %copy-done.9), channel_id=1, source_target_pairs={{0,8},{8,16},{16,24},{24,0},{1,9},{9,17},{17,25},{25,1},{2,10},{10... | collective-permute-start | bytes 393224 | tf_op jit(solution)/shard_map/ppermute | solution.py:731
  129.1 12.0 %collective-permute-start.1 = (f32[8,32,128]{2,1,0:T(8,128)S(1)}, f32[8,32,128]{2,1,0:T(8,128)S(1)}, u32[]{:S(2)}, u32[]{:S(2)}) collective-permute-start(f32[8,32,128]{2,1,0:T(8,128)S(1)} %copy-done.8), channel_id=1, source_target_pairs={{0,16},{8,24},{16,0},{24,8},{1,17},{9,25},{17,1},{25,9},{2,18},{10... | collective-permute-start | bytes 393224 | tf_op jit(solution)/shard_map/ppermute | solution.py:731
  130.6 10.5 %collective-permute-start.2 = (f32[8,32,128]{2,1,0:T(8,128)S(1)}, f32[8,32,128]{2,1,0:T(8,128)S(1)}, u32[]{:S(2)}, u32[]{:S(2)}) collective-permute-start(f32[8,32,128]{2,1,0:T(8,128)S(1)} %copy-done.7), channel_id=1, source_target_pairs={{0,24},{8,0},{16,8},{24,16},{1,25},{9,1},{17,9},{25,17},{2,26},{10... | collective-permute-start | bytes 393224 | tf_op jit(solution)/shard_map/ppermute | solution.py:731
  138.2 5.5 %copy-start.4 = (f32[8,32,128]{2,1,0:T(8,128)}, f32[8,32,128]{2,1,0:T(8,128)S(1)}, u32[]{:S(2)}) copy-start(f32[8,32,128]{2,1,0:T(8,128)S(1)} %collective-permute-done.refs_1_) | copy-start | bytes 393220
  141.1 2.6 %copy-start.5 = (f32[8,32,128]{2,1,0:T(8,128)}, f32[8,32,128]{2,1,0:T(8,128)S(1)}, u32[]{:S(2)}) copy-start(f32[8,32,128]{2,1,0:T(8,128)S(1)} %collective-permute-done.1.refs_2_) | copy-start | bytes 393220
  141.1 2.6 %copy-start.6 = (f32[8,32,128]{2,1,0:T(8,128)}, f32[8,32,128]{2,1,0:T(8,128)S(1)}, u32[]{:S(2)}) copy-start(f32[8,32,128]{2,1,0:T(8,128)S(1)} %collective-permute-done.2.refs_3_) | copy-start | bytes 393220
  143.8 0.8 copy-start.1

commit v5 on v4

--- a/solution.py
+++ b/solution.py
@@ -296,49 +296,163 @@
     )
 
 
+RANK_LOW = 64
+WINDOW = 64
+
+
+def exchange_rows(refs, low_bits, size_bits, descending):
+    for outer in range(RANK_LOW):
+        if any(outer >> bit & 1 for bit in low_bits[0]):
+            continue
+        touched = sorted(
+            outer + sum(1 << bit for i, bit in enumerate(low_bits[0]) if pattern >> i & 1)
+            for pattern in range(1 << len(low_bits[0]))
+        )
+        held = {v: [ref[v * 8 : v * 8 + 8, :] for ref in refs] for v in touched}
+        for size, bits in zip(size_bits, low_bits[1:]):
+            for bit in bits:
+                for v in touched:
+                    if v >> bit & 1:
+                        continue
+                    former, latter = held[v], held[v | 1 << bit]
+                    if size < 6:
+                        down = bool(v >> size & 1)
+                        swap = former[0] < latter[0] if down else former[0] > latter[0]
+                    else:
+                        swap = former[0] > latter[0]
+                        if descending is not None:
+                            swap = jnp.logical_xor(swap, descending)
+                    held[v] = [jnp.where(swap, y, x) for x, y in zip(former, latter)]
+                    held[v | 1 << bit] = [jnp.where(swap, x, y) for x, y in zip(former, latter)]
+        for v in touched:
+            for ref, value in zip(refs, held[v]):
+                ref[v * 8 : v * 8 + 8, :] = value
+
+
+def exchange_sublanes(refs, stride, descending):
+    sublane = lax.broadcasted_iota(jnp.int32, (8, LANES), 0)
+    upper = sublane // stride % 2 == 1
+    want_least = upper if descending is not None else jnp.logical_not(upper)
+    if descending is not None:
+        want_least = jnp.logical_not(jnp.logical_xor(upper, descending))
+
+    def partner(value):
+        if stride == 4:
+            return pltpu.roll(value, 4, 0)
+        return jnp.where(upper, pltpu.roll(value, stride, 0), pltpu.roll(value, 8 - stride, 0))
+
+    for v in range(RANK_LOW):
+        here = [ref[v * 8 : v * 8 + 8, :] for ref in refs]
+        there = [partner(value) for value in here]
+        take = jnp.where(
+            want_least, (here[0] > there[0]).astype(jnp.int32), (here[0] < there[0]).astype(jnp.int32)
+        )
+        take = take == 1
+        for ref, x, y in zip(refs, here, there):
+            ref[v * 8 : v * 8 + 8, :] = jnp.where(take, y, x)
+
+
+def sort_columns(refs):
+    sublane = lax.broadcasted_iota(jnp.int32, (8, LANES), 0)
+    exchange_rows(refs, [(0, 1, 2), (0,), (1, 0), (2, 1, 0)], [1, 2, 3], None)
+    exchange_rows(refs, [(3,), (3,)], [4], None)
+    exchange_rows(refs, [(0, 1, 2), (2, 1, 0)], [4], None)
+    exchange_rows(refs, [(3, 4), (4, 3)], [5], None)
+    exchange_rows(refs, [(0, 1, 2), (2, 1, 0)], [5], None)
+    for size in range(6, 10):
+        descending = None if size == 9 else sublane // (1 << (size - 6)) % 2 == 1
+        for bit in range(size - 1, 5, -1):
+            exchange_sublanes(refs, 1 << (bit - 6), descending)
+        exchange_rows(refs, [(3, 4, 5), (5, 4, 3)], [size], descending)
+        exchange_rows(refs, [(0, 1, 2), (2, 1, 0)], [size], descending)
+
+
 def pack_kernel(width, has_column, *refs):
     coeff_ref, miller_ref, slot_ref, pencil_ref = refs[:4]
     rest = list(refs[4:])
     column_ref = rest.pop(0) if has_column else None
-    out_ref, total = rest
+    out_ref, total, key_ref, real_ref, imag_ref = rest
     half = total.shape[0] // 4
     slots = 2 * half
     count = out_ref.shape[0]
     rows = pencil_ref.shape[1] // count
-    size = miller_ref.shape[1]
-    step_width = 1024 if size % 1024 == 0 else size
-    together = 4 if size % (4 * step_width) == 0 else 1
-
-    zero = jnp.zeros((half, step_width), jnp.bfloat16)
-    steps = lax.broadcasted_iota(jnp.int32, (half, step_width), 0)
-    steps = steps.astype(jnp.float32).astype(jnp.bfloat16)
-
-    def add(step):
-        part = pl.ds(pl.multiple_of(step * step_width, step_width), step_width)
-        slot = slot_ref[:, part]
-        second = slot >= half
-        row = jnp.where(second, slot - half, slot).astype(jnp.float32).astype(jnp.bfloat16)
-        lane = miller_ref[:, part] + width // 2
-        lane = jnp.where(second, lane + width, lane)
-        here = row == steps
-        spread = jnp.concatenate(
-            [
-                jnp.where(here, piece[c : c + 1], zero)
-                for piece in pieces(coeff_ref[0, 0, :, part])
-                for c in range(2)
-            ],
-            axis=0,
-        )
-        total[...] += mul(spread, one_hot_lanes(lane, 2 * width), NN)
+    length = miller_ref.shape[0]
+    ranks = key_ref.shape[0]
+
+    slot = slot_ref[...]
+    second = slot >= half
+    lane = miller_ref[...] + width // 2
+    key = jnp.where(second, slot - half, slot) * (2 * width) + jnp.where(second, lane + width, lane)
+    key_ref[0:length] = key.astype(jnp.float32)
+    real_ref[0:length] = coeff_ref[0, pl.ds(0, length, stride=2), :]
+    imag_ref[0:length] = coeff_ref[0, pl.ds(1, length, stride=2), :]
+    blank = jnp.zeros((ranks - length, LANES), jnp.float32)
+    key_ref[length:] = blank + 2.0 * slots * width
+    real_ref[length:] = blank
+    imag_ref[length:] = blank
+    sort_columns((key_ref, real_ref, imag_ref))
+
+    def base_of(block):
+        base = 8 * (block // 2) + 8 * (block % 2) - WINDOW // 2
+        return jnp.minimum(jnp.maximum(base, 0), half - WINDOW)
+
+    sublane = lax.broadcasted_iota(jnp.int32, (8, LANES), 0)
+    astray = jnp.zeros((8, LANES), jnp.float32)
+    for v in range(RANK_LOW):
+        base = base_of(sublane * (RANK_LOW // 8) + v // 8) * (2 * width)
+        offset = key_ref[v * 8 : v * 8 + 8, :] - base.astype(jnp.float32)
+        outside = jnp.logical_or(offset < 0.0, offset >= 2.0 * width * WINDOW)
+        astray = jnp.where(outside, 1.0, astray)
+    astray = jnp.max(jnp.where(sublane * RANK_LOW < length, astray, 0.0))
+
+    def add(block, base, window):
+        first = block % (RANK_LOW // 8) * 64 + block // (RANK_LOW // 8)
+        where = pl.ds(first, 8, stride=8)
+        keys = key_ref[where, :]
+        high = jnp.floor(keys * (1.0 / (2 * width)))
+        lane = keys - high * (2.0 * width)
+        high = (high - base).astype(jnp.bfloat16)
+        values = [piece for ref in (real_ref, imag_ref) for piece in pieces(ref[where, :])]
+        values = [values[0], values[2], values[1], values[3]]
+        steps = lax.broadcasted_iota(jnp.int32, (window, LANES), 0)
+        steps = steps.astype(jnp.float32).astype(jnp.bfloat16)
+        zero = jnp.zeros((window, LANES), jnp.bfloat16)
+        spread, chosen = [], []
+        for t in range(8):
+            here = high[t : t + 1] == steps
+            spread.append(
+                jnp.concatenate([jnp.where(here, value[t : t + 1], zero) for value in values], axis=0)
+            )
+            chosen.append(one_hot_lanes(lane[t : t + 1], 2 * width))
+        found = mul(jnp.concatenate(spread, axis=1), jnp.concatenate(chosen, axis=0), NN)
+        for i in range(4):
+            if window == half:
+                into = pl.ds(i * half, half)
+            else:
+                into = pl.ds(pl.multiple_of(i * half + base, 8), window)
+            total[into, :] += found[i * window : (i + 1) * window]
 
     total[...] = jnp.zeros_like(total)
-
-    def some_steps(i, unused):
-        for s in range(together):
-            add(together * i + s)
-        return unused
-
-    lax.fori_loop(0, size // (together * step_width), some_steps, 0)
+    blocks = length // 8
+    together = 4 if blocks % 4 == 0 else 1
+
+    @pl.when(astray == 0.0)
+    def _():
+        def some_blocks(i, unused):
+            for s in range(together):
+                block = together * i + s
+                add(block, base_of(block), WINDOW)
+            return unused
+
+        lax.fori_loop(0, blocks // together, some_blocks, 0)
+
+    @pl.when(astray > 0.0)
+    def _():
+        def one_block(block, unused):
+            add(block, 0, half)
+            return unused
+
+        lax.fori_loop(0, blocks, one_block, 0)
 
     both = []
     for at in range(2):
@@ -371,14 +485,14 @@
 
 
 def pack_band(band, count, coeffs, miller, slot, pencil, slots, column):
-    total = miller.shape[1]
+    length = miller.shape[0]
     width = pencil.shape[2] // 2
     rows = pencil.shape[1] // count * (slots // LANES)
     operands = [coeffs, miller, slot, pencil]
     if column is not None:
         operands.append(column)
         rows += 8
-    one_band = pl.BlockSpec((1, 1, 2, total), lambda i: (0, band, 0, 0))
+    one_band = pl.BlockSpec((1, 2 * length, LANES), lambda i: (band, 0, 0))
     return pl.pallas_call(
         functools.partial(pack_kernel, width, column is not None),
         grid=(1,),
@@ -386,10 +500,13 @@
         + [pl.BlockSpec(x.shape, lambda i, n=x.ndim: (0,) * n) for x in operands[1:]],
         out_specs=pl.BlockSpec((count, rows, LANES), lambda i: (0, 0, 0)),
         out_shape=jax.ShapeDtypeStruct((count, rows, LANES), jnp.float32),
-        scratch_shapes=[pltpu.VMEM((2 * slots, 2 * width), jnp.float32)],
+        scratch_shapes=[pltpu.VMEM((2 * slots, 2 * width), jnp.float32)]
+        + [pltpu.VMEM((8 * RANK_LOW, LANES), jnp.float32)] * 3,
         compiler_params=pltpu.CompilerParams(vmem_limit_bytes=VMEM_LIMIT),
         cost_estimate=pl.CostEstimate(
-            flops=2 * total * slots * 4 * width, bytes_accessed=16 * total, transcendentals=0
+            flops=2 * length * LANES * slots * 4 * width,
+            bytes_accessed=16 * length * LANES,
+            transcendentals=0,
         ),
         name="pack_band",
     )(*operands)
@@ -698,12 +815,17 @@
     )
 
     tiles = slots // LANES
+    length = column_slot.shape[1] // LANES
+    coeffs = band_coeffs.reshape(band_count, 2, length, LANES).transpose(0, 2, 1, 3)
+    coeffs = coeffs.reshape(band_count, 2 * length, LANES)
+    miller = miller_third.reshape(length, LANES)
+    slot = column_slot.reshape(length, LANES)
     scale = 2.0 / (column_slot.shape[1] * pws)
     arrived = []
     for band in range(band_count):
         column = column_map if band == 0 else None
         packed = pack_band(
-            band, count, band_coeffs, miller_third, column_slot, pencil, slots, column
+            band, count, coeffs, miller, slot, pencil, slots, column
         )
         arrived.append(exchange(packed, everyone))
     own = lax.axis_index("kpt").astype(jnp.int32).reshape(1)
@@ -753,7 +875,7 @@
 
 def local(band_coeffs, miller_third, column_slot, column_map, kpoint_counts):
     slots = column_map.shape[0]
-    plain = slots % LANES == 0 and slots // LANES <= 8 and slots // 2 <= 256
+    plain = slots % LANES == 0 and LANES <= slots <= 8 * RANK_LOW
     plain = plain and column_slot.shape[1] == slots * LANES
     fits = plain and fits_planes(lax.axis_size("kpt"), lax.axis_size("pw"))
     chosen = local_planes if fits else local_general

time: 148 us -> 134 us (0.905)
  Pallas kernels: 81.2 us -> 61.4 us
  waiting for transfers between devices: 39.6 us -> 48.9 us
  starting transfers between devices: 23.1 us -> 20.1 us
    pallas_call x2, Pallas kernels: 50.3 us -> 30.5 us  [pack_band(): pl.pallas_call(functools.partial(pack_kernel, width, column is not None),...]
    all_to_all x4, waiting for transfers between devices: 30.5 us -> 39.8 us  [exchange(): return lax.all_to_all(array, axes, split_axis=0, concat_axis=0, tiled=True)]
    all_to_all x4, starting transfers between devices: 18.5 us -> 15.5 us  [exchange(): return lax.all_to_all(array, axes, split_axis=0, concat_axis=0, tiled=True)]
  transfers between devices with their start and end apart: 7 -> 7, of which waited for: 5 -> 6; matrix products, arithmetic and copies ran while one was open for 0% -> 0% of each run, Pallas kernels for 24% -> 19%
where the time goes in v5:
time: 134 us
  Pallas kernels  61.4 us (46%)
  waiting for transfers between devices  48.9 us (36%)
  starting transfers between devices  20.1 us (15%)
  local copies, waits for them, and re-layouts  2.5 us (2%)
    all_to_all x4, waiting for transfers between devices, exchange(): return lax.all_to_all(array, axes, split_axis=0, concat_axis=0, tiled=True)  39.8 us
    pallas_call x2, Pallas kernels, pack_band(): pl.pallas_call(functools.partial(pack_kernel, width, column is not None),...  30.5 us
    pallas_call x2, Pallas kernels, wave_band(): pl.pallas_call(functools.partial(wave_kernel, kpts, tiles, scale, is_firs...  23.6 us
    all_to_all x4, starting transfers between devices, exchange(): return lax.all_to_all(array, axes, split_axis=0, concat_axis=0, tiled=True)  15.5 us
    ppermute x3, waiting for transfers between devices, local_planes(): lax.ppermute(made_here[s], 'kpt', [(a, (a + s) % kpts) for a in range(kpt...  9.07 us
    pallas_call x1, Pallas kernels, poisson(): pl.pallas_call(functools.partial(poisson_kernel, pws), in_specs=[pl.Block...  4.75 us
    ppermute x3, starting transfers between devices, local_planes(): lax.ppermute(made_here[s], 'kpt', [(a, (a + s) % kpts) for a in range(kpt...  4.63 us
  transfers between devices with their start and end apart: 7, of which 6 were waited for; matrix products, arithmetic and copies ran while one was open for 0% of the time, Pallas kernels for 19%

profile of v5, /device:TPU:0, one launch (start us, length us, event | category | flops | bytes accessed | tf_op | source)
XLA Modules:
  0.0 133.6 jit_solution(6868636788814716075)
XLA Ops:
  0.6 15.3 %pack_band.3 = f32[32,56,128]{2,1,0:T(8,128)} custom-call(f32[2,768,128]{2,1,0:T(8,128)} %bitcast.13, s32[384,128]{1,0:T(8,128)} %bitcast.15, s32[384,128]{1,0:T(8,128)} %bitcast.17, bf16[2,512,256]{2,1,0:T(8,128)(2,1)} %constant.28.clone.refs_3_, s32[384]{0:T(512)} %refs_4_.3), custom_call_target="tpu_custom_call" | custom-call | flops 19327352832 | bytes 786432 | tf_op jit(solution)/shard_map/pack_band/pallas_call | solution.py:496
  15.9 7.3 %all-to-all-start.1 = ((f32[32,56,128]{2,1,0:T(8,128)}), f32[32,56,128]{2,1,0:T(8,128)S(1)}, u32[]{:S(2)}, u32[]{:S(2)}) async-start(f32[32,56,128]{2,1,0:T(8,128)} %pack_band.3), calls=%async_computation.1 | async-start | bytes 1835008 | tf_op jit(solution)/shard_map/all_to_all | solution.py:797
  23.2 15.3 %pack_band.2 = f32[32,48,128]{2,1,0:T(8,128)} custom-call(f32[2,768,128]{2,1,0:T(8,128)} %bitcast.14, s32[384,128]{1,0:T(8,128)} %bitcast.16, s32[384,128]{1,0:T(8,128)} %bitcast.18, bf16[2,512,256]{2,1,0:T(8,128)(2,1)} %constant.28.clone.refs_3_), custom_call_target="tpu_custom_call" | custom-call | flops 19327352832 | bytes 786432 | tf_op jit(solution)/shard_map/pack_band/pallas_call | solution.py:496
  38.5 9.5 %all-to-all-done.1.refs_2_ = f32[32,56,128]{2,1,0:T(8,128)S(1)} async-done(((f32[32,56,128]{2,1,0:T(8,128)}), f32[32,56,128]{2,1,0:T(8,128)S(1)}, u32[]{:S(2)}, u32[]{:S(2)}) %all-to-all-start.1) | async-done | bytes 917536 | tf_op jit(solution)/shard_map/all_to_all | solution.py:797
  48.0 0.0 copy-start.2
  48.0 2.8 %all-to-all-start = ((f32[32,48,128]{2,1,0:T(8,128)}), f32[32,48,128]{2,1,0:T(8,128)S(1)}, u32[]{:S(2)}, u32[]{:S(2)}) async-start(f32[32,48,128]{2,1,0:T(8,128)} %pack_band.2), calls=%async_computation | async-start | bytes 1572864 | tf_op jit(solution)/shard_map/all_to_all | solution.py:797
  50.8 0.0 copy-done.2
  50.8 10.4 %wave_band.2 = (f32[8,128,128]{2,1,0:T(8,128)}, f32[1,3072]{1,0:T(1,128)}) custom-call(s32[1]{0:T(128)} %bitcast.refs_0_.own_ref, s32[4]{0:T(128)} %refs_1_.3, f32[32,56,128]{2,1,0:T(8,128)} %copy-done.2, bf16[2,128,256]{2,1,0:T(8,128)(2,1)} %constant.29.clone.refs_3_, bf16[2,256,128]{2,1,0:T(8,128)(2,1)} %constant.30.clone.refs_4_), custom_call_target="tpu_custom_call" | custom-call | flops 3221225472 | bytes 917504 | tf_op jit(solution)/shard_map/wave_band/pallas_call | solution.py:675
  61.2 11.3 %all-to-all-done.refs_2_ = f32[32,48,128]{2,1,0:T(8,128)S(1)} async-done(((f32[32,48,128]{2,1,0:T(8,128)}), f32[32,48,128]{2,1,0:T(8,128)S(1)}, u32[]{:S(2)}, u32[]{:S(2)}) %all-to-all-start) | async-done | bytes 786464 | tf_op jit(solution)/shard_map/all_to_all | solution.py:797
  72.6 0.0 copy-start.3
  72.6 0.9 copy-done.3
  73.5 13.1 %wave_band.3 = (f32[8,32,128]{2,1,0:T(8,128)}, f32[8,32,128]{2,1,0:T(8,128)}, f32[8,32,128]{2,1,0:T(8,128)}, f32[8,32,128]{2,1,0:T(8,128)}, f32[1024,128]{1,0:T(8,128)}) custom-call(s32[1]{0:T(128)} %bitcast.refs_0_.own_ref, s32[4]{0:T(128)} %refs_1_.3, f32[32,48,128]{2,1,0:T(8,128)} %copy-done.3, bf16[2,128,256]{2,1,0:T(8,128)(2,1)} %constant.29.clone.refs_3_, ...), custom_call_target="tpu_custom_call" | custom-call | flops 3221225472 | bytes 786432 | tf_op jit(solution)/shard_map/wave_band/pallas_call | solution.py:675
  86.6 2.6 %all-to-all-start.2 = ((f32[32,4,8,128]{3,2,1,0:T(8,128)}), f32[32,4,8,128]{3,2,1,0:T(8,128)S(1)}, u32[]{:S(2)}, u32[]{:S(2)}) async-start(f32[32,4,8,128]{3,2,1,0:T(8,128)} %bitcast.12), calls=%async_computation.2 | async-start | bytes 1048576 | tf_op jit(solution)/shard_map/all_to_all | solution.py:797
  89.2 16.3 %all-to-all-done.2.came_ref = f32[32,4,8,128]{3,2,1,0:T(8,128)S(1)} async-done(((f32[32,4,8,128]{3,2,1,0:T(8,128)}), f32[32,4,8,128]{3,2,1,0:T(8,128)S(1)}, u32[]{:S(2)}, u32[]{:S(2)}) %all-to-all-start.2) | async-done | bytes 524320 | tf_op jit(solution)/shard_map/all_to_all | solution.py:797
  105.6 0.8 copy-done
  106.4 4.8 %poisson.1 = f32[32,4,8,128]{3,2,1,0:T(8,128)} custom-call(s32[1]{0:T(128)} %bitcast.1.first_ref, f32[32,4,8,128]{3,2,1,0:T(8,128)} %copy-done, bf16[2,512,256]{2,1,0:T(8,128)(2,1)} %constant.33.clone.forth_ref, bf16[2,512,256]{2,1,0:T(8,128)(2,1)} %constant.34.clone.back_ref, bf16[2,128,256]{2,1,0:T(8,128)(2,1)} %constant.35.clone.both_x_ref), custom_call_target="tpu_custom_call" | custom-call | tf_op jit(solution)/shard_map/poisson/pallas_call | solution.py:759
  111.1 2.8 %all-to-all-start.3 = ((f32[32,4,8,128]{3,2,1,0:T(8,128)}), f32[32,4,8,128]{3,2,1,0:T(8,128)S(1)}, u32[]{:S(2)}, u32[]{:S(2)}) async-start(f32[32,4,8,128]{3,2,1,0:T(8,128)} %poisson.1), calls=%async_computation.3 | async-start | bytes 1048576 | tf_op jit(solution)/shard_map/all_to_all | solution.py:797
  113.9 0.0 copy-done.9
  113.9 1.7 %collective-permute-start = (f32[8,32,128]{2,1,0:T(8,128)S(1)}, f32[8,32,128]{2,1,0:T(8,128)S(1)}, u32[]{:S(2)}, u32[]{:S(2)}) collective-permute-start(f32[8,32,128]{2,1,0:T(8,128)S(1)} %copy-done.9), channel_id=1, source_target_pairs={{0,8},{8,16},{16,24},{24,0},{1,9},{9,17},{17,25},{25,1},{2,10},{10... | collective-permute-start | bytes 393224 | tf_op jit(solution)/shard_map/ppermute | solution.py:853
  115.6 0.0 copy-done.8
  115.6 1.5 %collective-permute-start.1 = (f32[8,32,128]{2,1,0:T(8,128)S(1)}, f32[8,32,128]{2,1,0:T(8,128)S(1)}, u32[]{:S(2)}, u32[]{:S(2)}) collective-permute-start(f32[8,32,128]{2,1,0:T(8,128)S(1)} %copy-done.8), channel_id=1, source_target_pairs={{0,16},{8,24},{16,0},{24,8},{1,17},{9,25},{17,1},{25,9},{2,18},{10... | collective-permute-start | bytes 393224 | tf_op jit(solution)/shard_map/ppermute | solution.py:853
  117.1 0.0 copy-done.7
  117.1 1.4 %collective-permute-start.2 = (f32[8,32,128]{2,1,0:T(8,128)S(1)}, f32[8,32,128]{2,1,0:T(8,128)S(1)}, u32[]{:S(2)}, u32[]{:S(2)}) collective-permute-start(f32[8,32,128]{2,1,0:T(8,128)S(1)} %copy-done.7), channel_id=1, source_target_pairs={{0,24},{8,0},{16,8},{24,16},{1,25},{9,1},{17,9},{25,17},{2,26},{10... | collective-permute-start | bytes 393224 | tf_op jit(solution)/shard_map/ppermute | solution.py:853
  118.5 6.2 %collective-permute-done.refs_1_ = f32[8,32,128]{2,1,0:T(8,128)S(1)} collective-permute-done((f32[8,32,128]{2,1,0:T(8,128)S(1)}, f32[8,32,128]{2,1,0:T(8,128)S(1)}, u32[]{:S(2)}, u32[]{:S(2)}) %collective-permute-start) | collective-permute-done | bytes 131104 | tf_op jit(solution)/shard_map/ppermute | solution.py:853
  124.7 2.9 %collective-permute-done.1.refs_2_ = f32[8,32,128]{2,1,0:T(8,128)S(1)} collective-permute-done((f32[8,32,128]{2,1,0:T(8,128)S(1)}, f32[8,32,128]{2,1,0:T(8,128)S(1)}, u32[]{:S(2)}, u32[]{:S(2)}) %collective-permute-start.1) | collective-permute-done | bytes 131104 | tf_op jit(solution)/shard_map/ppermute | solution.py:853
  127.6 0.0 collective-permute-done.2.refs_3_
  127.6 2.6 %all-to-all-done.3 = f32[32,4,8,128]{3,2,1,0:T(8,128)S(1)} async-done(((f32[32,4,8,128]{3,2,1,0:T(8,128)}), f32[32,4,8,128]{3,2,1,0:T(8,128)S(1)}, u32[]{:S(2)}, u32[]{:S(2)}) %all-to-all-start.3) | async-done | bytes 524320 | tf_op jit(solution)/shard_map/all_to_all | solution.py:797
  130.2 0.0 copy-done.4
  130.2 0.0 copy-done.5
  130.2 0.0 copy-done.6
  130.2 0.8 copy-done.1
  131.0 2.6 %finish.1 = (f32[32,32,128]{2,1,0:T(8,128)}, f32[32,32,128]{2,1,0:T(8,128)}) custom-call(s32[1]{0:T(128)} %bitcast.refs_0_.own_ref, f32[1024,128]{1,0:T(8,128)} %bitcast.11, bf16[2,128,128]{2,1,0:T(8,128)(2,1)} %constant.32.clone.back_ref, f32[8,32,128]{2,1,0:T(8,128)} %get-tuple-element.12.refs_0_, f32[8,32,128]{2,1,0:T(8,128)} %copy-done.4, ...), custom_call_target="tpu_custom_call" | custom-call | tf_op jit(solution)/shard_map/finish/pallas_call | solution.py:786
  (8 shorter events, 0.0 us)
Async XLA Ops:
  15.9 32.1 %all-to-all-start.1 = ((f32[32,56,128]{2,1,0:T(8,128)}), f32[32,56,128]{2,1,0:T(8,128)S(1)}, u32[]{:S(2)}, u32[]{:S(2)}) async-start(f32[32,56,128]{2,1,0:T(8,128)} %pack_band.3), calls=%async_computation.1 | async-start | bytes 1835008 | tf_op jit(solution)/shard_map/all_to_all | solution.py:797
  48.0 2.8 %copy-start.2 = (f32[32,56,128]{2,1,0:T(8,128)}, f32[32,56,128]{2,1,0:T(8,128)S(1)}, u32[]{:S(2)}) copy-start(f32[32,56,128]{2,1,0:T(8,128)S(1)} %all-to-all-done.1.refs_2_) | copy-start | bytes 2752516
  48.0 24.6 %all-to-all-start = ((f32[32,48,128]{2,1,0:T(8,128)}), f32[32,48,128]{2,1,0:T(8,128)S(1)}, u32[]{:S(2)}, u32[]{:S(2)}) async-start(f32[32,48,128]{2,1,0:T(8,128)} %pack_band.2), calls=%async_computation | async-start | bytes 1572864 | tf_op jit(solution)/shard_map/all_to_all | solution.py:797
  72.6 0.9 copy-start.3
  86.6 19.0 %all-to-all-start.2 = ((f32[32,4,8,128]{3,2,1,0:T(8,128)}), f32[32,4,8,128]{3,2,1,0:T(8,128)S(1)}, u32[]{:S(2)}, u32[]{:S(2)}) async-start(f32[32,4,8,128]{3,2,1,0:T(8,128)} %bitcast.12), calls=%async_computation.2 | async-start | bytes 1048576 | tf_op jit(solution)/shard_map/all_to_all | solution.py:797
  105.6 0.8 copy-start
  111.1 2.8 %copy-start.9 = (f32[8,32,128]{2,1,0:T(8,128)S(1)}, f32[8,32,128]{2,1,0:T(8,128)}, u32[]{:S(2)}) copy-start(f32[8,32,128]{2,1,0:T(8,128)} %get-tuple-element.13) | copy-start | bytes 393220
  111.1 4.5 %copy-start.8 = (f32[8,32,128]{2,1,0:T(8,128)S(1)}, f32[8,32,128]{2,1,0:T(8,128)}, u32[]{:S(2)}) copy-start(f32[8,32,128]{2,1,0:T(8,128)} %get-tuple-element.14) | copy-start | bytes 393220
  111.1 6.0 %copy-start.7 = (f32[8,32,128]{2,1,0:T(8,128)S(1)}, f32[8,32,128]{2,1,0:T(8,128)}, u32[]{:S(2)}) copy-start(f32[8,32,128]{2,1,0:T(8,128)} %get-tuple-element.15) | copy-start | bytes 393220
  111.1 19.1 %all-to-all-start.3 = ((f32[32,4,8,128]{3,2,1,0:T(8,128)}), f32[32,4,8,128]{3,2,1,0:T(8,128)S(1)}, u32[]{:S(2)}, u32[]{:S(2)}) async-start(f32[32,4,8,128]{3,2,1,0:T(8,128)} %poisson.1), calls=%async_computation.3 | async-start | bytes 1048576 | tf_op jit(solution)/shard_map/all_to_all | solution.py:797
  113.9 10.8 %collective-permute-start = (f32[8,32,128]{2,1,0:T(8,128)S(1)}, f32[8,32,128]{2,1,0:T(8,128)S(1)}, u32[]{:S(2)}, u32[]{:S(2)}) collective-permute-start(f32[8,32,128]{2,1,0:T(8,128)S(1)} %copy-done.9), channel_id=1, source_target_pairs={{0,8},{8,16},{16,24},{24,0},{1,9},{9,17},{17,25},{25,1},{2,10},{10... | collective-permute-start | bytes 393224 | tf_op jit(solution)/shard_map/ppermute | solution.py:853
  115.6 12.0 %collective-permute-start.1 = (f32[8,32,128]{2,1,0:T(8,128)S(1)}, f32[8,32,128]{2,1,0:T(8,128)S(1)}, u32[]{:S(2)}, u32[]{:S(2)}) collective-permute-start(f32[8,32,128]{2,1,0:T(8,128)S(1)} %copy-done.8), channel_id=1, source_target_pairs={{0,16},{8,24},{16,0},{24,8},{1,17},{9,25},{17,1},{25,9},{2,18},{10... | collective-permute-start | bytes 393224 | tf_op jit(solution)/shard_map/ppermute | solution.py:853
  117.1 10.5 %collective-permute-start.2 = (f32[8,32,128]{2,1,0:T(8,128)S(1)}, f32[8,32,128]{2,1,0:T(8,128)S(1)}, u32[]{:S(2)}, u32[]{:S(2)}) collective-permute-start(f32[8,32,128]{2,1,0:T(8,128)S(1)} %copy-done.7), channel_id=1, source_target_pairs={{0,24},{8,0},{16,8},{24,16},{1,25},{9,1},{17,9},{25,17},{2,26},{10... | collective-permute-start | bytes 393224 | tf_op jit(solution)/shard_map/ppermute | solution.py:853
  124.7 5.5 %copy-start.4 = (f32[8,32,128]{2,1,0:T(8,128)}, f32[8,32,128]{2,1,0:T(8,128)S(1)}, u32[]{:S(2)}) copy-start(f32[8,32,128]{2,1,0:T(8,128)S(1)} %collective-permute-done.refs_1_) | copy-start | bytes 393220
  127.6 2.6 %copy-start.5 = (f32[8,32,128]{2,1,0:T(8,128)}, f32[8,32,128]{2,1,0:T(8,128)S(1)}, u32[]{:S(2)}) copy-start(f32[8,32,128]{2,1,0:T(8,128)S(1)} %collective-permute-done.1.refs_2_) | copy-start | bytes 393220
  127.6 2.6 %copy-start.6 = (f32[8,32,128]{2,1,0:T(8,128)}, f32[8,32,128]{2,1,0:T(8,128)S(1)}, u32[]{:S(2)}) copy-start(f32[8,32,128]{2,1,0:T(8,128)S(1)} %collective-permute-done.2.refs_3_) | copy-start | bytes 393220
  130.2 0.8 copy-start.1

commit v6 on v5

--- a/solution.py
+++ b/solution.py
@@ -203,19 +203,22 @@
     return lax.dot_general(former, latter, dims, preferred_element_type=jnp.float32)
 
 
-def mul3(former, latter, dims):
-    (of_former,), (of_latter,) = dims[0]
-    return mul(
-        jnp.concatenate((former[0], former[0], former[1]), axis=of_former),
-        jnp.concatenate((latter[0], latter[1], latter[0]), axis=of_latter),
-        dims,
-    )
-
-
-def table(values):
+def mul3_left(former, latter, dims):
+    high, low = pieces(latter)
+    (unused,), (axis,) = dims[0]
+    return mul(former, jnp.concatenate((high, high, low), axis=axis), dims)
+
+
+def mul3_right(former, latter, dims):
+    high, low = pieces(former)
+    (axis,), (unused,) = dims[0]
+    return mul(jnp.concatenate((high, high, low), axis=axis), latter, dims)
+
+
+def stack_table(values, axis):
     high = values.astype(np.float32).astype(jnp.bfloat16)
     low = (values - high.astype(np.float64)).astype(np.float32).astype(jnp.bfloat16)
-    return jnp.asarray(np.stack((high, low)))
+    return jnp.asarray(np.concatenate((high, low, high), axis=axis))
 
 
 def angles(former, latter, length):
@@ -278,19 +281,23 @@
     return return_table
 
 
-def spread_lanes(row):
-    return jnp.transpose(jnp.broadcast_to(row, (LANES, row.shape[1])))
-
-
-def one_hot_lanes(row, lanes):
-    column = spread_lanes(row.astype(jnp.float32).astype(jnp.bfloat16))
-    step = lax.broadcasted_iota(jnp.int32, column.shape, 1)
+def ramp(shape, axis, first=0):
+    steps = lax.broadcasted_iota(jnp.int32, shape, axis) + first
+    return steps.astype(jnp.float32).astype(jnp.bfloat16)
+
+
+def sixteen(row):
+    return jnp.broadcast_to(row, (16, row.shape[1])).astype(jnp.bfloat16)
+
+
+def one_hot_lanes(row, ramps):
+    column = jnp.transpose(jnp.concatenate([sixteen(row)] * (LANES // 16), axis=0))
     one = jnp.ones(column.shape, jnp.bfloat16)
     zero = jnp.zeros(column.shape, jnp.bfloat16)
     return jnp.concatenate(
         [
-            jnp.where(column == (step + first).astype(jnp.float32).astype(jnp.bfloat16), one, zero)
-            for first in range(0, lanes, LANES)
+            jnp.where(column == ramps[:, first : first + LANES], one, zero)
+            for first in range(0, ramps.shape[1], LANES)
         ],
         axis=1,
     )
@@ -371,11 +378,11 @@
     coeff_ref, miller_ref, slot_ref, pencil_ref = refs[:4]
     rest = list(refs[4:])
     column_ref = rest.pop(0) if has_column else None
-    out_ref, total, key_ref, real_ref, imag_ref = rest
+    out_ref, total, key_ref, real_ref, imag_ref, lane_ref, real_low, imag_low, ramp_ref, step_ref = rest
     half = total.shape[0] // 4
     slots = 2 * half
     count = out_ref.shape[0]
-    rows = pencil_ref.shape[1] // count
+    rows = pencil_ref.shape[0] // count
     length = miller_ref.shape[0]
     ranks = key_ref.shape[0]
 
@@ -396,34 +403,48 @@
         base = 8 * (block // 2) + 8 * (block % 2) - WINDOW // 2
         return jnp.minimum(jnp.maximum(base, 0), half - WINDOW)
 
+    ramp_ref[...] = ramp(ramp_ref.shape, 1)
+    step_ref[...] = ramp(step_ref.shape, 0)
     sublane = lax.broadcasted_iota(jnp.int32, (8, LANES), 0)
     astray = jnp.zeros((8, LANES), jnp.float32)
     for v in range(RANK_LOW):
-        base = base_of(sublane * (RANK_LOW // 8) + v // 8) * (2 * width)
-        offset = key_ref[v * 8 : v * 8 + 8, :] - base.astype(jnp.float32)
-        outside = jnp.logical_or(offset < 0.0, offset >= 2.0 * width * WINDOW)
+        at = slice(v * 8, v * 8 + 8)
+        keys = key_ref[at, :]
+        high = jnp.floor(keys * (1.0 / (2 * width)))
+        lane_ref[at, :] = keys - high * (2.0 * width)
+        key_ref[at, :] = high
+        for ref, low_ref in ((real_ref, real_low), (imag_ref, imag_low)):
+            value = ref[at, :]
+            rounded = value.astype(jnp.bfloat16).astype(jnp.float32)
+            ref[at, :] = rounded
+            low_ref[at, :] = value - rounded
+        offset = high - base_of(sublane * (RANK_LOW // 8) + v // 8).astype(jnp.float32)
+        outside = jnp.logical_or(offset < 0.0, offset >= 1.0 * WINDOW)
         astray = jnp.where(outside, 1.0, astray)
     astray = jnp.max(jnp.where(sublane * RANK_LOW < length, astray, 0.0))
 
     def add(block, base, window):
         first = block % (RANK_LOW // 8) * 64 + block // (RANK_LOW // 8)
-        where = pl.ds(first, 8, stride=8)
-        keys = key_ref[where, :]
-        high = jnp.floor(keys * (1.0 / (2 * width)))
-        lane = keys - high * (2.0 * width)
-        high = (high - base).astype(jnp.bfloat16)
-        values = [piece for ref in (real_ref, imag_ref) for piece in pieces(ref[where, :])]
-        values = [values[0], values[2], values[1], values[3]]
-        steps = lax.broadcasted_iota(jnp.int32, (window, LANES), 0)
-        steps = steps.astype(jnp.float32).astype(jnp.bfloat16)
-        zero = jnp.zeros((window, LANES), jnp.bfloat16)
+        base_row = jnp.full((1, LANES), base, jnp.int32).astype(jnp.float32)
+        zero = jnp.zeros((16, LANES), jnp.bfloat16)
         spread, chosen = [], []
         for t in range(8):
-            here = high[t : t + 1] == steps
+            row = pl.ds(first + 8 * t, 1)
+            high = sixteen(key_ref[row, :] - base_row)
+            masks = [high == step_ref[r : r + 16, :] for r in range(0, window, 16)]
             spread.append(
-                jnp.concatenate([jnp.where(here, value[t : t + 1], zero) for value in values], axis=0)
+                jnp.concatenate(
+                    [
+                        jnp.where(mask, value, zero)
+                        for value in [
+                            sixteen(ref[row, :]) for ref in (real_ref, imag_ref, real_low, imag_low)
+                        ]
+                        for mask in masks
+                    ],
+                    axis=0,
+                )
             )
-            chosen.append(one_hot_lanes(lane[t : t + 1], 2 * width))
+            chosen.append(one_hot_lanes(lane_ref[row, :], ramp_ref[...]))
         found = mul(jnp.concatenate(spread, axis=1), jnp.concatenate(chosen, axis=0), NN)
         for i in range(4):
             if window == half:
@@ -469,7 +490,7 @@
                 axis=0,
             )
         )
-    pencils = mul3((pencil_ref[0], pencil_ref[1]), both, NT)
+    pencils = mul(pencil_ref[...], jnp.concatenate((both[0], both[0], both[1]), axis=1), NT)
     tiles = slots // LANES
     for t in range(tiles):
         tile = pencils[:, t * LANES : (t + 1) * LANES].reshape(count, rows, LANES)
@@ -486,8 +507,8 @@
 
 def pack_band(band, count, coeffs, miller, slot, pencil, slots, column):
     length = miller.shape[0]
-    width = pencil.shape[2] // 2
-    rows = pencil.shape[1] // count * (slots // LANES)
+    width = pencil.shape[1] // 6
+    rows = pencil.shape[0] // count * (slots // LANES)
     operands = [coeffs, miller, slot, pencil]
     if column is not None:
         operands.append(column)
@@ -501,7 +522,11 @@
         out_specs=pl.BlockSpec((count, rows, LANES), lambda i: (0, 0, 0)),
         out_shape=jax.ShapeDtypeStruct((count, rows, LANES), jnp.float32),
         scratch_shapes=[pltpu.VMEM((2 * slots, 2 * width), jnp.float32)]
-        + [pltpu.VMEM((8 * RANK_LOW, LANES), jnp.float32)] * 3,
+        + [pltpu.VMEM((8 * RANK_LOW, LANES), jnp.float32)] * 6
+        + [
+            pltpu.VMEM((LANES, 2 * width), jnp.bfloat16),
+            pltpu.VMEM((slots // 2, LANES), jnp.bfloat16),
+        ],
         compiler_params=pltpu.CompilerParams(vmem_limit_bytes=VMEM_LIMIT),
         cost_estimate=pl.CostEstimate(
             flops=2 * length * LANES * slots * 4 * width,
@@ -516,11 +541,12 @@
     own_ref, count_ref, came_ref, wave_y_ref, wave_x_ref = refs[:5]
     rest = list(refs[5:])
     forth_ref = rest.pop(0) if is_last else None
-    former_ref, cell_ref = (None, None) if is_first else (rest.pop(0), rest.pop(0))
+    former_ref, chosen_ref, high_ref = (None,) * 3 if is_first else [rest.pop(0) for _ in range(3)]
     density_refs = [rest.pop(0) for _ in range(kpts if is_last else 1)]
-    cell_out = rest.pop(0) if is_first and not is_last else None
+    if is_first:
+        chosen_ref, high_ref = rest.pop(0), rest.pop(0)
     send_ref = rest.pop(0) if is_last else None
-    values, grid, chosen, whole = rest
+    values, grid, whole = rest
     planes = density_refs[0].shape[0]
     block = NX // kpts
     part_rows = 2 * planes
@@ -539,26 +565,19 @@
             values[0:rows, first : first + LANES] = high
             values[rows : 2 * rows, first : first + LANES] = low
 
+    tile = 4 * HALF
     if is_first:
-        column = jnp.concatenate(
-            [
-                came_ref[j, tiles * part_rows + t : tiles * part_rows + t + 1]
-                for j in range(pws)
-                for t in range(tiles)
-            ],
-            axis=1,
-        ).astype(jnp.int32)
-        cell = ((column // NY + NX // 2) % NX - HALF // 2) * HALF
-        cell = cell + (column % NY + NY // 2) % NY - HALF // 2
-        cell = cell.astype(jnp.float32)
-        if cell_out is not None:
-            cell_out[...] = cell
-    else:
-        cell = cell_ref[...]
-    tile = 4 * HALF
-    high = jnp.floor(cell * (1.0 / tile))
-    chosen[...] = one_hot_lanes(cell - high * tile, tile)
-    high = high.astype(jnp.bfloat16)
+        ramps = ramp((LANES, tile), 1)
+        for j in range(pws):
+            for t in range(tiles):
+                column = came_ref[j, tiles * part_rows + t : tiles * part_rows + t + 1]
+                column = column.astype(jnp.int32)
+                cell = ((column // NY + NX // 2) % NX - HALF // 2) * HALF
+                cell = cell + (column % NY + NY // 2) % NY - HALF // 2
+                first = (j * tiles + t) * LANES
+                lane = (cell % tile).astype(jnp.float32)
+                chosen_ref[first : first + LANES, :] = one_hot_lanes(lane, ramps)
+                high_ref[:, first : first + LANES] = sixteen((cell // tile).astype(jnp.float32))
     left = lax.broadcasted_iota(jnp.int32, (kpts * planes, LANES), 1) < HALF
     together = 4
 
@@ -581,12 +600,15 @@
             grid[pl.ds(t * 4 + 2 * h + 1, kpts * planes, stride=HALF), :] = odd
 
     def some_tiles(i, unused):
-        held = values[...]
+        high = high_ref[...]
+        zero = jnp.zeros_like(high)
         kept = []
         for s in range(together):
             here = high == (together * i + s).astype(jnp.float32).astype(jnp.bfloat16)
-            kept.append(jnp.where(here, held, jnp.zeros_like(held)))
-        found = mul(jnp.concatenate(kept, axis=0), chosen[...], NN)
+            kept += [
+                jnp.where(here, values[r : r + 16, :], zero) for r in range(0, 2 * rows, 16)
+            ]
+        found = mul(jnp.concatenate(kept, axis=0), chosen_ref[...], NN)
         for s in range(together):
             place(together * i + s, found[2 * rows * s : 2 * rows * (s + 1)])
         return unused
@@ -609,12 +631,12 @@
     def transform(p):
         lines = jnp.concatenate(
             [
-                grid[pl.ds(pl.multiple_of((k * planes + p) * HALF, HALF), HALF), :]
+                grid[(k * planes + p) * HALF : (k * planes + p + 1) * HALF, :]
                 for k in range(kpts)
             ],
             axis=0,
         )
-        mixed = mul3(pieces(lines), (wave_y_ref[0], wave_y_ref[1]), NN)
+        mixed = mul3_right(lines, wave_y_ref[...], NN)
         mixed = jnp.concatenate(
             [
                 jnp.concatenate(
@@ -625,7 +647,7 @@
             ],
             axis=0,
         )
-        wave = mul3((wave_x_ref[0], wave_x_ref[1]), pieces(mixed), NN)
+        wave = mul3_left(wave_x_ref[...], mixed, NN)
         square = wave[:NX] * wave[:NX] + wave[NX:] * wave[NX:]
         density = weights[0] * square[:, :NY]
         for k in range(1, kpts):
@@ -641,19 +663,15 @@
             density_refs[0][p] = density
         if is_last:
             level = jnp.mean(density[:8], axis=(0, 1), keepdims=True)
-            half = mul3((forth_ref[0], forth_ref[1]), pieces(density - level), NT)
+            half = mul3_left(forth_ref[...], density - level, NT)
             half = half + jnp.where(first_row, level * NY, 0.0)
             send_ref[pl.ds(p, 2 * HALF, stride=planes), :] = half
 
-    def some_planes(i, unused):
-        for s in range(together):
-            transform(together * i + s)
-        return unused
-
-    lax.fori_loop(0, planes // together, some_planes, 0)
-
-
-def wave_band(kpts, tiles, total, scale, own, counts, came, wave_y, wave_x, forth, former, cell):
+    for p in range(planes):
+        transform(p)
+
+
+def wave_band(kpts, tiles, total, scale, own, counts, came, wave_y, wave_x, forth, former, chosen):
     planes = NZ // came.shape[0]
     block = NX // kpts
     is_first, is_last = former is None, forth is not None
@@ -662,13 +680,14 @@
     if is_last:
         operands.append(forth)
     if not is_first:
-        operands += [former, cell]
+        operands += [former, *chosen]
     if is_last:
         out_shape = [jax.ShapeDtypeStruct((planes, block, NY), jnp.float32)] * kpts
     else:
         out_shape = [jax.ShapeDtypeStruct((planes, NX, NY), jnp.float32)]
-    if is_first and not is_last:
-        out_shape.append(jax.ShapeDtypeStruct((1, total), jnp.float32))
+    if is_first:
+        out_shape.append(jax.ShapeDtypeStruct((total, 4 * HALF), jnp.bfloat16))
+        out_shape.append(jax.ShapeDtypeStruct((16, total), jnp.bfloat16))
     if is_last:
         out_shape.append(jax.ShapeDtypeStruct((2 * HALF * planes, NX), jnp.float32))
     rows = kpts * 2 * planes
@@ -680,7 +699,6 @@
         scratch_shapes=[
             pltpu.VMEM((2 * rows, total), jnp.bfloat16),
             pltpu.VMEM((kpts * planes * HALF, LANES), jnp.float32),
-            pltpu.VMEM((total, 4 * HALF), jnp.bfloat16),
             pltpu.VMEM((NX, NY), jnp.float32),
         ],
         compiler_params=pltpu.CompilerParams(vmem_limit_bytes=VMEM_LIMIT),
@@ -694,15 +712,11 @@
 def poisson_kernel(pws, first_ref, came_ref, forth_ref, back_ref, both_x_ref, send_ref):
     count, parts, planes, unused = came_ref.shape
     pairs = parts // 2
-    forth = (forth_ref[0], forth_ref[1])
-    back = (back_ref[0], back_ref[1])
-    both_x = (both_x_ref[0], both_x_ref[1])
-
     fields = [came_ref[:, i].reshape(NZ, NX) for i in range(parts)]
     level = jnp.mean(fields[0], axis=(0, 1), keepdims=True)
     fields[0] = fields[0] - jnp.where(first_ref[0] == 0, level, 0.0)
     field = jnp.concatenate(fields, axis=1)
-    turned = mul3(forth, pieces(field), NN)
+    turned = mul3_left(forth_ref[...], field, NN)
 
     def part(array, half, i):
         return array[half * NZ : (half + 1) * NZ, i * NX : (i + 1) * NX]
@@ -711,7 +725,7 @@
     for q in range(pairs):
         lines.append(part(turned, 0, 2 * q) + part(turned, 1, 2 * q + 1))
         lines.append(part(turned, 0, 2 * q + 1) - part(turned, 1, 2 * q))
-    spectrum = mul3(pieces(jnp.concatenate(lines, axis=0)), both_x, NN)
+    spectrum = mul3_right(jnp.concatenate(lines, axis=0), both_x_ref[...], NN)
 
     step_z = lax.broadcasted_iota(jnp.int32, (NZ, NX), 0)
     step_x = lax.broadcasted_iota(jnp.int32, (NZ, NX), 1)
@@ -724,14 +738,14 @@
         kernel = kernel * (1.0 / (NX * NY * NZ))
         lines.append((real[:, :NX] + imag[:, NX:]) * kernel)
         lines.append((imag[:, :NX] - real[:, NX:]) * kernel)
-    turned = mul3(pieces(jnp.concatenate(lines, axis=0)), both_x, NN)
+    turned = mul3_right(jnp.concatenate(lines, axis=0), both_x_ref[...], NN)
     lines = []
     for q in range(pairs):
         real = turned[2 * q * NZ : (2 * q + 1) * NZ]
         imag = turned[(2 * q + 1) * NZ : (2 * q + 2) * NZ]
         lines.append(real[:, :NX] - imag[:, NX:])
         lines.append(real[:, NX:] + imag[:, :NX])
-    turned = mul3(back, pieces(jnp.concatenate(lines, axis=1)), NN)
+    turned = mul3_left(back_ref[...], jnp.concatenate(lines, axis=1), NN)
 
     kpts = count // pws
     merged = NZ // pws // 8
@@ -766,31 +780,46 @@
     )(first, came, forth, back, both_x)
 
 
-def finish_kernel(own_ref, came_ref, back_ref, *refs):
-    block_refs, density_ref, out_ref = refs[:-2], refs[-2], refs[-1]
+def assemble_kernel(own_ref, *refs):
+    block_refs, density_ref = refs[:-1], refs[-1]
     kpts = len(block_refs)
-    back = (back_ref[0], back_ref[1])
+    part = density_ref.shape[0] // kpts
+    for s, block_ref in enumerate(block_refs):
+        sender = lax.rem(own_ref[0] + kpts - s, kpts)
+        density_ref[pl.ds(sender * part, part)] = block_ref[...]
+
+
+def assemble(own, blocks):
+    vmem = pl.BlockSpec(memory_space=pltpu.VMEM)
+    part, block, length = blocks[0].shape
+    return pl.pallas_call(
+        assemble_kernel,
+        in_specs=[pl.BlockSpec(memory_space=pltpu.SMEM)] + [vmem] * len(blocks),
+        out_specs=vmem,
+        out_shape=jax.ShapeDtypeStruct((part * len(blocks), block, length), jnp.float32),
+        name="assemble",
+    )(own, *blocks)
+
+
+def finish_kernel(came_ref, back_ref, out_ref):
     planes, block, unused = out_ref.shape
     merged = planes // 8
-    for s, block_ref in enumerate(block_refs):
-        sender = lax.rem(own_ref[0] + kpts - s, kpts)
-        density_ref[pl.ds(sender * (planes // kpts), planes // kpts)] = block_ref[...]
     for h in range(8):
         lines = came_ref[pl.ds(h, 2 * HALF, stride=8), :]
-        field = mul3(pieces(lines), back, TN)
+        field = mul3_right(lines, back_ref[...], TN)
         out_ref[h * merged : (h + 1) * merged] = field.reshape(merged, block, NY)
 
 
-def finish(planes, block, own, came, back_y, blocks):
+def finish(planes, block, came, back_y):
     vmem = pl.BlockSpec(memory_space=pltpu.VMEM)
     return pl.pallas_call(
         finish_kernel,
-        in_specs=[pl.BlockSpec(memory_space=pltpu.SMEM)] + [vmem] * (2 + len(blocks)),
-        out_specs=[vmem] * 2,
-        out_shape=[jax.ShapeDtypeStruct((planes, block, NY), jnp.float32)] * 2,
+        in_specs=[vmem] * 2,
+        out_specs=vmem,
+        out_shape=jax.ShapeDtypeStruct((planes, block, NY), jnp.float32),
         compiler_params=pltpu.CompilerParams(vmem_limit_bytes=VMEM_LIMIT),
         name="finish",
-    )(own, came, back_y, *blocks)
+    )(came, back_y)
 
 
 def exchange(array, axes):
@@ -808,11 +837,11 @@
     planes = NZ // count
     parts = 2 * HALF // count
     made = tables(kpts, pws, planes)
-    pencil = table(made["pencil"](z_width))
-    wave_y, wave_x, forth_y, back_y, forth_z, back_z, both_x = (
-        table(made[name])
-        for name in ("wave_y", "wave_x", "forth_y", "back_y", "forth_z", "back_z", "both_x")
-    )
+    pencil = stack_table(made["pencil"](z_width), 1)
+    wave_x, forth_y, forth_z, back_z = (
+        stack_table(made[name], 1) for name in ("wave_x", "forth_y", "forth_z", "back_z")
+    )
+    wave_y, back_y, both_x = (stack_table(made[name], 0) for name in ("wave_y", "back_y", "both_x"))
 
     tiles = slots // LANES
     length = column_slot.shape[1] // LANES
@@ -829,10 +858,10 @@
         )
         arrived.append(exchange(packed, everyone))
     own = lax.axis_index("kpt").astype(jnp.int32).reshape(1)
-    former = cell = None
+    former = chosen = None
     for band in range(band_count):
         forth = forth_y if band == band_count - 1 else None
-        *made_here, other = wave_band(
+        made_here = wave_band(
             kpts,
             tiles,
             pws * slots,
@@ -844,11 +873,11 @@
             wave_x,
             forth,
             former,
-            cell,
+            chosen,
         )
         former = made_here[0]
-        cell = other if band == 0 else cell
-    half = exchange(other.reshape(count, parts, planes, NX), everyone)
+        chosen = made_here[-2:] if band == 0 else chosen
+    half = exchange(made_here[-1].reshape(count, parts, planes, NX), everyone)
     blocks = [made_here[0]] + [
         lax.ppermute(made_here[s], "kpt", [(a, (a + s) % kpts) for a in range(kpts)])
         for s in range(1, kpts)
@@ -857,7 +886,7 @@
     first = (device * (parts // 2)).astype(jnp.int32).reshape(1)
     back = poisson(pws, first, half, forth_z, back_z, both_x)
     back = exchange(back, everyone).reshape(count * parts * 8, LANES)
-    return tuple(finish(NZ // pws, NX // kpts, own, back, back_y, blocks))
+    return assemble(own, blocks), finish(NZ // pws, NX // kpts, back, back_y)
 
 
 def fits_planes(kpts, pws):

time: 134 us -> 134 us (level)
  waiting for transfers between devices: 48.9 us -> 46.3 us
  Pallas kernels: 61.4 us -> 63.4 us
    all_to_all x4, waiting for transfers between devices: 39.8 us -> 37.2 us  [exchange(): return lax.all_to_all(array, axes, split_axis=0, concat_axis=0, tiled=True)]
    pallas_call x1 -> x2, Pallas kernels: 2.58 us -> 4.18 us  [the longest x1 2.25 us: finish(): pl.pallas_call(finish_kernel, in_specs=[vmem] * 2, out_specs=vmem, out_sh...]
  transfers between devices with their start and end apart: 7 -> 7, of which waited for: 6 -> 5; matrix products, arithmetic and copies ran while one was open for 0% -> 0% of each run, Pallas kernels for 19% -> 21%
where the time goes in v6:
time: 134 us
  Pallas kernels  63.4 us (47%)
  waiting for transfers between devices  46.3 us (35%)
  starting transfers between devices  19.9 us (15%)
  local copies, waits for them, and re-layouts  3.19 us (2%)
    all_to_all x4, waiting for transfers between devices, exchange(): return lax.all_to_all(array, axes, split_axis=0, concat_axis=0, tiled=True)  37.2 us
    pallas_call x2, Pallas kernels, pack_band(): pl.pallas_call(functools.partial(pack_kernel, width, column is not None),...  30.8 us
    pallas_call x2, Pallas kernels, wave_band(): pl.pallas_call(functools.partial(wave_kernel, kpts, tiles, scale, is_firs...  23.5 us
    all_to_all x4, starting transfers between devices, exchange(): return lax.all_to_all(array, axes, split_axis=0, concat_axis=0, tiled=True)  15.3 us
    ppermute x3, waiting for transfers between devices, local_planes(): lax.ppermute(made_here[s], 'kpt', [(a, (a + s) % kpts) for a in range(kpt...  9.07 us
    pallas_call x1, Pallas kernels, poisson(): pl.pallas_call(functools.partial(poisson_kernel, pws), in_specs=[pl.Block...  5 us
    ppermute x3, starting transfers between devices, local_planes(): lax.ppermute(made_here[s], 'kpt', [(a, (a + s) % kpts) for a in range(kpt...  4.63 us
    unnamed x20, local copies, waits for them, and re-layouts  3.19 us
  transfers between devices with their start and end apart: 7, of which 5 were waited for; matrix products, arithmetic and copies ran while one was open for 0% of the time, Pallas kernels for 21%

profile of v6, /device:TPU:0, one launch (start us, length us, event | category | flops | bytes accessed | tf_op | source)
XLA Modules:
  0.0 133.6 jit_solution(9528676503185342349)
XLA Ops:
  0.6 15.4 %pack_band.3 = f32[32,56,128]{2,1,0:T(8,128)} custom-call(f32[2,768,128]{2,1,0:T(8,128)} %bitcast.13, s32[384,128]{1,0:T(8,128)} %bitcast.15, s32[384,128]{1,0:T(8,128)} %bitcast.17, bf16[512,768]{1,0:T(8,128)(2,1)} %constant.28.clone.refs_3_, s32[384]{0:T(512)} %refs_4_.3), custom_call_target="tpu_custom_call" | custom-call | flops 19327352832 | bytes 786432 | tf_op jit(solution)/shard_map/pack_band/pallas_call | solution.py:517
  16.0 7.3 %all-to-all-start.1 = ((f32[32,56,128]{2,1,0:T(8,128)}), f32[32,56,128]{2,1,0:T(8,128)S(1)}, u32[]{:S(2)}, u32[]{:S(2)}) async-start(f32[32,56,128]{2,1,0:T(8,128)} %pack_band.3), calls=%async_computation.1 | async-start | bytes 1835008 | tf_op jit(solution)/shard_map/all_to_all | solution.py:826
  23.3 15.4 %pack_band.2 = f32[32,48,128]{2,1,0:T(8,128)} custom-call(f32[2,768,128]{2,1,0:T(8,128)} %bitcast.14, s32[384,128]{1,0:T(8,128)} %bitcast.16, s32[384,128]{1,0:T(8,128)} %bitcast.18, bf16[512,768]{1,0:T(8,128)(2,1)} %constant.28.clone.refs_3_), custom_call_target="tpu_custom_call" | custom-call | flops 19327352832 | bytes 786432 | tf_op jit(solution)/shard_map/pack_band/pallas_call | solution.py:517
  38.7 9.4 %all-to-all-done.1.refs_2_ = f32[32,56,128]{2,1,0:T(8,128)S(1)} async-done(((f32[32,56,128]{2,1,0:T(8,128)}), f32[32,56,128]{2,1,0:T(8,128)S(1)}, u32[]{:S(2)}, u32[]{:S(2)}) %all-to-all-start.1) | async-done | bytes 917536 | tf_op jit(solution)/shard_map/all_to_all | solution.py:826
  48.1 0.0 copy-start.2
  48.1 2.8 %all-to-all-start = ((f32[32,48,128]{2,1,0:T(8,128)}), f32[32,48,128]{2,1,0:T(8,128)S(1)}, u32[]{:S(2)}, u32[]{:S(2)}) async-start(f32[32,48,128]{2,1,0:T(8,128)} %pack_band.2), calls=%async_computation | async-start | bytes 1572864 | tf_op jit(solution)/shard_map/all_to_all | solution.py:826
  50.9 0.0 copy-done.2
  50.9 10.3 %wave_band.2 = (f32[8,128,128]{2,1,0:T(8,128)}, bf16[3072,256]{1,0:T(8,128)(2,1)}, bf16[16,3072]{1,0:T(8,128)(2,1)}) custom-call(s32[1]{0:T(128)} %bitcast.refs_0_.own_ref, s32[4]{0:T(128)} %refs_1_.3, f32[32,56,128]{2,1,0:T(8,128)} %copy-done.2, bf16[384,256]{1,0:T(8,128)(2,1)} %constant.33.clone.refs_3_, bf16[256,384]{1,0:T(8,128)(2,1)} %constant.29.clone.refs_4_), custom_call_target="tpu_custom_call" | custom-call | flops 3221225472 | bytes 917504 | tf_op jit(solution)/shard_map/wave_band/pallas_call | solution.py:694
  61.2 11.5 %all-to-all-done.refs_2_ = f32[32,48,128]{2,1,0:T(8,128)S(1)} async-done(((f32[32,48,128]{2,1,0:T(8,128)}), f32[32,48,128]{2,1,0:T(8,128)S(1)}, u32[]{:S(2)}, u32[]{:S(2)}) %all-to-all-start) | async-done | bytes 786464 | tf_op jit(solution)/shard_map/all_to_all | solution.py:826
  72.7 0.9 copy-done.3
  73.6 13.2 %wave_band.3 = (f32[8,32,128]{2,1,0:T(8,128)}, f32[8,32,128]{2,1,0:T(8,128)}, f32[8,32,128]{2,1,0:T(8,128)}, f32[8,32,128]{2,1,0:T(8,128)}, f32[1024,128]{1,0:T(8,128)}) custom-call(s32[1]{0:T(128)} %bitcast.refs_0_.own_ref, s32[4]{0:T(128)} %refs_1_.3, f32[32,48,128]{2,1,0:T(8,128)} %copy-done.3, bf16[384,256]{1,0:T(8,128)(2,1)} %constant.33.clone.refs_3_, ...), custom_call_target="tpu_custom_call" | custom-call | flops 3221225472 | bytes 786432 | tf_op jit(solution)/shard_map/wave_band/pallas_call | solution.py:694
  86.8 2.6 %all-to-all-start.2 = ((f32[32,4,8,128]{3,2,1,0:T(8,128)}), f32[32,4,8,128]{3,2,1,0:T(8,128)S(1)}, u32[]{:S(2)}, u32[]{:S(2)}) async-start(f32[32,4,8,128]{3,2,1,0:T(8,128)} %bitcast.12), calls=%async_computation.2 | async-start | bytes 1048576 | tf_op jit(solution)/shard_map/all_to_all | solution.py:826
  89.4 16.3 %all-to-all-done.2.came_ref = f32[32,4,8,128]{3,2,1,0:T(8,128)S(1)} async-done(((f32[32,4,8,128]{3,2,1,0:T(8,128)}), f32[32,4,8,128]{3,2,1,0:T(8,128)S(1)}, u32[]{:S(2)}, u32[]{:S(2)}) %all-to-all-start.2) | async-done | bytes 524320 | tf_op jit(solution)/shard_map/all_to_all | solution.py:826
  105.8 0.8 copy-done.1
  106.6 5.0 %poisson.1 = f32[32,4,8,128]{3,2,1,0:T(8,128)} custom-call(s32[1]{0:T(128)} %bitcast.8.first_ref, f32[32,4,8,128]{3,2,1,0:T(8,128)} %copy-done.1, bf16[512,768]{1,0:T(8,128)(2,1)} %constant.31.clone.forth_ref, bf16[512,768]{1,0:T(8,128)(2,1)} %constant.32.clone.back_ref, bf16[384,256]{1,0:T(8,128)(2,1)} %constant.35.clone.both_x_ref), custom_call_target="tpu_custom_call" | custom-call | tf_op jit(solution)/shard_map/poisson/pallas_call | solution.py:773
  111.6 2.6 %all-to-all-start.3 = ((f32[32,4,8,128]{3,2,1,0:T(8,128)}), f32[32,4,8,128]{3,2,1,0:T(8,128)S(1)}, u32[]{:S(2)}, u32[]{:S(2)}) async-start(f32[32,4,8,128]{3,2,1,0:T(8,128)} %poisson.1), calls=%async_computation.3 | async-start | bytes 1048576 | tf_op jit(solution)/shard_map/all_to_all | solution.py:826
  114.2 0.0 copy-done.9
  114.2 1.7 %collective-permute-start = (f32[8,32,128]{2,1,0:T(8,128)S(1)}, f32[8,32,128]{2,1,0:T(8,128)S(1)}, u32[]{:S(2)}, u32[]{:S(2)}) collective-permute-start(f32[8,32,128]{2,1,0:T(8,128)S(1)} %copy-done.9), channel_id=1, source_target_pairs={{0,8},{8,16},{16,24},{24,0},{1,9},{9,17},{17,25},{25,1},{2,10},{10... | collective-permute-start | bytes 393224 | tf_op jit(solution)/shard_map/ppermute | solution.py:882
  115.9 0.0 copy-done.8
  115.9 1.5 %collective-permute-start.1 = (f32[8,32,128]{2,1,0:T(8,128)S(1)}, f32[8,32,128]{2,1,0:T(8,128)S(1)}, u32[]{:S(2)}, u32[]{:S(2)}) collective-permute-start(f32[8,32,128]{2,1,0:T(8,128)S(1)} %copy-done.8), channel_id=1, source_target_pairs={{0,16},{8,24},{16,0},{24,8},{1,17},{9,25},{17,1},{25,9},{2,18},{10... | collective-permute-start | bytes 393224 | tf_op jit(solution)/shard_map/ppermute | solution.py:882
  117.4 0.0 copy-done.7
  117.4 1.4 %collective-permute-start.2 = (f32[8,32,128]{2,1,0:T(8,128)S(1)}, f32[8,32,128]{2,1,0:T(8,128)S(1)}, u32[]{:S(2)}, u32[]{:S(2)}) collective-permute-start(f32[8,32,128]{2,1,0:T(8,128)S(1)} %copy-done.7), channel_id=1, source_target_pairs={{0,24},{8,0},{16,8},{24,16},{1,25},{9,1},{17,9},{25,17},{2,26},{10... | collective-permute-start | bytes 393224 | tf_op jit(solution)/shard_map/ppermute | solution.py:882
  118.8 6.2 %collective-permute-done.refs_1_ = f32[8,32,128]{2,1,0:T(8,128)S(1)} collective-permute-done((f32[8,32,128]{2,1,0:T(8,128)S(1)}, f32[8,32,128]{2,1,0:T(8,128)S(1)}, u32[]{:S(2)}, u32[]{:S(2)}) %collective-permute-start) | collective-permute-done | bytes 131104 | tf_op jit(solution)/shard_map/ppermute | solution.py:882
  125.0 2.9 %collective-permute-done.1.refs_2_ = f32[8,32,128]{2,1,0:T(8,128)S(1)} collective-permute-done((f32[8,32,128]{2,1,0:T(8,128)S(1)}, f32[8,32,128]{2,1,0:T(8,128)S(1)}, u32[]{:S(2)}, u32[]{:S(2)}) %collective-permute-start.1) | collective-permute-done | bytes 131104 | tf_op jit(solution)/shard_map/ppermute | solution.py:882
  127.9 0.0 collective-permute-done.2.refs_3_
  127.9 0.0 copy-done.4
  127.9 0.6 copy-done.5
  128.5 0.0 copy-done.6
  128.6 1.9 %assemble.1 = f32[32,32,128]{2,1,0:T(8,128)} custom-call(s32[1]{0:T(128)} %bitcast.refs_0_.own_ref, f32[8,32,128]{2,1,0:T(8,128)} %get-tuple-element.13.refs_0_, f32[8,32,128]{2,1,0:T(8,128)} %copy-done.4, f32[8,32,128]{2,1,0:T(8,128)} %copy-done.5, f32[8,32,128]{2,1,0:T(8,128)} %copy-done.6), custom_call_target="tpu_custom_call" | custom-call | tf_op jit(solution)/shard_map/assemble/pallas_call | solution.py:795
  130.5 0.0 all-to-all-done.3
  130.5 0.8 copy-done
  131.3 2.3 %finish.1 = f32[32,32,128]{2,1,0:T(8,128)} custom-call(f32[1024,128]{1,0:T(8,128)} %bitcast.11, bf16[384,128]{1,0:T(8,128)(2,1)} %constant.34.clone.back_ref), custom_call_target="tpu_custom_call" | custom-call | tf_op jit(solution)/shard_map/finish/pallas_call | solution.py:815
  (9 shorter events, 0.0 us)
Async XLA Ops:
  16.0 32.1 %all-to-all-start.1 = ((f32[32,56,128]{2,1,0:T(8,128)}), f32[32,56,128]{2,1,0:T(8,128)S(1)}, u32[]{:S(2)}, u32[]{:S(2)}) async-start(f32[32,56,128]{2,1,0:T(8,128)} %pack_band.3), calls=%async_computation.1 | async-start | bytes 1835008 | tf_op jit(solution)/shard_map/all_to_all | solution.py:826
  48.1 2.8 %copy-start.2 = (f32[32,56,128]{2,1,0:T(8,128)}, f32[32,56,128]{2,1,0:T(8,128)S(1)}, u32[]{:S(2)}) copy-start(f32[32,56,128]{2,1,0:T(8,128)S(1)} %all-to-all-done.1.refs_2_) | copy-start | bytes 2752516
  48.1 24.6 %all-to-all-start = ((f32[32,48,128]{2,1,0:T(8,128)}), f32[32,48,128]{2,1,0:T(8,128)S(1)}, u32[]{:S(2)}, u32[]{:S(2)}) async-start(f32[32,48,128]{2,1,0:T(8,128)} %pack_band.2), calls=%async_computation | async-start | bytes 1572864 | tf_op jit(solution)/shard_map/all_to_all | solution.py:826
  72.7 0.9 copy-start.3
  86.8 19.0 %all-to-all-start.2 = ((f32[32,4,8,128]{3,2,1,0:T(8,128)}), f32[32,4,8,128]{3,2,1,0:T(8,128)S(1)}, u32[]{:S(2)}, u32[]{:S(2)}) async-start(f32[32,4,8,128]{3,2,1,0:T(8,128)} %bitcast.12), calls=%async_computation.2 | async-start | bytes 1048576 | tf_op jit(solution)/shard_map/all_to_all | solution.py:826
  105.8 0.8 copy-start.1
  106.6 7.6 %copy-start.9 = (f32[8,32,128]{2,1,0:T(8,128)S(1)}, f32[8,32,128]{2,1,0:T(8,128)}, u32[]{:S(2)}) copy-start(f32[8,32,128]{2,1,0:T(8,128)} %get-tuple-element.14) | copy-start | bytes 393220
  106.6 9.3 %copy-start.8 = (f32[8,32,128]{2,1,0:T(8,128)S(1)}, f32[8,32,128]{2,1,0:T(8,128)}, u32[]{:S(2)}) copy-start(f32[8,32,128]{2,1,0:T(8,128)} %get-tuple-element.15) | copy-start | bytes 393220
  106.6 10.8 %copy-start.7 = (f32[8,32,128]{2,1,0:T(8,128)S(1)}, f32[8,32,128]{2,1,0:T(8,128)}, u32[]{:S(2)}) copy-start(f32[8,32,128]{2,1,0:T(8,128)} %get-tuple-element.16) | copy-start | bytes 393220
  111.6 19.0 %all-to-all-start.3 = ((f32[32,4,8,128]{3,2,1,0:T(8,128)}), f32[32,4,8,128]{3,2,1,0:T(8,128)S(1)}, u32[]{:S(2)}, u32[]{:S(2)}) async-start(f32[32,4,8,128]{3,2,1,0:T(8,128)} %poisson.1), calls=%async_computation.3 | async-start | bytes 1048576 | tf_op jit(solution)/shard_map/all_to_all | solution.py:826
  114.2 10.8 %collective-permute-start = (f32[8,32,128]{2,1,0:T(8,128)S(1)}, f32[8,32,128]{2,1,0:T(8,128)S(1)}, u32[]{:S(2)}, u32[]{:S(2)}) collective-permute-start(f32[8,32,128]{2,1,0:T(8,128)S(1)} %copy-done.9), channel_id=1, source_target_pairs={{0,8},{8,16},{16,24},{24,0},{1,9},{9,17},{17,25},{25,1},{2,10},{10... | collective-permute-start | bytes 393224 | tf_op jit(solution)/shard_map/ppermute | solution.py:882
  115.9 12.0 %collective-permute-start.1 = (f32[8,32,128]{2,1,0:T(8,128)S(1)}, f32[8,32,128]{2,1,0:T(8,128)S(1)}, u32[]{:S(2)}, u32[]{:S(2)}) collective-permute-start(f32[8,32,128]{2,1,0:T(8,128)S(1)} %copy-done.8), channel_id=1, source_target_pairs={{0,16},{8,24},{16,0},{24,8},{1,17},{9,25},{17,1},{25,9},{2,18},{10... | collective-permute-start | bytes 393224 | tf_op jit(solution)/shard_map/ppermute | solution.py:882
  117.4 10.5 %collective-permute-start.2 = (f32[8,32,128]{2,1,0:T(8,128)S(1)}, f32[8,32,128]{2,1,0:T(8,128)S(1)}, u32[]{:S(2)}, u32[]{:S(2)}) collective-permute-start(f32[8,32,128]{2,1,0:T(8,128)S(1)} %copy-done.7), channel_id=1, source_target_pairs={{0,24},{8,0},{16,8},{24,16},{1,25},{9,1},{17,9},{25,17},{2,26},{10... | collective-permute-start | bytes 393224 | tf_op jit(solution)/shard_map/ppermute | solution.py:882
  125.0 2.9 %copy-start.4 = (f32[8,32,128]{2,1,0:T(8,128)}, f32[8,32,128]{2,1,0:T(8,128)S(1)}, u32[]{:S(2)}) copy-start(f32[8,32,128]{2,1,0:T(8,128)S(1)} %collective-permute-done.refs_1_) | copy-start | bytes 393220
  127.9 0.7 copy-start.5
  127.9 0.7 copy-start.6
  130.5 0.8 copy-start

commit v7 on v6

--- a/solution.py
+++ b/solution.py
@@ -494,15 +494,18 @@
     tiles = slots // LANES
     for t in range(tiles):
         tile = pencils[:, t * LANES : (t + 1) * LANES].reshape(count, rows, LANES)
-        out_ref[:, t * rows : (t + 1) * rows] = tile
+        if not has_column:
+            out_ref[:, t * rows : (t + 1) * rows] = tile
+            continue
+        for g in range(rows // 4):
+            out_ref[:, t * (rows // 4) + g] = tile[:, 4 * g : 4 * g + 4]
     if has_column:
         column = [
             column_ref[t * LANES : (t + 1) * LANES].astype(jnp.float32).reshape(1, LANES)
             for t in range(tiles)
         ]
-        blank = [jnp.zeros((8 - tiles, LANES), jnp.float32)]
-        column = jnp.concatenate(column + blank, axis=0)
-        out_ref[:, tiles * rows :] = jnp.broadcast_to(column[None], (count, 8, LANES))
+        column = jnp.concatenate(column + [jnp.zeros((4 - tiles, LANES), jnp.float32)], axis=0)
+        out_ref[:, tiles * rows // 4] = jnp.broadcast_to(column[None], (count, 4, LANES))
 
 
 def pack_band(band, count, coeffs, miller, slot, pencil, slots, column):
@@ -510,17 +513,18 @@
     width = pencil.shape[1] // 6
     rows = pencil.shape[0] // count * (slots // LANES)
     operands = [coeffs, miller, slot, pencil]
+    out_shape = (count, rows, LANES)
     if column is not None:
         operands.append(column)
-        rows += 8
+        out_shape = (count, rows // 4 + 1, 4, LANES)
     one_band = pl.BlockSpec((1, 2 * length, LANES), lambda i: (band, 0, 0))
     return pl.pallas_call(
         functools.partial(pack_kernel, width, column is not None),
         grid=(1,),
         in_specs=[one_band]
         + [pl.BlockSpec(x.shape, lambda i, n=x.ndim: (0,) * n) for x in operands[1:]],
-        out_specs=pl.BlockSpec((count, rows, LANES), lambda i: (0, 0, 0)),
-        out_shape=jax.ShapeDtypeStruct((count, rows, LANES), jnp.float32),
+        out_specs=pl.BlockSpec(out_shape, lambda i: (0,) * len(out_shape)),
+        out_shape=jax.ShapeDtypeStruct(out_shape, jnp.float32),
         scratch_shapes=[pltpu.VMEM((2 * slots, 2 * width), jnp.float32)]
         + [pltpu.VMEM((8 * RANK_LOW, LANES), jnp.float32)] * 6
         + [
@@ -544,7 +548,7 @@
     former_ref, chosen_ref, high_ref = (None,) * 3 if is_first else [rest.pop(0) for _ in range(3)]
     density_refs = [rest.pop(0) for _ in range(kpts if is_last else 1)]
     if is_first:
-        chosen_ref, high_ref = rest.pop(0), rest.pop(0)
+        coulomb_ref, chosen_ref, high_ref = rest.pop(0), rest.pop(0), rest.pop(0)
     send_ref = rest.pop(0) if is_last else None
     values, grid, whole = rest
     planes = density_refs[0].shape[0]
@@ -556,10 +560,17 @@
 
     for j in range(pws):
         for t in range(tiles):
-            taken = jnp.concatenate(
-                [came_ref[k * pws + j, t * part_rows : (t + 1) * part_rows] for k in range(kpts)],
-                axis=0,
-            )
+            if is_first:
+                groups = [
+                    came_ref[k * pws + j, t * (part_rows // 4) + g]
+                    for k in range(kpts)
+                    for g in range(part_rows // 4)
+                ]
+            else:
+                groups = [
+                    came_ref[k * pws + j, t * part_rows : (t + 1) * part_rows] for k in range(kpts)
+                ]
+            taken = jnp.concatenate(groups, axis=0)
             high, low = pieces(taken)
             first = (j * tiles + t) * LANES
             values[0:rows, first : first + LANES] = high
@@ -570,7 +581,7 @@
         ramps = ramp((LANES, tile), 1)
         for j in range(pws):
             for t in range(tiles):
-                column = came_ref[j, tiles * part_rows + t : tiles * part_rows + t + 1]
+                column = came_ref[j, tiles * part_rows // 4, t : t + 1]
                 column = column.astype(jnp.int32)
                 cell = ((column // NY + NX // 2) % NX - HALF // 2) * HALF
                 cell = cell + (column % NY + NY // 2) % NY - HALF // 2
@@ -578,42 +589,39 @@
                 lane = (cell % tile).astype(jnp.float32)
                 chosen_ref[first : first + LANES, :] = one_hot_lanes(lane, ramps)
                 high_ref[:, first : first + LANES] = sixteen((cell // tile).astype(jnp.float32))
-    left = lax.broadcasted_iota(jnp.int32, (kpts * planes, LANES), 1) < HALF
+        step_z = lax.broadcasted_iota(jnp.int32, (NZ, NX), 0)
+        step_x = lax.broadcasted_iota(jnp.int32, (NZ, NX), 1)
+        for q in range(coulomb_ref.shape[0]):
+            freq_y = jnp.full((NZ, NX), own_ref[1] + q, jnp.int32)
+            kernel = coulomb(signed_freq(step_z, NZ), signed_freq(step_x, NX), freq_y)
+            coulomb_ref[q] = kernel * (1.0 / (NX * NY * NZ))
+    left = lax.broadcasted_iota(jnp.int32, (planes, LANES), 1) < HALF
     together = 4
 
     def place(t, found):
         found = found[:rows] + found[rows:]
         for h in range(2):
-            real, imag = (
-                jnp.concatenate(
-                    [
-                        found[(2 * k + c) * planes : (2 * k + c + 1) * planes, h * LANES : (h + 1) * LANES]
-                        for k in range(kpts)
-                    ],
-                    axis=0,
+            for k in range(kpts):
+                real, imag = (
+                    found[(2 * k + c) * planes : (2 * k + c + 1) * planes, h * LANES : (h + 1) * LANES]
+                    for c in range(2)
                 )
-                for c in range(2)
-            )
-            even = jnp.where(left, real, pltpu.roll(imag, HALF, 1))
-            odd = jnp.where(left, pltpu.roll(real, HALF, 1), imag)
-            grid[pl.ds(t * 4 + 2 * h, kpts * planes, stride=HALF), :] = even
-            grid[pl.ds(t * 4 + 2 * h + 1, kpts * planes, stride=HALF), :] = odd
-
-    def some_tiles(i, unused):
-        high = high_ref[...]
-        zero = jnp.zeros_like(high)
+                first = (k * HALF + 4 * t + 2 * h) * planes
+                grid[first : first + planes, :] = jnp.where(left, real, pltpu.roll(imag, HALF, 1))
+                grid[first + planes : first + 2 * planes, :] = jnp.where(
+                    left, pltpu.roll(real, HALF, 1), imag
+                )
+
+    high = high_ref[...]
+    zero = jnp.zeros_like(high)
+    for start in range(0, HALF // 4, together):
         kept = []
-        for s in range(together):
-            here = high == (together * i + s).astype(jnp.float32).astype(jnp.bfloat16)
-            kept += [
-                jnp.where(here, values[r : r + 16, :], zero) for r in range(0, 2 * rows, 16)
-            ]
+        for t in range(start, start + together):
+            here = high == jnp.full_like(high, t)
+            kept += [jnp.where(here, values[r : r + 16, :], zero) for r in range(0, 2 * rows, 16)]
         found = mul(jnp.concatenate(kept, axis=0), chosen_ref[...], NN)
         for s in range(together):
-            place(together * i + s, found[2 * rows * s : 2 * rows * (s + 1)])
-        return unused
-
-    lax.fori_loop(0, HALF // 4 // together, some_tiles, 0)
+            place(start + s, found[2 * rows * s : 2 * rows * (s + 1)])
 
     sum_of = count_ref[0]
     for k in range(1, kpts):
@@ -629,13 +637,7 @@
     first_row = lax.broadcasted_iota(jnp.int32, (2 * HALF, NX), 0) == 0
 
     def transform(p):
-        lines = jnp.concatenate(
-            [
-                grid[(k * planes + p) * HALF : (k * planes + p + 1) * HALF, :]
-                for k in range(kpts)
-            ],
-            axis=0,
-        )
+        lines = grid[pl.ds(p, kpts * HALF, stride=planes), :]
         mixed = mul3_right(lines, wave_y_ref[...], NN)
         mixed = jnp.concatenate(
             [
@@ -655,10 +657,10 @@
         if former_ref is not None:
             density = density + former_ref[p]
         if is_last:
-            whole[...] = density
+            whole[p] = density
             for s, density_ref in enumerate(density_refs):
                 first = pl.multiple_of(lax.rem(own_ref[0] + s, kpts) * block, block)
-                density_ref[p] = whole[pl.ds(first, block), :]
+                density_ref[p] = whole[p, pl.ds(first, block), :]
         else:
             density_refs[0][p] = density
         if is_last:
@@ -686,6 +688,7 @@
     else:
         out_shape = [jax.ShapeDtypeStruct((planes, NX, NY), jnp.float32)]
     if is_first:
+        out_shape.append(jax.ShapeDtypeStruct((HALF // came.shape[0], NZ, NX), jnp.float32))
         out_shape.append(jax.ShapeDtypeStruct((total, 4 * HALF), jnp.bfloat16))
         out_shape.append(jax.ShapeDtypeStruct((16, total), jnp.bfloat16))
     if is_last:
@@ -699,7 +702,7 @@
         scratch_shapes=[
             pltpu.VMEM((2 * rows, total), jnp.bfloat16),
             pltpu.VMEM((kpts * planes * HALF, LANES), jnp.float32),
-            pltpu.VMEM((NX, NY), jnp.float32),
+            pltpu.VMEM((planes, NX, NY), jnp.float32),
         ],
         compiler_params=pltpu.CompilerParams(vmem_limit_bytes=VMEM_LIMIT),
         cost_estimate=pl.CostEstimate(
@@ -709,52 +712,41 @@
     )(*operands)
 
 
-def poisson_kernel(pws, first_ref, came_ref, forth_ref, back_ref, both_x_ref, send_ref):
+def poisson_kernel(pws, own_ref, kernel_ref, came_ref, forth_ref, back_ref, both_x_ref, send_ref):
     count, parts, planes, unused = came_ref.shape
-    pairs = parts // 2
-    fields = [came_ref[:, i].reshape(NZ, NX) for i in range(parts)]
-    level = jnp.mean(fields[0], axis=(0, 1), keepdims=True)
-    fields[0] = fields[0] - jnp.where(first_ref[0] == 0, level, 0.0)
-    field = jnp.concatenate(fields, axis=1)
-    turned = mul3_left(forth_ref[...], field, NN)
-
-    def part(array, half, i):
-        return array[half * NZ : (half + 1) * NZ, i * NX : (i + 1) * NX]
-
-    lines = []
-    for q in range(pairs):
-        lines.append(part(turned, 0, 2 * q) + part(turned, 1, 2 * q + 1))
-        lines.append(part(turned, 0, 2 * q + 1) - part(turned, 1, 2 * q))
-    spectrum = mul3_right(jnp.concatenate(lines, axis=0), both_x_ref[...], NN)
-
-    step_z = lax.broadcasted_iota(jnp.int32, (NZ, NX), 0)
-    step_x = lax.broadcasted_iota(jnp.int32, (NZ, NX), 1)
-    lines = []
-    for q in range(pairs):
-        real = spectrum[2 * q * NZ : (2 * q + 1) * NZ]
-        imag = spectrum[(2 * q + 1) * NZ : (2 * q + 2) * NZ]
-        freq_y = jnp.full((NZ, NX), first_ref[0] + q, jnp.int32)
-        kernel = coulomb(signed_freq(step_z, NZ), signed_freq(step_x, NX), freq_y)
-        kernel = kernel * (1.0 / (NX * NY * NZ))
-        lines.append((real[:, :NX] + imag[:, NX:]) * kernel)
-        lines.append((imag[:, :NX] - real[:, NX:]) * kernel)
-    turned = mul3_right(jnp.concatenate(lines, axis=0), both_x_ref[...], NN)
-    lines = []
-    for q in range(pairs):
-        real = turned[2 * q * NZ : (2 * q + 1) * NZ]
-        imag = turned[(2 * q + 1) * NZ : (2 * q + 2) * NZ]
-        lines.append(real[:, :NX] - imag[:, NX:])
-        lines.append(real[:, NX:] + imag[:, :NX])
-    turned = mul3_left(back_ref[...], jnp.concatenate(lines, axis=1), NN)
-
     kpts = count // pws
     merged = NZ // pws // 8
     block = NX // kpts
     rows = pws * 8
     lane = lax.broadcasted_iota(jnp.int32, (rows, LANES), 1) // block
-    for q in range(pairs):
-        real = part(turned, 0, 2 * q) - part(turned, 1, 2 * q + 1)
-        imag = part(turned, 0, 2 * q + 1) + part(turned, 1, 2 * q)
+
+    def quarter(array, half, c):
+        return array[half * NZ : (half + 1) * NZ, c * NX : (c + 1) * NX]
+
+    for q in range(parts // 2):
+        real, imag = (came_ref[:, 2 * q + c].reshape(NZ, NX) for c in range(2))
+        if q == 0:
+            level = jnp.mean(real, axis=(0, 1), keepdims=True)
+            real = real - jnp.where(own_ref[1] == 0, level, 0.0)
+        turned = mul3_left(forth_ref[...], jnp.concatenate((real, imag), axis=1), NN)
+        lines = (
+            quarter(turned, 0, 0) + quarter(turned, 1, 1),
+            quarter(turned, 0, 1) - quarter(turned, 1, 0),
+        )
+        turned = mul3_right(jnp.concatenate(lines, axis=0), both_x_ref[...], NN)
+        kernel = kernel_ref[q]
+        lines = (
+            (quarter(turned, 0, 0) + quarter(turned, 1, 1)) * kernel,
+            (quarter(turned, 1, 0) - quarter(turned, 0, 1)) * kernel,
+        )
+        turned = mul3_right(jnp.concatenate(lines, axis=0), both_x_ref[...], NN)
+        lines = (
+            quarter(turned, 0, 0) - quarter(turned, 1, 1),
+            quarter(turned, 0, 1) + quarter(turned, 1, 0),
+        )
+        turned = mul3_left(back_ref[...], jnp.concatenate(lines, axis=1), NN)
+        real = quarter(turned, 0, 0) - quarter(turned, 1, 1)
+        imag = quarter(turned, 0, 1) + quarter(turned, 1, 0)
         for c, value in enumerate((real, imag)):
             for a in range(kpts):
                 packed = None
@@ -767,36 +759,44 @@
                 send_ref[a * pws : (a + 1) * pws, 2 * q + c] = packed.reshape(pws, 8, LANES)
 
 
-def poisson(pws, first, came, forth, back, both_x):
+def poisson(pws, own, kernel, came, forth, back, both_x):
     vmem = pl.BlockSpec(memory_space=pltpu.VMEM)
     count, parts, unused, unused = came.shape
     return pl.pallas_call(
         functools.partial(poisson_kernel, pws),
-        in_specs=[pl.BlockSpec(memory_space=pltpu.SMEM)] + [vmem] * 4,
+        in_specs=[pl.BlockSpec(memory_space=pltpu.SMEM)] + [vmem] * 5,
         out_specs=vmem,
         out_shape=jax.ShapeDtypeStruct((count, parts, 8, LANES), jnp.float32),
         compiler_params=pltpu.CompilerParams(vmem_limit_bytes=VMEM_LIMIT),
         name="poisson",
-    )(first, came, forth, back, both_x)
+    )(own, kernel, came, forth, back, both_x)
 
 
 def assemble_kernel(own_ref, *refs):
-    block_refs, density_ref = refs[:-1], refs[-1]
+    *block_refs, density_ref, sems = refs
     kpts = len(block_refs)
     part = density_ref.shape[0] // kpts
+    copies = []
     for s, block_ref in enumerate(block_refs):
         sender = lax.rem(own_ref[0] + kpts - s, kpts)
-        density_ref[pl.ds(sender * part, part)] = block_ref[...]
+        copies.append(
+            pltpu.make_async_copy(block_ref, density_ref.at[pl.ds(sender * part, part)], sems.at[s])
+        )
+    for copy in copies:
+        copy.start()
+    for copy in copies:
+        copy.wait()
 
 
 def assemble(own, blocks):
-    vmem = pl.BlockSpec(memory_space=pltpu.VMEM)
     part, block, length = blocks[0].shape
     return pl.pallas_call(
         assemble_kernel,
-        in_specs=[pl.BlockSpec(memory_space=pltpu.SMEM)] + [vmem] * len(blocks),
-        out_specs=vmem,
+        in_specs=[pl.BlockSpec(memory_space=pltpu.SMEM)]
+        + [pl.BlockSpec(memory_space=pl.ANY)] * len(blocks),
+        out_specs=pl.BlockSpec(memory_space=pl.ANY),
         out_shape=jax.ShapeDtypeStruct((part * len(blocks), block, length), jnp.float32),
+        scratch_shapes=[pltpu.SemaphoreType.DMA((len(blocks),))],
         name="assemble",
     )(own, *blocks)
 
@@ -857,7 +857,8 @@
             band, count, coeffs, miller, slot, pencil, slots, column
         )
         arrived.append(exchange(packed, everyone))
-    own = lax.axis_index("kpt").astype(jnp.int32).reshape(1)
+    device = lax.axis_index("kpt") * pws + lax.axis_index("pw")
+    own = jnp.stack((lax.axis_index("kpt"), device * (parts // 2))).astype(jnp.int32)
     former = chosen = None
     for band in range(band_count):
         forth = forth_y if band == band_count - 1 else None
@@ -876,15 +877,14 @@
             chosen,
         )
         former = made_here[0]
-        chosen = made_here[-2:] if band == 0 else chosen
+        if band == 0:
+            kernel, *chosen = made_here[kpts if forth is not None else 1 :][:3]
     half = exchange(made_here[-1].reshape(count, parts, planes, NX), everyone)
     blocks = [made_here[0]] + [
         lax.ppermute(made_here[s], "kpt", [(a, (a + s) % kpts) for a in range(kpts)])
         for s in range(1, kpts)
     ]
-    device = lax.axis_index("kpt") * pws + lax.axis_index("pw")
-    first = (device * (parts // 2)).astype(jnp.int32).reshape(1)
-    back = poisson(pws, first, half, forth_z, back_z, both_x)
+    back = poisson(pws, own, kernel, half, forth_z, back_z, both_x)
     back = exchange(back, everyone).reshape(count * parts * 8, LANES)
     return assemble(own, blocks), finish(NZ // pws, NX // kpts, back, back_y)
 

time: 134 us -> 148 us (1.10)
  blocking collectives: 0 us -> 19.7 us
  waiting for transfers between devices: 46.3 us -> 28.6 us
  Pallas kernels: 63.4 us -> 78.1 us
  starting transfers between devices: 19.9 us -> 17.3 us
    all_to_all x0 -> x1, blocking collectives: none -> 19.7 us  [exchange(): return lax.all_to_all(array, axes, split_axis=0, concat_axis=0, tiled=True)]
    all_to_all x4 -> x3, waiting for transfers between devices: 37.2 us -> 19.5 us  [exchange(): return lax.all_to_all(array, axes, split_axis=0, concat_axis=0, tiled=True)]
    pallas_call x1, Pallas kernels: 1.92 us -> 17.7 us  [assemble(): pl.pallas_call(assemble_kernel, in_specs=[pl.BlockSpec(memory_space=pltpu...]
    all_to_all x4 -> x3, starting transfers between devices: 15.3 us -> 12.7 us  [exchange(): return lax.all_to_all(array, axes, split_axis=0, concat_axis=0, tiled=True)]
    pallas_call x2, Pallas kernels: 23.5 us -> 21.9 us  [wave_band(): pl.pallas_call(functools.partial(wave_kernel, kpts, tiles, scale, is_firs...]
    unnamed x20 -> x18, local copies, waits for them, and re-layouts: 3.19 us -> 2.38 us
  transfers between devices with their start and end apart: 7 -> 6, of which waited for: 5 -> 4; matrix products, arithmetic and copies ran while one was open for 0% -> 0% of each run, Pallas kernels for 21% -> 29%
where the time goes in v7:
time: 148 us; the launch traced here: 147 us
  Pallas kernels  78.1 us (53%)
  waiting for transfers between devices  28.6 us (19%)
  blocking collectives  19.7 us (13%)
  starting transfers between devices  17.3 us (12%)
  local copies, waits for them, and re-layouts  2.38 us (2%)
    pallas_call x2, Pallas kernels, pack_band(): pl.pallas_call(functools.partial(pack_kernel, width, column is not None),...  30.7 us
    pallas_call x2, Pallas kernels, wave_band(): pl.pallas_call(functools.partial(wave_kernel, kpts, tiles, scale, is_firs...  21.9 us
    all_to_all x1, blocking collectives, exchange(): return lax.all_to_all(array, axes, split_axis=0, concat_axis=0, tiled=True)  19.7 us
    all_to_all x3, waiting for transfers between devices, exchange(): return lax.all_to_all(array, axes, split_axis=0, concat_axis=0, tiled=True)  19.5 us
    pallas_call x1, Pallas kernels, assemble(): pl.pallas_call(assemble_kernel, in_specs=[pl.BlockSpec(memory_space=pltpu...  17.7 us
    all_to_all x3, starting transfers between devices, exchange(): return lax.all_to_all(array, axes, split_axis=0, concat_axis=0, tiled=True)  12.7 us
    ppermute x3, waiting for transfers between devices, local_planes(): lax.ppermute(made_here[s], 'kpt', [(a, (a + s) % kpts) for a in range(kpt...  9.07 us
    pallas_call x1, Pallas kernels, poisson(): pl.pallas_call(functools.partial(poisson_kernel, pws), in_specs=[pl.Block...  5.57 us
  transfers between devices with their start and end apart: 6, of which 4 were waited for; matrix products, arithmetic and copies ran while one was open for 0% of the time, Pallas kernels for 29%

profile of v7, /device:TPU:0, one launch (start us, length us, event | category | flops | bytes accessed | tf_op | source)
XLA Modules:
  0.0 147.4 jit_solution(15693041763978301496)
XLA Ops:
  0.6 15.4 %pack_band.3 = f32[32,13,4,128]{3,2,1,0:T(4,128)} custom-call(f32[2,768,128]{2,1,0:T(8,128)} %bitcast.13, s32[384,128]{1,0:T(8,128)} %bitcast.15, s32[384,128]{1,0:T(8,128)} %bitcast.17, bf16[512,768]{1,0:T(8,128)(2,1)} %constant.28.clone.refs_3_, s32[384]{0:T(512)} %refs_4_.3), custom_call_target="tpu_custom_call" | custom-call | flops 19327352832 | bytes 786432 | tf_op jit(solution)/shard_map/pack_band/pallas_call | solution.py:521
  16.0 7.3 %all-to-all-start.1 = ((f32[32,13,4,128]{3,2,1,0:T(4,128)}), f32[32,13,4,128]{3,2,1,0:T(4,128)S(1)}, u32[]{:S(2)}, u32[]{:S(2)}) async-start(f32[32,13,4,128]{3,2,1,0:T(4,128)} %pack_band.3), calls=%async_computation.1 | async-start | bytes 1703936 | tf_op jit(solution)/shard_map/all_to_all | solution.py:826
  23.3 15.4 %pack_band.2 = f32[32,48,128]{2,1,0:T(8,128)} custom-call(f32[2,768,128]{2,1,0:T(8,128)} %bitcast.14, s32[384,128]{1,0:T(8,128)} %bitcast.16, s32[384,128]{1,0:T(8,128)} %bitcast.18, bf16[512,768]{1,0:T(8,128)(2,1)} %constant.28.clone.refs_3_), custom_call_target="tpu_custom_call" | custom-call | flops 19327352832 | bytes 786432 | tf_op jit(solution)/shard_map/pack_band/pallas_call | solution.py:521
  38.7 8.0 %all-to-all-done.1.refs_2_ = f32[32,13,4,128]{3,2,1,0:T(4,128)S(1)} async-done(((f32[32,13,4,128]{3,2,1,0:T(4,128)}), f32[32,13,4,128]{3,2,1,0:T(4,128)S(1)}, u32[]{:S(2)}, u32[]{:S(2)}) %all-to-all-start.1) | async-done | bytes 852000 | tf_op jit(solution)/shard_map/all_to_all | solution.py:826
  46.7 0.0 copy-start.1
  46.7 2.8 %all-to-all-start = ((f32[32,48,128]{2,1,0:T(8,128)}), f32[32,48,128]{2,1,0:T(8,128)S(1)}, u32[]{:S(2)}, u32[]{:S(2)}) async-start(f32[32,48,128]{2,1,0:T(8,128)} %pack_band.2), calls=%async_computation | async-start | bytes 1572864 | tf_op jit(solution)/shard_map/all_to_all | solution.py:826
  49.5 0.6 pad_add_fusion.refs_0_.own_ref
  50.1 0.0 copy-done.1
  50.1 9.6 %wave_band.2 = (f32[8,128,128]{2,1,0:T(8,128)}, f32[2,256,128]{2,1,0:T(8,128)}, bf16[3072,256]{1,0:T(8,128)(2,1)}, bf16[16,3072]{1,0:T(8,128)(2,1)}) custom-call(s32[2]{0:T(128)} %pad_add_fusion.refs_0_.own_ref, s32[4]{0:T(128)} %refs_1_.3, f32[32,13,4,128]{3,2,1,0:T(4,128)} %copy-done.1, bf16[384,256]{1,0:T(8,128)(2,1)} %constant.33.clone.refs_3_, ...), custom_call_target="tpu_custom_call" | custom-call | flops 3221225472 | bytes 851968 | tf_op jit(solution)/shard_map/wave_band/pallas_call | solution.py:697
  59.8 11.5 %all-to-all-done.refs_2_ = f32[32,48,128]{2,1,0:T(8,128)S(1)} async-done(((f32[32,48,128]{2,1,0:T(8,128)}), f32[32,48,128]{2,1,0:T(8,128)S(1)}, u32[]{:S(2)}, u32[]{:S(2)}) %all-to-all-start) | async-done | bytes 786464 | tf_op jit(solution)/shard_map/all_to_all | solution.py:826
  71.3 0.9 copy-done.2
  72.2 12.3 %wave_band.3 = (f32[8,32,128]{2,1,0:T(8,128)}, f32[8,32,128]{2,1,0:T(8,128)}, f32[8,32,128]{2,1,0:T(8,128)}, f32[8,32,128]{2,1,0:T(8,128)}, f32[1024,128]{1,0:T(8,128)}) custom-call(s32[2]{0:T(128)} %pad_add_fusion.refs_0_.own_ref, s32[4]{0:T(128)} %refs_1_.3, f32[32,48,128]{2,1,0:T(8,128)} %copy-done.2, bf16[384,256]{1,0:T(8,128)(2,1)} %constant.33.clone.refs_3_, ...), custom_call_target="tpu_custom_call" | custom-call | flops 3221225472 | bytes 786432 | tf_op jit(solution)/shard_map/wave_band/pallas_call | solution.py:697
  84.4 19.7 %all_to_all.20.came_ref = f32[32,4,8,128]{3,2,1,0:T(8,128)} all-to-all(f32[32,4,8,128]{3,2,1,0:T(8,128)} %bitcast.12), channel_id=1, replica_groups=mesh['kpt'=4,'pw'=8] {'kpt','pw'}, dimensions={0} | all-to-all | bytes 1048576 | tf_op jit(solution)/shard_map/all_to_all | solution.py:826
  104.1 5.6 %poisson.1 = f32[32,4,8,128]{3,2,1,0:T(8,128)} custom-call(s32[2]{0:T(128)} %pad_add_fusion.refs_0_.own_ref, f32[2,256,128]{2,1,0:T(8,128)} %get-tuple-element.18.kernel_ref, f32[32,4,8,128]{3,2,1,0:T(8,128)} %all_to_all.20.came_ref, bf16[512,768]{1,0:T(8,128)(2,1)} %constant.31.clone.forth_ref, bf16[512,768]{1,0:T(8,128)(2,1)} %constant.32.clone.back_ref, ...), custom_call_target="tpu_custom_call" | custom-call | tf_op jit(solution)/shard_map/poisson/pallas_call | solution.py:765
  109.7 2.6 %all-to-all-start.3 = ((f32[32,4,8,128]{3,2,1,0:T(8,128)}), f32[32,4,8,128]{3,2,1,0:T(8,128)S(1)}, u32[]{:S(2)}, u32[]{:S(2)}) async-start(f32[32,4,8,128]{3,2,1,0:T(8,128)} %poisson.1), calls=%async_computation.3 | async-start | bytes 1048576 | tf_op jit(solution)/shard_map/all_to_all | solution.py:826
  112.3 0.0 copy-done.8
  112.3 1.7 %collective-permute-start = (f32[8,32,128]{2,1,0:T(8,128)S(1)}, f32[8,32,128]{2,1,0:T(8,128)S(1)}, u32[]{:S(2)}, u32[]{:S(2)}) collective-permute-start(f32[8,32,128]{2,1,0:T(8,128)S(1)} %copy-done.8), channel_id=1, source_target_pairs={{0,8},{8,16},{16,24},{24,0},{1,9},{9,17},{17,25},{25,1},{2,10},{10... | collective-permute-start | bytes 393224 | tf_op jit(solution)/shard_map/ppermute | solution.py:884
  114.0 0.0 copy-done.7
  114.0 1.5 %collective-permute-start.1 = (f32[8,32,128]{2,1,0:T(8,128)S(1)}, f32[8,32,128]{2,1,0:T(8,128)S(1)}, u32[]{:S(2)}, u32[]{:S(2)}) collective-permute-start(f32[8,32,128]{2,1,0:T(8,128)S(1)} %copy-done.7), channel_id=1, source_target_pairs={{0,16},{8,24},{16,0},{24,8},{1,17},{9,25},{17,1},{25,9},{2,18},{10... | collective-permute-start | bytes 393224 | tf_op jit(solution)/shard_map/ppermute | solution.py:884
  115.5 0.0 copy-done.6
  115.5 1.4 collective-permute-start.2
  116.9 6.2 %collective-permute-done.refs_1_ = f32[8,32,128]{2,1,0:T(8,128)S(1)} collective-permute-done((f32[8,32,128]{2,1,0:T(8,128)S(1)}, f32[8,32,128]{2,1,0:T(8,128)S(1)}, u32[]{:S(2)}, u32[]{:S(2)}) %collective-permute-start) | collective-permute-done | bytes 131104 | tf_op jit(solution)/shard_map/ppermute | solution.py:884
  123.1 2.9 %collective-permute-done.1.refs_2_ = f32[8,32,128]{2,1,0:T(8,128)S(1)} collective-permute-done((f32[8,32,128]{2,1,0:T(8,128)S(1)}, f32[8,32,128]{2,1,0:T(8,128)S(1)}, u32[]{:S(2)}, u32[]{:S(2)}) %collective-permute-start.1) | collective-permute-done | bytes 131104 | tf_op jit(solution)/shard_map/ppermute | solution.py:884
  126.0 0.0 collective-permute-done.2.refs_3_
  126.0 0.0 copy-done.3
  126.0 0.6 copy-done.4
  126.6 0.0 copy-done.5
  126.7 17.7 %assemble.1 = f32[32,32,128]{2,1,0:T(8,128)} custom-call(s32[2]{0:T(128)} %pad_add_fusion.refs_0_.own_ref, f32[8,32,128]{2,1,0:T(8,128)} %get-tuple-element.14.refs_0_, f32[8,32,128]{2,1,0:T(8,128)} %copy-done.3, f32[8,32,128]{2,1,0:T(8,128)} %copy-done.4, f32[8,32,128]{2,1,0:T(8,128)} %copy-done.5), custom_call_target="tpu_custom_call" | custom-call | tf_op jit(solution)/shard_map/assemble/pallas_call | solution.py:793
  144.4 0.0 all-to-all-done.3
  144.4 0.0 copy-start
  144.4 0.8 copy-done
  145.2 2.3 %finish.1 = f32[32,32,128]{2,1,0:T(8,128)} custom-call(f32[1024,128]{1,0:T(8,128)} %bitcast.11, bf16[384,128]{1,0:T(8,128)(2,1)} %constant.34.clone.back_ref), custom_call_target="tpu_custom_call" | custom-call | tf_op jit(solution)/shard_map/finish/pallas_call | solution.py:815
  (7 shorter events, 0.0 us)
Async XLA Ops:
  16.0 30.7 %all-to-all-start.1 = ((f32[32,13,4,128]{3,2,1,0:T(4,128)}), f32[32,13,4,128]{3,2,1,0:T(4,128)S(1)}, u32[]{:S(2)}, u32[]{:S(2)}) async-start(f32[32,13,4,128]{3,2,1,0:T(4,128)} %pack_band.3), calls=%async_computation.1 | async-start | bytes 1703936 | tf_op jit(solution)/shard_map/all_to_all | solution.py:826
  46.7 3.5 %copy-start.1 = (f32[32,13,4,128]{3,2,1,0:T(4,128)}, f32[32,13,4,128]{3,2,1,0:T(4,128)S(1)}, u32[]{:S(2)}) copy-start(f32[32,13,4,128]{3,2,1,0:T(4,128)S(1)} %all-to-all-done.1.refs_2_) | copy-start | bytes 2555908
  46.7 24.6 %all-to-all-start = ((f32[32,48,128]{2,1,0:T(8,128)}), f32[32,48,128]{2,1,0:T(8,128)S(1)}, u32[]{:S(2)}, u32[]{:S(2)}) async-start(f32[32,48,128]{2,1,0:T(8,128)} %pack_band.2), calls=%async_computation | async-start | bytes 1572864 | tf_op jit(solution)/shard_map/all_to_all | solution.py:826
  71.3 0.9 copy-start.2
  104.1 8.2 %copy-start.8 = (f32[8,32,128]{2,1,0:T(8,128)S(1)}, f32[8,32,128]{2,1,0:T(8,128)}, u32[]{:S(2)}) copy-start(f32[8,32,128]{2,1,0:T(8,128)} %get-tuple-element.15) | copy-start | bytes 393220
  104.1 9.9 %copy-start.7 = (f32[8,32,128]{2,1,0:T(8,128)S(1)}, f32[8,32,128]{2,1,0:T(8,128)}, u32[]{:S(2)}) copy-start(f32[8,32,128]{2,1,0:T(8,128)} %get-tuple-element.16) | copy-start | bytes 393220
  104.1 11.4 %copy-start.6 = (f32[8,32,128]{2,1,0:T(8,128)S(1)}, f32[8,32,128]{2,1,0:T(8,128)}, u32[]{:S(2)}) copy-start(f32[8,32,128]{2,1,0:T(8,128)} %get-tuple-element.17) | copy-start | bytes 393220
  109.7 34.7 %all-to-all-start.3 = ((f32[32,4,8,128]{3,2,1,0:T(8,128)}), f32[32,4,8,128]{3,2,1,0:T(8,128)S(1)}, u32[]{:S(2)}, u32[]{:S(2)}) async-start(f32[32,4,8,128]{3,2,1,0:T(8,128)} %poisson.1), calls=%async_computation.3 | async-start | bytes 1048576 | tf_op jit(solution)/shard_map/all_to_all | solution.py:826
  112.3 10.8 %collective-permute-start = (f32[8,32,128]{2,1,0:T(8,128)S(1)}, f32[8,32,128]{2,1,0:T(8,128)S(1)}, u32[]{:S(2)}, u32[]{:S(2)}) collective-permute-start(f32[8,32,128]{2,1,0:T(8,128)S(1)} %copy-done.8), channel_id=1, source_target_pairs={{0,8},{8,16},{16,24},{24,0},{1,9},{9,17},{17,25},{25,1},{2,10},{10... | collective-permute-start | bytes 393224 | tf_op jit(solution)/shard_map/ppermute | solution.py:884
  114.0 12.0 %collective-permute-start.1 = (f32[8,32,128]{2,1,0:T(8,128)S(1)}, f32[8,32,128]{2,1,0:T(8,128)S(1)}, u32[]{:S(2)}, u32[]{:S(2)}) collective-permute-start(f32[8,32,128]{2,1,0:T(8,128)S(1)} %copy-done.7), channel_id=1, source_target_pairs={{0,16},{8,24},{16,0},{24,8},{1,17},{9,25},{17,1},{25,9},{2,18},{10... | collective-permute-start | bytes 393224 | tf_op jit(solution)/shard_map/ppermute | solution.py:884
  115.5 10.5 %collective-permute-start.2 = (f32[8,32,128]{2,1,0:T(8,128)S(1)}, f32[8,32,128]{2,1,0:T(8,128)S(1)}, u32[]{:S(2)}, u32[]{:S(2)}) collective-permute-start(f32[8,32,128]{2,1,0:T(8,128)S(1)} %copy-done.6), channel_id=1, source_target_pairs={{0,24},{8,0},{16,8},{24,16},{1,25},{9,1},{17,9},{25,17},{2,26},{10... | collective-permute-start | bytes 393224 | tf_op jit(solution)/shard_map/ppermute | solution.py:884
  123.1 2.9 %copy-start.3 = (f32[8,32,128]{2,1,0:T(8,128)}, f32[8,32,128]{2,1,0:T(8,128)S(1)}, u32[]{:S(2)}) copy-start(f32[8,32,128]{2,1,0:T(8,128)S(1)} %collective-permute-done.refs_1_) | copy-start | bytes 393220
  126.0 0.6 copy-start.4
  126.0 0.7 copy-start.5
  144.4 0.8 copy-start

commit v8 on v7

--- a/solution.py
+++ b/solution.py
@@ -260,7 +260,7 @@
 
     angle = angles(own_y, grid_y, NY)
     cos, sin = np.cos(angle), np.sin(angle)
-    return_table["forth_y"] = np.stack((cos, -sin), axis=1).reshape(2 * HALF, NY)
+    return_table["forth_y"] = np.stack((cos, -sin), axis=1).reshape(2 * HALF, NY).T
     twice = np.where(own_y == 0, 1.0, 2.0)[:, None]
     return_table["back_y"] = np.stack((twice * cos, -twice * sin), axis=1).reshape(2 * HALF, NY)
 
@@ -378,7 +378,9 @@
     coeff_ref, miller_ref, slot_ref, pencil_ref = refs[:4]
     rest = list(refs[4:])
     column_ref = rest.pop(0) if has_column else None
-    out_ref, total, key_ref, real_ref, imag_ref, lane_ref, real_low, imag_low, ramp_ref, step_ref = rest
+    out_ref, total, key_ref, real_ref, imag_ref, lane_ref, real_low, imag_low, ramp_ref, step_ref, held, sem = rest
+    fetch = pltpu.make_async_copy(pencil_ref, held, sem)
+    fetch.start()
     half = total.shape[0] // 4
     slots = 2 * half
     count = out_ref.shape[0]
@@ -490,7 +492,8 @@
                 axis=0,
             )
         )
-    pencils = mul(pencil_ref[...], jnp.concatenate((both[0], both[0], both[1]), axis=1), NT)
+    fetch.wait()
+    pencils = mul(held[...], jnp.concatenate((both[0], both[0], both[1]), axis=1), NT)
     tiles = slots // LANES
     for t in range(tiles):
         tile = pencils[:, t * LANES : (t + 1) * LANES].reshape(count, rows, LANES)
@@ -522,7 +525,12 @@
         functools.partial(pack_kernel, width, column is not None),
         grid=(1,),
         in_specs=[one_band]
-        + [pl.BlockSpec(x.shape, lambda i, n=x.ndim: (0,) * n) for x in operands[1:]],
+        + [
+            pl.BlockSpec(memory_space=pl.ANY)
+            if x is pencil
+            else pl.BlockSpec(x.shape, lambda i, n=x.ndim: (0,) * n)
+            for x in operands[1:]
+        ],
         out_specs=pl.BlockSpec(out_shape, lambda i: (0,) * len(out_shape)),
         out_shape=jax.ShapeDtypeStruct(out_shape, jnp.float32),
         scratch_shapes=[pltpu.VMEM((2 * slots, 2 * width), jnp.float32)]
@@ -530,6 +538,8 @@
         + [
             pltpu.VMEM((LANES, 2 * width), jnp.bfloat16),
             pltpu.VMEM((slots // 2, LANES), jnp.bfloat16),
+            pltpu.VMEM(pencil.shape, jnp.bfloat16),
+            pltpu.SemaphoreType.DMA,
         ],
         compiler_params=pltpu.CompilerParams(vmem_limit_bytes=VMEM_LIMIT),
         cost_estimate=pl.CostEstimate(
@@ -634,11 +644,11 @@
         jnp.concatenate([spread(count_ref[k]) / spread(sum_of) * scale] * (NX // 8), axis=0)
         for k in range(kpts)
     ]
-    first_row = lax.broadcasted_iota(jnp.int32, (2 * HALF, NX), 0) == 0
-
-    def transform(p):
-        lines = grid[pl.ds(p, kpts * HALF, stride=planes), :]
-        mixed = mul3_right(lines, wave_y_ref[...], NN)
+    lines = [grid[pl.ds(p, kpts * HALF, stride=planes), :] for p in range(planes)]
+    lines = mul3_right(jnp.concatenate(lines, axis=0), wave_y_ref[...], NN)
+
+    for p in range(planes):
+        mixed = lines[p * kpts * HALF : (p + 1) * kpts * HALF]
         mixed = jnp.concatenate(
             [
                 jnp.concatenate(
@@ -658,19 +668,21 @@
             density = density + former_ref[p]
         if is_last:
             whole[p] = density
-            for s, density_ref in enumerate(density_refs):
-                first = pl.multiple_of(lax.rem(own_ref[0] + s, kpts) * block, block)
-                density_ref[p] = whole[p, pl.ds(first, block), :]
         else:
             density_refs[0][p] = density
-        if is_last:
-            level = jnp.mean(density[:8], axis=(0, 1), keepdims=True)
-            half = mul3_left(forth_ref[...], density - level, NT)
-            half = half + jnp.where(first_row, level * NY, 0.0)
-            send_ref[pl.ds(p, 2 * HALF, stride=planes), :] = half
-
-    for p in range(planes):
-        transform(p)
+
+    if is_last:
+        for s, density_ref in enumerate(density_refs):
+            first = pl.multiple_of(lax.rem(own_ref[0] + s, kpts) * block, block)
+            density_ref[...] = whole[:, pl.ds(first, block), :]
+        level = jnp.mean(whole[0, :8, :], axis=(0, 1), keepdims=True)
+        field = whole[...].reshape(planes * NX, NY) - level
+        half = mul3_right(field, forth_ref[...], NN)
+        first_row = lax.broadcasted_iota(jnp.int32, (2 * HALF, NX), 0) == 0
+        for p in range(planes):
+            turned = jnp.transpose(half[p * NX : (p + 1) * NX])
+            turned = turned + jnp.where(first_row, level * NY, 0.0)
+            send_ref[pl.ds(p, 2 * HALF, stride=planes), :] = turned
 
 
 def wave_band(kpts, tiles, total, scale, own, counts, came, wave_y, wave_x, forth, former, chosen):
@@ -714,39 +726,46 @@
 
 def poisson_kernel(pws, own_ref, kernel_ref, came_ref, forth_ref, back_ref, both_x_ref, send_ref):
     count, parts, planes, unused = came_ref.shape
+    pairs = parts // 2
+    fields = [came_ref[:, i].reshape(NZ, NX) for i in range(parts)]
+    level = jnp.mean(fields[0], axis=(0, 1), keepdims=True)
+    fields[0] = fields[0] - jnp.where(own_ref[1] == 0, level, 0.0)
+    field = jnp.concatenate(fields, axis=1)
+    turned = mul3_left(forth_ref[...], field, NN)
+
+    def part(array, half, i):
+        return array[half * NZ : (half + 1) * NZ, i * NX : (i + 1) * NX]
+
+    lines = []
+    for q in range(pairs):
+        lines.append(part(turned, 0, 2 * q) + part(turned, 1, 2 * q + 1))
+        lines.append(part(turned, 0, 2 * q + 1) - part(turned, 1, 2 * q))
+    spectrum = mul3_right(jnp.concatenate(lines, axis=0), both_x_ref[...], NN)
+
+    lines = []
+    for q in range(pairs):
+        real = spectrum[2 * q * NZ : (2 * q + 1) * NZ]
+        imag = spectrum[(2 * q + 1) * NZ : (2 * q + 2) * NZ]
+        kernel = kernel_ref[q]
+        lines.append((real[:, :NX] + imag[:, NX:]) * kernel)
+        lines.append((imag[:, :NX] - real[:, NX:]) * kernel)
+    turned = mul3_right(jnp.concatenate(lines, axis=0), both_x_ref[...], NN)
+    lines = []
+    for q in range(pairs):
+        real = turned[2 * q * NZ : (2 * q + 1) * NZ]
+        imag = turned[(2 * q + 1) * NZ : (2 * q + 2) * NZ]
+        lines.append(real[:, :NX] - imag[:, NX:])
+        lines.append(real[:, NX:] + imag[:, :NX])
+    turned = mul3_left(back_ref[...], jnp.concatenate(lines, axis=1), NN)
+
     kpts = count // pws
     merged = NZ // pws // 8
     block = NX // kpts
     rows = pws * 8
     lane = lax.broadcasted_iota(jnp.int32, (rows, LANES), 1) // block
-
-    def quarter(array, half, c):
-        return array[half * NZ : (half + 1) * NZ, c * NX : (c + 1) * NX]
-
-    for q in range(parts // 2):
-        real, imag = (came_ref[:, 2 * q + c].reshape(NZ, NX) for c in range(2))
-        if q == 0:
-            level = jnp.mean(real, axis=(0, 1), keepdims=True)
-            real = real - jnp.where(own_ref[1] == 0, level, 0.0)
-        turned = mul3_left(forth_ref[...], jnp.concatenate((real, imag), axis=1), NN)
-        lines = (
-            quarter(turned, 0, 0) + quarter(turned, 1, 1),
-            quarter(turned, 0, 1) - quarter(turned, 1, 0),
-        )
-        turned = mul3_right(jnp.concatenate(lines, axis=0), both_x_ref[...], NN)
-        kernel = kernel_ref[q]
-        lines = (
-            (quarter(turned, 0, 0) + quarter(turned, 1, 1)) * kernel,
-            (quarter(turned, 1, 0) - quarter(turned, 0, 1)) * kernel,
-        )
-        turned = mul3_right(jnp.concatenate(lines, axis=0), both_x_ref[...], NN)
-        lines = (
-            quarter(turned, 0, 0) - quarter(turned, 1, 1),
-            quarter(turned, 0, 1) + quarter(turned, 1, 0),
-        )
-        turned = mul3_left(back_ref[...], jnp.concatenate(lines, axis=1), NN)
-        real = quarter(turned, 0, 0) - quarter(turned, 1, 1)
-        imag = quarter(turned, 0, 1) + quarter(turned, 1, 0)
+    for q in range(pairs):
+        real = part(turned, 0, 2 * q) - part(turned, 1, 2 * q + 1)
+        imag = part(turned, 0, 2 * q + 1) + part(turned, 1, 2 * q)
         for c, value in enumerate((real, imag)):
             for a in range(kpts):
                 packed = None
@@ -772,54 +791,30 @@
     )(own, kernel, came, forth, back, both_x)
 
 
-def assemble_kernel(own_ref, *refs):
-    *block_refs, density_ref, sems = refs
+def finish_kernel(own_ref, came_ref, back_ref, *refs):
+    block_refs, density_ref, out_ref = refs[:-2], refs[-2], refs[-1]
     kpts = len(block_refs)
-    part = density_ref.shape[0] // kpts
-    copies = []
+    planes, block, unused = out_ref.shape
+    merged = planes // 8
     for s, block_ref in enumerate(block_refs):
         sender = lax.rem(own_ref[0] + kpts - s, kpts)
-        copies.append(
-            pltpu.make_async_copy(block_ref, density_ref.at[pl.ds(sender * part, part)], sems.at[s])
-        )
-    for copy in copies:
-        copy.start()
-    for copy in copies:
-        copy.wait()
-
-
-def assemble(own, blocks):
-    part, block, length = blocks[0].shape
-    return pl.pallas_call(
-        assemble_kernel,
-        in_specs=[pl.BlockSpec(memory_space=pltpu.SMEM)]
-        + [pl.BlockSpec(memory_space=pl.ANY)] * len(blocks),
-        out_specs=pl.BlockSpec(memory_space=pl.ANY),
-        out_shape=jax.ShapeDtypeStruct((part * len(blocks), block, length), jnp.float32),
-        scratch_shapes=[pltpu.SemaphoreType.DMA((len(blocks),))],
-        name="assemble",
-    )(own, *blocks)
-
-
-def finish_kernel(came_ref, back_ref, out_ref):
-    planes, block, unused = out_ref.shape
-    merged = planes // 8
+        density_ref[pl.ds(sender * (planes // kpts), planes // kpts)] = block_ref[...]
     for h in range(8):
         lines = came_ref[pl.ds(h, 2 * HALF, stride=8), :]
         field = mul3_right(lines, back_ref[...], TN)
         out_ref[h * merged : (h + 1) * merged] = field.reshape(merged, block, NY)
 
 
-def finish(planes, block, came, back_y):
+def finish(planes, block, own, came, back_y, blocks):
     vmem = pl.BlockSpec(memory_space=pltpu.VMEM)
     return pl.pallas_call(
         finish_kernel,
-        in_specs=[vmem] * 2,
-        out_specs=vmem,
-        out_shape=jax.ShapeDtypeStruct((planes, block, NY), jnp.float32),
+        in_specs=[pl.BlockSpec(memory_space=pltpu.SMEM)] + [vmem] * (2 + len(blocks)),
+        out_specs=[vmem] * 2,
+        out_shape=[jax.ShapeDtypeStruct((planes, block, NY), jnp.float32)] * 2,
         compiler_params=pltpu.CompilerParams(vmem_limit_bytes=VMEM_LIMIT),
         name="finish",
-    )(came, back_y)
+    )(own, came, back_y, *blocks)
 
 
 def exchange(array, axes):
@@ -838,10 +833,12 @@
     parts = 2 * HALF // count
     made = tables(kpts, pws, planes)
     pencil = stack_table(made["pencil"](z_width), 1)
-    wave_x, forth_y, forth_z, back_z = (
-        stack_table(made[name], 1) for name in ("wave_x", "forth_y", "forth_z", "back_z")
-    )
-    wave_y, back_y, both_x = (stack_table(made[name], 0) for name in ("wave_y", "back_y", "both_x"))
+    wave_x, forth_z, back_z = (
+        stack_table(made[name], 1) for name in ("wave_x", "forth_z", "back_z")
+    )
+    wave_y, forth_y, back_y, both_x = (
+        stack_table(made[name], 0) for name in ("wave_y", "forth_y", "back_y", "both_x")
+    )
 
     tiles = slots // LANES
     length = column_slot.shape[1] // LANES
@@ -886,7 +883,7 @@
     ]
     back = poisson(pws, own, kernel, half, forth_z, back_z, both_x)
     back = exchange(back, everyone).reshape(count * parts * 8, LANES)
-    return assemble(own, blocks), finish(NZ // pws, NX // kpts, back, back_y)
+    return tuple(finish(NZ // pws, NX // kpts, own, back, back_y, blocks))
 
 
 def fits_planes(kpts, pws):

time: 148 us -> 129 us (0.87)
  Pallas kernels: 78.1 us -> 56 us
  waiting for transfers between devices: 28.6 us -> 32.2 us
    pallas_call x2 -> x1, Pallas kernels: 19.9 us -> 2.6 us  [finish(): pl.pallas_call(finish_kernel, in_specs=[pl.BlockSpec(memory_space=pltpu.S...]
    pallas_call x2, Pallas kernels: 21.9 us -> 18 us  [wave_band(): pl.pallas_call(functools.partial(wave_kernel, kpts, tiles, scale, is_firs...]
    all_to_all x3, waiting for transfers between devices: 19.5 us -> 23.1 us  [exchange(): return lax.all_to_all(array, axes, split_axis=0, concat_axis=0, tiled=True)]
  transfers between devices with their start and end apart: 6 -> 6, of which waited for: 4 -> 5; matrix products, arithmetic and copies ran while one was open for 0% -> 1% of each run, Pallas kernels for 29% -> 19%
where the time goes in v8:
time: 129 us; the launch traced here: 128 us
  Pallas kernels  56 us (43%)
  waiting for transfers between devices  32.2 us (25%)
  blocking collectives  19.7 us (15%)
  starting transfers between devices  17.3 us (13%)
  local copies, waits for them, and re-layouts  1.69 us (1%)
    pallas_call x2, Pallas kernels, pack_band(): pl.pallas_call(functools.partial(pack_kernel, width, column is not None),...  30.3 us
    all_to_all x3, waiting for transfers between devices, exchange(): return lax.all_to_all(array, axes, split_axis=0, concat_axis=0, tiled=True)  23.1 us
    all_to_all x1, blocking collectives, exchange(): return lax.all_to_all(array, axes, split_axis=0, concat_axis=0, tiled=True)  19.7 us
    pallas_call x2, Pallas kernels, wave_band(): pl.pallas_call(functools.partial(wave_kernel, kpts, tiles, scale, is_firs...  18 us
    all_to_all x3, starting transfers between devices, exchange(): return lax.all_to_all(array, axes, split_axis=0, concat_axis=0, tiled=True)  12.7 us
    ppermute x3, waiting for transfers between devices, local_planes(): lax.ppermute(made_here[s], 'kpt', [(a, (a + s) % kpts) for a in range(kpt...  9.07 us
    pallas_call x1, Pallas kernels, poisson(): pl.pallas_call(functools.partial(poisson_kernel, pws), in_specs=[pl.Block...  5.07 us
    ppermute x3, starting transfers between devices, local_planes(): lax.ppermute(made_here[s], 'kpt', [(a, (a + s) % kpts) for a in range(kpt...  4.63 us
  transfers between devices with their start and end apart: 6, of which 5 were waited for; matrix products, arithmetic and copies ran while one was open for 1% of the time, Pallas kernels for 19%

profile of v8, /device:TPU:0, one launch (start us, length us, event | category | flops | bytes accessed | tf_op | source)
XLA Modules:
  0.0 128.2 jit_solution(14634872330086201237)
XLA Ops:
  0.6 15.2 %pack_band.2 = f32[32,13,4,128]{3,2,1,0:T(4,128)} custom-call(f32[2,768,128]{2,1,0:T(8,128)} %bitcast.13, s32[384,128]{1,0:T(8,128)} %bitcast.15, s32[384,128]{1,0:T(8,128)} %bitcast.17, bf16[512,768]{1,0:T(8,128)(2,1)} %constant.28.clone.refs_3_, s32[384]{0:T(512)} %refs_4_.3), custom_call_target="tpu_custom_call" | custom-call | flops 19327352832 | bytes 786432 | tf_op jit(solution)/shard_map/pack_band/pallas_call | solution.py:524
  15.8 7.3 %all-to-all-start = ((f32[32,13,4,128]{3,2,1,0:T(4,128)}), f32[32,13,4,128]{3,2,1,0:T(4,128)S(1)}, u32[]{:S(2)}, u32[]{:S(2)}) async-start(f32[32,13,4,128]{3,2,1,0:T(4,128)} %pack_band.2), calls=%async_computation | async-start | bytes 1703936 | tf_op jit(solution)/shard_map/all_to_all | solution.py:821
  23.1 15.1 %pack_band.3 = f32[32,48,128]{2,1,0:T(8,128)} custom-call(f32[2,768,128]{2,1,0:T(8,128)} %bitcast.14, s32[384,128]{1,0:T(8,128)} %bitcast.16, s32[384,128]{1,0:T(8,128)} %bitcast.18, bf16[512,768]{1,0:T(8,128)(2,1)} %constant.28.clone.refs_3_), custom_call_target="tpu_custom_call" | custom-call | flops 19327352832 | bytes 786432 | tf_op jit(solution)/shard_map/pack_band/pallas_call | solution.py:524
  38.3 8.2 %all-to-all-done.refs_2_ = f32[32,13,4,128]{3,2,1,0:T(4,128)S(1)} async-done(((f32[32,13,4,128]{3,2,1,0:T(4,128)}), f32[32,13,4,128]{3,2,1,0:T(4,128)S(1)}, u32[]{:S(2)}, u32[]{:S(2)}) %all-to-all-start) | async-done | bytes 852000 | tf_op jit(solution)/shard_map/all_to_all | solution.py:821
  46.5 0.0 copy-start.1
  46.5 2.8 %all-to-all-start.1 = ((f32[32,48,128]{2,1,0:T(8,128)}), f32[32,48,128]{2,1,0:T(8,128)S(1)}, u32[]{:S(2)}, u32[]{:S(2)}) async-start(f32[32,48,128]{2,1,0:T(8,128)} %pack_band.3), calls=%async_computation.1 | async-start | bytes 1572864 | tf_op jit(solution)/shard_map/all_to_all | solution.py:821
  49.3 0.6 pad_add_fusion.refs_0_.own_ref
  50.0 0.0 copy-done.1
  50.0 8.8 %wave_band.2 = (f32[8,128,128]{2,1,0:T(8,128)}, f32[2,256,128]{2,1,0:T(8,128)}, bf16[3072,256]{1,0:T(8,128)(2,1)}, bf16[16,3072]{1,0:T(8,128)(2,1)}) custom-call(s32[2]{0:T(128)} %pad_add_fusion.refs_0_.own_ref, s32[4]{0:T(128)} %refs_1_.3, f32[32,13,4,128]{3,2,1,0:T(4,128)} %copy-done.1, bf16[384,256]{1,0:T(8,128)(2,1)} %constant.32.clone.refs_3_, ...), custom_call_target="tpu_custom_call" | custom-call | flops 3221225472 | bytes 851968 | tf_op jit(solution)/shard_map/wave_band/pallas_call | solution.py:709
  58.8 12.3 %all-to-all-done.1.refs_2_ = f32[32,48,128]{2,1,0:T(8,128)S(1)} async-done(((f32[32,48,128]{2,1,0:T(8,128)}), f32[32,48,128]{2,1,0:T(8,128)S(1)}, u32[]{:S(2)}, u32[]{:S(2)}) %all-to-all-start.1) | async-done | bytes 786464 | tf_op jit(solution)/shard_map/all_to_all | solution.py:821
  71.1 0.0 copy-start.2
  71.1 0.9 copy-done.2
  72.0 9.1 %wave_band.3 = (f32[8,32,128]{2,1,0:T(8,128)}, f32[8,32,128]{2,1,0:T(8,128)}, f32[8,32,128]{2,1,0:T(8,128)}, f32[8,32,128]{2,1,0:T(8,128)}, f32[1024,128]{1,0:T(8,128)}) custom-call(s32[2]{0:T(128)} %pad_add_fusion.refs_0_.own_ref, s32[4]{0:T(128)} %refs_1_.3, f32[32,48,128]{2,1,0:T(8,128)} %copy-done.2, bf16[384,256]{1,0:T(8,128)(2,1)} %constant.32.clone.refs_3_, ...), custom_call_target="tpu_custom_call" | custom-call | flops 3221225472 | bytes 786432 | tf_op jit(solution)/shard_map/wave_band/pallas_call | solution.py:709
  81.1 19.7 %all_to_all.20.came_ref = f32[32,4,8,128]{3,2,1,0:T(8,128)} all-to-all(f32[32,4,8,128]{3,2,1,0:T(8,128)} %bitcast.12), channel_id=1, replica_groups=mesh['kpt'=4,'pw'=8] {'kpt','pw'}, dimensions={0} | all-to-all | bytes 1048576 | tf_op jit(solution)/shard_map/all_to_all | solution.py:821
  100.8 0.0 copy-start.8
  100.8 5.1 %poisson.1 = f32[32,4,8,128]{3,2,1,0:T(8,128)} custom-call(s32[2]{0:T(128)} %pad_add_fusion.refs_0_.own_ref, f32[2,256,128]{2,1,0:T(8,128)} %get-tuple-element.11.kernel_ref, f32[32,4,8,128]{3,2,1,0:T(8,128)} %all_to_all.20.came_ref, bf16[512,768]{1,0:T(8,128)(2,1)} %constant.30.clone.forth_ref, bf16[512,768]{1,0:T(8,128)(2,1)} %constant.31.clone.back_ref, ...), custom_call_target="tpu_custom_call" | custom-call | tf_op jit(solution)/shard_map/poisson/pallas_call | solution.py:784
  105.9 2.6 %all-to-all-start.3 = ((f32[32,4,8,128]{3,2,1,0:T(8,128)}), f32[32,4,8,128]{3,2,1,0:T(8,128)S(1)}, u32[]{:S(2)}, u32[]{:S(2)}) async-start(f32[32,4,8,128]{3,2,1,0:T(8,128)} %poisson.1), calls=%async_computation.3 | async-start | bytes 1048576 | tf_op jit(solution)/shard_map/all_to_all | solution.py:821
  108.5 0.0 copy-done.8
  108.5 1.7 %collective-permute-start = (f32[8,32,128]{2,1,0:T(8,128)S(1)}, f32[8,32,128]{2,1,0:T(8,128)S(1)}, u32[]{:S(2)}, u32[]{:S(2)}) collective-permute-start(f32[8,32,128]{2,1,0:T(8,128)S(1)} %copy-done.8), channel_id=1, source_target_pairs={{0,8},{8,16},{16,24},{24,0},{1,9},{9,17},{17,25},{25,1},{2,10},{10... | collective-permute-start | bytes 393224 | tf_op jit(solution)/shard_map/ppermute | solution.py:881
  110.2 0.0 copy-done.7
  110.2 1.5 %collective-permute-start.1 = (f32[8,32,128]{2,1,0:T(8,128)S(1)}, f32[8,32,128]{2,1,0:T(8,128)S(1)}, u32[]{:S(2)}, u32[]{:S(2)}) collective-permute-start(f32[8,32,128]{2,1,0:T(8,128)S(1)} %copy-done.7), channel_id=1, source_target_pairs={{0,16},{8,24},{16,0},{24,8},{1,17},{9,25},{17,1},{25,9},{2,18},{10... | collective-permute-start | bytes 393224 | tf_op jit(solution)/shard_map/ppermute | solution.py:881
  111.7 0.0 copy-done.6
  111.7 1.4 %collective-permute-start.2 = (f32[8,32,128]{2,1,0:T(8,128)S(1)}, f32[8,32,128]{2,1,0:T(8,128)S(1)}, u32[]{:S(2)}, u32[]{:S(2)}) collective-permute-start(f32[8,32,128]{2,1,0:T(8,128)S(1)} %copy-done.6), channel_id=1, source_target_pairs={{0,24},{8,0},{16,8},{24,16},{1,25},{9,1},{17,9},{25,17},{2,26},{10... | collective-permute-start | bytes 393224 | tf_op jit(solution)/shard_map/ppermute | solution.py:881
  113.1 6.2 %collective-permute-done.refs_1_ = f32[8,32,128]{2,1,0:T(8,128)S(1)} collective-permute-done((f32[8,32,128]{2,1,0:T(8,128)S(1)}, f32[8,32,128]{2,1,0:T(8,128)S(1)}, u32[]{:S(2)}, u32[]{:S(2)}) %collective-permute-start) | collective-permute-done | bytes 131104 | tf_op jit(solution)/shard_map/ppermute | solution.py:881
  119.3 2.9 %collective-permute-done.1.refs_2_ = f32[8,32,128]{2,1,0:T(8,128)S(1)} collective-permute-done((f32[8,32,128]{2,1,0:T(8,128)S(1)}, f32[8,32,128]{2,1,0:T(8,128)S(1)}, u32[]{:S(2)}, u32[]{:S(2)}) %collective-permute-start.1) | collective-permute-done | bytes 131104 | tf_op jit(solution)/shard_map/ppermute | solution.py:881
  122.2 0.0 collective-permute-done.2.refs_3_
  122.2 2.6 %all-to-all-done.3 = f32[32,4,8,128]{3,2,1,0:T(8,128)S(1)} async-done(((f32[32,4,8,128]{3,2,1,0:T(8,128)}), f32[32,4,8,128]{3,2,1,0:T(8,128)S(1)}, u32[]{:S(2)}, u32[]{:S(2)}) %all-to-all-start.3) | async-done | bytes 524320 | tf_op jit(solution)/shard_map/all_to_all | solution.py:821
  124.8 0.0 copy-done.3
  124.8 0.0 copy-done.4
  124.8 0.0 copy-done.5
  124.8 0.8 copy-done
  125.6 2.6 %finish.1 = (f32[32,32,128]{2,1,0:T(8,128)}, f32[32,32,128]{2,1,0:T(8,128)}) custom-call(s32[2]{0:T(128)} %pad_add_fusion.refs_0_.own_ref, f32[1024,128]{1,0:T(8,128)} %bitcast.11, bf16[384,128]{1,0:T(8,128)(2,1)} %constant.34.clone.back_ref, f32[8,32,128]{2,1,0:T(8,128)} %get-tuple-element.16.refs_0_, f32[8,32,128]{2,1,0:T(8,128)} %copy-done.3, ...), custom_call_target="tpu_custom_call" | custom-call | tf_op jit(solution)/shard_map/finish/pallas_call | solution.py:810
  (6 shorter events, 0.0 us)
Async XLA Ops:
  15.8 30.7 %all-to-all-start = ((f32[32,13,4,128]{3,2,1,0:T(4,128)}), f32[32,13,4,128]{3,2,1,0:T(4,128)S(1)}, u32[]{:S(2)}, u32[]{:S(2)}) async-start(f32[32,13,4,128]{3,2,1,0:T(4,128)} %pack_band.2), calls=%async_computation | async-start | bytes 1703936 | tf_op jit(solution)/shard_map/all_to_all | solution.py:821
  46.5 3.5 %copy-start.1 = (f32[32,13,4,128]{3,2,1,0:T(4,128)}, f32[32,13,4,128]{3,2,1,0:T(4,128)S(1)}, u32[]{:S(2)}) copy-start(f32[32,13,4,128]{3,2,1,0:T(4,128)S(1)} %all-to-all-done.refs_2_) | copy-start | bytes 2555908
  46.5 24.6 %all-to-all-start.1 = ((f32[32,48,128]{2,1,0:T(8,128)}), f32[32,48,128]{2,1,0:T(8,128)S(1)}, u32[]{:S(2)}, u32[]{:S(2)}) async-start(f32[32,48,128]{2,1,0:T(8,128)} %pack_band.3), calls=%async_computation.1 | async-start | bytes 1572864 | tf_op jit(solution)/shard_map/all_to_all | solution.py:821
  71.1 0.9 copy-start.2
  100.8 7.7 %copy-start.8 = (f32[8,32,128]{2,1,0:T(8,128)S(1)}, f32[8,32,128]{2,1,0:T(8,128)}, u32[]{:S(2)}) copy-start(f32[8,32,128]{2,1,0:T(8,128)} %get-tuple-element.17) | copy-start | bytes 393220
  100.8 9.4 %copy-start.7 = (f32[8,32,128]{2,1,0:T(8,128)S(1)}, f32[8,32,128]{2,1,0:T(8,128)}, u32[]{:S(2)}) copy-start(f32[8,32,128]{2,1,0:T(8,128)} %get-tuple-element.18) | copy-start | bytes 393220
  100.8 10.9 %copy-start.6 = (f32[8,32,128]{2,1,0:T(8,128)S(1)}, f32[8,32,128]{2,1,0:T(8,128)}, u32[]{:S(2)}) copy-start(f32[8,32,128]{2,1,0:T(8,128)} %get-tuple-element.19) | copy-start | bytes 393220
  105.9 19.0 %all-to-all-start.3 = ((f32[32,4,8,128]{3,2,1,0:T(8,128)}), f32[32,4,8,128]{3,2,1,0:T(8,128)S(1)}, u32[]{:S(2)}, u32[]{:S(2)}) async-start(f32[32,4,8,128]{3,2,1,0:T(8,128)} %poisson.1), calls=%async_computation.3 | async-start | bytes 1048576 | tf_op jit(solution)/shard_map/all_to_all | solution.py:821
  108.5 10.8 %collective-permute-start = (f32[8,32,128]{2,1,0:T(8,128)S(1)}, f32[8,32,128]{2,1,0:T(8,128)S(1)}, u32[]{:S(2)}, u32[]{:S(2)}) collective-permute-start(f32[8,32,128]{2,1,0:T(8,128)S(1)} %copy-done.8), channel_id=1, source_target_pairs={{0,8},{8,16},{16,24},{24,0},{1,9},{9,17},{17,25},{25,1},{2,10},{10... | collective-permute-start | bytes 393224 | tf_op jit(solution)/shard_map/ppermute | solution.py:881
  110.2 12.0 %collective-permute-start.1 = (f32[8,32,128]{2,1,0:T(8,128)S(1)}, f32[8,32,128]{2,1,0:T(8,128)S(1)}, u32[]{:S(2)}, u32[]{:S(2)}) collective-permute-start(f32[8,32,128]{2,1,0:T(8,128)S(1)} %copy-done.7), channel_id=1, source_target_pairs={{0,16},{8,24},{16,0},{24,8},{1,17},{9,25},{17,1},{25,9},{2,18},{10... | collective-permute-start | bytes 393224 | tf_op jit(solution)/shard_map/ppermute | solution.py:881
  111.7 10.5 %collective-permute-start.2 = (f32[8,32,128]{2,1,0:T(8,128)S(1)}, f32[8,32,128]{2,1,0:T(8,128)S(1)}, u32[]{:S(2)}, u32[]{:S(2)}) collective-permute-start(f32[8,32,128]{2,1,0:T(8,128)S(1)} %copy-done.6), channel_id=1, source_target_pairs={{0,24},{8,0},{16,8},{24,16},{1,25},{9,1},{17,9},{25,17},{2,26},{10... | collective-permute-start | bytes 393224 | tf_op jit(solution)/shard_map/ppermute | solution.py:881
  119.3 5.5 %copy-start.3 = (f32[8,32,128]{2,1,0:T(8,128)}, f32[8,32,128]{2,1,0:T(8,128)S(1)}, u32[]{:S(2)}) copy-start(f32[8,32,128]{2,1,0:T(8,128)S(1)} %collective-permute-done.refs_1_) | copy-start | bytes 393220
  122.2 2.6 %copy-start.4 = (f32[8,32,128]{2,1,0:T(8,128)}, f32[8,32,128]{2,1,0:T(8,128)S(1)}, u32[]{:S(2)}) copy-start(f32[8,32,128]{2,1,0:T(8,128)S(1)} %collective-permute-done.1.refs_2_) | copy-start | bytes 393220
  122.2 2.6 %copy-start.5 = (f32[8,32,128]{2,1,0:T(8,128)}, f32[8,32,128]{2,1,0:T(8,128)S(1)}, u32[]{:S(2)}) copy-start(f32[8,32,128]{2,1,0:T(8,128)S(1)} %collective-permute-done.2.refs_3_) | copy-start | bytes 393220
  124.8 0.8 copy-start

commit v9 on v8

--- a/solution.py
+++ b/solution.py
@@ -187,7 +187,7 @@
 
 LANES = 128
 HALF = 64
-VMEM_LIMIT = 56 * 1024 * 1024
+VMEM_LIMIT = 16 * 1024 * 1024
 NN = (((1,), (0,)), ((), ()))
 NT = (((1,), (1,)), ((), ()))
 TN = (((0,), (0,)), ((), ()))
@@ -339,22 +339,13 @@
 def exchange_sublanes(refs, stride, descending):
     sublane = lax.broadcasted_iota(jnp.int32, (8, LANES), 0)
     upper = sublane // stride % 2 == 1
-    want_least = upper if descending is not None else jnp.logical_not(upper)
-    if descending is not None:
-        want_least = jnp.logical_not(jnp.logical_xor(upper, descending))
-
-    def partner(value):
-        if stride == 4:
-            return pltpu.roll(value, 4, 0)
-        return jnp.where(upper, pltpu.roll(value, stride, 0), pltpu.roll(value, 8 - stride, 0))
+    want_most = upper if descending is None else jnp.logical_xor(upper, descending)
+    other = jnp.where(upper, sublane - stride, sublane + stride)
 
     for v in range(RANK_LOW):
         here = [ref[v * 8 : v * 8 + 8, :] for ref in refs]
-        there = [partner(value) for value in here]
-        take = jnp.where(
-            want_least, (here[0] > there[0]).astype(jnp.int32), (here[0] < there[0]).astype(jnp.int32)
-        )
-        take = take == 1
+        there = [jnp.take_along_axis(value, other, axis=0) for value in here]
+        take = jnp.logical_xor(here[0] > there[0], want_most)
         for ref, x, y in zip(refs, here, there):
             ref[v * 8 : v * 8 + 8, :] = jnp.where(take, y, x)
 

time: 129 us -> 127 us (0.984)
  Pallas kernels: 56 us -> 46.9 us
  local copies, waits for them, and re-layouts: 1.69 us -> 7.45 us
  waiting for transfers between devices: 32.2 us -> 35.1 us
  blocking collectives: 19.7 us -> 18.3 us
    unnamed x18 -> x38, local copies, waits for them, and re-layouts: 1.69 us -> 7.45 us
    pallas_call x2, Pallas kernels: 18 us -> 13.7 us  [wave_band(): pl.pallas_call(functools.partial(wave_kernel, kpts, tiles, scale, is_firs...]
    pallas_call x2, Pallas kernels: 30.3 us -> 27.3 us  [pack_band(): pl.pallas_call(functools.partial(pack_kernel, width, column is not None),...]
    all_to_all x3, waiting for transfers between devices: 23.1 us -> 26 us  [exchange(): return lax.all_to_all(array, axes, split_axis=0, concat_axis=0, tiled=True)]
    all_to_all x1, blocking collectives: 19.7 us -> 18.3 us  [exchange(): return lax.all_to_all(array, axes, split_axis=0, concat_axis=0, tiled=True)]
  transfers between devices with their start and end apart: 6 -> 6, of which waited for: 5 -> 5; matrix products, arithmetic and copies ran while one was open for 1% -> 0% of each run, Pallas kernels for 19% -> 16%
where the time goes in v9:
time: 127 us; the launch traced here: 126 us
  Pallas kernels  46.9 us (37%)
  waiting for transfers between devices  35.1 us (28%)
  blocking collectives  18.3 us (14%)
  starting transfers between devices  17.3 us (14%)
  local copies, waits for them, and re-layouts  7.45 us (6%)
    pallas_call x2, Pallas kernels, pack_band(): pl.pallas_call(functools.partial(pack_kernel, width, column is not None),...  27.3 us
    all_to_all x3, waiting for transfers between devices, exchange(): return lax.all_to_all(array, axes, split_axis=0, concat_axis=0, tiled=True)  26 us
    all_to_all x1, blocking collectives, exchange(): return lax.all_to_all(array, axes, split_axis=0, concat_axis=0, tiled=True)  18.3 us
    pallas_call x2, Pallas kernels, wave_band(): pl.pallas_call(functools.partial(wave_kernel, kpts, tiles, scale, is_firs...  13.7 us
    all_to_all x3, starting transfers between devices, exchange(): return lax.all_to_all(array, axes, split_axis=0, concat_axis=0, tiled=True)  12.7 us
    ppermute x3, waiting for transfers between devices, local_planes(): lax.ppermute(made_here[s], 'kpt', [(a, (a + s) % kpts) for a in range(kpt...  9.09 us
    unnamed x38, local copies, waits for them, and re-layouts  7.45 us
    ppermute x3, starting transfers between devices, local_planes(): lax.ppermute(made_here[s], 'kpt', [(a, (a + s) % kpts) for a in range(kpt...  4.63 us
  transfers between devices with their start and end apart: 6, of which 5 were waited for; matrix products, arithmetic and copies ran while one was open for 0% of the time, Pallas kernels for 16%

profile of v9, /device:TPU:0, one launch (start us, length us, event | category | flops | bytes accessed | tf_op | source)
XLA Modules:
  0.0 126.0 jit_solution(14009622509822890319)
XLA Ops:
  0.6 0.0 copy-start.4
  0.6 1.1 copy-done.4
  1.8 0.9 copy-done.6
  2.7 0.9 copy-done.8
  3.6 0.7 copy-done.10
  4.3 1.1 copy-done.12
  5.4 13.7 %pack_band.2 = f32[32,13,4,128]{3,2,1,0:T(4,128)} custom-call(f32[2,768,128]{2,1,0:T(8,128)S(1)} %bitcast.13, s32[384,128]{1,0:T(8,128)S(1)} %bitcast.15, s32[384,128]{1,0:T(8,128)S(1)} %bitcast.17, bf16[512,768]{1,0:T(8,128)(2,1)S(1)} %copy-done.12, s32[384]{0:T(512)S(1)} %copy-done.10), custom_call_target="tpu_custom_call" | custom-call | flops 19327352832 | bytes 786432 | tf_op jit(solution)/shard_map/pack_band/pallas_call | solution.py:515
  19.1 0.0 copy-start.7
  19.2 0.0 copy-start.9
  19.2 7.3 %all-to-all-start = ((f32[32,13,4,128]{3,2,1,0:T(4,128)}), f32[32,13,4,128]{3,2,1,0:T(4,128)S(1)}, u32[]{:S(2)}, u32[]{:S(2)}) async-start(f32[32,13,4,128]{3,2,1,0:T(4,128)} %pack_band.2), calls=%async_computation | async-start | bytes 1703936 | tf_op jit(solution)/shard_map/all_to_all | solution.py:812
  26.5 13.7 %pack_band.3 = f32[32,48,128]{2,1,0:T(8,128)} custom-call(f32[2,768,128]{2,1,0:T(8,128)S(1)} %bitcast.14, s32[384,128]{1,0:T(8,128)S(1)} %bitcast.16, s32[384,128]{1,0:T(8,128)S(1)} %bitcast.18, bf16[512,768]{1,0:T(8,128)(2,1)S(1)} %copy-done.13), custom_call_target="tpu_custom_call" | custom-call | flops 19327352832 | bytes 786432 | tf_op jit(solution)/shard_map/pack_band/pallas_call | solution.py:515
  40.2 0.0 copy-start.14
  40.2 0.0 copy-start.15
  40.2 9.6 %all-to-all-done.refs_2_ = f32[32,13,4,128]{3,2,1,0:T(4,128)S(1)} async-done(((f32[32,13,4,128]{3,2,1,0:T(4,128)}), f32[32,13,4,128]{3,2,1,0:T(4,128)S(1)}, u32[]{:S(2)}, u32[]{:S(2)}) %all-to-all-start) | async-done | bytes 852000 | tf_op jit(solution)/shard_map/all_to_all | solution.py:812
  49.9 2.8 %all-to-all-start.1 = ((f32[32,48,128]{2,1,0:T(8,128)}), f32[32,48,128]{2,1,0:T(8,128)S(1)}, u32[]{:S(2)}, u32[]{:S(2)}) async-start(f32[32,48,128]{2,1,0:T(8,128)} %pack_band.3), calls=%async_computation.1 | async-start | bytes 1572864 | tf_op jit(solution)/shard_map/all_to_all | solution.py:812
  52.7 0.1 pad_add_fusion.refs_0_.own_ref
  52.8 6.7 %wave_band.2 = (f32[8,128,128]{2,1,0:T(8,128)S(1)}, f32[2,256,128]{2,1,0:T(8,128)S(1)}, bf16[3072,256]{1,0:T(8,128)(2,1)S(1)}, bf16[16,3072]{1,0:T(8,128)(2,1)S(1)}) custom-call(s32[2]{0:T(128)S(1)} %pad_add_fusion.refs_0_.own_ref, s32[4]{0:T(128)S(1)} %copy-done.11, f32[32,13,4,128]{3,2,1,0:T(4,128)S(1)} %all-to-all-done.refs_2_, ...), custom_call_target="tpu_custom_call" | custom-call | flops 3221225472 | bytes 851968 | tf_op jit(solution)/shard_map/wave_band/pallas_call | solution.py:700
  59.5 1.2 copy-done.17
  60.7 13.8 %all-to-all-done.1.refs_2_ = f32[32,48,128]{2,1,0:T(8,128)S(1)} async-done(((f32[32,48,128]{2,1,0:T(8,128)}), f32[32,48,128]{2,1,0:T(8,128)S(1)}, u32[]{:S(2)}, u32[]{:S(2)}) %all-to-all-start.1) | async-done | bytes 786464 | tf_op jit(solution)/shard_map/all_to_all | solution.py:812
  74.5 1.4 %copy-done.18 = bf16[3072,256]{1,0:T(8,128)(2,1)S(1)} copy-done((bf16[3072,256]{1,0:T(8,128)(2,1)S(1)}, bf16[3072,256]{1,0:T(8,128)(2,1)}, u32[]{:S(2)}) %copy-start.18) | copy-done | bytes 1572888
  75.9 7.0 %wave_band.3 = (f32[8,32,128]{2,1,0:T(8,128)S(1)}, f32[8,32,128]{2,1,0:T(8,128)S(1)}, f32[8,32,128]{2,1,0:T(8,128)S(1)}, f32[8,32,128]{2,1,0:T(8,128)S(1)}, f32[1024,128]{1,0:T(8,128)S(1)}) custom-call(s32[2]{0:T(128)S(1)} %pad_add_fusion.refs_0_.own_ref, s32[4]{0:T(128)S(1)} %copy-done.11, f32[32,48,128]{2,1,0:T(8,128)S(1)} %all-to-all-done.1.refs_2_, ...), custom_call_target="tpu_custom_call" | custom-call | flops 3221225472 | bytes 786432 | tf_op jit(solution)/shard_map/wave_band/pallas_call | solution.py:700
  82.9 18.3 %all_to_all.20.came_ref = f32[32,4,8,128]{3,2,1,0:T(8,128)S(1)} all-to-all(f32[32,4,8,128]{3,2,1,0:T(8,128)S(1)} %bitcast.12), channel_id=1, replica_groups=mesh['kpt'=4,'pw'=8] {'kpt','pw'}, dimensions={0} | all-to-all | bytes 1048576 | tf_op jit(solution)/shard_map/all_to_all | solution.py:812
  101.2 0.0 copy-start.3
  101.2 3.9 %poisson.1 = f32[32,4,8,128]{3,2,1,0:T(8,128)} custom-call(s32[2]{0:T(128)S(1)} %pad_add_fusion.refs_0_.own_ref, f32[2,256,128]{2,1,0:T(8,128)S(1)} %get-tuple-element.11.kernel_ref, f32[32,4,8,128]{3,2,1,0:T(8,128)S(1)} %all_to_all.20.came_ref, bf16[512,768]{1,0:T(8,128)(2,1)S(1)} %copy-done.1, bf16[512,768]{1,0:T(8,128)(2,1)S(1)} %copy-done, ...), custom_call_target="tpu_custom_call" | custom-call | tf_op jit(solution)/shard_map/poisson/pallas_call | solution.py:775
  105.2 2.6 %all-to-all-start.3 = ((f32[32,4,8,128]{3,2,1,0:T(8,128)}), f32[32,4,8,128]{3,2,1,0:T(8,128)S(1)}, u32[]{:S(2)}, u32[]{:S(2)}) async-start(f32[32,4,8,128]{3,2,1,0:T(8,128)} %poisson.1), calls=%async_computation.3 | async-start | bytes 1048576 | tf_op jit(solution)/shard_map/all_to_all | solution.py:812
  107.8 1.7 %collective-permute-start = (f32[8,32,128]{2,1,0:T(8,128)S(1)}, f32[8,32,128]{2,1,0:T(8,128)S(1)}, u32[]{:S(2)}, u32[]{:S(2)}) collective-permute-start(f32[8,32,128]{2,1,0:T(8,128)S(1)} %get-tuple-element.17), channel_id=1, source_target_pairs={{0,8},{8,16},{16,24},{24,0},{1,9},{9,17},{17,25},{25,1},{2,10},{10... | collective-permute-start | bytes 393224 | tf_op jit(solution)/shard_map/ppermute | solution.py:872
  109.5 1.5 %collective-permute-start.1 = (f32[8,32,128]{2,1,0:T(8,128)S(1)}, f32[8,32,128]{2,1,0:T(8,128)S(1)}, u32[]{:S(2)}, u32[]{:S(2)}) collective-permute-start(f32[8,32,128]{2,1,0:T(8,128)S(1)} %get-tuple-element.18), channel_id=1, source_target_pairs={{0,16},{8,24},{16,0},{24,8},{1,17},{9,25},{17,1},{25,9},{2,18},{10... | collective-permute-start | bytes 393224 | tf_op jit(solution)/shard_map/ppermute | solution.py:872
  111.0 1.4 %collective-permute-start.2 = (f32[8,32,128]{2,1,0:T(8,128)S(1)}, f32[8,32,128]{2,1,0:T(8,128)S(1)}, u32[]{:S(2)}, u32[]{:S(2)}) collective-permute-start(f32[8,32,128]{2,1,0:T(8,128)S(1)} %get-tuple-element.19), channel_id=1, source_target_pairs={{0,24},{8,0},{16,8},{24,16},{1,25},{9,1},{17,9},{25,17},{2,26},{10... | collective-permute-start | bytes 393224 | tf_op jit(solution)/shard_map/ppermute | solution.py:872
  112.4 6.2 %collective-permute-done.refs_1_ = f32[8,32,128]{2,1,0:T(8,128)S(1)} collective-permute-done((f32[8,32,128]{2,1,0:T(8,128)S(1)}, f32[8,32,128]{2,1,0:T(8,128)S(1)}, u32[]{:S(2)}, u32[]{:S(2)}) %collective-permute-start) | collective-permute-done | bytes 131104 | tf_op jit(solution)/shard_map/ppermute | solution.py:872
  118.6 2.9 %collective-permute-done.1.refs_2_ = f32[8,32,128]{2,1,0:T(8,128)S(1)} collective-permute-done((f32[8,32,128]{2,1,0:T(8,128)S(1)}, f32[8,32,128]{2,1,0:T(8,128)S(1)}, u32[]{:S(2)}, u32[]{:S(2)}) %collective-permute-start.1) | collective-permute-done | bytes 131104 | tf_op jit(solution)/shard_map/ppermute | solution.py:872
  121.5 2.6 %all-to-all-done.3 = f32[32,4,8,128]{3,2,1,0:T(8,128)S(1)} async-done(((f32[32,4,8,128]{3,2,1,0:T(8,128)}), f32[32,4,8,128]{3,2,1,0:T(8,128)S(1)}, u32[]{:S(2)}, u32[]{:S(2)}) %all-to-all-start.3) | async-done | bytes 524320 | tf_op jit(solution)/shard_map/all_to_all | solution.py:812
  124.1 1.9 %finish.1 = (f32[32,32,128]{2,1,0:T(8,128)}, f32[32,32,128]{2,1,0:T(8,128)}) custom-call(s32[2]{0:T(128)S(1)} %pad_add_fusion.refs_0_.own_ref, f32[1024,128]{1,0:T(8,128)S(1)} %bitcast.11, bf16[384,128]{1,0:T(8,128)(2,1)S(1)} %copy-done.3, f32[8,32,128]{2,1,0:T(8,128)S(1)} %get-tuple-element.16.refs_0_, f32[8,32,128]{2,1,0:T(8,128)S(1)} %collective-permute-done.refs_1_, ...), custom_call_target="tpu_custom_call" | custom-call | tf_op jit(solution)/shard_map/finish/pallas_call | solution.py:801
  (26 shorter events, 0.1 us)
Async XLA Ops:
  0.6 1.1 copy-start.4
  1.8 0.9 copy-start.6
  2.7 0.9 copy-start.8
  3.6 0.7 copy-start.10
  4.3 1.1 copy-start.12
  5.4 21.0 %copy-start.13 = (bf16[512,768]{1,0:T(8,128)(2,1)S(1)}, bf16[512,768]{1,0:T(8,128)(2,1)}, u32[]{:S(2)}) copy-start(bf16[512,768]{1,0:T(8,128)(2,1)} %constant.28.clone.refs_3_) | copy-start | bytes 2359300
  19.1 7.4 %copy-start.5 = (f32[1,2,2,49152]{3,2,1,0:T(2,128)S(1)}, f32[1,2,2,49152]{3,2,1,0:T(2,128)}, u32[]{:S(2)}) copy-start(f32[1,2,2,49152]{3,2,1,0:T(2,128)} %param.13) | copy-start | bytes 2359300
  19.1 7.4 %copy-start.7 = (s32[1,49152]{1,0:T(1,128)S(1)}, s32[1,49152]{1,0:T(1,128)}, u32[]{:S(2)}) copy-start(s32[1,49152]{1,0:T(1,128)} %param.14) | copy-start | bytes 589828
  19.2 7.4 %copy-start.9 = (s32[1,49152]{1,0:T(1,128)S(1)}, s32[1,49152]{1,0:T(1,128)}, u32[]{:S(2)}) copy-start(s32[1,49152]{1,0:T(1,128)} %param.15) | copy-start | bytes 589828
  19.2 30.7 %all-to-all-start = ((f32[32,13,4,128]{3,2,1,0:T(4,128)}), f32[32,13,4,128]{3,2,1,0:T(4,128)S(1)}, u32[]{:S(2)}, u32[]{:S(2)}) async-start(f32[32,13,4,128]{3,2,1,0:T(4,128)} %pack_band.2), calls=%async_computation | async-start | bytes 1703936 | tf_op jit(solution)/shard_map/all_to_all | solution.py:812
  40.2 12.6 %copy-start.11 = (s32[4]{0:T(128)S(1)}, s32[4]{0:T(128)}, u32[]{:S(2)}) copy-start(s32[4]{0:T(128)} %refs_1_.3) | copy-start | bytes 52
  40.2 12.6 %copy-start.14 = (bf16[384,256]{1,0:T(8,128)(2,1)S(1)}, bf16[384,256]{1,0:T(8,128)(2,1)}, u32[]{:S(2)}) copy-start(bf16[384,256]{1,0:T(8,128)(2,1)} %constant.32.clone.refs_3_) | copy-start | bytes 589828
  40.2 12.5 %copy-start.15 = (bf16[256,384]{1,0:T(8,128)(2,1)S(1)}, bf16[256,384]{1,0:T(8,128)(2,1)}, u32[]{:S(2)}) copy-start(bf16[256,384]{1,0:T(8,128)(2,1)} %constant.29.clone.refs_4_) | copy-start | bytes 589828
  49.9 24.6 %all-to-all-start.1 = ((f32[32,48,128]{2,1,0:T(8,128)}), f32[32,48,128]{2,1,0:T(8,128)S(1)}, u32[]{:S(2)}, u32[]{:S(2)}) async-start(f32[32,48,128]{2,1,0:T(8,128)} %pack_band.3), calls=%async_computation.1 | async-start | bytes 1572864 | tf_op jit(solution)/shard_map/all_to_all | solution.py:812
  52.8 21.7 %copy-start.16 = (bf16[384,128]{1,0:T(8,128)(2,1)S(1)}, bf16[384,128]{1,0:T(8,128)(2,1)}, u32[]{:S(2)}) copy-start(bf16[384,128]{1,0:T(8,128)(2,1)} %constant.33.clone.refs_5_) | copy-start | bytes 294916
  59.5 1.2 copy-start.17
  74.5 1.4 %copy-start.18 = (bf16[3072,256]{1,0:T(8,128)(2,1)S(1)}, bf16[3072,256]{1,0:T(8,128)(2,1)}, u32[]{:S(2)}) copy-start(bf16[3072,256]{1,0:T(8,128)(2,1)} %copy-done.17) | copy-start | bytes 4718596
  75.9 25.3 %copy-start.1 = (bf16[512,768]{1,0:T(8,128)(2,1)S(1)}, bf16[512,768]{1,0:T(8,128)(2,1)}, u32[]{:S(2)}) copy-start(bf16[512,768]{1,0:T(8,128)(2,1)} %constant.30.clone.forth_ref) | copy-start | bytes 2359300
  75.9 25.3 %copy-start.2 = (bf16[384,256]{1,0:T(8,128)(2,1)S(1)}, bf16[384,256]{1,0:T(8,128)(2,1)}, u32[]{:S(2)}) copy-start(bf16[384,256]{1,0:T(8,128)(2,1)} %constant.35.clone.both_x_ref) | copy-start | bytes 589828
  82.9 18.3 %copy-start = (bf16[512,768]{1,0:T(8,128)(2,1)S(1)}, bf16[512,768]{1,0:T(8,128)(2,1)}, u32[]{:S(2)}) copy-start(bf16[512,768]{1,0:T(8,128)(2,1)} %constant.31.clone.back_ref) | copy-start | bytes 2359300
  101.2 22.9 %copy-start.3 = (bf16[384,128]{1,0:T(8,128)(2,1)S(1)}, bf16[384,128]{1,0:T(8,128)(2,1)}, u32[]{:S(2)}) copy-start(bf16[384,128]{1,0:T(8,128)(2,1)} %constant.34.clone.back_ref) | copy-start | bytes 294916
  105.2 19.0 %all-to-all-start.3 = ((f32[32,4,8,128]{3,2,1,0:T(8,128)}), f32[32,4,8,128]{3,2,1,0:T(8,128)S(1)}, u32[]{:S(2)}, u32[]{:S(2)}) async-start(f32[32,4,8,128]{3,2,1,0:T(8,128)} %poisson.1), calls=%async_computation.3 | async-start | bytes 1048576 | tf_op jit(solution)/shard_map/all_to_all | solution.py:812
  107.8 10.8 %collective-permute-start = (f32[8,32,128]{2,1,0:T(8,128)S(1)}, f32[8,32,128]{2,1,0:T(8,128)S(1)}, u32[]{:S(2)}, u32[]{:S(2)}) collective-permute-start(f32[8,32,128]{2,1,0:T(8,128)S(1)} %get-tuple-element.17), channel_id=1, source_target_pairs={{0,8},{8,16},{16,24},{24,0},{1,9},{9,17},{17,25},{25,1},{2,10},{10... | collective-permute-start | bytes 393224 | tf_op jit(solution)/shard_map/ppermute | solution.py:872
  109.5 12.0 %collective-permute-start.1 = (f32[8,32,128]{2,1,0:T(8,128)S(1)}, f32[8,32,128]{2,1,0:T(8,128)S(1)}, u32[]{:S(2)}, u32[]{:S(2)}) collective-permute-start(f32[8,32,128]{2,1,0:T(8,128)S(1)} %get-tuple-element.18), channel_id=1, source_target_pairs={{0,16},{8,24},{16,0},{24,8},{1,17},{9,25},{17,1},{25,9},{2,18},{10... | collective-permute-start | bytes 393224 | tf_op jit(solution)/shard_map/ppermute | solution.py:872
  111.0 10.5 %collective-permute-start.2 = (f32[8,32,128]{2,1,0:T(8,128)S(1)}, f32[8,32,128]{2,1,0:T(8,128)S(1)}, u32[]{:S(2)}, u32[]{:S(2)}) collective-permute-start(f32[8,32,128]{2,1,0:T(8,128)S(1)} %get-tuple-element.19), channel_id=1, source_target_pairs={{0,24},{8,0},{16,8},{24,16},{1,25},{9,1},{17,9},{25,17},{2,26},{10... | collective-permute-start | bytes 393224 | tf_op jit(solution)/shard_map/ppermute | solution.py:872

commit v10 on v9

--- a/solution.py
+++ b/solution.py
@@ -188,6 +188,7 @@
 LANES = 128
 HALF = 64
 VMEM_LIMIT = 16 * 1024 * 1024
+PACK_LIMIT = 56 * 1024 * 1024
 NN = (((1,), (0,)), ((), ()))
 NT = (((1,), (1,)), ((), ()))
 TN = (((0,), (0,)), ((), ()))
@@ -532,7 +533,7 @@
             pltpu.VMEM(pencil.shape, jnp.bfloat16),
             pltpu.SemaphoreType.DMA,
         ],
-        compiler_params=pltpu.CompilerParams(vmem_limit_bytes=VMEM_LIMIT),
+        compiler_params=pltpu.CompilerParams(vmem_limit_bytes=PACK_LIMIT),
         cost_estimate=pl.CostEstimate(
             flops=2 * length * LANES * slots * 4 * width,
             bytes_accessed=16 * length * LANES,
@@ -546,12 +547,12 @@
     own_ref, count_ref, came_ref, wave_y_ref, wave_x_ref = refs[:5]
     rest = list(refs[5:])
     forth_ref = rest.pop(0) if is_last else None
-    former_ref, chosen_ref, high_ref = (None,) * 3 if is_first else [rest.pop(0) for _ in range(3)]
+    former_ref, cell_ref = (None, None) if is_first else (rest.pop(0), rest.pop(0))
     density_refs = [rest.pop(0) for _ in range(kpts if is_last else 1)]
     if is_first:
-        coulomb_ref, chosen_ref, high_ref = rest.pop(0), rest.pop(0), rest.pop(0)
+        coulomb_ref, cell_ref = rest.pop(0), rest.pop(0)
     send_ref = rest.pop(0) if is_last else None
-    values, grid, whole = rest
+    values, grid, whole, chosen_ref, high_ref = rest
     planes = density_refs[0].shape[0]
     block = NX // kpts
     part_rows = 2 * planes
@@ -578,18 +579,21 @@
             values[rows : 2 * rows, first : first + LANES] = low
 
     tile = 4 * HALF
-    if is_first:
-        ramps = ramp((LANES, tile), 1)
-        for j in range(pws):
-            for t in range(tiles):
-                column = came_ref[j, tiles * part_rows // 4, t : t + 1]
-                column = column.astype(jnp.int32)
+    ramps = ramp((LANES, tile), 1)
+    for j in range(pws):
+        for t in range(tiles):
+            first = (j * tiles + t) * LANES
+            if is_first:
+                column = came_ref[j, tiles * part_rows // 4, t : t + 1].astype(jnp.int32)
                 cell = ((column // NY + NX // 2) % NX - HALF // 2) * HALF
                 cell = cell + (column % NY + NY // 2) % NY - HALF // 2
-                first = (j * tiles + t) * LANES
-                lane = (cell % tile).astype(jnp.float32)
-                chosen_ref[first : first + LANES, :] = one_hot_lanes(lane, ramps)
-                high_ref[:, first : first + LANES] = sixteen((cell // tile).astype(jnp.float32))
+                cell_ref[:, first : first + LANES] = cell
+            else:
+                cell = cell_ref[:, first : first + LANES]
+            lane = (cell % tile).astype(jnp.float32)
+            chosen_ref[first : first + LANES, :] = one_hot_lanes(lane, ramps)
+            high_ref[:, first : first + LANES] = sixteen((cell // tile).astype(jnp.float32))
+    if is_first:
         step_z = lax.broadcasted_iota(jnp.int32, (NZ, NX), 0)
         step_x = lax.broadcasted_iota(jnp.int32, (NZ, NX), 1)
         for q in range(coulomb_ref.shape[0]):
@@ -676,7 +680,7 @@
             send_ref[pl.ds(p, 2 * HALF, stride=planes), :] = turned
 
 
-def wave_band(kpts, tiles, total, scale, own, counts, came, wave_y, wave_x, forth, former, chosen):
+def wave_band(kpts, tiles, total, scale, own, counts, came, wave_y, wave_x, forth, former, cell):
     planes = NZ // came.shape[0]
     block = NX // kpts
     is_first, is_last = former is None, forth is not None
@@ -685,15 +689,14 @@
     if is_last:
         operands.append(forth)
     if not is_first:
-        operands += [former, *chosen]
+        operands += [former, cell]
     if is_last:
         out_shape = [jax.ShapeDtypeStruct((planes, block, NY), jnp.float32)] * kpts
     else:
         out_shape = [jax.ShapeDtypeStruct((planes, NX, NY), jnp.float32)]
     if is_first:
         out_shape.append(jax.ShapeDtypeStruct((HALF // came.shape[0], NZ, NX), jnp.float32))
-        out_shape.append(jax.ShapeDtypeStruct((total, 4 * HALF), jnp.bfloat16))
-        out_shape.append(jax.ShapeDtypeStruct((16, total), jnp.bfloat16))
+        out_shape.append(jax.ShapeDtypeStruct((1, total), jnp.int32))
     if is_last:
         out_shape.append(jax.ShapeDtypeStruct((2 * HALF * planes, NX), jnp.float32))
     rows = kpts * 2 * planes
@@ -706,6 +709,8 @@
             pltpu.VMEM((2 * rows, total), jnp.bfloat16),
             pltpu.VMEM((kpts * planes * HALF, LANES), jnp.float32),
             pltpu.VMEM((planes, NX, NY), jnp.float32),
+            pltpu.VMEM((total, 4 * HALF), jnp.bfloat16),
+            pltpu.VMEM((16, total), jnp.bfloat16),
         ],
         compiler_params=pltpu.CompilerParams(vmem_limit_bytes=VMEM_LIMIT),
         cost_estimate=pl.CostEstimate(
@@ -847,7 +852,7 @@
         arrived.append(exchange(packed, everyone))
     device = lax.axis_index("kpt") * pws + lax.axis_index("pw")
     own = jnp.stack((lax.axis_index("kpt"), device * (parts // 2))).astype(jnp.int32)
-    former = chosen = None
+    former = cell = None
     for band in range(band_count):
         forth = forth_y if band == band_count - 1 else None
         made_here = wave_band(
@@ -862,11 +867,11 @@
             wave_x,
             forth,
             former,
-            chosen,
+            cell,
         )
         former = made_here[0]
         if band == 0:
-            kernel, *chosen = made_here[kpts if forth is not None else 1 :][:3]
+            kernel, cell = made_here[kpts if forth is not None else 1 :][:2]
     half = exchange(made_here[-1].reshape(count, parts, planes, NX), everyone)
     blocks = [made_here[0]] + [
         lax.ppermute(made_here[s], "kpt", [(a, (a + s) % kpts) for a in range(kpts)])

time: 127 us -> 121 us (0.953)
  local copies, waits for them, and re-layouts: 7.45 us -> 0.61 us
  Pallas kernels: 46.9 us -> 49.2 us
    unnamed x38 -> x16, local copies, waits for them, and re-layouts: 7.45 us -> 0.61 us
    pallas_call x2, Pallas kernels: 27.3 us -> 29.6 us  [pack_band(): pl.pallas_call(functools.partial(pack_kernel, width, column is not None),...]
  transfers between devices with their start and end apart: 6 -> 6, of which waited for: 5 -> 5; matrix products, arithmetic and copies ran while one was open for 0% -> 0% of each run, Pallas kernels for 16% -> 18%
where the time goes in v10:
time: 121 us
  Pallas kernels  49.2 us (41%)
  waiting for transfers between devices  34.6 us (29%)
  blocking collectives  18.3 us (15%)
  starting transfers between devices  17.5 us (14%)
    pallas_call x2, Pallas kernels, pack_band(): pl.pallas_call(functools.partial(pack_kernel, width, column is not None),...  29.6 us
    all_to_all x3, waiting for transfers between devices, exchange(): return lax.all_to_all(array, axes, split_axis=0, concat_axis=0, tiled=True)  25.5 us
    all_to_all x1, blocking collectives, exchange(): return lax.all_to_all(array, axes, split_axis=0, concat_axis=0, tiled=True)  18.3 us
    pallas_call x2, Pallas kernels, wave_band(): pl.pallas_call(functools.partial(wave_kernel, kpts, tiles, scale, is_firs...  13.8 us
    all_to_all x3, starting transfers between devices, exchange(): return lax.all_to_all(array, axes, split_axis=0, concat_axis=0, tiled=True)  12.9 us
    ppermute x3, waiting for transfers between devices, local_planes(): lax.ppermute(made_here[s], 'kpt', [(a, (a + s) % kpts) for a in range(kpt...  9.09 us
    ppermute x3, starting transfers between devices, local_planes(): lax.ppermute(made_here[s], 'kpt', [(a, (a + s) % kpts) for a in range(kpt...  4.63 us
    pallas_call x1, Pallas kernels, poisson(): pl.pallas_call(functools.partial(poisson_kernel, pws), in_specs=[pl.Block...  3.93 us
  transfers between devices with their start and end apart: 6, of which 5 were waited for; matrix products, arithmetic and copies ran while one was open for 0% of the time, Pallas kernels for 18%

profile of v10, /device:TPU:0, one launch (start us, length us, event | category | flops | bytes accessed | tf_op | source)
XLA Modules:
  0.0 121.0 jit_solution(9659477701304992100)
XLA Ops:
  0.6 14.8 %pack_band.2 = f32[32,13,4,128]{3,2,1,0:T(4,128)} custom-call(f32[2,768,128]{2,1,0:T(8,128)} %bitcast.13, s32[384,128]{1,0:T(8,128)} %bitcast.15, s32[384,128]{1,0:T(8,128)} %bitcast.17, bf16[512,768]{1,0:T(8,128)(2,1)} %constant.28.clone.refs_3_, s32[384]{0:T(512)} %refs_4_.3), custom_call_target="tpu_custom_call" | custom-call | flops 19327352832 | bytes 786432 | tf_op jit(solution)/shard_map/pack_band/pallas_call | solution.py:516
  15.4 7.3 %all-to-all-start = ((f32[32,13,4,128]{3,2,1,0:T(4,128)}), f32[32,13,4,128]{3,2,1,0:T(4,128)S(1)}, u32[]{:S(2)}, u32[]{:S(2)}) async-start(f32[32,13,4,128]{3,2,1,0:T(4,128)} %pack_band.2), calls=%async_computation | async-start | bytes 1703936 | tf_op jit(solution)/shard_map/all_to_all | solution.py:817
  22.8 14.8 %pack_band.3 = f32[32,48,128]{2,1,0:T(8,128)} custom-call(f32[2,768,128]{2,1,0:T(8,128)} %bitcast.14, s32[384,128]{1,0:T(8,128)} %bitcast.16, s32[384,128]{1,0:T(8,128)} %bitcast.18, bf16[512,768]{1,0:T(8,128)(2,1)} %constant.28.clone.refs_3_), custom_call_target="tpu_custom_call" | custom-call | flops 19327352832 | bytes 786432 | tf_op jit(solution)/shard_map/pack_band/pallas_call | solution.py:516
  37.6 0.0 copy-start.5
  37.6 0.0 copy-start.6
  37.6 8.5 %all-to-all-done.refs_2_ = f32[32,13,4,128]{3,2,1,0:T(4,128)S(1)} async-done(((f32[32,13,4,128]{3,2,1,0:T(4,128)}), f32[32,13,4,128]{3,2,1,0:T(4,128)S(1)}, u32[]{:S(2)}, u32[]{:S(2)}) %all-to-all-start) | async-done | bytes 852000 | tf_op jit(solution)/shard_map/all_to_all | solution.py:817
  46.1 2.8 %all-to-all-start.1 = ((f32[32,48,128]{2,1,0:T(8,128)}), f32[32,48,128]{2,1,0:T(8,128)S(1)}, u32[]{:S(2)}, u32[]{:S(2)}) async-start(f32[32,48,128]{2,1,0:T(8,128)} %pack_band.3), calls=%async_computation.1 | async-start | bytes 1572864 | tf_op jit(solution)/shard_map/all_to_all | solution.py:817
  49.0 0.0 copy-start.4
  49.0 0.1 pad_add_fusion.refs_0_.own_ref
  49.0 0.0 copy-done.5
  49.0 0.0 copy-done.6
  49.1 0.6 copy-done.4
  49.6 6.8 %wave_band.2 = (f32[8,128,128]{2,1,0:T(8,128)S(1)}, f32[2,256,128]{2,1,0:T(8,128)S(1)}, s32[1,3072]{1,0:T(1,128)S(1)}) custom-call(s32[2]{0:T(128)S(1)} %pad_add_fusion.refs_0_.own_ref, s32[4]{0:T(128)S(1)} %copy-done.4, f32[32,13,4,128]{3,2,1,0:T(4,128)S(1)} %all-to-all-done.refs_2_, bf16[384,256]{1,0:T(8,128)(2,1)S(1)} %copy-done.5, ...), custom_call_target="tpu_custom_call" | custom-call | flops 3221225472 | bytes 851968 | tf_op jit(solution)/shard_map/wave_band/pallas_call | solution.py:703
  56.4 14.3 %all-to-all-done.1.refs_2_ = f32[32,48,128]{2,1,0:T(8,128)S(1)} async-done(((f32[32,48,128]{2,1,0:T(8,128)}), f32[32,48,128]{2,1,0:T(8,128)S(1)}, u32[]{:S(2)}, u32[]{:S(2)}) %all-to-all-start.1) | async-done | bytes 786464 | tf_op jit(solution)/shard_map/all_to_all | solution.py:817
  70.7 0.0 copy-done.7
  70.7 7.0 %wave_band.3 = (f32[8,32,128]{2,1,0:T(8,128)S(1)}, f32[8,32,128]{2,1,0:T(8,128)S(1)}, f32[8,32,128]{2,1,0:T(8,128)S(1)}, f32[8,32,128]{2,1,0:T(8,128)S(1)}, f32[1024,128]{1,0:T(8,128)S(1)}) custom-call(s32[2]{0:T(128)S(1)} %pad_add_fusion.refs_0_.own_ref, s32[4]{0:T(128)S(1)} %copy-done.4, f32[32,48,128]{2,1,0:T(8,128)S(1)} %all-to-all-done.1.refs_2_, ...), custom_call_target="tpu_custom_call" | custom-call | flops 3221225472 | bytes 786432 | tf_op jit(solution)/shard_map/wave_band/pallas_call | solution.py:703
  77.8 0.0 copy-start
  77.8 0.0 copy-start.2
  77.8 18.3 %all_to_all.20.came_ref = f32[32,4,8,128]{3,2,1,0:T(8,128)S(1)} all-to-all(f32[32,4,8,128]{3,2,1,0:T(8,128)S(1)} %bitcast.12), channel_id=1, replica_groups=mesh['kpt'=4,'pw'=8] {'kpt','pw'}, dimensions={0} | all-to-all | bytes 1048576 | tf_op jit(solution)/shard_map/all_to_all | solution.py:817
  96.1 0.0 copy-done.1
  96.1 0.0 copy-done
  96.1 0.0 copy-done.2
  96.1 3.9 %poisson.1 = f32[32,4,8,128]{3,2,1,0:T(8,128)} custom-call(s32[2]{0:T(128)S(1)} %pad_add_fusion.refs_0_.own_ref, f32[2,256,128]{2,1,0:T(8,128)S(1)} %get-tuple-element.10.kernel_ref, f32[32,4,8,128]{3,2,1,0:T(8,128)S(1)} %all_to_all.20.came_ref, bf16[512,768]{1,0:T(8,128)(2,1)S(1)} %copy-done.1, bf16[512,768]{1,0:T(8,128)(2,1)S(1)} %copy-done, ...), custom_call_target="tpu_custom_call" | custom-call | tf_op jit(solution)/shard_map/poisson/pallas_call | solution.py:780
  100.1 2.7 %all-to-all-start.3 = ((f32[32,4,8,128]{3,2,1,0:T(8,128)}), f32[32,4,8,128]{3,2,1,0:T(8,128)S(1)}, u32[]{:S(2)}, u32[]{:S(2)}) async-start(f32[32,4,8,128]{3,2,1,0:T(8,128)} %poisson.1), calls=%async_computation.3 | async-start | bytes 1048576 | tf_op jit(solution)/shard_map/all_to_all | solution.py:817
  102.8 1.7 %collective-permute-start = (f32[8,32,128]{2,1,0:T(8,128)S(1)}, f32[8,32,128]{2,1,0:T(8,128)S(1)}, u32[]{:S(2)}, u32[]{:S(2)}) collective-permute-start(f32[8,32,128]{2,1,0:T(8,128)S(1)} %get-tuple-element.15), channel_id=1, source_target_pairs={{0,8},{8,16},{16,24},{24,0},{1,9},{9,17},{17,25},{25,1},{2,10},{10... | collective-permute-start | bytes 393224 | tf_op jit(solution)/shard_map/ppermute | solution.py:877
  104.5 1.5 %collective-permute-start.1 = (f32[8,32,128]{2,1,0:T(8,128)S(1)}, f32[8,32,128]{2,1,0:T(8,128)S(1)}, u32[]{:S(2)}, u32[]{:S(2)}) collective-permute-start(f32[8,32,128]{2,1,0:T(8,128)S(1)} %get-tuple-element.16), channel_id=1, source_target_pairs={{0,16},{8,24},{16,0},{24,8},{1,17},{9,25},{17,1},{25,9},{2,18},{10... | collective-permute-start | bytes 393224 | tf_op jit(solution)/shard_map/ppermute | solution.py:877
  106.0 1.4 %collective-permute-start.2 = (f32[8,32,128]{2,1,0:T(8,128)S(1)}, f32[8,32,128]{2,1,0:T(8,128)S(1)}, u32[]{:S(2)}, u32[]{:S(2)}) collective-permute-start(f32[8,32,128]{2,1,0:T(8,128)S(1)} %get-tuple-element.17), channel_id=1, source_target_pairs={{0,24},{8,0},{16,8},{24,16},{1,25},{9,1},{17,9},{25,17},{2,26},{10... | collective-permute-start | bytes 393224 | tf_op jit(solution)/shard_map/ppermute | solution.py:877
  107.4 6.2 %collective-permute-done.refs_1_ = f32[8,32,128]{2,1,0:T(8,128)S(1)} collective-permute-done((f32[8,32,128]{2,1,0:T(8,128)S(1)}, f32[8,32,128]{2,1,0:T(8,128)S(1)}, u32[]{:S(2)}, u32[]{:S(2)}) %collective-permute-start) | collective-permute-done | bytes 131104 | tf_op jit(solution)/shard_map/ppermute | solution.py:877
  113.6 2.9 %collective-permute-done.1.refs_2_ = f32[8,32,128]{2,1,0:T(8,128)S(1)} collective-permute-done((f32[8,32,128]{2,1,0:T(8,128)S(1)}, f32[8,32,128]{2,1,0:T(8,128)S(1)}, u32[]{:S(2)}, u32[]{:S(2)}) %collective-permute-start.1) | collective-permute-done | bytes 131104 | tf_op jit(solution)/shard_map/ppermute | solution.py:877
  116.5 0.0 collective-permute-done.2.refs_3_
  116.5 2.6 %all-to-all-done.3 = f32[32,4,8,128]{3,2,1,0:T(8,128)S(1)} async-done(((f32[32,4,8,128]{3,2,1,0:T(8,128)}), f32[32,4,8,128]{3,2,1,0:T(8,128)S(1)}, u32[]{:S(2)}, u32[]{:S(2)}) %all-to-all-start.3) | async-done | bytes 524320 | tf_op jit(solution)/shard_map/all_to_all | solution.py:817
  119.2 1.9 %finish.1 = (f32[32,32,128]{2,1,0:T(8,128)}, f32[32,32,128]{2,1,0:T(8,128)}) custom-call(s32[2]{0:T(128)S(1)} %pad_add_fusion.refs_0_.own_ref, f32[1024,128]{1,0:T(8,128)S(1)} %bitcast.11, bf16[384,128]{1,0:T(8,128)(2,1)S(1)} %copy-done.3, f32[8,32,128]{2,1,0:T(8,128)S(1)} %get-tuple-element.14.refs_0_, f32[8,32,128]{2,1,0:T(8,128)S(1)} %collective-permute-done.refs_1_, ...), custom_call_target="tpu_custom_call" | custom-call | tf_op jit(solution)/shard_map/finish/pallas_call | solution.py:806
  (4 shorter events, 0.0 us)
Async XLA Ops:
  15.4 30.7 %all-to-all-start = ((f32[32,13,4,128]{3,2,1,0:T(4,128)}), f32[32,13,4,128]{3,2,1,0:T(4,128)S(1)}, u32[]{:S(2)}, u32[]{:S(2)}) async-start(f32[32,13,4,128]{3,2,1,0:T(4,128)} %pack_band.2), calls=%async_computation | async-start | bytes 1703936 | tf_op jit(solution)/shard_map/all_to_all | solution.py:817
  37.6 11.5 %copy-start.5 = (bf16[384,256]{1,0:T(8,128)(2,1)S(1)}, bf16[384,256]{1,0:T(8,128)(2,1)}, u32[]{:S(2)}) copy-start(bf16[384,256]{1,0:T(8,128)(2,1)} %constant.32.clone.refs_3_) | copy-start | bytes 589828
  37.6 11.5 %copy-start.6 = (bf16[256,384]{1,0:T(8,128)(2,1)S(1)}, bf16[256,384]{1,0:T(8,128)(2,1)}, u32[]{:S(2)}) copy-start(bf16[256,384]{1,0:T(8,128)(2,1)} %constant.29.clone.refs_4_) | copy-start | bytes 589828
  46.1 24.6 %all-to-all-start.1 = ((f32[32,48,128]{2,1,0:T(8,128)}), f32[32,48,128]{2,1,0:T(8,128)S(1)}, u32[]{:S(2)}, u32[]{:S(2)}) async-start(f32[32,48,128]{2,1,0:T(8,128)} %pack_band.3), calls=%async_computation.1 | async-start | bytes 1572864 | tf_op jit(solution)/shard_map/all_to_all | solution.py:817
  49.0 0.7 copy-start.4
  49.6 21.1 %copy-start.7 = (bf16[384,128]{1,0:T(8,128)(2,1)S(1)}, bf16[384,128]{1,0:T(8,128)(2,1)}, u32[]{:S(2)}) copy-start(bf16[384,128]{1,0:T(8,128)(2,1)} %constant.33.clone.refs_5_) | copy-start | bytes 294916
  70.7 25.4 %copy-start.1 = (bf16[512,768]{1,0:T(8,128)(2,1)S(1)}, bf16[512,768]{1,0:T(8,128)(2,1)}, u32[]{:S(2)}) copy-start(bf16[512,768]{1,0:T(8,128)(2,1)} %constant.30.clone.forth_ref) | copy-start | bytes 2359300
  77.8 18.3 %copy-start = (bf16[512,768]{1,0:T(8,128)(2,1)S(1)}, bf16[512,768]{1,0:T(8,128)(2,1)}, u32[]{:S(2)}) copy-start(bf16[512,768]{1,0:T(8,128)(2,1)} %constant.31.clone.back_ref) | copy-start | bytes 2359300
  77.8 18.3 %copy-start.2 = (bf16[384,256]{1,0:T(8,128)(2,1)S(1)}, bf16[384,256]{1,0:T(8,128)(2,1)}, u32[]{:S(2)}) copy-start(bf16[384,256]{1,0:T(8,128)(2,1)} %constant.35.clone.both_x_ref) | copy-start | bytes 589828
  100.0 19.1 %copy-start.3 = (bf16[384,128]{1,0:T(8,128)(2,1)S(1)}, bf16[384,128]{1,0:T(8,128)(2,1)}, u32[]{:S(2)}) copy-start(bf16[384,128]{1,0:T(8,128)(2,1)} %constant.34.clone.back_ref) | copy-start | bytes 294916
  100.1 19.1 %all-to-all-start.3 = ((f32[32,4,8,128]{3,2,1,0:T(8,128)}), f32[32,4,8,128]{3,2,1,0:T(8,128)S(1)}, u32[]{:S(2)}, u32[]{:S(2)}) async-start(f32[32,4,8,128]{3,2,1,0:T(8,128)} %poisson.1), calls=%async_computation.3 | async-start | bytes 1048576 | tf_op jit(solution)/shard_map/all_to_all | solution.py:817
  102.8 10.8 %collective-permute-start = (f32[8,32,128]{2,1,0:T(8,128)S(1)}, f32[8,32,128]{2,1,0:T(8,128)S(1)}, u32[]{:S(2)}, u32[]{:S(2)}) collective-permute-start(f32[8,32,128]{2,1,0:T(8,128)S(1)} %get-tuple-element.15), channel_id=1, source_target_pairs={{0,8},{8,16},{16,24},{24,0},{1,9},{9,17},{17,25},{25,1},{2,10},{10... | collective-permute-start | bytes 393224 | tf_op jit(solution)/shard_map/ppermute | solution.py:877
  104.5 12.0 %collective-permute-start.1 = (f32[8,32,128]{2,1,0:T(8,128)S(1)}, f32[8,32,128]{2,1,0:T(8,128)S(1)}, u32[]{:S(2)}, u32[]{:S(2)}) collective-permute-start(f32[8,32,128]{2,1,0:T(8,128)S(1)} %get-tuple-element.16), channel_id=1, source_target_pairs={{0,16},{8,24},{16,0},{24,8},{1,17},{9,25},{17,1},{25,9},{2,18},{10... | collective-permute-start | bytes 393224 | tf_op jit(solution)/shard_map/ppermute | solution.py:877
  106.0 10.5 %collective-permute-start.2 = (f32[8,32,128]{2,1,0:T(8,128)S(1)}, f32[8,32,128]{2,1,0:T(8,128)S(1)}, u32[]{:S(2)}, u32[]{:S(2)}) collective-permute-start(f32[8,32,128]{2,1,0:T(8,128)S(1)} %get-tuple-element.17), channel_id=1, source_target_pairs={{0,24},{8,0},{16,8},{24,16},{1,25},{9,1},{17,9},{25,17},{2,26},{10... | collective-permute-start | bytes 393224 | tf_op jit(solution)/shard_map/ppermute | solution.py:877

commit v11 on v10

--- a/solution.py
+++ b/solution.py
@@ -226,16 +226,26 @@
     return np.outer(former, latter) % length * (2.0 * np.pi / length)
 
 
+def ring_order(length):
+    return [0, *range(1, length, 2), *range(length - 2 + length % 2, 0, -2)] if length > 1 else [0]
+
+
+def group_order(kpts, pws):
+    cores = 2 if pws % 2 == 0 else 1
+    return ring_order(kpts), [c * cores + i for c in ring_order(pws // cores) for i in range(cores)]
+
+
 def tables(kpts, pws, planes):
     count = kpts * pws
+    kpt_order, pw_order = (np.array(order) for order in group_order(kpts, pws))
     low_freq = np.arange(HALF) - HALF // 2
     grid_x, grid_y, grid_z = np.arange(NX), np.arange(NY), np.arange(NZ)
     own_y = np.arange(HALF)
 
     device = np.arange(count)
     plane_of = (
-        (device % pws)[:, None] * (NZ // pws)
-        + (device // pws)[:, None] * planes
+        pw_order[device % pws][:, None] * (NZ // pws)
+        + kpt_order[device // pws][:, None] * planes
         + np.arange(planes)[None, :]
     )
     return_table = {}
@@ -270,7 +280,7 @@
     own = NZ // pws
     merged = own // 8
     order = (
-        np.arange(pws)[None, :, None] * own
+        pw_order[None, :, None] * own
         + np.arange(8)[None, None, :] * merged
         + np.arange(merged)[:, None, None]
     )
@@ -637,7 +647,7 @@
 
     weights = [
         jnp.concatenate([spread(count_ref[k]) / spread(sum_of) * scale] * (NX // 8), axis=0)
-        for k in range(kpts)
+        for k in ring_order(kpts)
     ]
     lines = [grid[pl.ds(p, kpts * HALF, stride=planes), :] for p in range(planes)]
     lines = mul3_right(jnp.concatenate(lines, axis=0), wave_y_ref[...], NN)
@@ -763,7 +773,7 @@
         real = part(turned, 0, 2 * q) - part(turned, 1, 2 * q + 1)
         imag = part(turned, 0, 2 * q + 1) + part(turned, 1, 2 * q)
         for c, value in enumerate((real, imag)):
-            for a in range(kpts):
+            for place, a in enumerate(ring_order(kpts)):
                 packed = None
                 for m in range(merged):
                     piece = value[m * rows : (m + 1) * rows]
@@ -771,7 +781,7 @@
                     if shift:
                         piece = pltpu.roll(piece, shift, 1)
                     packed = piece if m == 0 else jnp.where(lane == m, piece, packed)
-                send_ref[a * pws : (a + 1) * pws, 2 * q + c] = packed.reshape(pws, 8, LANES)
+                send_ref[place * pws : (place + 1) * pws, 2 * q + c] = packed.reshape(pws, 8, LANES)
 
 
 def poisson(pws, own, kernel, came, forth, back, both_x):
@@ -813,15 +823,24 @@
     )(own, came, back_y, *blocks)
 
 
-def exchange(array, axes):
-    return lax.all_to_all(array, axes, split_axis=0, concat_axis=0, tiled=True)
+def exchange(array):
+    kpts, pws = lax.axis_size("kpt"), lax.axis_size("pw")
+    kpt_order, pw_order = group_order(kpts, pws)
+    group = [k * pws + j for k in kpt_order for j in pw_order]
+    return lax.all_to_all(
+        array, ("kpt", "pw"), split_axis=0, concat_axis=0, tiled=True, axis_index_groups=[group]
+    )
+
+
+def place_in(order, axis):
+    places = jnp.asarray(np.argsort(np.array(order)), jnp.int32)
+    return lax.dynamic_index_in_dim(places, lax.axis_index(axis), 0, keepdims=False)
 
 
 def local_planes(band_coeffs, miller_third, column_slot, column_map, kpoint_counts):
     pws = lax.axis_size("pw")
     kpts = lax.axis_size("kpt")
     count = pws * kpts
-    everyone = ("kpt", "pw")
     slots = column_map.shape[0]
     band_count = band_coeffs.shape[1]
     z_width = column_slot.shape[1] // slots
@@ -849,8 +868,9 @@
         packed = pack_band(
             band, count, coeffs, miller, slot, pencil, slots, column
         )
-        arrived.append(exchange(packed, everyone))
-    device = lax.axis_index("kpt") * pws + lax.axis_index("pw")
+        arrived.append(exchange(packed))
+    kpt_order, pw_order = group_order(kpts, pws)
+    device = place_in(kpt_order, "kpt") * pws + place_in(pw_order, "pw")
     own = jnp.stack((lax.axis_index("kpt"), device * (parts // 2))).astype(jnp.int32)
     former = cell = None
     for band in range(band_count):
@@ -872,13 +892,13 @@
         former = made_here[0]
         if band == 0:
             kernel, cell = made_here[kpts if forth is not None else 1 :][:2]
-    half = exchange(made_here[-1].reshape(count, parts, planes, NX), everyone)
+    half = exchange(made_here[-1].reshape(count, parts, planes, NX))
     blocks = [made_here[0]] + [
         lax.ppermute(made_here[s], "kpt", [(a, (a + s) % kpts) for a in range(kpts)])
         for s in range(1, kpts)
     ]
     back = poisson(pws, own, kernel, half, forth_z, back_z, both_x)
-    back = exchange(back, everyone).reshape(count * parts * 8, LANES)
+    back = exchange(back).reshape(count * parts * 8, LANES)
     return tuple(finish(NZ // pws, NX // kpts, own, back, back_y, blocks))
 
 

time: 121 us -> 118 us (0.975)
  waiting for transfers between devices: 34.6 us -> 26.3 us
  local copies, waits for them, and re-layouts: 0.61 us -> 2.49 us
  starting transfers between devices: 17.5 us -> 18.8 us
  between operations: 0.74 us -> 1.96 us
    all_to_all x3, waiting for transfers between devices: 25.5 us -> 17.3 us  [exchange(): lax.all_to_all(array, ('kpt', 'pw'), split_axis=0, concat_axis=0, tiled=T...]
  transfers between devices with their start and end apart: 6 -> 6, of which waited for: 5 -> 5; matrix products, arithmetic and copies ran while one was open for 0% -> 1% of each run, Pallas kernels for 18% -> 18%
where the time goes in v11:
time: 118 us; the launch traced here: 117 us
  Pallas kernels  49.1 us (42%)
  waiting for transfers between devices  26.3 us (22%)
  starting transfers between devices  18.8 us (16%)
  blocking collectives  18.6 us (16%)
  local copies, waits for them, and re-layouts  2.49 us (2%)
  between operations  1.96 us (2%)
    pallas_call x2, Pallas kernels, pack_band(): pl.pallas_call(functools.partial(pack_kernel, width, column is not None),...  29.6 us
    all_to_all x1, blocking collectives, exchange(): lax.all_to_all(array, ('kpt', 'pw'), split_axis=0, concat_axis=0, tiled=T...  18.6 us
    all_to_all x3, waiting for transfers between devices, exchange(): lax.all_to_all(array, ('kpt', 'pw'), split_axis=0, concat_axis=0, tiled=T...  17.3 us
    all_to_all x3, starting transfers between devices, exchange(): lax.all_to_all(array, ('kpt', 'pw'), split_axis=0, concat_axis=0, tiled=T...  14.1 us
    pallas_call x2, Pallas kernels, wave_band(): pl.pallas_call(functools.partial(wave_kernel, kpts, tiles, scale, is_firs...  13.7 us
    ppermute x3, waiting for transfers between devices, local_planes(): lax.ppermute(made_here[s], 'kpt', [(a, (a + s) % kpts) for a in range(kpt...  9.03 us
    ppermute x3, starting transfers between devices, local_planes(): lax.ppermute(made_here[s], 'kpt', [(a, (a + s) % kpts) for a in range(kpt...  4.75 us
    pallas_call x1, Pallas kernels, poisson(): pl.pallas_call(functools.partial(poisson_kernel, pws), in_specs=[pl.Block...  3.93 us
  transfers between devices with their start and end apart: 6, of which 5 were waited for; matrix products, arithmetic and copies ran while one was open for 1% of the time, Pallas kernels for 18%

profile of v11, /device:TPU:0, one launch (start us, length us, event | category | flops | bytes accessed | tf_op | source)
XLA Modules:
  0.0 117.4 jit_solution(10741684690159158374)
XLA Ops:
  0.6 14.8 %pack_band.2 = f32[32,13,4,128]{3,2,1,0:T(4,128)} custom-call(f32[2,768,128]{2,1,0:T(8,128)} %bitcast.12, s32[384,128]{1,0:T(8,128)} %bitcast.14, s32[384,128]{1,0:T(8,128)} %bitcast.16, bf16[512,768]{1,0:T(8,128)(2,1)} %constant.45.clone.refs_3_, s32[384]{0:T(512)} %refs_4_.3), custom_call_target="tpu_custom_call" | custom-call | flops 19327352832 | bytes 786432 | tf_op jit(solution)/shard_map/pack_band/pallas_call | solution.py:526
  15.4 7.3 %all-to-all-start = ((f32[32,13,4,128]{3,2,1,0:T(4,128)}), f32[32,13,4,128]{3,2,1,0:T(4,128)S(1)}, u32[]{:S(2)}, u32[]{:S(2)}) async-start(f32[32,13,4,128]{3,2,1,0:T(4,128)} %pack_band.2), calls=%async_computation | async-start | bytes 1703936 | tf_op jit(solution)/shard_map/all_to_all | solution.py:830
  22.8 14.8 %pack_band.3 = f32[32,48,128]{2,1,0:T(8,128)} custom-call(f32[2,768,128]{2,1,0:T(8,128)} %bitcast.13, s32[384,128]{1,0:T(8,128)} %bitcast.15, s32[384,128]{1,0:T(8,128)} %bitcast.17, bf16[512,768]{1,0:T(8,128)(2,1)} %constant.45.clone.refs_3_), custom_call_target="tpu_custom_call" | custom-call | flops 19327352832 | bytes 786432 | tf_op jit(solution)/shard_map/pack_band/pallas_call | solution.py:526
  37.6 0.0 copy-start.5
  37.6 0.0 copy-start.6
  37.6 6.5 %all-to-all-done.refs_2_ = f32[32,13,4,128]{3,2,1,0:T(4,128)S(1)} async-done(((f32[32,13,4,128]{3,2,1,0:T(4,128)}), f32[32,13,4,128]{3,2,1,0:T(4,128)S(1)}, u32[]{:S(2)}, u32[]{:S(2)}) %all-to-all-start) | async-done | bytes 852000 | tf_op jit(solution)/shard_map/all_to_all | solution.py:830
  44.1 3.9 %all-to-all-start.1 = ((f32[32,48,128]{2,1,0:T(8,128)}), f32[32,48,128]{2,1,0:T(8,128)S(1)}, u32[]{:S(2)}, u32[]{:S(2)}) async-start(f32[32,48,128]{2,1,0:T(8,128)} %pack_band.3), calls=%async_computation.1 | async-start | bytes 1572864 | tf_op jit(solution)/shard_map/all_to_all | solution.py:830
  48.0 0.0 copy-start.9
  48.0 0.6 copy-done.9
  48.7 0.6 dynamic_slice.9
  49.3 0.1 copy-done.8
  49.3 0.6 dynamic_slice.8
  51.1 0.0 copy-start.4
  51.1 0.1 pad_add_fusion.refs_0_.own_ref
  51.2 0.0 copy-done.5
  51.2 0.6 copy-done.4
  51.8 6.7 %wave_band.2 = (f32[8,128,128]{2,1,0:T(8,128)S(1)}, f32[2,256,128]{2,1,0:T(8,128)S(1)}, s32[1,3072]{1,0:T(1,128)S(1)}) custom-call(s32[2]{0:T(128)S(1)} %pad_add_fusion.refs_0_.own_ref, s32[4]{0:T(128)S(1)} %copy-done.4, f32[32,13,4,128]{3,2,1,0:T(4,128)S(1)} %all-to-all-done.refs_2_, bf16[384,256]{1,0:T(8,128)(2,1)S(1)} %copy-done.5, ...), custom_call_target="tpu_custom_call" | custom-call | flops 3221225472 | bytes 851968 | tf_op jit(solution)/shard_map/wave_band/pallas_call | solution.py:713
  58.5 9.4 %all-to-all-done.1.refs_2_ = f32[32,48,128]{2,1,0:T(8,128)S(1)} async-done(((f32[32,48,128]{2,1,0:T(8,128)}), f32[32,48,128]{2,1,0:T(8,128)S(1)}, u32[]{:S(2)}, u32[]{:S(2)}) %all-to-all-start.1) | async-done | bytes 786464 | tf_op jit(solution)/shard_map/all_to_all | solution.py:830
  67.9 7.0 %wave_band.3 = (f32[8,32,128]{2,1,0:T(8,128)S(1)}, f32[8,32,128]{2,1,0:T(8,128)S(1)}, f32[8,32,128]{2,1,0:T(8,128)S(1)}, f32[8,32,128]{2,1,0:T(8,128)S(1)}, f32[1024,128]{1,0:T(8,128)S(1)}) custom-call(s32[2]{0:T(128)S(1)} %pad_add_fusion.refs_0_.own_ref, s32[4]{0:T(128)S(1)} %copy-done.4, f32[32,48,128]{2,1,0:T(8,128)S(1)} %all-to-all-done.1.refs_2_, ...), custom_call_target="tpu_custom_call" | custom-call | flops 3221225472 | bytes 786432 | tf_op jit(solution)/shard_map/wave_band/pallas_call | solution.py:713
  74.9 0.0 copy-start
  74.9 0.0 copy-start.2
  74.9 18.6 %all_to_all.20.came_ref = f32[32,4,8,128]{3,2,1,0:T(8,128)S(1)} all-to-all(f32[32,4,8,128]{3,2,1,0:T(8,128)S(1)} %bitcast.11), channel_id=1, replica_groups={{0,1,2,3,6,7,4,5,8,9,10,11,14,15,12,13,24,25,26,27,30,31,28,29,16,17,18..., dimensions={0} | all-to-all | bytes 1048576 | tf_op jit(solution)/shard_map/all_to_all | solution.py:830
  93.5 3.9 %poisson.1 = f32[32,4,8,128]{3,2,1,0:T(8,128)} custom-call(s32[2]{0:T(128)S(1)} %pad_add_fusion.refs_0_.own_ref, f32[2,256,128]{2,1,0:T(8,128)S(1)} %get-tuple-element.10.kernel_ref, f32[32,4,8,128]{3,2,1,0:T(8,128)S(1)} %all_to_all.20.came_ref, bf16[512,768]{1,0:T(8,128)(2,1)S(1)} %copy-done.1, bf16[512,768]{1,0:T(8,128)(2,1)S(1)} %copy-done, ...), custom_call_target="tpu_custom_call" | custom-call | tf_op jit(solution)/shard_map/poisson/pallas_call | solution.py:790
  97.5 2.8 %all-to-all-start.3 = ((f32[32,4,8,128]{3,2,1,0:T(8,128)}), f32[32,4,8,128]{3,2,1,0:T(8,128)S(1)}, u32[]{:S(2)}, u32[]{:S(2)}) async-start(f32[32,4,8,128]{3,2,1,0:T(8,128)} %poisson.1), calls=%async_computation.3 | async-start | bytes 1048576 | tf_op jit(solution)/shard_map/all_to_all | solution.py:830
  100.3 1.8 %collective-permute-start = (f32[8,32,128]{2,1,0:T(8,128)S(1)}, f32[8,32,128]{2,1,0:T(8,128)S(1)}, u32[]{:S(2)}, u32[]{:S(2)}) collective-permute-start(f32[8,32,128]{2,1,0:T(8,128)S(1)} %get-tuple-element.15), channel_id=1, source_target_pairs={{0,8},{8,16},{16,24},{24,0},{1,9},{9,17},{17,25},{25,1},{2,10},{10... | collective-permute-start | bytes 393224 | tf_op jit(solution)/shard_map/ppermute | solution.py:897
  102.2 1.5 %collective-permute-start.1 = (f32[8,32,128]{2,1,0:T(8,128)S(1)}, f32[8,32,128]{2,1,0:T(8,128)S(1)}, u32[]{:S(2)}, u32[]{:S(2)}) collective-permute-start(f32[8,32,128]{2,1,0:T(8,128)S(1)} %get-tuple-element.16), channel_id=1, source_target_pairs={{0,16},{8,24},{16,0},{24,8},{1,17},{9,25},{17,1},{25,9},{2,18},{10... | collective-permute-start | bytes 393224 | tf_op jit(solution)/shard_map/ppermute | solution.py:897
  103.6 1.5 %collective-permute-start.2 = (f32[8,32,128]{2,1,0:T(8,128)S(1)}, f32[8,32,128]{2,1,0:T(8,128)S(1)}, u32[]{:S(2)}, u32[]{:S(2)}) collective-permute-start(f32[8,32,128]{2,1,0:T(8,128)S(1)} %get-tuple-element.17), channel_id=1, source_target_pairs={{0,24},{8,0},{16,8},{24,16},{1,25},{9,1},{17,9},{25,17},{2,26},{10... | collective-permute-start | bytes 393224 | tf_op jit(solution)/shard_map/ppermute | solution.py:897
  105.1 6.5 %collective-permute-done.refs_1_ = f32[8,32,128]{2,1,0:T(8,128)S(1)} collective-permute-done((f32[8,32,128]{2,1,0:T(8,128)S(1)}, f32[8,32,128]{2,1,0:T(8,128)S(1)}, u32[]{:S(2)}, u32[]{:S(2)}) %collective-permute-start) | collective-permute-done | bytes 131104 | tf_op jit(solution)/shard_map/ppermute | solution.py:897
  111.6 2.5 %collective-permute-done.1.refs_2_ = f32[8,32,128]{2,1,0:T(8,128)S(1)} collective-permute-done((f32[8,32,128]{2,1,0:T(8,128)S(1)}, f32[8,32,128]{2,1,0:T(8,128)S(1)}, u32[]{:S(2)}, u32[]{:S(2)}) %collective-permute-start.1) | collective-permute-done | bytes 131104 | tf_op jit(solution)/shard_map/ppermute | solution.py:897
  114.1 0.0 collective-permute-done.2.refs_3_
  114.1 1.4 %all-to-all-done.3 = f32[32,4,8,128]{3,2,1,0:T(8,128)S(1)} async-done(((f32[32,4,8,128]{3,2,1,0:T(8,128)}), f32[32,4,8,128]{3,2,1,0:T(8,128)S(1)}, u32[]{:S(2)}, u32[]{:S(2)}) %all-to-all-start.3) | async-done | bytes 524320 | tf_op jit(solution)/shard_map/all_to_all | solution.py:830
  115.5 1.9 %finish.1 = (f32[32,32,128]{2,1,0:T(8,128)}, f32[32,32,128]{2,1,0:T(8,128)}) custom-call(s32[2]{0:T(128)S(1)} %pad_add_fusion.refs_0_.own_ref, f32[1024,128]{1,0:T(8,128)S(1)} %bitcast.10, bf16[384,128]{1,0:T(8,128)(2,1)S(1)} %copy-done.3, f32[8,32,128]{2,1,0:T(8,128)S(1)} %get-tuple-element.14.refs_0_, f32[8,32,128]{2,1,0:T(8,128)S(1)} %collective-permute-done.refs_1_, ...), custom_call_target="tpu_custom_call" | custom-call | tf_op jit(solution)/shard_map/finish/pallas_call | solution.py:816
  (10 shorter events, 0.0 us)
Async XLA Ops:
  15.4 28.7 %all-to-all-start = ((f32[32,13,4,128]{3,2,1,0:T(4,128)}), f32[32,13,4,128]{3,2,1,0:T(4,128)S(1)}, u32[]{:S(2)}, u32[]{:S(2)}) async-start(f32[32,13,4,128]{3,2,1,0:T(4,128)} %pack_band.2), calls=%async_computation | async-start | bytes 1703936 | tf_op jit(solution)/shard_map/all_to_all | solution.py:830
  37.6 13.7 %copy-start.5 = (bf16[384,256]{1,0:T(8,128)(2,1)S(1)}, bf16[384,256]{1,0:T(8,128)(2,1)}, u32[]{:S(2)}) copy-start(bf16[384,256]{1,0:T(8,128)(2,1)} %constant.49.clone.refs_3_) | copy-start | bytes 589828
  37.6 13.6 %copy-start.6 = (bf16[256,384]{1,0:T(8,128)(2,1)S(1)}, bf16[256,384]{1,0:T(8,128)(2,1)}, u32[]{:S(2)}) copy-start(bf16[256,384]{1,0:T(8,128)(2,1)} %constant.46.clone.refs_4_) | copy-start | bytes 589828
  44.1 23.8 %all-to-all-start.1 = ((f32[32,48,128]{2,1,0:T(8,128)}), f32[32,48,128]{2,1,0:T(8,128)S(1)}, u32[]{:S(2)}, u32[]{:S(2)}) async-start(f32[32,48,128]{2,1,0:T(8,128)} %pack_band.3), calls=%async_computation.1 | async-start | bytes 1572864 | tf_op jit(solution)/shard_map/all_to_all | solution.py:830
  48.0 0.7 copy-start.9
  48.7 0.7 copy-start.8
  51.1 0.7 copy-start.4
  51.8 16.1 %copy-start.7 = (bf16[384,128]{1,0:T(8,128)(2,1)S(1)}, bf16[384,128]{1,0:T(8,128)(2,1)}, u32[]{:S(2)}) copy-start(bf16[384,128]{1,0:T(8,128)(2,1)} %constant.50.clone.refs_5_) | copy-start | bytes 294916
  67.9 25.7 %copy-start.1 = (bf16[512,768]{1,0:T(8,128)(2,1)S(1)}, bf16[512,768]{1,0:T(8,128)(2,1)}, u32[]{:S(2)}) copy-start(bf16[512,768]{1,0:T(8,128)(2,1)} %constant.47.clone.forth_ref) | copy-start | bytes 2359300
  74.9 18.7 %copy-start = (bf16[512,768]{1,0:T(8,128)(2,1)S(1)}, bf16[512,768]{1,0:T(8,128)(2,1)}, u32[]{:S(2)}) copy-start(bf16[512,768]{1,0:T(8,128)(2,1)} %constant.48.clone.back_ref) | copy-start | bytes 2359300
  74.9 18.7 %copy-start.2 = (bf16[384,256]{1,0:T(8,128)(2,1)S(1)}, bf16[384,256]{1,0:T(8,128)(2,1)}, u32[]{:S(2)}) copy-start(bf16[384,256]{1,0:T(8,128)(2,1)} %constant.52.clone.both_x_ref) | copy-start | bytes 589828
  97.5 18.1 %copy-start.3 = (bf16[384,128]{1,0:T(8,128)(2,1)S(1)}, bf16[384,128]{1,0:T(8,128)(2,1)}, u32[]{:S(2)}) copy-start(bf16[384,128]{1,0:T(8,128)(2,1)} %constant.51.clone.back_ref) | copy-start | bytes 294916
  97.5 18.1 %all-to-all-start.3 = ((f32[32,4,8,128]{3,2,1,0:T(8,128)}), f32[32,4,8,128]{3,2,1,0:T(8,128)S(1)}, u32[]{:S(2)}, u32[]{:S(2)}) async-start(f32[32,4,8,128]{3,2,1,0:T(8,128)} %poisson.1), calls=%async_computation.3 | async-start | bytes 1048576 | tf_op jit(solution)/shard_map/all_to_all | solution.py:830
  100.3 11.3 %collective-permute-start = (f32[8,32,128]{2,1,0:T(8,128)S(1)}, f32[8,32,128]{2,1,0:T(8,128)S(1)}, u32[]{:S(2)}, u32[]{:S(2)}) collective-permute-start(f32[8,32,128]{2,1,0:T(8,128)S(1)} %get-tuple-element.15), channel_id=1, source_target_pairs={{0,8},{8,16},{16,24},{24,0},{1,9},{9,17},{17,25},{25,1},{2,10},{10... | collective-permute-start | bytes 393224 | tf_op jit(solution)/shard_map/ppermute | solution.py:897
  102.2 12.0 %collective-permute-start.1 = (f32[8,32,128]{2,1,0:T(8,128)S(1)}, f32[8,32,128]{2,1,0:T(8,128)S(1)}, u32[]{:S(2)}, u32[]{:S(2)}) collective-permute-start(f32[8,32,128]{2,1,0:T(8,128)S(1)} %get-tuple-element.16), channel_id=1, source_target_pairs={{0,16},{8,24},{16,0},{24,8},{1,17},{9,25},{17,1},{25,9},{2,18},{10... | collective-permute-start | bytes 393224 | tf_op jit(solution)/shard_map/ppermute | solution.py:897
  103.6 10.5 %collective-permute-start.2 = (f32[8,32,128]{2,1,0:T(8,128)S(1)}, f32[8,32,128]{2,1,0:T(8,128)S(1)}, u32[]{:S(2)}, u32[]{:S(2)}) collective-permute-start(f32[8,32,128]{2,1,0:T(8,128)S(1)} %get-tuple-element.17), channel_id=1, source_target_pairs={{0,24},{8,0},{16,8},{24,16},{1,25},{9,1},{17,9},{25,17},{2,26},{10... | collective-permute-start | bytes 393224 | tf_op jit(solution)/shard_map/ppermute | solution.py:897

commit v12 on v11

--- a/solution.py
+++ b/solution.py
@@ -232,7 +232,7 @@
 
 def group_order(kpts, pws):
     cores = 2 if pws % 2 == 0 else 1
-    return ring_order(kpts), [c * cores + i for c in ring_order(pws // cores) for i in range(cores)]
+    return ring_order(kpts), [c * cores + i for i in range(cores) for c in ring_order(pws // cores)]
 
 
 def tables(kpts, pws, planes):
@@ -373,7 +373,8 @@
         for bit in range(size - 1, 5, -1):
             exchange_sublanes(refs, 1 << (bit - 6), descending)
         exchange_rows(refs, [(3, 4, 5), (5, 4, 3)], [size], descending)
-        exchange_rows(refs, [(0, 1, 2), (2, 1, 0)], [size], descending)
+        if size < 9:
+            exchange_rows(refs, [(0, 1, 2), (2, 1, 0)], [size], descending)
 
 
 def pack_kernel(width, has_column, *refs):

time: 118 us -> 121 us (1.025)
  waiting for transfers between devices: 26.3 us -> 31.5 us
  starting transfers between devices: 18.8 us -> 17.4 us
    all_to_all x3, waiting for transfers between devices: 17.3 us -> 22.1 us  [exchange(): lax.all_to_all(array, ('kpt', 'pw'), split_axis=0, concat_axis=0, tiled=T...]
    all_to_all x3, starting transfers between devices: 14.1 us -> 12.8 us  [exchange(): lax.all_to_all(array, ('kpt', 'pw'), split_axis=0, concat_axis=0, tiled=T...]
where the time goes in v12:
time: 121 us
  Pallas kernels  49 us (40%)
  waiting for transfers between devices  31.5 us (26%)
  blocking collectives  18.3 us (15%)
  starting transfers between devices  17.4 us (14%)
  local copies, waits for them, and re-layouts  2.49 us (2%)
  between operations  1.96 us (2%)
    pallas_call x2, Pallas kernels, pack_band(): pl.pallas_call(functools.partial(pack_kernel, width, column is not None),...  29.4 us
    all_to_all x3, waiting for transfers between devices, exchange(): lax.all_to_all(array, ('kpt', 'pw'), split_axis=0, concat_axis=0, tiled=T...  22.1 us
    all_to_all x1, blocking collectives, exchange(): lax.all_to_all(array, ('kpt', 'pw'), split_axis=0, concat_axis=0, tiled=T...  18.3 us
    pallas_call x2, Pallas kernels, wave_band(): pl.pallas_call(functools.partial(wave_kernel, kpts, tiles, scale, is_firs...  13.7 us
    all_to_all x3, starting transfers between devices, exchange(): lax.all_to_all(array, ('kpt', 'pw'), split_axis=0, concat_axis=0, tiled=T...  12.8 us
    ppermute x3, waiting for transfers between devices, local_planes(): lax.ppermute(made_here[s], 'kpt', [(a, (a + s) % kpts) for a in range(kpt...  9.35 us
    ppermute x3, starting transfers between devices, local_planes(): lax.ppermute(made_here[s], 'kpt', [(a, (a + s) % kpts) for a in range(kpt...  4.63 us
    pallas_call x1, Pallas kernels, poisson(): pl.pallas_call(functools.partial(poisson_kernel, pws), in_specs=[pl.Block...  3.93 us
  transfers between devices with their start and end apart: 6, of which 5 were waited for; matrix products, arithmetic and copies ran while one was open for 1% of the time, Pallas kernels for 18%

profile of v12, /device:TPU:0, one launch (start us, length us, event | category | flops | bytes accessed | tf_op | source)
XLA Modules:
  0.0 120.7 jit_solution(13134201642744374126)
XLA Ops:
  0.6 14.7 %pack_band.2 = f32[32,13,4,128]{3,2,1,0:T(4,128)} custom-call(f32[2,768,128]{2,1,0:T(8,128)} %bitcast.12, s32[384,128]{1,0:T(8,128)} %bitcast.14, s32[384,128]{1,0:T(8,128)} %bitcast.16, bf16[512,768]{1,0:T(8,128)(2,1)} %constant.45.clone.refs_3_, s32[384]{0:T(512)} %refs_4_.3), custom_call_target="tpu_custom_call" | custom-call | flops 19327352832 | bytes 786432 | tf_op jit(solution)/shard_map/pack_band/pallas_call | solution.py:527
  15.4 7.3 %all-to-all-start = ((f32[32,13,4,128]{3,2,1,0:T(4,128)}), f32[32,13,4,128]{3,2,1,0:T(4,128)S(1)}, u32[]{:S(2)}, u32[]{:S(2)}) async-start(f32[32,13,4,128]{3,2,1,0:T(4,128)} %pack_band.2), calls=%async_computation | async-start | bytes 1703936 | tf_op jit(solution)/shard_map/all_to_all | solution.py:831
  22.6 14.7 %pack_band.3 = f32[32,48,128]{2,1,0:T(8,128)} custom-call(f32[2,768,128]{2,1,0:T(8,128)} %bitcast.13, s32[384,128]{1,0:T(8,128)} %bitcast.15, s32[384,128]{1,0:T(8,128)} %bitcast.17, bf16[512,768]{1,0:T(8,128)(2,1)} %constant.45.clone.refs_3_), custom_call_target="tpu_custom_call" | custom-call | flops 19327352832 | bytes 786432 | tf_op jit(solution)/shard_map/pack_band/pallas_call | solution.py:527
  37.4 0.0 copy-start.5
  37.4 0.0 copy-start.6
  37.4 8.4 %all-to-all-done.refs_2_ = f32[32,13,4,128]{3,2,1,0:T(4,128)S(1)} async-done(((f32[32,13,4,128]{3,2,1,0:T(4,128)}), f32[32,13,4,128]{3,2,1,0:T(4,128)S(1)}, u32[]{:S(2)}, u32[]{:S(2)}) %all-to-all-start) | async-done | bytes 852000 | tf_op jit(solution)/shard_map/all_to_all | solution.py:831
  45.8 2.8 %all-to-all-start.1 = ((f32[32,48,128]{2,1,0:T(8,128)}), f32[32,48,128]{2,1,0:T(8,128)S(1)}, u32[]{:S(2)}, u32[]{:S(2)}) async-start(f32[32,48,128]{2,1,0:T(8,128)} %pack_band.3), calls=%async_computation.1 | async-start | bytes 1572864 | tf_op jit(solution)/shard_map/all_to_all | solution.py:831
  48.6 0.0 copy-start.9
  48.7 0.6 copy-done.9
  49.3 0.6 dynamic_slice.9
  49.9 0.1 copy-done.8
  50.0 0.6 dynamic_slice.8
  51.8 0.0 copy-start.4
  51.8 0.1 pad_add_fusion.refs_0_.own_ref
  51.8 0.0 copy-done.6
  51.8 0.6 copy-done.4
  52.4 6.7 %wave_band.2 = (f32[8,128,128]{2,1,0:T(8,128)S(1)}, f32[2,256,128]{2,1,0:T(8,128)S(1)}, s32[1,3072]{1,0:T(1,128)S(1)}) custom-call(s32[2]{0:T(128)S(1)} %pad_add_fusion.refs_0_.own_ref, s32[4]{0:T(128)S(1)} %copy-done.4, f32[32,13,4,128]{3,2,1,0:T(4,128)S(1)} %all-to-all-done.refs_2_, bf16[384,256]{1,0:T(8,128)(2,1)S(1)} %copy-done.5, ...), custom_call_target="tpu_custom_call" | custom-call | flops 3221225472 | bytes 851968 | tf_op jit(solution)/shard_map/wave_band/pallas_call | solution.py:714
  59.1 11.2 %all-to-all-done.1.refs_2_ = f32[32,48,128]{2,1,0:T(8,128)S(1)} async-done(((f32[32,48,128]{2,1,0:T(8,128)}), f32[32,48,128]{2,1,0:T(8,128)S(1)}, u32[]{:S(2)}, u32[]{:S(2)}) %all-to-all-start.1) | async-done | bytes 786464 | tf_op jit(solution)/shard_map/all_to_all | solution.py:831
  70.3 7.0 %wave_band.3 = (f32[8,32,128]{2,1,0:T(8,128)S(1)}, f32[8,32,128]{2,1,0:T(8,128)S(1)}, f32[8,32,128]{2,1,0:T(8,128)S(1)}, f32[8,32,128]{2,1,0:T(8,128)S(1)}, f32[1024,128]{1,0:T(8,128)S(1)}) custom-call(s32[2]{0:T(128)S(1)} %pad_add_fusion.refs_0_.own_ref, s32[4]{0:T(128)S(1)} %copy-done.4, f32[32,48,128]{2,1,0:T(8,128)S(1)} %all-to-all-done.1.refs_2_, ...), custom_call_target="tpu_custom_call" | custom-call | flops 3221225472 | bytes 786432 | tf_op jit(solution)/shard_map/wave_band/pallas_call | solution.py:714
  77.3 0.0 copy-start
  77.3 0.0 copy-start.2
  77.4 18.3 %all_to_all.20.came_ref = f32[32,4,8,128]{3,2,1,0:T(8,128)S(1)} all-to-all(f32[32,4,8,128]{3,2,1,0:T(8,128)S(1)} %bitcast.11), channel_id=1, replica_groups={{0,2,6,4,1,3,7,5,8,10,14,12,9,11,15,13,24,26,30,28,25,27,31,29,16,18,22..., dimensions={0} | all-to-all | bytes 1048576 | tf_op jit(solution)/shard_map/all_to_all | solution.py:831
  95.7 3.9 %poisson.1 = f32[32,4,8,128]{3,2,1,0:T(8,128)} custom-call(s32[2]{0:T(128)S(1)} %pad_add_fusion.refs_0_.own_ref, f32[2,256,128]{2,1,0:T(8,128)S(1)} %get-tuple-element.10.kernel_ref, f32[32,4,8,128]{3,2,1,0:T(8,128)S(1)} %all_to_all.20.came_ref, bf16[512,768]{1,0:T(8,128)(2,1)S(1)} %copy-done.1, bf16[512,768]{1,0:T(8,128)(2,1)S(1)} %copy-done, ...), custom_call_target="tpu_custom_call" | custom-call | tf_op jit(solution)/shard_map/poisson/pallas_call | solution.py:791
  99.6 2.7 %all-to-all-start.3 = ((f32[32,4,8,128]{3,2,1,0:T(8,128)}), f32[32,4,8,128]{3,2,1,0:T(8,128)S(1)}, u32[]{:S(2)}, u32[]{:S(2)}) async-start(f32[32,4,8,128]{3,2,1,0:T(8,128)} %poisson.1), calls=%async_computation.3 | async-start | bytes 1048576 | tf_op jit(solution)/shard_map/all_to_all | solution.py:831
  102.4 1.7 %collective-permute-start = (f32[8,32,128]{2,1,0:T(8,128)S(1)}, f32[8,32,128]{2,1,0:T(8,128)S(1)}, u32[]{:S(2)}, u32[]{:S(2)}) collective-permute-start(f32[8,32,128]{2,1,0:T(8,128)S(1)} %get-tuple-element.15), channel_id=1, source_target_pairs={{0,8},{8,16},{16,24},{24,0},{1,9},{9,17},{17,25},{25,1},{2,10},{10... | collective-permute-start | bytes 393224 | tf_op jit(solution)/shard_map/ppermute | solution.py:898
  104.1 1.5 %collective-permute-start.1 = (f32[8,32,128]{2,1,0:T(8,128)S(1)}, f32[8,32,128]{2,1,0:T(8,128)S(1)}, u32[]{:S(2)}, u32[]{:S(2)}) collective-permute-start(f32[8,32,128]{2,1,0:T(8,128)S(1)} %get-tuple-element.16), channel_id=1, source_target_pairs={{0,16},{8,24},{16,0},{24,8},{1,17},{9,25},{17,1},{25,9},{2,18},{10... | collective-permute-start | bytes 393224 | tf_op jit(solution)/shard_map/ppermute | solution.py:898
  105.6 1.4 %collective-permute-start.2 = (f32[8,32,128]{2,1,0:T(8,128)S(1)}, f32[8,32,128]{2,1,0:T(8,128)S(1)}, u32[]{:S(2)}, u32[]{:S(2)}) collective-permute-start(f32[8,32,128]{2,1,0:T(8,128)S(1)} %get-tuple-element.17), channel_id=1, source_target_pairs={{0,24},{8,0},{16,8},{24,16},{1,25},{9,1},{17,9},{25,17},{2,26},{10... | collective-permute-start | bytes 393224 | tf_op jit(solution)/shard_map/ppermute | solution.py:898
  107.0 6.6 %collective-permute-done.refs_1_ = f32[8,32,128]{2,1,0:T(8,128)S(1)} collective-permute-done((f32[8,32,128]{2,1,0:T(8,128)S(1)}, f32[8,32,128]{2,1,0:T(8,128)S(1)}, u32[]{:S(2)}, u32[]{:S(2)}) %collective-permute-start) | collective-permute-done | bytes 131104 | tf_op jit(solution)/shard_map/ppermute | solution.py:898
  113.6 2.8 %collective-permute-done.1.refs_2_ = f32[8,32,128]{2,1,0:T(8,128)S(1)} collective-permute-done((f32[8,32,128]{2,1,0:T(8,128)S(1)}, f32[8,32,128]{2,1,0:T(8,128)S(1)}, u32[]{:S(2)}, u32[]{:S(2)}) %collective-permute-start.1) | collective-permute-done | bytes 131104 | tf_op jit(solution)/shard_map/ppermute | solution.py:898
  116.4 0.0 collective-permute-done.2.refs_3_
  116.4 2.5 %all-to-all-done.3 = f32[32,4,8,128]{3,2,1,0:T(8,128)S(1)} async-done(((f32[32,4,8,128]{3,2,1,0:T(8,128)}), f32[32,4,8,128]{3,2,1,0:T(8,128)S(1)}, u32[]{:S(2)}, u32[]{:S(2)}) %all-to-all-start.3) | async-done | bytes 524320 | tf_op jit(solution)/shard_map/all_to_all | solution.py:831
  118.9 1.9 %finish.1 = (f32[32,32,128]{2,1,0:T(8,128)}, f32[32,32,128]{2,1,0:T(8,128)}) custom-call(s32[2]{0:T(128)S(1)} %pad_add_fusion.refs_0_.own_ref, f32[1024,128]{1,0:T(8,128)S(1)} %bitcast.10, bf16[384,128]{1,0:T(8,128)(2,1)S(1)} %copy-done.3, f32[8,32,128]{2,1,0:T(8,128)S(1)} %get-tuple-element.14.refs_0_, f32[8,32,128]{2,1,0:T(8,128)S(1)} %collective-permute-done.refs_1_, ...), custom_call_target="tpu_custom_call" | custom-call | tf_op jit(solution)/shard_map/finish/pallas_call | solution.py:817
  (10 shorter events, 0.0 us)
Async XLA Ops:
  15.4 30.5 %all-to-all-start = ((f32[32,13,4,128]{3,2,1,0:T(4,128)}), f32[32,13,4,128]{3,2,1,0:T(4,128)S(1)}, u32[]{:S(2)}, u32[]{:S(2)}) async-start(f32[32,13,4,128]{3,2,1,0:T(4,128)} %pack_band.2), calls=%async_computation | async-start | bytes 1703936 | tf_op jit(solution)/shard_map/all_to_all | solution.py:831
  37.4 14.5 %copy-start.5 = (bf16[384,256]{1,0:T(8,128)(2,1)S(1)}, bf16[384,256]{1,0:T(8,128)(2,1)}, u32[]{:S(2)}) copy-start(bf16[384,256]{1,0:T(8,128)(2,1)} %constant.49.clone.refs_3_) | copy-start | bytes 589828
  37.4 14.5 %copy-start.6 = (bf16[256,384]{1,0:T(8,128)(2,1)S(1)}, bf16[256,384]{1,0:T(8,128)(2,1)}, u32[]{:S(2)}) copy-start(bf16[256,384]{1,0:T(8,128)(2,1)} %constant.46.clone.refs_4_) | copy-start | bytes 589828
  45.8 24.5 %all-to-all-start.1 = ((f32[32,48,128]{2,1,0:T(8,128)}), f32[32,48,128]{2,1,0:T(8,128)S(1)}, u32[]{:S(2)}, u32[]{:S(2)}) async-start(f32[32,48,128]{2,1,0:T(8,128)} %pack_band.3), calls=%async_computation.1 | async-start | bytes 1572864 | tf_op jit(solution)/shard_map/all_to_all | solution.py:831
  48.6 0.7 copy-start.9
  49.3 0.7 copy-start.8
  51.8 0.7 copy-start.4
  52.4 17.9 %copy-start.7 = (bf16[384,128]{1,0:T(8,128)(2,1)S(1)}, bf16[384,128]{1,0:T(8,128)(2,1)}, u32[]{:S(2)}) copy-start(bf16[384,128]{1,0:T(8,128)(2,1)} %constant.50.clone.refs_5_) | copy-start | bytes 294916
  70.3 25.4 %copy-start.1 = (bf16[512,768]{1,0:T(8,128)(2,1)S(1)}, bf16[512,768]{1,0:T(8,128)(2,1)}, u32[]{:S(2)}) copy-start(bf16[512,768]{1,0:T(8,128)(2,1)} %constant.47.clone.forth_ref) | copy-start | bytes 2359300
  77.3 18.4 %copy-start = (bf16[512,768]{1,0:T(8,128)(2,1)S(1)}, bf16[512,768]{1,0:T(8,128)(2,1)}, u32[]{:S(2)}) copy-start(bf16[512,768]{1,0:T(8,128)(2,1)} %constant.48.clone.back_ref) | copy-start | bytes 2359300
  77.3 18.4 %copy-start.2 = (bf16[384,256]{1,0:T(8,128)(2,1)S(1)}, bf16[384,256]{1,0:T(8,128)(2,1)}, u32[]{:S(2)}) copy-start(bf16[384,256]{1,0:T(8,128)(2,1)} %constant.52.clone.both_x_ref) | copy-start | bytes 589828
  99.6 19.2 %copy-start.3 = (bf16[384,128]{1,0:T(8,128)(2,1)S(1)}, bf16[384,128]{1,0:T(8,128)(2,1)}, u32[]{:S(2)}) copy-start(bf16[384,128]{1,0:T(8,128)(2,1)} %constant.51.clone.back_ref) | copy-start | bytes 294916
  99.6 19.2 %all-to-all-start.3 = ((f32[32,4,8,128]{3,2,1,0:T(8,128)}), f32[32,4,8,128]{3,2,1,0:T(8,128)S(1)}, u32[]{:S(2)}, u32[]{:S(2)}) async-start(f32[32,4,8,128]{3,2,1,0:T(8,128)} %poisson.1), calls=%async_computation.3 | async-start | bytes 1048576 | tf_op jit(solution)/shard_map/all_to_all | solution.py:831
  102.4 11.2 %collective-permute-start = (f32[8,32,128]{2,1,0:T(8,128)S(1)}, f32[8,32,128]{2,1,0:T(8,128)S(1)}, u32[]{:S(2)}, u32[]{:S(2)}) collective-permute-start(f32[8,32,128]{2,1,0:T(8,128)S(1)} %get-tuple-element.15), channel_id=1, source_target_pairs={{0,8},{8,16},{16,24},{24,0},{1,9},{9,17},{17,25},{25,1},{2,10},{10... | collective-permute-start | bytes 393224 | tf_op jit(solution)/shard_map/ppermute | solution.py:898
  104.1 12.3 %collective-permute-start.1 = (f32[8,32,128]{2,1,0:T(8,128)S(1)}, f32[8,32,128]{2,1,0:T(8,128)S(1)}, u32[]{:S(2)}, u32[]{:S(2)}) collective-permute-start(f32[8,32,128]{2,1,0:T(8,128)S(1)} %get-tuple-element.16), channel_id=1, source_target_pairs={{0,16},{8,24},{16,0},{24,8},{1,17},{9,25},{17,1},{25,9},{2,18},{10... | collective-permute-start | bytes 393224 | tf_op jit(solution)/shard_map/ppermute | solution.py:898
  105.6 10.8 %collective-permute-start.2 = (f32[8,32,128]{2,1,0:T(8,128)S(1)}, f32[8,32,128]{2,1,0:T(8,128)S(1)}, u32[]{:S(2)}, u32[]{:S(2)}) collective-permute-start(f32[8,32,128]{2,1,0:T(8,128)S(1)} %get-tuple-element.17), channel_id=1, source_target_pairs={{0,24},{8,0},{16,8},{24,16},{1,25},{9,1},{17,9},{25,17},{2,26},{10... | collective-permute-start | bytes 393224 | tf_op jit(solution)/shard_map/ppermute | solution.py:898

commit v13 on v12

--- a/solution.py
+++ b/solution.py
@@ -232,7 +232,7 @@
 
 def group_order(kpts, pws):
     cores = 2 if pws % 2 == 0 else 1
-    return ring_order(kpts), [c * cores + i for i in range(cores) for c in ring_order(pws // cores)]
+    return ring_order(kpts), [c * cores + i for c in ring_order(pws // cores) for i in range(cores)]
 
 
 def tables(kpts, pws, planes):
@@ -312,6 +312,51 @@
         ],
         axis=1,
     )
+
+
+def turn(row):
+    return jnp.transpose(jnp.broadcast_to(row, (LANES, LANES)))
+
+
+def cell_of(column):
+    cell = ((column // NY + NX // 2) % NX - HALF // 2) * HALF
+    return cell + (column % NY + NY // 2) % NY - HALF // 2
+
+
+def rank_rows(rows, turned):
+    return [
+        sum(jnp.sum(jnp.where(t < row, 1.0, 0.0), axis=0, keepdims=True) for t in turned)
+        for row in rows
+    ]
+
+
+def sorted_rows(rows):
+    turned = [turn(row) for row in rows]
+    ranks = [turn(rank) for rank in rank_rows(rows, turned)]
+    lane = lax.broadcasted_iota(jnp.int32, (LANES, LANES), 1).astype(jnp.float32)
+    return [
+        sum(
+            jnp.sum(jnp.where(rank == lane + t * LANES, value, 0.0), axis=0, keepdims=True)
+            for rank, value in zip(ranks, turned)
+        )
+        for t in range(len(rows))
+    ]
+
+
+def usual_tiles(total, tiles):
+    signed = np.arange(NX) - NX // 2
+    radius = (signed[:, None] * NY) ** 2 + ((np.arange(NY) - NY // 2)[None, :] * NX) ** 2
+    kept = np.sort(np.argsort(radius.ravel(), kind="stable")[:total] // NY - NX // 2 + HALF // 2)
+    slots = tiles * LANES
+    ranges = []
+    for t in range(tiles):
+        ends = []
+        for edge, sign in ((t / tiles, -1), ((t + 1) / tiles, 1)):
+            edge += sign * 5 * math.sqrt(edge * (1 - edge) / slots)
+            ends.append(int(kept[min(max(int(edge * total), 0), total - 1)]) // 16)
+        ranges.append(ends)
+    held = [[t for t in range(tiles) if ranges[t][0] <= g <= ranges[t][1]] for g in range(HALF // 16)]
+    return [(ts[0], ts[-1] + 1) if ts else (0, tiles) for ts in held]
 
 
 RANK_LOW = 64
@@ -378,9 +423,8 @@
 
 
 def pack_kernel(width, has_column, *refs):
-    coeff_ref, miller_ref, slot_ref, pencil_ref = refs[:4]
-    rest = list(refs[4:])
-    column_ref = rest.pop(0) if has_column else None
+    coeff_ref, miller_ref, slot_ref, pencil_ref, column_ref = refs[:5]
+    rest = list(refs[5:])
     out_ref, total, key_ref, real_ref, imag_ref, lane_ref, real_low, imag_low, ramp_ref, step_ref, held, sem = rest
     fetch = pltpu.make_async_copy(pencil_ref, held, sem)
     fetch.start()
@@ -392,6 +436,17 @@
     ranks = key_ref.shape[0]
 
     slot = slot_ref[...]
+    columns = [
+        column_ref[t * LANES : (t + 1) * LANES].reshape(1, LANES) for t in range(slots // LANES)
+    ]
+    if not has_column:
+        cells = [cell_of(column).astype(jnp.float32) for column in columns]
+        near = slot % LANES
+        rank = jnp.zeros(slot.shape, jnp.float32)
+        for t, row in enumerate(rank_rows(cells, [turn(row) for row in cells])):
+            found = jnp.take_along_axis(jnp.broadcast_to(row, slot.shape), near, axis=1)
+            rank = jnp.where(slot // LANES == t, found, rank)
+        slot = rank.astype(jnp.int32)
     second = slot >= half
     lane = miller_ref[...] + width // 2
     key = jnp.where(second, slot - half, slot) * (2 * width) + jnp.where(second, lane + width, lane)
@@ -506,26 +561,23 @@
         for g in range(rows // 4):
             out_ref[:, t * (rows // 4) + g] = tile[:, 4 * g : 4 * g + 4]
     if has_column:
-        column = [
-            column_ref[t * LANES : (t + 1) * LANES].astype(jnp.float32).reshape(1, LANES)
-            for t in range(tiles)
-        ]
+        column = [column.astype(jnp.float32) for column in columns]
         column = jnp.concatenate(column + [jnp.zeros((4 - tiles, LANES), jnp.float32)], axis=0)
         out_ref[:, tiles * rows // 4] = jnp.broadcast_to(column[None], (count, 4, LANES))
 
 
 def pack_band(band, count, coeffs, miller, slot, pencil, slots, column):
+    has_column = band == 0
     length = miller.shape[0]
     width = pencil.shape[1] // 6
     rows = pencil.shape[0] // count * (slots // LANES)
-    operands = [coeffs, miller, slot, pencil]
+    operands = [coeffs, miller, slot, pencil, column]
     out_shape = (count, rows, LANES)
-    if column is not None:
-        operands.append(column)
+    if has_column:
         out_shape = (count, rows // 4 + 1, 4, LANES)
     one_band = pl.BlockSpec((1, 2 * length, LANES), lambda i: (band, 0, 0))
     return pl.pallas_call(
-        functools.partial(pack_kernel, width, column is not None),
+        functools.partial(pack_kernel, width, has_column),
         grid=(1,),
         in_specs=[one_band]
         + [
@@ -585,22 +637,30 @@
                 ]
             taken = jnp.concatenate(groups, axis=0)
             high, low = pieces(taken)
-            first = (j * tiles + t) * LANES
+            first = (t * pws + j) * LANES
             values[0:rows, first : first + LANES] = high
             values[rows : 2 * rows, first : first + LANES] = low
 
     tile = 4 * HALF
     ramps = ramp((LANES, tile), 1)
+    usual = usual_tiles(total, tiles)
+    astray = jnp.zeros((1, LANES), jnp.float32)
     for j in range(pws):
+        if is_first:
+            columns = [came_ref[j, tiles * part_rows // 4, t : t + 1] for t in range(tiles)]
+            cells = [cell_of(column.astype(jnp.int32)) for column in columns]
+            ordered = sorted_rows([cell.astype(jnp.float32) for cell in cells])
         for t in range(tiles):
-            first = (j * tiles + t) * LANES
+            first = (t * pws + j) * LANES
             if is_first:
-                column = came_ref[j, tiles * part_rows // 4, t : t + 1].astype(jnp.int32)
-                cell = ((column // NY + NX // 2) % NX - HALF // 2) * HALF
-                cell = cell + (column % NY + NY // 2) % NY - HALF // 2
-                cell_ref[:, first : first + LANES] = cell
+                cell = cells[t]
+                cell_ref[:, first : first + LANES] = ordered[t].astype(jnp.int32)
             else:
                 cell = cell_ref[:, first : first + LANES]
+                group = cell // (4 * tile)
+                for g, (least, end) in enumerate(usual):
+                    if not least <= t < end:
+                        astray = jnp.where(group == g, 1.0, astray)
             lane = (cell % tile).astype(jnp.float32)
             chosen_ref[first : first + LANES, :] = one_hot_lanes(lane, ramps)
             high_ref[:, first : first + LANES] = sixteen((cell // tile).astype(jnp.float32))
@@ -612,7 +672,6 @@
             kernel = coulomb(signed_freq(step_z, NZ), signed_freq(step_x, NX), freq_y)
             coulomb_ref[q] = kernel * (1.0 / (NX * NY * NZ))
     left = lax.broadcasted_iota(jnp.int32, (planes, LANES), 1) < HALF
-    together = 4
 
     def place(t, found):
         found = found[:rows] + found[rows:]
@@ -628,16 +687,34 @@
                     left, pltpu.roll(real, HALF, 1), imag
                 )
 
-    high = high_ref[...]
-    zero = jnp.zeros_like(high)
-    for start in range(0, HALF // 4, together):
-        kept = []
-        for t in range(start, start + together):
-            here = high == jnp.full_like(high, t)
-            kept += [jnp.where(here, values[r : r + 16, :], zero) for r in range(0, 2 * rows, 16)]
-        found = mul(jnp.concatenate(kept, axis=0), chosen_ref[...], NN)
-        for s in range(together):
-            place(start + s, found[2 * rows * s : 2 * rows * (s + 1)])
+    def place_all(ranges):
+        for g, (least, end) in enumerate(ranges):
+            held = slice(least * pws * LANES, end * pws * LANES)
+            high = high_ref[:, held]
+            zero = jnp.zeros_like(high)
+            kept = []
+            for t in range(4 * g, 4 * g + 4):
+                here = high == jnp.full_like(high, t)
+                kept += [
+                    jnp.where(here, values[r : r + 16, held], zero) for r in range(0, 2 * rows, 16)
+                ]
+            found = mul(jnp.concatenate(kept, axis=0), chosen_ref[held, :], NN)
+            for s in range(4):
+                place(4 * g + s, found[2 * rows * s : 2 * rows * (s + 1)])
+
+    whole_range = [(0, tiles)] * len(usual)
+    if is_first:
+        place_all(whole_range)
+    else:
+        astray = jnp.max(astray)
+
+        @pl.when(astray == 0.0)
+        def _():
+            place_all(usual)
+
+        @pl.when(astray > 0.0)
+        def _():
+            place_all(whole_range)
 
     sum_of = count_ref[0]
     for k in range(1, kpts):
@@ -865,9 +942,8 @@
     scale = 2.0 / (column_slot.shape[1] * pws)
     arrived = []
     for band in range(band_count):
-        column = column_map if band == 0 else None
         packed = pack_band(
-            band, count, coeffs, miller, slot, pencil, slots, column
+            band, count, coeffs, miller, slot, pencil, slots, column_map
         )
         arrived.append(exchange(packed))
     kpt_order, pw_order = group_order(kpts, pws)

time: 121 us -> 117 us (0.967)
  waiting for transfers between devices: 31.5 us -> 25.7 us
  starting transfers between devices: 17.4 us -> 18.8 us
    all_to_all x3, waiting for transfers between devices: 22.1 us -> 16.7 us  [exchange(): lax.all_to_all(array, ('kpt', 'pw'), split_axis=0, concat_axis=0, tiled=T...]
    all_to_all x3, starting transfers between devices: 12.8 us -> 14 us  [exchange(): lax.all_to_all(array, ('kpt', 'pw'), split_axis=0, concat_axis=0, tiled=T...]
  transfers between devices with their start and end apart: 6 -> 6, of which waited for: 5 -> 5; matrix products, arithmetic and copies ran while one was open for 1% -> 1% of each run, Pallas kernels for 18% -> 19%
where the time goes in v13:
time: 117 us; the launch traced here: 116 us
  Pallas kernels  48.4 us (41%)
  waiting for transfers between devices  25.7 us (22%)
  starting transfers between devices  18.8 us (16%)
  blocking collectives  18.6 us (16%)
  local copies, waits for them, and re-layouts  2.49 us (2%)
  between operations  1.96 us (2%)
    pallas_call x2, Pallas kernels, pack_band(): pl.pallas_call(functools.partial(pack_kernel, width, has_column), grid=(1...  29.8 us
    all_to_all x1, blocking collectives, exchange(): lax.all_to_all(array, ('kpt', 'pw'), split_axis=0, concat_axis=0, tiled=T...  18.6 us
    all_to_all x3, waiting for transfers between devices, exchange(): lax.all_to_all(array, ('kpt', 'pw'), split_axis=0, concat_axis=0, tiled=T...  16.7 us
    all_to_all x3, starting transfers between devices, exchange(): lax.all_to_all(array, ('kpt', 'pw'), split_axis=0, concat_axis=0, tiled=T...  14 us
    pallas_call x2, Pallas kernels, wave_band(): pl.pallas_call(functools.partial(wave_kernel, kpts, tiles, scale, is_firs...  12.8 us
    ppermute x3, waiting for transfers between devices, local_planes(): lax.ppermute(made_here[s], 'kpt', [(a, (a + s) % kpts) for a in range(kpt...  9.03 us
    ppermute x3, starting transfers between devices, local_planes(): lax.ppermute(made_here[s], 'kpt', [(a, (a + s) % kpts) for a in range(kpt...  4.75 us
    pallas_call x1, Pallas kernels, poisson(): pl.pallas_call(functools.partial(poisson_kernel, pws), in_specs=[pl.Block...  3.93 us
  transfers between devices with their start and end apart: 6, of which 5 were waited for; matrix products, arithmetic and copies ran while one was open for 1% of the time, Pallas kernels for 19%

profile of v13, /device:TPU:0, one launch (start us, length us, event | category | flops | bytes accessed | tf_op | source)
XLA Modules:
  0.0 116.1 jit_solution(12336105853295147492)
XLA Ops:
  0.6 14.7 %pack_band.2 = f32[32,13,4,128]{3,2,1,0:T(4,128)} custom-call(f32[2,768,128]{2,1,0:T(8,128)} %bitcast.12, s32[384,128]{1,0:T(8,128)} %bitcast.14, s32[384,128]{1,0:T(8,128)} %bitcast.16, bf16[512,768]{1,0:T(8,128)(2,1)} %constant.45.clone.refs_3_, s32[384]{0:T(512)} %refs_4_.5), custom_call_target="tpu_custom_call" | custom-call | flops 19327352832 | bytes 786432 | tf_op jit(solution)/shard_map/pack_band/pallas_call | solution.py:579
  15.3 7.3 %all-to-all-start = ((f32[32,13,4,128]{3,2,1,0:T(4,128)}), f32[32,13,4,128]{3,2,1,0:T(4,128)S(1)}, u32[]{:S(2)}, u32[]{:S(2)}) async-start(f32[32,13,4,128]{3,2,1,0:T(4,128)} %pack_band.2), calls=%async_computation | async-start | bytes 1703936 | tf_op jit(solution)/shard_map/all_to_all | solution.py:908
  22.6 15.2 %pack_band.3 = f32[32,48,128]{2,1,0:T(8,128)} custom-call(f32[2,768,128]{2,1,0:T(8,128)} %bitcast.13, s32[384,128]{1,0:T(8,128)} %bitcast.15, s32[384,128]{1,0:T(8,128)} %bitcast.17, bf16[512,768]{1,0:T(8,128)(2,1)} %constant.45.clone.refs_3_, s32[384]{0:T(512)} %refs_4_.5), custom_call_target="tpu_custom_call" | custom-call | flops 19327352832 | bytes 786432 | tf_op jit(solution)/shard_map/pack_band/pallas_call | solution.py:579
  37.8 0.0 copy-start.5
  37.8 0.0 copy-start.6
  37.8 6.2 %all-to-all-done.refs_2_ = f32[32,13,4,128]{3,2,1,0:T(4,128)S(1)} async-done(((f32[32,13,4,128]{3,2,1,0:T(4,128)}), f32[32,13,4,128]{3,2,1,0:T(4,128)S(1)}, u32[]{:S(2)}, u32[]{:S(2)}) %all-to-all-start) | async-done | bytes 852000 | tf_op jit(solution)/shard_map/all_to_all | solution.py:908
  44.0 3.9 %all-to-all-start.1 = ((f32[32,48,128]{2,1,0:T(8,128)}), f32[32,48,128]{2,1,0:T(8,128)S(1)}, u32[]{:S(2)}, u32[]{:S(2)}) async-start(f32[32,48,128]{2,1,0:T(8,128)} %pack_band.3), calls=%async_computation.1 | async-start | bytes 1572864 | tf_op jit(solution)/shard_map/all_to_all | solution.py:908
  47.9 0.0 copy-start.9
  47.9 0.6 copy-done.9
  48.6 0.6 dynamic_slice.9
  49.1 0.1 copy-done.8
  49.2 0.6 dynamic_slice.8
  51.0 0.0 copy-start.4
  51.0 0.1 pad_add_fusion.refs_0_.own_ref
  51.1 0.6 copy-done.4
  51.7 7.0 %wave_band.2 = (f32[8,128,128]{2,1,0:T(8,128)S(1)}, f32[2,256,128]{2,1,0:T(8,128)S(1)}, s32[1,3072]{1,0:T(1,128)S(1)}) custom-call(s32[2]{0:T(128)S(1)} %pad_add_fusion.refs_0_.own_ref, s32[4]{0:T(128)S(1)} %copy-done.4, f32[32,13,4,128]{3,2,1,0:T(4,128)S(1)} %all-to-all-done.refs_2_, bf16[384,256]{1,0:T(8,128)(2,1)S(1)} %copy-done.5, ...), custom_call_target="tpu_custom_call" | custom-call | flops 3221225472 | bytes 851968 | tf_op jit(solution)/shard_map/wave_band/pallas_call | solution.py:791
  58.7 9.1 %all-to-all-done.1.refs_2_ = f32[32,48,128]{2,1,0:T(8,128)S(1)} async-done(((f32[32,48,128]{2,1,0:T(8,128)}), f32[32,48,128]{2,1,0:T(8,128)S(1)}, u32[]{:S(2)}, u32[]{:S(2)}) %all-to-all-start.1) | async-done | bytes 786464 | tf_op jit(solution)/shard_map/all_to_all | solution.py:908
  67.8 0.0 copy-done.7
  67.8 5.8 %wave_band.3 = (f32[8,32,128]{2,1,0:T(8,128)S(1)}, f32[8,32,128]{2,1,0:T(8,128)S(1)}, f32[8,32,128]{2,1,0:T(8,128)S(1)}, f32[8,32,128]{2,1,0:T(8,128)S(1)}, f32[1024,128]{1,0:T(8,128)S(1)}) custom-call(s32[2]{0:T(128)S(1)} %pad_add_fusion.refs_0_.own_ref, s32[4]{0:T(128)S(1)} %copy-done.4, f32[32,48,128]{2,1,0:T(8,128)S(1)} %all-to-all-done.1.refs_2_, ...), custom_call_target="tpu_custom_call" | custom-call | flops 3221225472 | bytes 786432 | tf_op jit(solution)/shard_map/wave_band/pallas_call | solution.py:791
  73.5 0.0 copy-start
  73.6 0.0 copy-start.2
  73.6 18.6 %all_to_all.20.came_ref = f32[32,4,8,128]{3,2,1,0:T(8,128)S(1)} all-to-all(f32[32,4,8,128]{3,2,1,0:T(8,128)S(1)} %bitcast.11), channel_id=1, replica_groups={{0,1,2,3,6,7,4,5,8,9,10,11,14,15,12,13,24,25,26,27,30,31,28,29,16,17,18..., dimensions={0} | all-to-all | bytes 1048576 | tf_op jit(solution)/shard_map/all_to_all | solution.py:908
  92.2 3.9 %poisson.1 = f32[32,4,8,128]{3,2,1,0:T(8,128)} custom-call(s32[2]{0:T(128)S(1)} %pad_add_fusion.refs_0_.own_ref, f32[2,256,128]{2,1,0:T(8,128)S(1)} %get-tuple-element.10.kernel_ref, f32[32,4,8,128]{3,2,1,0:T(8,128)S(1)} %all_to_all.20.came_ref, bf16[512,768]{1,0:T(8,128)(2,1)S(1)} %copy-done.1, bf16[512,768]{1,0:T(8,128)(2,1)S(1)} %copy-done, ...), custom_call_target="tpu_custom_call" | custom-call | tf_op jit(solution)/shard_map/poisson/pallas_call | solution.py:868
  96.2 2.8 %all-to-all-start.3 = ((f32[32,4,8,128]{3,2,1,0:T(8,128)}), f32[32,4,8,128]{3,2,1,0:T(8,128)S(1)}, u32[]{:S(2)}, u32[]{:S(2)}) async-start(f32[32,4,8,128]{3,2,1,0:T(8,128)} %poisson.1), calls=%async_computation.3 | async-start | bytes 1048576 | tf_op jit(solution)/shard_map/all_to_all | solution.py:908
  99.0 1.8 %collective-permute-start = (f32[8,32,128]{2,1,0:T(8,128)S(1)}, f32[8,32,128]{2,1,0:T(8,128)S(1)}, u32[]{:S(2)}, u32[]{:S(2)}) collective-permute-start(f32[8,32,128]{2,1,0:T(8,128)S(1)} %get-tuple-element.15), channel_id=1, source_target_pairs={{0,8},{8,16},{16,24},{24,0},{1,9},{9,17},{17,25},{25,1},{2,10},{10... | collective-permute-start | bytes 393224 | tf_op jit(solution)/shard_map/ppermute | solution.py:974
  100.8 1.5 %collective-permute-start.1 = (f32[8,32,128]{2,1,0:T(8,128)S(1)}, f32[8,32,128]{2,1,0:T(8,128)S(1)}, u32[]{:S(2)}, u32[]{:S(2)}) collective-permute-start(f32[8,32,128]{2,1,0:T(8,128)S(1)} %get-tuple-element.16), channel_id=1, source_target_pairs={{0,16},{8,24},{16,0},{24,8},{1,17},{9,25},{17,1},{25,9},{2,18},{10... | collective-permute-start | bytes 393224 | tf_op jit(solution)/shard_map/ppermute | solution.py:974
  102.3 1.5 %collective-permute-start.2 = (f32[8,32,128]{2,1,0:T(8,128)S(1)}, f32[8,32,128]{2,1,0:T(8,128)S(1)}, u32[]{:S(2)}, u32[]{:S(2)}) collective-permute-start(f32[8,32,128]{2,1,0:T(8,128)S(1)} %get-tuple-element.17), channel_id=1, source_target_pairs={{0,24},{8,0},{16,8},{24,16},{1,25},{9,1},{17,9},{25,17},{2,26},{10... | collective-permute-start | bytes 393224 | tf_op jit(solution)/shard_map/ppermute | solution.py:974
  103.8 6.5 %collective-permute-done.refs_1_ = f32[8,32,128]{2,1,0:T(8,128)S(1)} collective-permute-done((f32[8,32,128]{2,1,0:T(8,128)S(1)}, f32[8,32,128]{2,1,0:T(8,128)S(1)}, u32[]{:S(2)}, u32[]{:S(2)}) %collective-permute-start) | collective-permute-done | bytes 131104 | tf_op jit(solution)/shard_map/ppermute | solution.py:974
  110.3 2.5 %collective-permute-done.1.refs_2_ = f32[8,32,128]{2,1,0:T(8,128)S(1)} collective-permute-done((f32[8,32,128]{2,1,0:T(8,128)S(1)}, f32[8,32,128]{2,1,0:T(8,128)S(1)}, u32[]{:S(2)}, u32[]{:S(2)}) %collective-permute-start.1) | collective-permute-done | bytes 131104 | tf_op jit(solution)/shard_map/ppermute | solution.py:974
  112.8 0.0 collective-permute-done.2.refs_3_
  112.8 1.4 %all-to-all-done.3 = f32[32,4,8,128]{3,2,1,0:T(8,128)S(1)} async-done(((f32[32,4,8,128]{3,2,1,0:T(8,128)}), f32[32,4,8,128]{3,2,1,0:T(8,128)S(1)}, u32[]{:S(2)}, u32[]{:S(2)}) %all-to-all-start.3) | async-done | bytes 524320 | tf_op jit(solution)/shard_map/all_to_all | solution.py:908
  114.2 1.9 %finish.1 = (f32[32,32,128]{2,1,0:T(8,128)}, f32[32,32,128]{2,1,0:T(8,128)}) custom-call(s32[2]{0:T(128)S(1)} %pad_add_fusion.refs_0_.own_ref, f32[1024,128]{1,0:T(8,128)S(1)} %bitcast.10, bf16[384,128]{1,0:T(8,128)(2,1)S(1)} %copy-done.3, f32[8,32,128]{2,1,0:T(8,128)S(1)} %get-tuple-element.14.refs_0_, f32[8,32,128]{2,1,0:T(8,128)S(1)} %collective-permute-done.refs_1_, ...), custom_call_target="tpu_custom_call" | custom-call | tf_op jit(solution)/shard_map/finish/pallas_call | solution.py:894
  (10 shorter events, 0.0 us)
Async XLA Ops:
  15.3 28.7 %all-to-all-start = ((f32[32,13,4,128]{3,2,1,0:T(4,128)}), f32[32,13,4,128]{3,2,1,0:T(4,128)S(1)}, u32[]{:S(2)}, u32[]{:S(2)}) async-start(f32[32,13,4,128]{3,2,1,0:T(4,128)} %pack_band.2), calls=%async_computation | async-start | bytes 1703936 | tf_op jit(solution)/shard_map/all_to_all | solution.py:908
  37.8 13.3 %copy-start.5 = (bf16[384,256]{1,0:T(8,128)(2,1)S(1)}, bf16[384,256]{1,0:T(8,128)(2,1)}, u32[]{:S(2)}) copy-start(bf16[384,256]{1,0:T(8,128)(2,1)} %constant.49.clone.refs_3_) | copy-start | bytes 589828
  37.8 13.3 %copy-start.6 = (bf16[256,384]{1,0:T(8,128)(2,1)S(1)}, bf16[256,384]{1,0:T(8,128)(2,1)}, u32[]{:S(2)}) copy-start(bf16[256,384]{1,0:T(8,128)(2,1)} %constant.46.clone.refs_4_) | copy-start | bytes 589828
  44.0 23.8 %all-to-all-start.1 = ((f32[32,48,128]{2,1,0:T(8,128)}), f32[32,48,128]{2,1,0:T(8,128)S(1)}, u32[]{:S(2)}, u32[]{:S(2)}) async-start(f32[32,48,128]{2,1,0:T(8,128)} %pack_band.3), calls=%async_computation.1 | async-start | bytes 1572864 | tf_op jit(solution)/shard_map/all_to_all | solution.py:908
  47.9 0.7 copy-start.9
  48.6 0.7 copy-start.8
  51.0 0.7 copy-start.4
  51.7 16.1 %copy-start.7 = (bf16[384,128]{1,0:T(8,128)(2,1)S(1)}, bf16[384,128]{1,0:T(8,128)(2,1)}, u32[]{:S(2)}) copy-start(bf16[384,128]{1,0:T(8,128)(2,1)} %constant.50.clone.refs_5_) | copy-start | bytes 294916
  67.8 24.5 %copy-start.1 = (bf16[512,768]{1,0:T(8,128)(2,1)S(1)}, bf16[512,768]{1,0:T(8,128)(2,1)}, u32[]{:S(2)}) copy-start(bf16[512,768]{1,0:T(8,128)(2,1)} %constant.47.clone.forth_ref) | copy-start | bytes 2359300
  73.5 18.7 %copy-start = (bf16[512,768]{1,0:T(8,128)(2,1)S(1)}, bf16[512,768]{1,0:T(8,128)(2,1)}, u32[]{:S(2)}) copy-start(bf16[512,768]{1,0:T(8,128)(2,1)} %constant.48.clone.back_ref) | copy-start | bytes 2359300
  73.6 18.7 %copy-start.2 = (bf16[384,256]{1,0:T(8,128)(2,1)S(1)}, bf16[384,256]{1,0:T(8,128)(2,1)}, u32[]{:S(2)}) copy-start(bf16[384,256]{1,0:T(8,128)(2,1)} %constant.52.clone.both_x_ref) | copy-start | bytes 589828
  96.2 18.1 %copy-start.3 = (bf16[384,128]{1,0:T(8,128)(2,1)S(1)}, bf16[384,128]{1,0:T(8,128)(2,1)}, u32[]{:S(2)}) copy-start(bf16[384,128]{1,0:T(8,128)(2,1)} %constant.51.clone.back_ref) | copy-start | bytes 294916
  96.2 18.1 %all-to-all-start.3 = ((f32[32,4,8,128]{3,2,1,0:T(8,128)}), f32[32,4,8,128]{3,2,1,0:T(8,128)S(1)}, u32[]{:S(2)}, u32[]{:S(2)}) async-start(f32[32,4,8,128]{3,2,1,0:T(8,128)} %poisson.1), calls=%async_computation.3 | async-start | bytes 1048576 | tf_op jit(solution)/shard_map/all_to_all | solution.py:908
  99.0 11.3 %collective-permute-start = (f32[8,32,128]{2,1,0:T(8,128)S(1)}, f32[8,32,128]{2,1,0:T(8,128)S(1)}, u32[]{:S(2)}, u32[]{:S(2)}) collective-permute-start(f32[8,32,128]{2,1,0:T(8,128)S(1)} %get-tuple-element.15), channel_id=1, source_target_pairs={{0,8},{8,16},{16,24},{24,0},{1,9},{9,17},{17,25},{25,1},{2,10},{10... | collective-permute-start | bytes 393224 | tf_op jit(solution)/shard_map/ppermute | solution.py:974
  100.8 12.0 %collective-permute-start.1 = (f32[8,32,128]{2,1,0:T(8,128)S(1)}, f32[8,32,128]{2,1,0:T(8,128)S(1)}, u32[]{:S(2)}, u32[]{:S(2)}) collective-permute-start(f32[8,32,128]{2,1,0:T(8,128)S(1)} %get-tuple-element.16), channel_id=1, source_target_pairs={{0,16},{8,24},{16,0},{24,8},{1,17},{9,25},{17,1},{25,9},{2,18},{10... | collective-permute-start | bytes 393224 | tf_op jit(solution)/shard_map/ppermute | solution.py:974
  102.3 10.5 %collective-permute-start.2 = (f32[8,32,128]{2,1,0:T(8,128)S(1)}, f32[8,32,128]{2,1,0:T(8,128)S(1)}, u32[]{:S(2)}, u32[]{:S(2)}) collective-permute-start(f32[8,32,128]{2,1,0:T(8,128)S(1)} %get-tuple-element.17), channel_id=1, source_target_pairs={{0,24},{8,0},{16,8},{24,16},{1,25},{9,1},{17,9},{25,17},{2,26},{10... | collective-permute-start | bytes 393224 | tf_op jit(solution)/shard_map/ppermute | solution.py:974

commit v14 on v13

--- a/solution.py
+++ b/solution.py
@@ -232,6 +232,8 @@
 
 def group_order(kpts, pws):
     cores = 2 if pws % 2 == 0 else 1
+    if pws == 8:
+        return ring_order(kpts), [0, 1, 4, 2, 5, 3, 6, 7]
     return ring_order(kpts), [c * cores + i for c in ring_order(pws // cores) for i in range(cores)]
 
 
@@ -361,6 +363,7 @@
 
 RANK_LOW = 64
 WINDOW = 64
+END_WINDOW = 48
 
 
 def exchange_rows(refs, low_bits, size_bits, descending):
@@ -459,9 +462,12 @@
     imag_ref[length:] = blank
     sort_columns((key_ref, real_ref, imag_ref))
 
-    def base_of(block):
-        base = 8 * (block // 2) + 8 * (block % 2) - WINDOW // 2
-        return jnp.minimum(jnp.maximum(base, 0), half - WINDOW)
+    blocks = length // 8
+    ends = blocks // 6
+
+    def base_of(block, window):
+        base = 8 * (block // 2) + 8 * (block % 2) - window // 2
+        return jnp.minimum(jnp.maximum(base, 0), half - window)
 
     ramp_ref[...] = ramp(ramp_ref.shape, 1)
     step_ref[...] = ramp(step_ref.shape, 0)
@@ -478,8 +484,11 @@
             rounded = value.astype(jnp.bfloat16).astype(jnp.float32)
             ref[at, :] = rounded
             low_ref[at, :] = value - rounded
-        offset = high - base_of(sublane * (RANK_LOW // 8) + v // 8).astype(jnp.float32)
-        outside = jnp.logical_or(offset < 0.0, offset >= 1.0 * WINDOW)
+        block = sublane * (RANK_LOW // 8) + v // 8
+        at_end = jnp.logical_or(block < ends, block >= blocks - ends)
+        base = jnp.where(at_end, base_of(block, END_WINDOW), base_of(block, WINDOW))
+        offset = high - base.astype(jnp.float32)
+        outside = jnp.logical_or(offset < 0.0, offset >= jnp.where(at_end, 1.0 * END_WINDOW, 1.0 * WINDOW))
         astray = jnp.where(outside, 1.0, astray)
     astray = jnp.max(jnp.where(sublane * RANK_LOW < length, astray, 0.0))
 
@@ -514,21 +523,25 @@
             total[into, :] += found[i * window : (i + 1) * window]
 
     total[...] = jnp.zeros_like(total)
-    blocks = length // 8
-    together = 4 if blocks % 4 == 0 else 1
-
-    @pl.when(astray == 0.0)
-    def _():
+    together = 4 if ends % 4 == 0 and blocks % 4 == 0 else 1
+
+    def add_blocks(first, end, window):
         def some_blocks(i, unused):
             for s in range(together):
-                block = together * i + s
-                add(block, base_of(block), WINDOW)
+                block = first + together * i + s
+                add(block, base_of(block, window), window)
             return unused
 
-        lax.fori_loop(0, blocks // together, some_blocks, 0)
+        lax.fori_loop(0, (end - first) // together, some_blocks, 0)
+
+    add_blocks(0, ends, END_WINDOW)
+    add_blocks(ends, blocks - ends, WINDOW)
+    add_blocks(blocks - ends, blocks, END_WINDOW)
 
     @pl.when(astray > 0.0)
     def _():
+        total[...] = jnp.zeros_like(total)
+
         def one_block(block, unused):
             add(block, 0, half)
             return unused
@@ -708,9 +721,7 @@
     else:
         astray = jnp.max(astray)
 
-        @pl.when(astray == 0.0)
-        def _():
-            place_all(usual)
+        place_all(usual)
 
         @pl.when(astray > 0.0)
         def _():

time: 117 us -> 118 us (level); the launches traced: 116 us -> 116 us
  starting transfers between devices: 18.8 us -> 24.1 us
  waiting for transfers between devices: 25.7 us -> 20.4 us
  Pallas kernels: 48.4 us -> 47 us
    all_to_all x3, starting transfers between devices: 14 us -> 19.3 us  [exchange(): lax.all_to_all(array, ('kpt', 'pw'), split_axis=0, concat_axis=0, tiled=T...]
    all_to_all x3, waiting for transfers between devices: 16.7 us -> 11.4 us  [exchange(): lax.all_to_all(array, ('kpt', 'pw'), split_axis=0, concat_axis=0, tiled=T...]
  transfers between devices with their start and end apart: 6 -> 6, of which waited for: 5 -> 4; matrix products, arithmetic and copies ran while one was open for 1% -> 1% of each run, Pallas kernels for 19% -> 19%
where the time goes in v14:
time: 118 us; the launch traced here: 116 us
  Pallas kernels  47 us (40%)
  starting transfers between devices  24.1 us (20%)
  waiting for transfers between devices  20.4 us (17%)
  blocking collectives  19.5 us (17%)
  local copies, waits for them, and re-layouts  2.49 us (2%)
  between operations  1.97 us (2%)
    pallas_call x2, Pallas kernels, pack_band(): pl.pallas_call(functools.partial(pack_kernel, width, has_column), grid=(1...  28.8 us
    all_to_all x1, blocking collectives, exchange(): lax.all_to_all(array, ('kpt', 'pw'), split_axis=0, concat_axis=0, tiled=T...  19.5 us
    all_to_all x3, starting transfers between devices, exchange(): lax.all_to_all(array, ('kpt', 'pw'), split_axis=0, concat_axis=0, tiled=T...  19.3 us
    pallas_call x2, Pallas kernels, wave_band(): pl.pallas_call(functools.partial(wave_kernel, kpts, tiles, scale, is_firs...  12.4 us
    all_to_all x3, waiting for transfers between devices, exchange(): lax.all_to_all(array, ('kpt', 'pw'), split_axis=0, concat_axis=0, tiled=T...  11.4 us
    ppermute x3, waiting for transfers between devices, local_planes(): lax.ppermute(made_here[s], 'kpt', [(a, (a + s) % kpts) for a in range(kpt...  9.04 us
    ppermute x3, starting transfers between devices, local_planes(): lax.ppermute(made_here[s], 'kpt', [(a, (a + s) % kpts) for a in range(kpt...  4.75 us
    pallas_call x1, Pallas kernels, poisson(): pl.pallas_call(functools.partial(poisson_kernel, pws), in_specs=[pl.Block...  3.93 us
  transfers between devices with their start and end apart: 6, of which 4 were waited for; matrix products, arithmetic and copies ran while one was open for 1% of the time, Pallas kernels for 19%

profile of v14, /device:TPU:0, one launch (start us, length us, event | category | flops | bytes accessed | tf_op | source)
XLA Modules:
  0.0 115.6 jit_solution(6839169488014512602)
XLA Ops:
  0.6 14.2 %pack_band.2 = f32[32,13,4,128]{3,2,1,0:T(4,128)} custom-call(f32[2,768,128]{2,1,0:T(8,128)} %bitcast.12, s32[384,128]{1,0:T(8,128)} %bitcast.14, s32[384,128]{1,0:T(8,128)} %bitcast.16, bf16[512,768]{1,0:T(8,128)(2,1)} %constant.45.clone.refs_3_, s32[384]{0:T(512)} %refs_4_.5), custom_call_target="tpu_custom_call" | custom-call | flops 19327352832 | bytes 786432 | tf_op jit(solution)/shard_map/pack_band/pallas_call | solution.py:592
  14.8 7.3 %all-to-all-start = ((f32[32,13,4,128]{3,2,1,0:T(4,128)}), f32[32,13,4,128]{3,2,1,0:T(4,128)S(1)}, u32[]{:S(2)}, u32[]{:S(2)}) async-start(f32[32,13,4,128]{3,2,1,0:T(4,128)} %pack_band.2), calls=%async_computation | async-start | bytes 1703936 | tf_op jit(solution)/shard_map/all_to_all | solution.py:919
  22.1 14.6 %pack_band.3 = f32[32,48,128]{2,1,0:T(8,128)} custom-call(f32[2,768,128]{2,1,0:T(8,128)} %bitcast.13, s32[384,128]{1,0:T(8,128)} %bitcast.15, s32[384,128]{1,0:T(8,128)} %bitcast.17, bf16[512,768]{1,0:T(8,128)(2,1)} %constant.45.clone.refs_3_, s32[384]{0:T(512)} %refs_4_.5), custom_call_target="tpu_custom_call" | custom-call | flops 19327352832 | bytes 786432 | tf_op jit(solution)/shard_map/pack_band/pallas_call | solution.py:592
  36.8 0.0 copy-start.5
  36.8 0.0 copy-start.6
  36.8 4.4 %all-to-all-done.refs_2_ = f32[32,13,4,128]{3,2,1,0:T(4,128)S(1)} async-done(((f32[32,13,4,128]{3,2,1,0:T(4,128)}), f32[32,13,4,128]{3,2,1,0:T(4,128)S(1)}, u32[]{:S(2)}, u32[]{:S(2)}) %all-to-all-start) | async-done | bytes 852000 | tf_op jit(solution)/shard_map/all_to_all | solution.py:919
  41.2 6.8 %all-to-all-start.1 = ((f32[32,48,128]{2,1,0:T(8,128)}), f32[32,48,128]{2,1,0:T(8,128)S(1)}, u32[]{:S(2)}, u32[]{:S(2)}) async-start(f32[32,48,128]{2,1,0:T(8,128)} %pack_band.3), calls=%async_computation.1 | async-start | bytes 1572864 | tf_op jit(solution)/shard_map/all_to_all | solution.py:919
  48.0 0.0 copy-start.9
  48.0 0.6 copy-done.9
  48.6 0.6 dynamic_slice.9
  49.2 0.1 copy-done.8
  49.3 0.6 dynamic_slice.8
  51.1 0.0 copy-start.4
  51.1 0.1 pad_add_fusion.refs_0_.own_ref
  51.2 0.0 copy-done.5
  51.2 0.6 copy-done.4
  51.8 7.0 %wave_band.2 = (f32[8,128,128]{2,1,0:T(8,128)S(1)}, f32[2,256,128]{2,1,0:T(8,128)S(1)}, s32[1,3072]{1,0:T(1,128)S(1)}) custom-call(s32[2]{0:T(128)S(1)} %pad_add_fusion.refs_0_.own_ref, s32[4]{0:T(128)S(1)} %copy-done.4, f32[32,13,4,128]{3,2,1,0:T(4,128)S(1)} %all-to-all-done.refs_2_, bf16[384,256]{1,0:T(8,128)(2,1)S(1)} %copy-done.5, ...), custom_call_target="tpu_custom_call" | custom-call | flops 3221225472 | bytes 851968 | tf_op jit(solution)/shard_map/wave_band/pallas_call | solution.py:802
  58.8 7.0 %all-to-all-done.1.refs_2_ = f32[32,48,128]{2,1,0:T(8,128)S(1)} async-done(((f32[32,48,128]{2,1,0:T(8,128)}), f32[32,48,128]{2,1,0:T(8,128)S(1)}, u32[]{:S(2)}, u32[]{:S(2)}) %all-to-all-start.1) | async-done | bytes 786464 | tf_op jit(solution)/shard_map/all_to_all | solution.py:919
  65.7 5.4 %wave_band.3 = (f32[8,32,128]{2,1,0:T(8,128)S(1)}, f32[8,32,128]{2,1,0:T(8,128)S(1)}, f32[8,32,128]{2,1,0:T(8,128)S(1)}, f32[8,32,128]{2,1,0:T(8,128)S(1)}, f32[1024,128]{1,0:T(8,128)S(1)}) custom-call(s32[2]{0:T(128)S(1)} %pad_add_fusion.refs_0_.own_ref, s32[4]{0:T(128)S(1)} %copy-done.4, f32[32,48,128]{2,1,0:T(8,128)S(1)} %all-to-all-done.1.refs_2_, ...), custom_call_target="tpu_custom_call" | custom-call | flops 3221225472 | bytes 786432 | tf_op jit(solution)/shard_map/wave_band/pallas_call | solution.py:802
  71.1 0.0 copy-start
  71.1 0.0 copy-start.2
  71.2 19.5 %all_to_all.20.came_ref = f32[32,4,8,128]{3,2,1,0:T(8,128)S(1)} all-to-all(f32[32,4,8,128]{3,2,1,0:T(8,128)S(1)} %bitcast.11), channel_id=1, replica_groups={{0,1,4,2,5,3,6,7,8,9,12,10,13,11,14,15,24,25,28,26,29,27,30,31,16,17,20..., dimensions={0} | all-to-all | bytes 1048576 | tf_op jit(solution)/shard_map/all_to_all | solution.py:919
  90.7 3.9 %poisson.1 = f32[32,4,8,128]{3,2,1,0:T(8,128)} custom-call(s32[2]{0:T(128)S(1)} %pad_add_fusion.refs_0_.own_ref, f32[2,256,128]{2,1,0:T(8,128)S(1)} %get-tuple-element.10.kernel_ref, f32[32,4,8,128]{3,2,1,0:T(8,128)S(1)} %all_to_all.20.came_ref, bf16[512,768]{1,0:T(8,128)(2,1)S(1)} %copy-done.1, bf16[512,768]{1,0:T(8,128)(2,1)S(1)} %copy-done, ...), custom_call_target="tpu_custom_call" | custom-call | tf_op jit(solution)/shard_map/poisson/pallas_call | solution.py:879
  94.6 5.3 %all-to-all-start.3 = ((f32[32,4,8,128]{3,2,1,0:T(8,128)}), f32[32,4,8,128]{3,2,1,0:T(8,128)S(1)}, u32[]{:S(2)}, u32[]{:S(2)}) async-start(f32[32,4,8,128]{3,2,1,0:T(8,128)} %poisson.1), calls=%async_computation.3 | async-start | bytes 1048576 | tf_op jit(solution)/shard_map/all_to_all | solution.py:919
  99.9 1.8 %collective-permute-start = (f32[8,32,128]{2,1,0:T(8,128)S(1)}, f32[8,32,128]{2,1,0:T(8,128)S(1)}, u32[]{:S(2)}, u32[]{:S(2)}) collective-permute-start(f32[8,32,128]{2,1,0:T(8,128)S(1)} %get-tuple-element.15), channel_id=1, source_target_pairs={{0,8},{8,16},{16,24},{24,0},{1,9},{9,17},{17,25},{25,1},{2,10},{10... | collective-permute-start | bytes 393224 | tf_op jit(solution)/shard_map/ppermute | solution.py:985
  101.7 1.5 %collective-permute-start.1 = (f32[8,32,128]{2,1,0:T(8,128)S(1)}, f32[8,32,128]{2,1,0:T(8,128)S(1)}, u32[]{:S(2)}, u32[]{:S(2)}) collective-permute-start(f32[8,32,128]{2,1,0:T(8,128)S(1)} %get-tuple-element.16), channel_id=1, source_target_pairs={{0,16},{8,24},{16,0},{24,8},{1,17},{9,25},{17,1},{25,9},{2,18},{10... | collective-permute-start | bytes 393224 | tf_op jit(solution)/shard_map/ppermute | solution.py:985
  103.2 1.5 %collective-permute-start.2 = (f32[8,32,128]{2,1,0:T(8,128)S(1)}, f32[8,32,128]{2,1,0:T(8,128)S(1)}, u32[]{:S(2)}, u32[]{:S(2)}) collective-permute-start(f32[8,32,128]{2,1,0:T(8,128)S(1)} %get-tuple-element.17), channel_id=1, source_target_pairs={{0,24},{8,0},{16,8},{24,16},{1,25},{9,1},{17,9},{25,17},{2,26},{10... | collective-permute-start | bytes 393224 | tf_op jit(solution)/shard_map/ppermute | solution.py:985
  104.6 6.3 %collective-permute-done.refs_1_ = f32[8,32,128]{2,1,0:T(8,128)S(1)} collective-permute-done((f32[8,32,128]{2,1,0:T(8,128)S(1)}, f32[8,32,128]{2,1,0:T(8,128)S(1)}, u32[]{:S(2)}, u32[]{:S(2)}) %collective-permute-start) | collective-permute-done | bytes 131104 | tf_op jit(solution)/shard_map/ppermute | solution.py:985
  111.0 2.7 %collective-permute-done.1.refs_2_ = f32[8,32,128]{2,1,0:T(8,128)S(1)} collective-permute-done((f32[8,32,128]{2,1,0:T(8,128)S(1)}, f32[8,32,128]{2,1,0:T(8,128)S(1)}, u32[]{:S(2)}, u32[]{:S(2)}) %collective-permute-start.1) | collective-permute-done | bytes 131104 | tf_op jit(solution)/shard_map/ppermute | solution.py:985
  113.7 0.0 collective-permute-done.2.refs_3_
  113.7 0.0 all-to-all-done.3
  113.7 1.9 %finish.1 = (f32[32,32,128]{2,1,0:T(8,128)}, f32[32,32,128]{2,1,0:T(8,128)}) custom-call(s32[2]{0:T(128)S(1)} %pad_add_fusion.refs_0_.own_ref, f32[1024,128]{1,0:T(8,128)S(1)} %bitcast.10, bf16[384,128]{1,0:T(8,128)(2,1)S(1)} %copy-done.3, f32[8,32,128]{2,1,0:T(8,128)S(1)} %get-tuple-element.14.refs_0_, f32[8,32,128]{2,1,0:T(8,128)S(1)} %collective-permute-done.refs_1_, ...), custom_call_target="tpu_custom_call" | custom-call | tf_op jit(solution)/shard_map/finish/pallas_call | solution.py:905
  (10 shorter events, 0.0 us)
Async XLA Ops:
  14.8 26.4 %all-to-all-start = ((f32[32,13,4,128]{3,2,1,0:T(4,128)}), f32[32,13,4,128]{3,2,1,0:T(4,128)S(1)}, u32[]{:S(2)}, u32[]{:S(2)}) async-start(f32[32,13,4,128]{3,2,1,0:T(4,128)} %pack_band.2), calls=%async_computation | async-start | bytes 1703936 | tf_op jit(solution)/shard_map/all_to_all | solution.py:919
  36.8 14.4 %copy-start.5 = (bf16[384,256]{1,0:T(8,128)(2,1)S(1)}, bf16[384,256]{1,0:T(8,128)(2,1)}, u32[]{:S(2)}) copy-start(bf16[384,256]{1,0:T(8,128)(2,1)} %constant.49.clone.refs_3_) | copy-start | bytes 589828
  36.8 14.4 %copy-start.6 = (bf16[256,384]{1,0:T(8,128)(2,1)S(1)}, bf16[256,384]{1,0:T(8,128)(2,1)}, u32[]{:S(2)}) copy-start(bf16[256,384]{1,0:T(8,128)(2,1)} %constant.46.clone.refs_4_) | copy-start | bytes 589828
  41.2 24.5 %all-to-all-start.1 = ((f32[32,48,128]{2,1,0:T(8,128)}), f32[32,48,128]{2,1,0:T(8,128)S(1)}, u32[]{:S(2)}, u32[]{:S(2)}) async-start(f32[32,48,128]{2,1,0:T(8,128)} %pack_band.3), calls=%async_computation.1 | async-start | bytes 1572864 | tf_op jit(solution)/shard_map/all_to_all | solution.py:919
  48.0 0.7 copy-start.9
  48.6 0.7 copy-start.8
  51.1 0.7 copy-start.4
  51.7 14.0 %copy-start.7 = (bf16[384,128]{1,0:T(8,128)(2,1)S(1)}, bf16[384,128]{1,0:T(8,128)(2,1)}, u32[]{:S(2)}) copy-start(bf16[384,128]{1,0:T(8,128)(2,1)} %constant.50.clone.refs_5_) | copy-start | bytes 294916
  65.7 24.9 %copy-start.1 = (bf16[512,768]{1,0:T(8,128)(2,1)S(1)}, bf16[512,768]{1,0:T(8,128)(2,1)}, u32[]{:S(2)}) copy-start(bf16[512,768]{1,0:T(8,128)(2,1)} %constant.47.clone.forth_ref) | copy-start | bytes 2359300
  71.1 19.5 %copy-start = (bf16[512,768]{1,0:T(8,128)(2,1)S(1)}, bf16[512,768]{1,0:T(8,128)(2,1)}, u32[]{:S(2)}) copy-start(bf16[512,768]{1,0:T(8,128)(2,1)} %constant.48.clone.back_ref) | copy-start | bytes 2359300
  71.1 19.5 %copy-start.2 = (bf16[384,256]{1,0:T(8,128)(2,1)S(1)}, bf16[384,256]{1,0:T(8,128)(2,1)}, u32[]{:S(2)}) copy-start(bf16[384,256]{1,0:T(8,128)(2,1)} %constant.52.clone.both_x_ref) | copy-start | bytes 589828
  94.6 19.1 %copy-start.3 = (bf16[384,128]{1,0:T(8,128)(2,1)S(1)}, bf16[384,128]{1,0:T(8,128)(2,1)}, u32[]{:S(2)}) copy-start(bf16[384,128]{1,0:T(8,128)(2,1)} %constant.51.clone.back_ref) | copy-start | bytes 294916
  94.6 19.1 %all-to-all-start.3 = ((f32[32,4,8,128]{3,2,1,0:T(8,128)}), f32[32,4,8,128]{3,2,1,0:T(8,128)S(1)}, u32[]{:S(2)}, u32[]{:S(2)}) async-start(f32[32,4,8,128]{3,2,1,0:T(8,128)} %poisson.1), calls=%async_computation.3 | async-start | bytes 1048576 | tf_op jit(solution)/shard_map/all_to_all | solution.py:919
  99.9 11.1 %collective-permute-start = (f32[8,32,128]{2,1,0:T(8,128)S(1)}, f32[8,32,128]{2,1,0:T(8,128)S(1)}, u32[]{:S(2)}, u32[]{:S(2)}) collective-permute-start(f32[8,32,128]{2,1,0:T(8,128)S(1)} %get-tuple-element.15), channel_id=1, source_target_pairs={{0,8},{8,16},{16,24},{24,0},{1,9},{9,17},{17,25},{25,1},{2,10},{10... | collective-permute-start | bytes 393224 | tf_op jit(solution)/shard_map/ppermute | solution.py:985
  101.7 12.0 %collective-permute-start.1 = (f32[8,32,128]{2,1,0:T(8,128)S(1)}, f32[8,32,128]{2,1,0:T(8,128)S(1)}, u32[]{:S(2)}, u32[]{:S(2)}) collective-permute-start(f32[8,32,128]{2,1,0:T(8,128)S(1)} %get-tuple-element.16), channel_id=1, source_target_pairs={{0,16},{8,24},{16,0},{24,8},{1,17},{9,25},{17,1},{25,9},{2,18},{10... | collective-permute-start | bytes 393224 | tf_op jit(solution)/shard_map/ppermute | solution.py:985
  103.2 10.5 %collective-permute-start.2 = (f32[8,32,128]{2,1,0:T(8,128)S(1)}, f32[8,32,128]{2,1,0:T(8,128)S(1)}, u32[]{:S(2)}, u32[]{:S(2)}) collective-permute-start(f32[8,32,128]{2,1,0:T(8,128)S(1)} %get-tuple-element.17), channel_id=1, source_target_pairs={{0,24},{8,0},{16,8},{24,16},{1,25},{9,1},{17,9},{25,17},{2,26},{10... | collective-permute-start | bytes 393224 | tf_op jit(solution)/shard_map/ppermute | solution.py:985

commit v15 on v14

--- a/solution.py
+++ b/solution.py
@@ -232,8 +232,6 @@
 
 def group_order(kpts, pws):
     cores = 2 if pws % 2 == 0 else 1
-    if pws == 8:
-        return ring_order(kpts), [0, 1, 4, 2, 5, 3, 6, 7]
     return ring_order(kpts), [c * cores + i for c in ring_order(pws // cores) for i in range(cores)]
 
 

time: 118 us -> 116 us (0.983); the launches traced: 116 us -> 115 us
  waiting for transfers between devices: 20.4 us -> 26.2 us
  starting transfers between devices: 24.1 us -> 18.8 us
    all_to_all x3, waiting for transfers between devices: 11.4 us -> 17.2 us  [exchange(): lax.all_to_all(array, ('kpt', 'pw'), split_axis=0, concat_axis=0, tiled=T...]
    all_to_all x3, starting transfers between devices: 19.3 us -> 14.1 us  [exchange(): lax.all_to_all(array, ('kpt', 'pw'), split_axis=0, concat_axis=0, tiled=T...]
  transfers between devices with their start and end apart: 6 -> 6, of which waited for: 4 -> 5; matrix products, arithmetic and copies ran while one was open for 1% -> 1% of each run, Pallas kernels for 19% -> 19%
where the time goes in v15:
time: 116 us; the launch traced here: 115 us
  Pallas kernels  47 us (41%)
  waiting for transfers between devices  26.2 us (23%)
  starting transfers between devices  18.8 us (16%)
  blocking collectives  18.7 us (16%)
  local copies, waits for them, and re-layouts  2.49 us (2%)
  between operations  1.96 us (2%)
    pallas_call x2, Pallas kernels, pack_band(): pl.pallas_call(functools.partial(pack_kernel, width, has_column), grid=(1...  28.8 us
    all_to_all x1, blocking collectives, exchange(): lax.all_to_all(array, ('kpt', 'pw'), split_axis=0, concat_axis=0, tiled=T...  18.7 us
    all_to_all x3, waiting for transfers between devices, exchange(): lax.all_to_all(array, ('kpt', 'pw'), split_axis=0, concat_axis=0, tiled=T...  17.2 us
    all_to_all x3, starting transfers between devices, exchange(): lax.all_to_all(array, ('kpt', 'pw'), split_axis=0, concat_axis=0, tiled=T...  14.1 us
    pallas_call x2, Pallas kernels, wave_band(): pl.pallas_call(functools.partial(wave_kernel, kpts, tiles, scale, is_firs...  12.4 us
    ppermute x3, waiting for transfers between devices, local_planes(): lax.ppermute(made_here[s], 'kpt', [(a, (a + s) % kpts) for a in range(kpt...  9.03 us
    ppermute x3, starting transfers between devices, local_planes(): lax.ppermute(made_here[s], 'kpt', [(a, (a + s) % kpts) for a in range(kpt...  4.75 us
    pallas_call x1, Pallas kernels, poisson(): pl.pallas_call(functools.partial(poisson_kernel, pws), in_specs=[pl.Block...  3.93 us
  transfers between devices with their start and end apart: 6, of which 5 were waited for; matrix products, arithmetic and copies ran while one was open for 1% of the time, Pallas kernels for 19%

profile of v15, /device:TPU:0, one launch (start us, length us, event | category | flops | bytes accessed | tf_op | source)
XLA Modules:
  0.0 115.2 jit_solution(15561565279830544685)
XLA Ops:
  0.6 14.2 %pack_band.2 = f32[32,13,4,128]{3,2,1,0:T(4,128)} custom-call(f32[2,768,128]{2,1,0:T(8,128)} %bitcast.12, s32[384,128]{1,0:T(8,128)} %bitcast.14, s32[384,128]{1,0:T(8,128)} %bitcast.16, bf16[512,768]{1,0:T(8,128)(2,1)} %constant.45.clone.refs_3_, s32[384]{0:T(512)} %refs_4_.5), custom_call_target="tpu_custom_call" | custom-call | flops 19327352832 | bytes 786432 | tf_op jit(solution)/shard_map/pack_band/pallas_call | solution.py:590
  14.8 7.3 %all-to-all-start = ((f32[32,13,4,128]{3,2,1,0:T(4,128)}), f32[32,13,4,128]{3,2,1,0:T(4,128)S(1)}, u32[]{:S(2)}, u32[]{:S(2)}) async-start(f32[32,13,4,128]{3,2,1,0:T(4,128)} %pack_band.2), calls=%async_computation | async-start | bytes 1703936 | tf_op jit(solution)/shard_map/all_to_all | solution.py:917
  22.1 14.6 %pack_band.3 = f32[32,48,128]{2,1,0:T(8,128)} custom-call(f32[2,768,128]{2,1,0:T(8,128)} %bitcast.13, s32[384,128]{1,0:T(8,128)} %bitcast.15, s32[384,128]{1,0:T(8,128)} %bitcast.17, bf16[512,768]{1,0:T(8,128)(2,1)} %constant.45.clone.refs_3_, s32[384]{0:T(512)} %refs_4_.5), custom_call_target="tpu_custom_call" | custom-call | flops 19327352832 | bytes 786432 | tf_op jit(solution)/shard_map/pack_band/pallas_call | solution.py:590
  36.8 0.0 copy-start.5
  36.8 0.0 copy-start.6
  36.8 6.7 %all-to-all-done.refs_2_ = f32[32,13,4,128]{3,2,1,0:T(4,128)S(1)} async-done(((f32[32,13,4,128]{3,2,1,0:T(4,128)}), f32[32,13,4,128]{3,2,1,0:T(4,128)S(1)}, u32[]{:S(2)}, u32[]{:S(2)}) %all-to-all-start) | async-done | bytes 852000 | tf_op jit(solution)/shard_map/all_to_all | solution.py:917
  43.5 3.9 %all-to-all-start.1 = ((f32[32,48,128]{2,1,0:T(8,128)}), f32[32,48,128]{2,1,0:T(8,128)S(1)}, u32[]{:S(2)}, u32[]{:S(2)}) async-start(f32[32,48,128]{2,1,0:T(8,128)} %pack_band.3), calls=%async_computation.1 | async-start | bytes 1572864 | tf_op jit(solution)/shard_map/all_to_all | solution.py:917
  47.4 0.0 copy-start.9
  47.4 0.6 copy-done.9
  48.1 0.6 dynamic_slice.9
  48.6 0.1 copy-done.8
  48.7 0.6 dynamic_slice.8
  50.5 0.0 copy-start.4
  50.5 0.1 pad_add_fusion.refs_0_.own_ref
  50.6 0.0 copy-done.5
  50.6 0.6 copy-done.4
  51.2 7.0 %wave_band.2 = (f32[8,128,128]{2,1,0:T(8,128)S(1)}, f32[2,256,128]{2,1,0:T(8,128)S(1)}, s32[1,3072]{1,0:T(1,128)S(1)}) custom-call(s32[2]{0:T(128)S(1)} %pad_add_fusion.refs_0_.own_ref, s32[4]{0:T(128)S(1)} %copy-done.4, f32[32,13,4,128]{3,2,1,0:T(4,128)S(1)} %all-to-all-done.refs_2_, bf16[384,256]{1,0:T(8,128)(2,1)S(1)} %copy-done.5, ...), custom_call_target="tpu_custom_call" | custom-call | flops 3221225472 | bytes 851968 | tf_op jit(solution)/shard_map/wave_band/pallas_call | solution.py:800
  58.2 9.1 %all-to-all-done.1.refs_2_ = f32[32,48,128]{2,1,0:T(8,128)S(1)} async-done(((f32[32,48,128]{2,1,0:T(8,128)}), f32[32,48,128]{2,1,0:T(8,128)S(1)}, u32[]{:S(2)}, u32[]{:S(2)}) %all-to-all-start.1) | async-done | bytes 786464 | tf_op jit(solution)/shard_map/all_to_all | solution.py:917
  67.3 5.4 %wave_band.3 = (f32[8,32,128]{2,1,0:T(8,128)S(1)}, f32[8,32,128]{2,1,0:T(8,128)S(1)}, f32[8,32,128]{2,1,0:T(8,128)S(1)}, f32[8,32,128]{2,1,0:T(8,128)S(1)}, f32[1024,128]{1,0:T(8,128)S(1)}) custom-call(s32[2]{0:T(128)S(1)} %pad_add_fusion.refs_0_.own_ref, s32[4]{0:T(128)S(1)} %copy-done.4, f32[32,48,128]{2,1,0:T(8,128)S(1)} %all-to-all-done.1.refs_2_, ...), custom_call_target="tpu_custom_call" | custom-call | flops 3221225472 | bytes 786432 | tf_op jit(solution)/shard_map/wave_band/pallas_call | solution.py:800
  72.7 0.0 copy-start
  72.7 0.0 copy-start.2
  72.7 18.7 %all_to_all.20.came_ref = f32[32,4,8,128]{3,2,1,0:T(8,128)S(1)} all-to-all(f32[32,4,8,128]{3,2,1,0:T(8,128)S(1)} %bitcast.11), channel_id=1, replica_groups={{0,1,2,3,6,7,4,5,8,9,10,11,14,15,12,13,24,25,26,27,30,31,28,29,16,17,18..., dimensions={0} | all-to-all | bytes 1048576 | tf_op jit(solution)/shard_map/all_to_all | solution.py:917
  91.4 3.9 %poisson.1 = f32[32,4,8,128]{3,2,1,0:T(8,128)} custom-call(s32[2]{0:T(128)S(1)} %pad_add_fusion.refs_0_.own_ref, f32[2,256,128]{2,1,0:T(8,128)S(1)} %get-tuple-element.10.kernel_ref, f32[32,4,8,128]{3,2,1,0:T(8,128)S(1)} %all_to_all.20.came_ref, bf16[512,768]{1,0:T(8,128)(2,1)S(1)} %copy-done.1, bf16[512,768]{1,0:T(8,128)(2,1)S(1)} %copy-done, ...), custom_call_target="tpu_custom_call" | custom-call | tf_op jit(solution)/shard_map/poisson/pallas_call | solution.py:877
  95.3 2.9 %all-to-all-start.3 = ((f32[32,4,8,128]{3,2,1,0:T(8,128)}), f32[32,4,8,128]{3,2,1,0:T(8,128)S(1)}, u32[]{:S(2)}, u32[]{:S(2)}) async-start(f32[32,4,8,128]{3,2,1,0:T(8,128)} %poisson.1), calls=%async_computation.3 | async-start | bytes 1048576 | tf_op jit(solution)/shard_map/all_to_all | solution.py:917
  98.2 1.8 %collective-permute-start = (f32[8,32,128]{2,1,0:T(8,128)S(1)}, f32[8,32,128]{2,1,0:T(8,128)S(1)}, u32[]{:S(2)}, u32[]{:S(2)}) collective-permute-start(f32[8,32,128]{2,1,0:T(8,128)S(1)} %get-tuple-element.15), channel_id=1, source_target_pairs={{0,8},{8,16},{16,24},{24,0},{1,9},{9,17},{17,25},{25,1},{2,10},{10... | collective-permute-start | bytes 393224 | tf_op jit(solution)/shard_map/ppermute | solution.py:983
  100.0 1.5 %collective-permute-start.1 = (f32[8,32,128]{2,1,0:T(8,128)S(1)}, f32[8,32,128]{2,1,0:T(8,128)S(1)}, u32[]{:S(2)}, u32[]{:S(2)}) collective-permute-start(f32[8,32,128]{2,1,0:T(8,128)S(1)} %get-tuple-element.16), channel_id=1, source_target_pairs={{0,16},{8,24},{16,0},{24,8},{1,17},{9,25},{17,1},{25,9},{2,18},{10... | collective-permute-start | bytes 393224 | tf_op jit(solution)/shard_map/ppermute | solution.py:983
  101.4 1.5 %collective-permute-start.2 = (f32[8,32,128]{2,1,0:T(8,128)S(1)}, f32[8,32,128]{2,1,0:T(8,128)S(1)}, u32[]{:S(2)}, u32[]{:S(2)}) collective-permute-start(f32[8,32,128]{2,1,0:T(8,128)S(1)} %get-tuple-element.17), channel_id=1, source_target_pairs={{0,24},{8,0},{16,8},{24,16},{1,25},{9,1},{17,9},{25,17},{2,26},{10... | collective-permute-start | bytes 393224 | tf_op jit(solution)/shard_map/ppermute | solution.py:983
  102.9 6.5 %collective-permute-done.refs_1_ = f32[8,32,128]{2,1,0:T(8,128)S(1)} collective-permute-done((f32[8,32,128]{2,1,0:T(8,128)S(1)}, f32[8,32,128]{2,1,0:T(8,128)S(1)}, u32[]{:S(2)}, u32[]{:S(2)}) %collective-permute-start) | collective-permute-done | bytes 131104 | tf_op jit(solution)/shard_map/ppermute | solution.py:983
  109.4 2.5 %collective-permute-done.1.refs_2_ = f32[8,32,128]{2,1,0:T(8,128)S(1)} collective-permute-done((f32[8,32,128]{2,1,0:T(8,128)S(1)}, f32[8,32,128]{2,1,0:T(8,128)S(1)}, u32[]{:S(2)}, u32[]{:S(2)}) %collective-permute-start.1) | collective-permute-done | bytes 131104 | tf_op jit(solution)/shard_map/ppermute | solution.py:983
  111.9 0.0 collective-permute-done.2.refs_3_
  111.9 1.4 %all-to-all-done.3 = f32[32,4,8,128]{3,2,1,0:T(8,128)S(1)} async-done(((f32[32,4,8,128]{3,2,1,0:T(8,128)}), f32[32,4,8,128]{3,2,1,0:T(8,128)S(1)}, u32[]{:S(2)}, u32[]{:S(2)}) %all-to-all-start.3) | async-done | bytes 524320 | tf_op jit(solution)/shard_map/all_to_all | solution.py:917
  113.4 1.9 %finish.1 = (f32[32,32,128]{2,1,0:T(8,128)}, f32[32,32,128]{2,1,0:T(8,128)}) custom-call(s32[2]{0:T(128)S(1)} %pad_add_fusion.refs_0_.own_ref, f32[1024,128]{1,0:T(8,128)S(1)} %bitcast.10, bf16[384,128]{1,0:T(8,128)(2,1)S(1)} %copy-done.3, f32[8,32,128]{2,1,0:T(8,128)S(1)} %get-tuple-element.14.refs_0_, f32[8,32,128]{2,1,0:T(8,128)S(1)} %collective-permute-done.refs_1_, ...), custom_call_target="tpu_custom_call" | custom-call | tf_op jit(solution)/shard_map/finish/pallas_call | solution.py:903
  (10 shorter events, 0.0 us)
Async XLA Ops:
  14.8 28.7 %all-to-all-start = ((f32[32,13,4,128]{3,2,1,0:T(4,128)}), f32[32,13,4,128]{3,2,1,0:T(4,128)S(1)}, u32[]{:S(2)}, u32[]{:S(2)}) async-start(f32[32,13,4,128]{3,2,1,0:T(4,128)} %pack_band.2), calls=%async_computation | async-start | bytes 1703936 | tf_op jit(solution)/shard_map/all_to_all | solution.py:917
  36.8 13.8 %copy-start.5 = (bf16[384,256]{1,0:T(8,128)(2,1)S(1)}, bf16[384,256]{1,0:T(8,128)(2,1)}, u32[]{:S(2)}) copy-start(bf16[384,256]{1,0:T(8,128)(2,1)} %constant.49.clone.refs_3_) | copy-start | bytes 589828
  36.8 13.8 %copy-start.6 = (bf16[256,384]{1,0:T(8,128)(2,1)S(1)}, bf16[256,384]{1,0:T(8,128)(2,1)}, u32[]{:S(2)}) copy-start(bf16[256,384]{1,0:T(8,128)(2,1)} %constant.46.clone.refs_4_) | copy-start | bytes 589828
  43.5 23.8 %all-to-all-start.1 = ((f32[32,48,128]{2,1,0:T(8,128)}), f32[32,48,128]{2,1,0:T(8,128)S(1)}, u32[]{:S(2)}, u32[]{:S(2)}) async-start(f32[32,48,128]{2,1,0:T(8,128)} %pack_band.3), calls=%async_computation.1 | async-start | bytes 1572864 | tf_op jit(solution)/shard_map/all_to_all | solution.py:917
  47.4 0.7 copy-start.9
  48.1 0.7 copy-start.8
  50.5 0.7 copy-start.4
  51.2 16.1 %copy-start.7 = (bf16[384,128]{1,0:T(8,128)(2,1)S(1)}, bf16[384,128]{1,0:T(8,128)(2,1)}, u32[]{:S(2)}) copy-start(bf16[384,128]{1,0:T(8,128)(2,1)} %constant.50.clone.refs_5_) | copy-start | bytes 294916
  67.3 24.1 %copy-start.1 = (bf16[512,768]{1,0:T(8,128)(2,1)S(1)}, bf16[512,768]{1,0:T(8,128)(2,1)}, u32[]{:S(2)}) copy-start(bf16[512,768]{1,0:T(8,128)(2,1)} %constant.47.clone.forth_ref) | copy-start | bytes 2359300
  72.7 18.7 %copy-start = (bf16[512,768]{1,0:T(8,128)(2,1)S(1)}, bf16[512,768]{1,0:T(8,128)(2,1)}, u32[]{:S(2)}) copy-start(bf16[512,768]{1,0:T(8,128)(2,1)} %constant.48.clone.back_ref) | copy-start | bytes 2359300
  72.7 18.7 %copy-start.2 = (bf16[384,256]{1,0:T(8,128)(2,1)S(1)}, bf16[384,256]{1,0:T(8,128)(2,1)}, u32[]{:S(2)}) copy-start(bf16[384,256]{1,0:T(8,128)(2,1)} %constant.52.clone.both_x_ref) | copy-start | bytes 589828
  95.3 18.1 %copy-start.3 = (bf16[384,128]{1,0:T(8,128)(2,1)S(1)}, bf16[384,128]{1,0:T(8,128)(2,1)}, u32[]{:S(2)}) copy-start(bf16[384,128]{1,0:T(8,128)(2,1)} %constant.51.clone.back_ref) | copy-start | bytes 294916
  95.3 18.1 %all-to-all-start.3 = ((f32[32,4,8,128]{3,2,1,0:T(8,128)}), f32[32,4,8,128]{3,2,1,0:T(8,128)S(1)}, u32[]{:S(2)}, u32[]{:S(2)}) async-start(f32[32,4,8,128]{3,2,1,0:T(8,128)} %poisson.1), calls=%async_computation.3 | async-start | bytes 1048576 | tf_op jit(solution)/shard_map/all_to_all | solution.py:917
  98.2 11.3 %collective-permute-start = (f32[8,32,128]{2,1,0:T(8,128)S(1)}, f32[8,32,128]{2,1,0:T(8,128)S(1)}, u32[]{:S(2)}, u32[]{:S(2)}) collective-permute-start(f32[8,32,128]{2,1,0:T(8,128)S(1)} %get-tuple-element.15), channel_id=1, source_target_pairs={{0,8},{8,16},{16,24},{24,0},{1,9},{9,17},{17,25},{25,1},{2,10},{10... | collective-permute-start | bytes 393224 | tf_op jit(solution)/shard_map/ppermute | solution.py:983
  100.0 12.0 %collective-permute-start.1 = (f32[8,32,128]{2,1,0:T(8,128)S(1)}, f32[8,32,128]{2,1,0:T(8,128)S(1)}, u32[]{:S(2)}, u32[]{:S(2)}) collective-permute-start(f32[8,32,128]{2,1,0:T(8,128)S(1)} %get-tuple-element.16), channel_id=1, source_target_pairs={{0,16},{8,24},{16,0},{24,8},{1,17},{9,25},{17,1},{25,9},{2,18},{10... | collective-permute-start | bytes 393224 | tf_op jit(solution)/shard_map/ppermute | solution.py:983
  101.4 10.5 %collective-permute-start.2 = (f32[8,32,128]{2,1,0:T(8,128)S(1)}, f32[8,32,128]{2,1,0:T(8,128)S(1)}, u32[]{:S(2)}, u32[]{:S(2)}) collective-permute-start(f32[8,32,128]{2,1,0:T(8,128)S(1)} %get-tuple-element.17), channel_id=1, source_target_pairs={{0,24},{8,0},{16,8},{24,16},{1,25},{9,1},{17,9},{25,17},{2,26},{10... | collective-permute-start | bytes 393224 | tf_op jit(solution)/shard_map/ppermute | solution.py:983

commit v16 on v15

--- a/solution.py
+++ b/solution.py
@@ -426,7 +426,7 @@
 def pack_kernel(width, has_column, *refs):
     coeff_ref, miller_ref, slot_ref, pencil_ref, column_ref = refs[:5]
     rest = list(refs[5:])
-    out_ref, total, key_ref, real_ref, imag_ref, lane_ref, real_low, imag_low, ramp_ref, step_ref, held, sem = rest
+    out_ref, total, key_ref, real_ref, imag_ref, lane_ref, real_low, imag_low, ramp_ref, step_ref, pairs, held, sem = rest
     fetch = pltpu.make_async_copy(pencil_ref, held, sem)
     fetch.start()
     half = total.shape[0] // 4
@@ -452,8 +452,9 @@
     lane = miller_ref[...] + width // 2
     key = jnp.where(second, slot - half, slot) * (2 * width) + jnp.where(second, lane + width, lane)
     key_ref[0:length] = key.astype(jnp.float32)
-    real_ref[0:length] = coeff_ref[0, pl.ds(0, length, stride=2), :]
-    imag_ref[0:length] = coeff_ref[0, pl.ds(1, length, stride=2), :]
+    pairs[0 : 2 * length, :] = coeff_ref[0]
+    real_ref[0:length] = pairs[pl.ds(0, length, stride=2), :]
+    imag_ref[0:length] = pairs[pl.ds(1, length, stride=2), :]
     blank = jnp.zeros((ranks - length, LANES), jnp.float32)
     key_ref[length:] = blank + 2.0 * slots * width
     real_ref[length:] = blank
@@ -604,6 +605,7 @@
         + [
             pltpu.VMEM((LANES, 2 * width), jnp.bfloat16),
             pltpu.VMEM((slots // 2, LANES), jnp.bfloat16),
+            pltpu.VMEM((2 * length + 8, LANES), jnp.float32),
             pltpu.VMEM(pencil.shape, jnp.bfloat16),
             pltpu.SemaphoreType.DMA,
         ],
@@ -626,7 +628,7 @@
     if is_first:
         coulomb_ref, cell_ref = rest.pop(0), rest.pop(0)
     send_ref = rest.pop(0) if is_last else None
-    values, grid, whole, chosen_ref, high_ref = rest
+    values, grid, whole, chosen_ref, high_ref, sent = rest
     planes = density_refs[0].shape[0]
     block = NX // kpts
     part_rows = 2 * planes
@@ -774,7 +776,8 @@
         for p in range(planes):
             turned = jnp.transpose(half[p * NX : (p + 1) * NX])
             turned = turned + jnp.where(first_row, level * NY, 0.0)
-            send_ref[pl.ds(p, 2 * HALF, stride=planes), :] = turned
+            sent[pl.ds(p, 2 * HALF, stride=planes), :] = turned
+        send_ref[...] = sent[0 : 2 * HALF * planes, :]
 
 
 def wave_band(kpts, tiles, total, scale, own, counts, came, wave_y, wave_x, forth, former, cell):
@@ -804,10 +807,11 @@
         out_shape=out_shape,
         scratch_shapes=[
             pltpu.VMEM((2 * rows, total), jnp.bfloat16),
-            pltpu.VMEM((kpts * planes * HALF, LANES), jnp.float32),
+            pltpu.VMEM((kpts * planes * HALF + planes, LANES), jnp.float32),
             pltpu.VMEM((planes, NX, NY), jnp.float32),
             pltpu.VMEM((total, 4 * HALF), jnp.bfloat16),
             pltpu.VMEM((16, total), jnp.bfloat16),
+            pltpu.VMEM(((2 * HALF + 1) * planes, NX), jnp.float32),
         ],
         compiler_params=pltpu.CompilerParams(vmem_limit_bytes=VMEM_LIMIT),
         cost_estimate=pl.CostEstimate(
@@ -885,15 +889,16 @@
 
 
 def finish_kernel(own_ref, came_ref, back_ref, *refs):
-    block_refs, density_ref, out_ref = refs[:-2], refs[-2], refs[-1]
+    *block_refs, density_ref, out_ref, held = refs
     kpts = len(block_refs)
     planes, block, unused = out_ref.shape
     merged = planes // 8
     for s, block_ref in enumerate(block_refs):
         sender = lax.rem(own_ref[0] + kpts - s, kpts)
         density_ref[pl.ds(sender * (planes // kpts), planes // kpts)] = block_ref[...]
+    held[0 : 16 * HALF, :] = came_ref[...]
     for h in range(8):
-        lines = came_ref[pl.ds(h, 2 * HALF, stride=8), :]
+        lines = held[pl.ds(h, 2 * HALF, stride=8), :]
         field = mul3_right(lines, back_ref[...], TN)
         out_ref[h * merged : (h + 1) * merged] = field.reshape(merged, block, NY)
 
@@ -905,6 +910,7 @@
         in_specs=[pl.BlockSpec(memory_space=pltpu.SMEM)] + [vmem] * (2 + len(blocks)),
         out_specs=[vmem] * 2,
         out_shape=[jax.ShapeDtypeStruct((planes, block, NY), jnp.float32)] * 2,
+        scratch_shapes=[pltpu.VMEM((16 * HALF + 8, LANES), jnp.float32)],
         compiler_params=pltpu.CompilerParams(vmem_limit_bytes=VMEM_LIMIT),
         name="finish",
     )(own, came, back_y, *blocks)

time: 116 us -> 116 us (level)
  no operation moved by 1% of the time
where the time goes in v16:
time: 116 us; the launch traced here: 115 us
  Pallas kernels  47.1 us (41%)
  waiting for transfers between devices  26.2 us (23%)
  starting transfers between devices  18.8 us (16%)
  blocking collectives  18.6 us (16%)
  local copies, waits for them, and re-layouts  2.49 us (2%)
  between operations  1.96 us (2%)
    pallas_call x2, Pallas kernels, pack_band(): pl.pallas_call(functools.partial(pack_kernel, width, has_column), grid=(1...  28.8 us
    all_to_all x1, blocking collectives, exchange(): lax.all_to_all(array, ('kpt', 'pw'), split_axis=0, concat_axis=0, tiled=T...  18.6 us
    all_to_all x3, waiting for transfers between devices, exchange(): lax.all_to_all(array, ('kpt', 'pw'), split_axis=0, concat_axis=0, tiled=T...  17.2 us
    all_to_all x3, starting transfers between devices, exchange(): lax.all_to_all(array, ('kpt', 'pw'), split_axis=0, concat_axis=0, tiled=T...  14 us
    pallas_call x2, Pallas kernels, wave_band(): pl.pallas_call(functools.partial(wave_kernel, kpts, tiles, scale, is_firs...  12.4 us
    ppermute x3, waiting for transfers between devices, local_planes(): lax.ppermute(made_here[s], 'kpt', [(a, (a + s) % kpts) for a in range(kpt...  9.03 us
    ppermute x3, starting transfers between devices, local_planes(): lax.ppermute(made_here[s], 'kpt', [(a, (a + s) % kpts) for a in range(kpt...  4.75 us
    pallas_call x1, Pallas kernels, poisson(): pl.pallas_call(functools.partial(poisson_kernel, pws), in_specs=[pl.Block...  3.93 us
  transfers between devices with their start and end apart: 6, of which 5 were waited for; matrix products, arithmetic and copies ran while one was open for 1% of the time, Pallas kernels for 19%

profile of v16, /device:TPU:0, one launch (start us, length us, event | category | flops | bytes accessed | tf_op | source)
XLA Modules:
  0.0 115.3 jit_solution(7185985103614499250)
XLA Ops:
  0.6 14.2 %pack_band.2 = f32[32,13,4,128]{3,2,1,0:T(4,128)} custom-call(f32[2,768,128]{2,1,0:T(8,128)} %bitcast.12, s32[384,128]{1,0:T(8,128)} %bitcast.14, s32[384,128]{1,0:T(8,128)} %bitcast.16, bf16[512,768]{1,0:T(8,128)(2,1)} %constant.45.clone.refs_3_, s32[384]{0:T(512)} %refs_4_.5), custom_call_target="tpu_custom_call" | custom-call | flops 19327352832 | bytes 786432 | tf_op jit(solution)/shard_map/pack_band/pallas_call | solution.py:591
  14.8 7.3 %all-to-all-start = ((f32[32,13,4,128]{3,2,1,0:T(4,128)}), f32[32,13,4,128]{3,2,1,0:T(4,128)S(1)}, u32[]{:S(2)}, u32[]{:S(2)}) async-start(f32[32,13,4,128]{3,2,1,0:T(4,128)} %pack_band.2), calls=%async_computation | async-start | bytes 1703936 | tf_op jit(solution)/shard_map/all_to_all | solution.py:923
  22.1 14.6 %pack_band.3 = f32[32,48,128]{2,1,0:T(8,128)} custom-call(f32[2,768,128]{2,1,0:T(8,128)} %bitcast.13, s32[384,128]{1,0:T(8,128)} %bitcast.15, s32[384,128]{1,0:T(8,128)} %bitcast.17, bf16[512,768]{1,0:T(8,128)(2,1)} %constant.45.clone.refs_3_, s32[384]{0:T(512)} %refs_4_.5), custom_call_target="tpu_custom_call" | custom-call | flops 19327352832 | bytes 786432 | tf_op jit(solution)/shard_map/pack_band/pallas_call | solution.py:591
  36.8 0.0 copy-start.5
  36.8 0.0 copy-start.6
  36.8 6.7 %all-to-all-done.refs_2_ = f32[32,13,4,128]{3,2,1,0:T(4,128)S(1)} async-done(((f32[32,13,4,128]{3,2,1,0:T(4,128)}), f32[32,13,4,128]{3,2,1,0:T(4,128)S(1)}, u32[]{:S(2)}, u32[]{:S(2)}) %all-to-all-start) | async-done | bytes 852000 | tf_op jit(solution)/shard_map/all_to_all | solution.py:923
  43.5 3.9 %all-to-all-start.1 = ((f32[32,48,128]{2,1,0:T(8,128)}), f32[32,48,128]{2,1,0:T(8,128)S(1)}, u32[]{:S(2)}, u32[]{:S(2)}) async-start(f32[32,48,128]{2,1,0:T(8,128)} %pack_band.3), calls=%async_computation.1 | async-start | bytes 1572864 | tf_op jit(solution)/shard_map/all_to_all | solution.py:923
  47.4 0.0 copy-start.9
  47.4 0.6 copy-done.9
  48.1 0.6 dynamic_slice.9
  48.6 0.1 copy-done.8
  48.7 0.6 dynamic_slice.8
  50.5 0.0 copy-start.4
  50.5 0.1 pad_add_fusion.refs_0_.own_ref
  50.6 0.0 copy-done.6
  50.6 0.6 copy-done.4
  51.2 7.0 %wave_band.2 = (f32[8,128,128]{2,1,0:T(8,128)S(1)}, f32[2,256,128]{2,1,0:T(8,128)S(1)}, s32[1,3072]{1,0:T(1,128)S(1)}) custom-call(s32[2]{0:T(128)S(1)} %pad_add_fusion.refs_0_.own_ref, s32[4]{0:T(128)S(1)} %copy-done.4, f32[32,13,4,128]{3,2,1,0:T(4,128)S(1)} %all-to-all-done.refs_2_, bf16[384,256]{1,0:T(8,128)(2,1)S(1)} %copy-done.5, ...), custom_call_target="tpu_custom_call" | custom-call | flops 3221225472 | bytes 851968 | tf_op jit(solution)/shard_map/wave_band/pallas_call | solution.py:803
  58.2 9.1 %all-to-all-done.1.refs_2_ = f32[32,48,128]{2,1,0:T(8,128)S(1)} async-done(((f32[32,48,128]{2,1,0:T(8,128)}), f32[32,48,128]{2,1,0:T(8,128)S(1)}, u32[]{:S(2)}, u32[]{:S(2)}) %all-to-all-start.1) | async-done | bytes 786464 | tf_op jit(solution)/shard_map/all_to_all | solution.py:923
  67.2 5.4 %wave_band.3 = (f32[8,32,128]{2,1,0:T(8,128)S(1)}, f32[8,32,128]{2,1,0:T(8,128)S(1)}, f32[8,32,128]{2,1,0:T(8,128)S(1)}, f32[8,32,128]{2,1,0:T(8,128)S(1)}, f32[1024,128]{1,0:T(8,128)S(1)}) custom-call(s32[2]{0:T(128)S(1)} %pad_add_fusion.refs_0_.own_ref, s32[4]{0:T(128)S(1)} %copy-done.4, f32[32,48,128]{2,1,0:T(8,128)S(1)} %all-to-all-done.1.refs_2_, ...), custom_call_target="tpu_custom_call" | custom-call | flops 3221225472 | bytes 786432 | tf_op jit(solution)/shard_map/wave_band/pallas_call | solution.py:803
  72.7 0.0 copy-start
  72.7 0.0 copy-start.2
  72.7 18.6 %all_to_all.20.came_ref = f32[32,4,8,128]{3,2,1,0:T(8,128)S(1)} all-to-all(f32[32,4,8,128]{3,2,1,0:T(8,128)S(1)} %bitcast.11), channel_id=1, replica_groups={{0,1,2,3,6,7,4,5,8,9,10,11,14,15,12,13,24,25,26,27,30,31,28,29,16,17,18..., dimensions={0} | all-to-all | bytes 1048576 | tf_op jit(solution)/shard_map/all_to_all | solution.py:923
  91.4 3.9 %poisson.1 = f32[32,4,8,128]{3,2,1,0:T(8,128)} custom-call(s32[2]{0:T(128)S(1)} %pad_add_fusion.refs_0_.own_ref, f32[2,256,128]{2,1,0:T(8,128)S(1)} %get-tuple-element.10.kernel_ref, f32[32,4,8,128]{3,2,1,0:T(8,128)S(1)} %all_to_all.20.came_ref, bf16[512,768]{1,0:T(8,128)(2,1)S(1)} %copy-done.1, bf16[512,768]{1,0:T(8,128)(2,1)S(1)} %copy-done, ...), custom_call_target="tpu_custom_call" | custom-call | tf_op jit(solution)/shard_map/poisson/pallas_call | solution.py:881
  95.3 2.8 %all-to-all-start.3 = ((f32[32,4,8,128]{3,2,1,0:T(8,128)}), f32[32,4,8,128]{3,2,1,0:T(8,128)S(1)}, u32[]{:S(2)}, u32[]{:S(2)}) async-start(f32[32,4,8,128]{3,2,1,0:T(8,128)} %poisson.1), calls=%async_computation.3 | async-start | bytes 1048576 | tf_op jit(solution)/shard_map/all_to_all | solution.py:923
  98.2 1.8 %collective-permute-start = (f32[8,32,128]{2,1,0:T(8,128)S(1)}, f32[8,32,128]{2,1,0:T(8,128)S(1)}, u32[]{:S(2)}, u32[]{:S(2)}) collective-permute-start(f32[8,32,128]{2,1,0:T(8,128)S(1)} %get-tuple-element.15), channel_id=1, source_target_pairs={{0,8},{8,16},{16,24},{24,0},{1,9},{9,17},{17,25},{25,1},{2,10},{10... | collective-permute-start | bytes 393224 | tf_op jit(solution)/shard_map/ppermute | solution.py:989
  100.0 1.5 %collective-permute-start.1 = (f32[8,32,128]{2,1,0:T(8,128)S(1)}, f32[8,32,128]{2,1,0:T(8,128)S(1)}, u32[]{:S(2)}, u32[]{:S(2)}) collective-permute-start(f32[8,32,128]{2,1,0:T(8,128)S(1)} %get-tuple-element.16), channel_id=1, source_target_pairs={{0,16},{8,24},{16,0},{24,8},{1,17},{9,25},{17,1},{25,9},{2,18},{10... | collective-permute-start | bytes 393224 | tf_op jit(solution)/shard_map/ppermute | solution.py:989
  101.5 1.5 %collective-permute-start.2 = (f32[8,32,128]{2,1,0:T(8,128)S(1)}, f32[8,32,128]{2,1,0:T(8,128)S(1)}, u32[]{:S(2)}, u32[]{:S(2)}) collective-permute-start(f32[8,32,128]{2,1,0:T(8,128)S(1)} %get-tuple-element.17), channel_id=1, source_target_pairs={{0,24},{8,0},{16,8},{24,16},{1,25},{9,1},{17,9},{25,17},{2,26},{10... | collective-permute-start | bytes 393224 | tf_op jit(solution)/shard_map/ppermute | solution.py:989
  102.9 6.5 %collective-permute-done.refs_1_ = f32[8,32,128]{2,1,0:T(8,128)S(1)} collective-permute-done((f32[8,32,128]{2,1,0:T(8,128)S(1)}, f32[8,32,128]{2,1,0:T(8,128)S(1)}, u32[]{:S(2)}, u32[]{:S(2)}) %collective-permute-start) | collective-permute-done | bytes 131104 | tf_op jit(solution)/shard_map/ppermute | solution.py:989
  109.4 2.5 %collective-permute-done.1.refs_2_ = f32[8,32,128]{2,1,0:T(8,128)S(1)} collective-permute-done((f32[8,32,128]{2,1,0:T(8,128)S(1)}, f32[8,32,128]{2,1,0:T(8,128)S(1)}, u32[]{:S(2)}, u32[]{:S(2)}) %collective-permute-start.1) | collective-permute-done | bytes 131104 | tf_op jit(solution)/shard_map/ppermute | solution.py:989
  112.0 0.0 collective-permute-done.2.refs_3_
  112.0 1.4 %all-to-all-done.3 = f32[32,4,8,128]{3,2,1,0:T(8,128)S(1)} async-done(((f32[32,4,8,128]{3,2,1,0:T(8,128)}), f32[32,4,8,128]{3,2,1,0:T(8,128)S(1)}, u32[]{:S(2)}, u32[]{:S(2)}) %all-to-all-start.3) | async-done | bytes 524320 | tf_op jit(solution)/shard_map/all_to_all | solution.py:923
  113.4 1.9 %finish.1 = (f32[32,32,128]{2,1,0:T(8,128)}, f32[32,32,128]{2,1,0:T(8,128)}) custom-call(s32[2]{0:T(128)S(1)} %pad_add_fusion.refs_0_.own_ref, f32[1024,128]{1,0:T(8,128)S(1)} %bitcast.10, bf16[384,128]{1,0:T(8,128)(2,1)S(1)} %copy-done.3, f32[8,32,128]{2,1,0:T(8,128)S(1)} %get-tuple-element.14.refs_0_, f32[8,32,128]{2,1,0:T(8,128)S(1)} %collective-permute-done.refs_1_, ...), custom_call_target="tpu_custom_call" | custom-call | tf_op jit(solution)/shard_map/finish/pallas_call | solution.py:908
  (10 shorter events, 0.0 us)
Async XLA Ops:
  14.8 28.7 %all-to-all-start = ((f32[32,13,4,128]{3,2,1,0:T(4,128)}), f32[32,13,4,128]{3,2,1,0:T(4,128)S(1)}, u32[]{:S(2)}, u32[]{:S(2)}) async-start(f32[32,13,4,128]{3,2,1,0:T(4,128)} %pack_band.2), calls=%async_computation | async-start | bytes 1703936 | tf_op jit(solution)/shard_map/all_to_all | solution.py:923
  36.8 13.8 %copy-start.5 = (bf16[384,256]{1,0:T(8,128)(2,1)S(1)}, bf16[384,256]{1,0:T(8,128)(2,1)}, u32[]{:S(2)}) copy-start(bf16[384,256]{1,0:T(8,128)(2,1)} %constant.49.clone.refs_3_) | copy-start | bytes 589828
  36.8 13.8 %copy-start.6 = (bf16[256,384]{1,0:T(8,128)(2,1)S(1)}, bf16[256,384]{1,0:T(8,128)(2,1)}, u32[]{:S(2)}) copy-start(bf16[256,384]{1,0:T(8,128)(2,1)} %constant.46.clone.refs_4_) | copy-start | bytes 589828
  43.5 23.8 %all-to-all-start.1 = ((f32[32,48,128]{2,1,0:T(8,128)}), f32[32,48,128]{2,1,0:T(8,128)S(1)}, u32[]{:S(2)}, u32[]{:S(2)}) async-start(f32[32,48,128]{2,1,0:T(8,128)} %pack_band.3), calls=%async_computation.1 | async-start | bytes 1572864 | tf_op jit(solution)/shard_map/all_to_all | solution.py:923
  47.4 0.7 copy-start.9
  48.1 0.7 copy-start.8
  50.5 0.7 copy-start.4
  51.2 16.1 %copy-start.7 = (bf16[384,128]{1,0:T(8,128)(2,1)S(1)}, bf16[384,128]{1,0:T(8,128)(2,1)}, u32[]{:S(2)}) copy-start(bf16[384,128]{1,0:T(8,128)(2,1)} %constant.50.clone.refs_5_) | copy-start | bytes 294916
  67.2 24.1 %copy-start.1 = (bf16[512,768]{1,0:T(8,128)(2,1)S(1)}, bf16[512,768]{1,0:T(8,128)(2,1)}, u32[]{:S(2)}) copy-start(bf16[512,768]{1,0:T(8,128)(2,1)} %constant.47.clone.forth_ref) | copy-start | bytes 2359300
  72.7 18.7 %copy-start = (bf16[512,768]{1,0:T(8,128)(2,1)S(1)}, bf16[512,768]{1,0:T(8,128)(2,1)}, u32[]{:S(2)}) copy-start(bf16[512,768]{1,0:T(8,128)(2,1)} %constant.48.clone.back_ref) | copy-start | bytes 2359300
  72.7 18.7 %copy-start.2 = (bf16[384,256]{1,0:T(8,128)(2,1)S(1)}, bf16[384,256]{1,0:T(8,128)(2,1)}, u32[]{:S(2)}) copy-start(bf16[384,256]{1,0:T(8,128)(2,1)} %constant.52.clone.both_x_ref) | copy-start | bytes 589828
  95.3 18.1 %copy-start.3 = (bf16[384,128]{1,0:T(8,128)(2,1)S(1)}, bf16[384,128]{1,0:T(8,128)(2,1)}, u32[]{:S(2)}) copy-start(bf16[384,128]{1,0:T(8,128)(2,1)} %constant.51.clone.back_ref) | copy-start | bytes 294916
  95.3 18.1 %all-to-all-start.3 = ((f32[32,4,8,128]{3,2,1,0:T(8,128)}), f32[32,4,8,128]{3,2,1,0:T(8,128)S(1)}, u32[]{:S(2)}, u32[]{:S(2)}) async-start(f32[32,4,8,128]{3,2,1,0:T(8,128)} %poisson.1), calls=%async_computation.3 | async-start | bytes 1048576 | tf_op jit(solution)/shard_map/all_to_all | solution.py:923
  98.2 11.3 %collective-permute-start = (f32[8,32,128]{2,1,0:T(8,128)S(1)}, f32[8,32,128]{2,1,0:T(8,128)S(1)}, u32[]{:S(2)}, u32[]{:S(2)}) collective-permute-start(f32[8,32,128]{2,1,0:T(8,128)S(1)} %get-tuple-element.15), channel_id=1, source_target_pairs={{0,8},{8,16},{16,24},{24,0},{1,9},{9,17},{17,25},{25,1},{2,10},{10... | collective-permute-start | bytes 393224 | tf_op jit(solution)/shard_map/ppermute | solution.py:989
  100.0 12.0 %collective-permute-start.1 = (f32[8,32,128]{2,1,0:T(8,128)S(1)}, f32[8,32,128]{2,1,0:T(8,128)S(1)}, u32[]{:S(2)}, u32[]{:S(2)}) collective-permute-start(f32[8,32,128]{2,1,0:T(8,128)S(1)} %get-tuple-element.16), channel_id=1, source_target_pairs={{0,16},{8,24},{16,0},{24,8},{1,17},{9,25},{17,1},{25,9},{2,18},{10... | collective-permute-start | bytes 393224 | tf_op jit(solution)/shard_map/ppermute | solution.py:989
  101.5 10.5 %collective-permute-start.2 = (f32[8,32,128]{2,1,0:T(8,128)S(1)}, f32[8,32,128]{2,1,0:T(8,128)S(1)}, u32[]{:S(2)}, u32[]{:S(2)}) collective-permute-start(f32[8,32,128]{2,1,0:T(8,128)S(1)} %get-tuple-element.17), channel_id=1, source_target_pairs={{0,24},{8,0},{16,8},{24,16},{1,25},{9,1},{17,9},{25,17},{2,26},{10... | collective-permute-start | bytes 393224 | tf_op jit(solution)/shard_map/ppermute | solution.py:989
